TPU v7x, 32 devices: a whole 2x2x4 slice. The times are simulated.
32 devices in a mesh: seq: 8 (over y, x, core), chan: 4 (over z).
Axes of the slice: x: 2, y: 2, z: 4, core: 2. Of those that a mesh axis runs over, the one named last changes fastest.
Arguments:
- tokens: bfloat16 [8192, 4096], P('seq', 'chan'), may hold values from -6 to 6
- in_weight: bfloat16 [3, 4096, 2048], P(None, None, 'chan'), may hold values from -0.09375 to 0.09375
- conv_weight: float32 [3, 3, 2048], P(None, None, 'chan'), may hold values from -3 to 3
- spectrum: float32 [2, 2048, 16, 1024], P(None, 'chan', 'seq'), may hold values from -6 to 6
- skip: float32 [2048], P('chan'), may hold values from -4 to 4
- out_weight: bfloat16 [2048, 4096], P('chan'), may hold values from -0.125 to 0.125
Outputs:
- mixed: bfloat16 [8192, 4096], P('seq', 'chan')
All inputs are finite; a program needn't handle non-finite values.
Results may differ from a plain program's by a relative error of at most 0.03.
Values may be sent and summed in bfloat16 or wider, within the bound.
No kernel may reach another device: no remote copies, remote signals or barrier semaphores. Data moves between devices by JAX's collectives and lax.ppermute only.
A program may use at most 256 MiB of HBM per device.

v0:
```python
import math

import jax
import jax.numpy as jnp
from jax import lax
from jax.sharding import PartitionSpec as P

TAPS = 3


def from_behind(value, axis, by):
    size = lax.axis_size(axis)
    pairs = [(i, i + by) for i in range(size) if 0 <= i + by < size]
    return lax.ppermute(value, axis, pairs)


def angle_tables(rows_index, cols_index, modulus):
    phases = rows_index[:, None] * cols_index[None, :] % modulus
    angles = phases.astype(jnp.float32) * (2.0 * math.pi / modulus)
    return (jnp.cos(angles), jnp.sin(angles))


def split_pair(values):
    high_part = values.astype(jnp.bfloat16)
    low_part = (values - high_part.astype(jnp.float32)).astype(jnp.bfloat16)
    return (high_part, low_part)


def three_pass(form, left, right):
    left_high, left_low = split_pair(left)
    right_high, right_low = split_pair(right)
    total = jnp.einsum(form, left_high, right_high, preferred_element_type=jnp.float32)
    total = total + jnp.einsum(form, left_high, right_low, preferred_element_type=jnp.float32)
    return total + jnp.einsum(form, left_low, right_high, preferred_element_type=jnp.float32)


def apply_table(operand, table):
    return three_pass("crb,bk->crk", operand, table)


def spectral_core(real_in, imag_in, freq_list, resp_real, resp_imag, tok_rows, fft_len):
    position_index = jnp.arange(tok_rows, dtype=jnp.int32)
    twiddle_cos, twiddle_sin = angle_tables(freq_list, position_index, fft_len)
    dft_cos, dft_sin = angle_tables(position_index, position_index, tok_rows)
    turned_real = real_in * twiddle_cos + imag_in * twiddle_sin
    turned_imag = imag_in * twiddle_cos - real_in * twiddle_sin
    freq_real = apply_table(turned_real, dft_cos) + apply_table(turned_imag, dft_sin)
    freq_imag = apply_table(turned_imag, dft_cos) - apply_table(turned_real, dft_sin)
    prod_real = freq_real * resp_real - freq_imag * resp_imag
    prod_imag = freq_real * resp_imag + freq_imag * resp_real
    back_real = apply_table(prod_real, dft_cos) - apply_table(prod_imag, dft_sin)
    back_imag = apply_table(prod_imag, dft_cos) + apply_table(prod_real, dft_sin)
    shifted_real = back_real * twiddle_cos - back_imag * twiddle_sin
    shifted_imag = back_imag * twiddle_cos + back_real * twiddle_sin
    return (shifted_real, shifted_imag)


def shards(tokens, in_weight, conv_weight, spectrum, skip, out_weight):
    tok_rows = tokens.shape[0]
    seq_count = lax.axis_size("seq")
    seq_index = lax.axis_index("seq")
    fft_len = 2 * seq_count * tok_rows
    freq_blocks = 2 * seq_count
    norm_factor = 1.0 / fft_len
    projected = jnp.einsum(
        "td,pdc->pct",
        lax.all_gather(tokens, "chan", axis=1, tiled=True),
        in_weight,
        preferred_element_type=jnp.float32,
    ).astype(jnp.bfloat16)
    margin = TAPS - 1
    earlier = from_behind(projected[:, :, tok_rows - margin :], "seq", 1)
    extended = jnp.concatenate([earlier, projected], axis=2).astype(jnp.float32)
    filtered = conv_weight[0][:, :, None] * extended[:, :, margin : margin + tok_rows]
    for tap_index in range(1, TAPS):
        filtered = (
            filtered
            + conv_weight[tap_index][:, :, None]
            * extended[:, :, margin - tap_index : margin - tap_index + tok_rows]
        )
    query_rows = filtered[0]
    signal = (filtered[1] * filtered[2]).astype(jnp.bfloat16)
    source_index = jnp.arange(seq_count, dtype=jnp.int32)
    freq_index = jnp.arange(freq_blocks, dtype=jnp.int32)
    cross_cos, cross_sin = angle_tables(source_index, freq_index, freq_blocks)
    values = lax.all_to_all(
        signal[:, None, :], "seq", split_axis=2, concat_axis=1, tiled=True
    ).astype(jnp.float32)
    real_part = three_pass("iab,ak->ikb", values, cross_cos)
    imag_part = -three_pass("iab,ak->ikb", values, cross_sin)
    stacked = jnp.stack([real_part, imag_part], axis=1)
    spectral = lax.all_to_all(
        stacked.astype(jnp.bfloat16), "seq", split_axis=2, concat_axis=3, tiled=True
    ).astype(stacked.dtype)
    own_freq = 2 * seq_index + jnp.arange(2, dtype=jnp.int32)
    shifted_real, shifted_imag = spectral_core(
        spectral[:, 0], spectral[:, 1], own_freq, spectrum[0], spectrum[1], tok_rows, fft_len
    )
    rows_index = jnp.arange(lax.axis_size("seq") * 1, dtype=jnp.int32)
    part_cos, part_sin = angle_tables(rows_index, own_freq, freq_blocks)
    partial_terms = three_pass("ar,crb->acb", part_cos, shifted_real)
    partial_terms = partial_terms - three_pass("ar,crb->acb", part_sin, shifted_imag)
    longconv = lax.psum_scatter(
        (partial_terms * norm_factor).astype(jnp.bfloat16), "seq", scatter_dimension=0, tiled=True
    ).astype(jnp.float32)[0]
    gated = (query_rows * (longconv + skip[:, None] * signal.astype(jnp.float32))).astype(
        jnp.bfloat16
    )
    partial_terms = lax.dot_general(
        gated, out_weight, (((0,), (0,)), ((), ())), preferred_element_type=jnp.float32
    )
    result = lax.psum_scatter(
        partial_terms.astype(jnp.bfloat16), "chan", scatter_dimension=1, tiled=True
    )
    return result


def solution(mesh):
    placed = (
        P("seq", "chan"),
        P(None, None, "chan"),
        P(None, None, "chan"),
        P(None, "chan", "seq", None),
        P("chan"),
        P("chan", None),
    )
    return jax.shard_map(
        shards, mesh=mesh, in_specs=placed, out_specs=P("seq", "chan"), check_vma=False
    )
```

profile of v0, /device:TPU:0, one launch (start us, length us, event | category | flops | bytes accessed | tf_op | source)
XLA Modules:
  0.0 1127.9 jit_solution(18172929154490830758)
XLA Ops:
  6.5 0.7 all-gather.2.cloned.1.call-update
  7.3 154.0 %all-gather.2.cloned.1.call-done = bf16[1024,4096]{1,0:T(8,128)(2,1)} async-done(((bf16[1024,1024]{1,0:T(8,128)(2,1)}), bf16[1024,4096]{1,0:T(8,128)(2,1)}) %all-gather.2.cloned.1.call-update) | async-done | bytes 8388624 | tf_op jit(solution)/shard_map/all_gather | solution.py:67
  161.3 18.3 %fusion.13 = bf16[3,512,1024]{2,1,0:T(8,128)(2,1)S(1)} fusion(bf16[3,4096,512]{2,1,0:T(8,128)(2,1)} %param.7, bf16[1024,4096]{1,0:T(8,128)(2,1)} %all-gather.2.cloned.1.call-done), kind=kOutput, calls=%fused_computation.51 | convolution fusion | flops 12886474752 | bytes 24117248 | tf_op jit(solution)/shard_map/td,pdc->pct/dot_general | solution.py:65
  179.8 2.2 collective-permute-start
  182.0 1.1 collective-permute-done
  183.1 2.0 maximum_convert_fusion
  185.2 5.1 fusion.5
  190.2 2.7 copy-done
  193.3 1.8 copy.24
  195.1 0.5 broadcast.259
  195.6 7.0 reduce
  202.7 0.8 reshape.114
  203.5 24.8 %all_to_all.21 = bf16[8,2,32768]{2,1,0:T(2,128)(2,1)S(1)} all-to-all(bf16[8,2,32768]{2,1,0:T(2,128)(2,1)S(1)} %reshape.114), channel_id=1, replica_groups=mesh['seq'=8,'chan'=4] {'seq'}, dimensions={0} | all-to-all | bytes 2097152 | tf_op jit(solution)/shard_map/all_to_all | solution.py:86
  228.3 1.0 reshape.115
  229.7 0.8 copy.43
  230.4 0.8 fusion.135
  231.2 0.8 fusion.138
  232.0 0.8 fusion.132
  232.8 0.8 fusion.141
  233.6 1.0 fusion.103
  234.6 0.9 fusion.102
  235.5 0.4 pad_maximum_fusion
  235.9 3.0 copy.26
  238.9 4.6 all-to-all-start.1
  243.6 0.5 copy-done.7
  244.3 9.6 fusion.340
  253.9 38.8 %all-to-all-done.1 = bf16[512,2,16,128]{3,0,1,2:T(8,128)(2,1)} async-done(((bf16[512,2,16,128]{3,0,1,2:T(8,128)(2,1)}), bf16[512,2,16,128]{3,0,1,2:T(8,128)(2,1)}, u32[]{:S(2)}, u32[]{:S(2)}) %all-to-all-start.1) | async-done | bytes 4194336 | tf_op jit(solution)/shard_map/all_to_all | solution.py:92
  292.7 7.8 copy.88
  300.5 9.6 reshape.96
  310.2 4.3 subtract_convert_fusion.4
  314.5 17.6 %fusion.46 = f32[512,2,1024]{2,0,1:T(8,128)S(1)} fusion(bf16[512,2,1024]{2,0,1:T(8,128)(2,1)S(1)} %get-tuple-element.5), kind=kOutput, calls=%fused_computation.85 | convolution fusion | flops 2163212288 | bytes 6291456 | tf_op jit(solution)/shard_map/crb,bk->crk/dot_general | solution.py:34
  332.1 17.6 %fusion.34 = f32[512,2,1024]{2,0,1:T(8,128)S(1)} fusion(bf16[512,2,1024]{2,0,1:T(8,128)(2,1)S(1)} %get-tuple-element.5), kind=kOutput, calls=%fused_computation.73 | convolution fusion | flops 2163212288 | bytes 6291456 | tf_op jit(solution)/shard_map/crb,bk->crk/dot_general | solution.py:34
  349.6 17.8 %fusion.30 = f32[512,2,1024]{2,0,1:T(8,128)S(1)} fusion(bf16[512,2,1024]{2,0,1:T(8,128)(2,1)S(1)} %get-tuple-element.15), kind=kOutput, calls=%fused_computation.69 | convolution fusion | flops 2163212288 | bytes 6291456 | tf_op jit(solution)/shard_map/crb,bk->crk/dot_general | solution.py:34
  367.4 17.6 %fusion.50 = f32[512,2,1024]{2,0,1:T(8,128)S(1)} fusion(bf16[512,2,1024]{2,0,1:T(8,128)(2,1)S(1)} %get-tuple-element.15), kind=kOutput, calls=%fused_computation.89 | convolution fusion | flops 2163212288 | bytes 6291456 | tf_op jit(solution)/shard_map/crb,bk->crk/dot_general | solution.py:34
  385.0 17.8 %fusion.48 = f32[512,2,1024]{2,0,1:T(8,128)S(1)} fusion(bf16[512,2,1024]{2,0,1:T(8,128)(2,1)S(1)} %get-tuple-element.6), kind=kOutput, calls=%fused_computation.87 | convolution fusion | flops 2163212288 | bytes 6291456 | tf_op jit(solution)/shard_map/crb,bk->crk/dot_general | solution.py:32
  402.8 18.4 %fusion.84 = f32[512,2,1024]{2,0,1:T(8,128)} fusion(bf16[512,2,1024]{2,0,1:T(8,128)(2,1)S(1)} %get-tuple-element.6), kind=kOutput, calls=%fused_computation.104 | convolution fusion | flops 2166358016 | bytes 6291456 | tf_op jit(solution)/shard_map/crb,bk->crk/dot_general | solution.py:33
  421.2 18.6 %fusion.36 = f32[512,2,1024]{2,0,1:T(8,128)} fusion(bf16[512,2,1024]{2,0,1:T(8,128)(2,1)S(1)} %get-tuple-element.6), kind=kOutput, calls=%fused_computation.75 | convolution fusion | flops 2163212288 | bytes 6291456 | tf_op jit(solution)/shard_map/crb,bk->crk/dot_general | solution.py:32
  439.8 17.8 %fusion.82 = f32[512,2,1024]{2,0,1:T(8,128)S(1)} fusion(bf16[512,2,1024]{2,0,1:T(8,128)(2,1)S(1)} %get-tuple-element.16), kind=kOutput, calls=%fused_computation.103 | convolution fusion | flops 2166358016 | bytes 6291456 | tf_op jit(solution)/shard_map/crb,bk->crk/dot_general | solution.py:33
  457.6 18.4 %fusion.52 = f32[512,2,1024]{2,0,1:T(8,128)} fusion(bf16[512,2,1024]{2,0,1:T(8,128)(2,1)S(1)} %get-tuple-element.16), kind=kOutput, calls=%fused_computation.91 | convolution fusion | flops 2163212288 | bytes 6291456 | tf_op jit(solution)/shard_map/crb,bk->crk/dot_general | solution.py:32
  476.0 17.6 %fusion.32 = f32[512,2,1024]{2,0,1:T(8,128)S(1)} fusion(bf16[512,2,1024]{2,0,1:T(8,128)(2,1)S(1)} %get-tuple-element.16), kind=kOutput, calls=%fused_computation.71 | convolution fusion | flops 2163212288 | bytes 6291456 | tf_op jit(solution)/shard_map/crb,bk->crk/dot_general | solution.py:32
  493.6 22.5 %add_add_fusion.1 = f32[512,2,1024]{2,0,1:T(8,128)} fusion(f32[512,2,1024]{2,0,1:T(8,128)S(1)} %fusion.34, f32[512,2,1024]{2,0,1:T(8,128)} %fusion.36, f32[512,2,1024]{2,0,1:T(8,128)} %fusion.84, f32[512,2,1024]{2,0,1:T(8,128)S(1)} %fusion.50, f32[512,2,1024]{2,0,1:T(8,128)} %fusion.52, bf16[512,2,1024]{2,0,1:T(8,128)(2,1)S(1)} %get-tuple-element.16), kind=kOutput, calls=%fused_computation.38 | convolution fusion | flops 2171600896 | bytes 27262976 | tf_op jit(solution)/shard_map/crb,bk->crk/dot_general | solution.py:33
  516.1 23.4 %multiply_subtract_fusion.1 = (f32[512,2,1024]{2,0,1:T(8,128)S(1)}, f32[512,2,1024]{2,0,1:T(8,128)S(1)}) fusion(f32[512,2,1024]{2,0,1:T(8,128)} %add_add_fusion.1, f32[1,512,2,1024]{3,2,1,0:T(2,128)S(1)} %copy-done.2, f32[1,512,2,1024]{3,2,1,0:T(2,128)S(1)} %copy-done.1, f32[512,2,1024]{2,0,1:T(8,128)S(1)} %fusion.30, f32[512,2,1024]{2,0,1:T(8,128)S(1)} %fusion.32, ...), kind=kOutput, calls=%fused_computation.36 | convolution fusion | flops 2177892352 | bytes 44040192 | tf_op jit(solution)/shard_map/crb,bk->crk/dot_general | solution.py:33
  539.5 16.8 %fusion.24 = f32[512,2,1024]{2,0,1:T(8,128)S(1)} fusion(f32[512,2,1024]{2,0,1:T(8,128)S(1)} %get-tuple-element.9), kind=kOutput, calls=%fused_computation.63 | convolution fusion | flops 2164260864 | bytes 8388608 | tf_op jit(solution)/shard_map/crb,bk->crk/dot_general | solution.py:32
  556.3 18.4 %fusion.78 = f32[512,2,1024]{2,0,1:T(8,128)} fusion(f32[512,2,1024]{2,0,1:T(8,128)S(1)} %get-tuple-element.9), kind=kOutput, calls=%fused_computation.101 | convolution fusion | flops 2167406592 | bytes 8388608 | tf_op jit(solution)/shard_map/crb,bk->crk/dot_general | solution.py:33
  574.7 18.9 %fusion.22 = f32[512,2,1024]{2,0,1:T(8,128)} fusion(f32[512,2,1024]{2,0,1:T(8,128)S(1)} %get-tuple-element.9), kind=kOutput, calls=%fused_computation.61 | convolution fusion | flops 2167406592 | bytes 8388608 | tf_op jit(solution)/shard_map/crb,bk->crk/dot_general | solution.py:34
  593.6 16.6 %fusion.42 = f32[512,2,1024]{2,0,1:T(8,128)S(1)} fusion(f32[512,2,1024]{2,0,1:T(8,128)S(1)} %get-tuple-element.9), kind=kOutput, calls=%fused_computation.81 | convolution fusion | flops 2167406592 | bytes 8388608 | tf_op jit(solution)/shard_map/crb,bk->crk/dot_general | solution.py:34
  610.2 16.6 %fusion.44 = f32[512,2,1024]{2,0,1:T(8,128)S(1)} fusion(f32[512,2,1024]{2,0,1:T(8,128)S(1)} %get-tuple-element.9), kind=kOutput, calls=%fused_computation.83 | convolution fusion | flops 2164260864 | bytes 8388608 | tf_op jit(solution)/shard_map/crb,bk->crk/dot_general | solution.py:32
  626.8 17.3 %fusion.80 = f32[512,2,1024]{2,0,1:T(8,128)S(1)} fusion(f32[512,2,1024]{2,0,1:T(8,128)S(1)} %get-tuple-element.10), kind=kOutput, calls=%fused_computation.102 | convolution fusion | flops 2167406592 | bytes 8388608 | tf_op jit(solution)/shard_map/crb,bk->crk/dot_general | solution.py:33
  644.1 18.2 %fusion.40 = f32[512,2,1024]{2,0,1:T(8,128)} fusion(f32[512,2,1024]{2,0,1:T(8,128)S(1)} %get-tuple-element.10), kind=kOutput, calls=%fused_computation.79 | convolution fusion | flops 2164260864 | bytes 8388608 | tf_op jit(solution)/shard_map/crb,bk->crk/dot_general | solution.py:32
  662.3 18.7 %fusion.38 = f32[512,2,1024]{2,0,1:T(8,128)} fusion(f32[512,2,1024]{2,0,1:T(8,128)S(1)} %get-tuple-element.10), kind=kOutput, calls=%fused_computation.77 | convolution fusion | flops 2167406592 | bytes 8388608 | tf_op jit(solution)/shard_map/crb,bk->crk/dot_general | solution.py:34
  681.0 16.8 %fusion.26 = f32[512,2,1024]{2,0,1:T(8,128)S(1)} fusion(f32[512,2,1024]{2,0,1:T(8,128)S(1)} %get-tuple-element.10), kind=kOutput, calls=%fused_computation.65 | convolution fusion | flops 2167406592 | bytes 8388608 | tf_op jit(solution)/shard_map/crb,bk->crk/dot_general | solution.py:34
  697.8 16.8 %fusion.28 = f32[512,2,1024]{2,0,1:T(8,128)S(1)} fusion(f32[512,2,1024]{2,0,1:T(8,128)S(1)} %get-tuple-element.10), kind=kOutput, calls=%fused_computation.67 | convolution fusion | flops 2164260864 | bytes 8388608 | tf_op jit(solution)/shard_map/crb,bk->crk/dot_general | solution.py:32
  714.6 17.9 %add_subtract_fusion = f32[512,2,1024]{2,0,1:T(8,128)S(1)} fusion(f32[512,2,1024]{2,0,1:T(8,128)S(1)} %fusion.26, f32[512,2,1024]{2,0,1:T(8,128)S(1)} %fusion.28, f32[512,2,1024]{2,0,1:T(8,128)S(1)} %fusion.80, f32[512,2,1024]{2,0,1:T(8,128)S(1)} %fusion.42, f32[512,2,1024]{2,0,1:T(8,128)S(1)} %fusion.44, f32[512,2,1024]{2,0,1:T(8,128)S(1)} %get-tuple-element.9), kind=kOutput, calls=%fused_computation.32 | convolution fusion | flops 2172649472 | bytes 29360128 | tf_op jit(solution)/shard_map/crb,bk->crk/dot_general | solution.py:33
  732.5 21.3 %subtract_convert_fusion.1 = (bf16[512,2,1024]{2,0,1:T(8,128)(2,1)S(1)}, bf16[512,2,1024]{2,0,1:T(8,128)(2,1)S(1)}, bf16[512,2,1024]{2,0,1:T(8,128)(2,1)S(1)}, bf16[512,2,1024]{2,0,1:T(8,128)(2,1)S(1)}) fusion(f32[2,1024]{1,0:T(2,128)S(1)} %copy-done.6, f32[512,2,1024]{2,0,1:T(8,128)S(1)} %add_subtract_fusion, f32[2,1024]{1,0:T(2,128)S(1)} %copy-done.4, ...), kind=kOutput, calls=%fused_computation.29 | convolution fusion | flops 2187329536 | bytes 37765120 | tf_op jit(solution)/shard_map/crb,bk->crk/dot_general | solution.py:33
  753.8 7.6 fusion.106
  761.5 7.6 fusion.108
  769.1 7.6 fusion.110
  776.7 8.1 fusion.112
  784.8 7.8 fusion.56
  792.6 7.6 fusion.54
  800.2 95.7 %fusion.2 = bf16[8,512,1024]{2,1,0:T(8,128)(2,1)} fusion(f32[8,512,1024]{2,0,1:T(8,128)} %fusion.106, f32[8,512,1024]{2,0,1:T(8,128)} %fusion.54, f32[8,512,1024]{2,0,1:T(8,128)} %fusion.108, f32[8,512,1024]{2,0,1:T(8,128)} %fusion.110, f32[8,512,1024]{2,0,1:T(8,128)} %fusion.56, f32[8,512,1024]{2,0,1:T(8,128)} %fusion.112), kind=kLoop, calls=%fused_computation.3 | loop fusion | flops 29360128 | bytes 109051904 | tf_op jit(solution)/shard_map/convert_element_type | solution.py:104
  896.0 67.8 %reduce-scatter.3.cloned.1.call-done = bf16[1,512,1024]{2,1,0:T(8,128)(2,1)} async-done(((bf16[8,512,1024]{2,1,0:T(8,128)(2,1)}), bf16[1,512,1024]{2,1,0:T(8,128)(2,1)}) %reduce-scatter.3.cloned.1.call-update) | async-done | bytes 1048592 | tf_op jit(solution)/shard_map/reduce_scatter | solution.py:103
  963.8 12.7 %convolution_convert_fusion = bf16[1024,4096]{1,0:T(8,128)(2,1)} fusion(bf16[512,4096]{1,0:T(8,128)(2,1)} %param.11, f32[3,512,1024]{2,1,0:T(8,128)} %copy-done, bf16[1,512,1024]{2,1,0:T(8,128)(2,1)} %reduce-scatter.3.cloned.1.call-done, f32[512]{0:T(512)S(1)} %copy-done.10), kind=kOutput, calls=%fused_computation.10 | convolution fusion | flops 4303355904 | bytes 19924992 | tf_op jit(solution)/shard_map/dot_general | solution.py:109
  976.5 144.6 %reduce-scatter.5.cloned.1.call-done = bf16[1024,1024]{1,0:T(8,128)(2,1)} async-done(((bf16[1024,4096]{1,0:T(8,128)(2,1)}), bf16[1024,1024]{1,0:T(8,128)(2,1)}) %reduce-scatter.5.cloned.1.call-update) | async-done | bytes 2097168 | tf_op jit(solution)/shard_map/reduce_scatter | solution.py:112
  (31 shorter events, 1.2 us)
Async XLA Ops:
  6.5 154.8 %all-gather.2.cloned.1.call-start = ((), (), s32[]{:S(2)}) async-start(), calls=%async_computation.4 | async-start | bytes 10485760 | tf_op jit(solution)/shard_map/all_gather | solution.py:67
  7.3 174.7 %copy-start.9 = (f32[3,3,512]{2,1,0:T(4,128)S(1)}, f32[3,3,512]{2,1,0:T(4,128)}, u32[]{:S(2)}) copy-start(f32[3,3,512]{2,1,0:T(4,128)} %param.8) | copy-start | bytes 55300
  179.8 3.3 collective-permute-start
  190.2 2.7 copy-start
  238.9 53.7 %all-to-all-start.1 = ((bf16[512,2,16,128]{3,0,1,2:T(8,128)(2,1)}), bf16[512,2,16,128]{3,0,1,2:T(8,128)(2,1)}, u32[]{:S(2)}, u32[]{:S(2)}) async-start(bf16[512,2,16,128]{3,0,1,2:T(8,128)(2,1)} %copy.26), calls=%async_computation.1 | async-start | bytes 8388608 | tf_op jit(solution)/shard_map/all_to_all | solution.py:92
  243.5 720.2 %reduce-scatter.3.cloned.1.call-start = ((), (), s32[]{:S(2)}) async-start(), calls=%async_computation.5 | async-start | bytes 9437184 | tf_op jit(solution)/shard_map/reduce_scatter | solution.py:103
  243.6 0.5 copy-start.7
  244.3 65.8 %copy-start.3 = (f32[2,1024]{1,0:T(2,128)}, f32[2,1024]{1,0:T(2,128)S(1)}, u32[]{:S(2)}) copy-start(f32[2,1024]{1,0:T(2,128)S(1)} %get-tuple-element.22) | copy-start | bytes 24580
  244.3 65.8 %copy-start.5 = (f32[2,1024]{1,0:T(2,128)}, f32[2,1024]{1,0:T(2,128)S(1)}, u32[]{:S(2)}) copy-start(f32[2,1024]{1,0:T(2,128)S(1)} %get-tuple-element.23) | copy-start | bytes 24580
  493.6 22.5 %copy-start.1 = (f32[1,512,2,1024]{3,2,1,0:T(2,128)S(1)}, f32[1,512,2,1024]{3,2,1,0:T(2,128)}, u32[]{:S(2)}) copy-start(f32[1,512,2,1024]{3,2,1,0:T(2,128)} %get-tuple-element.17) | copy-start | bytes 12582916
  493.6 22.5 %copy-start.2 = (f32[1,512,2,1024]{3,2,1,0:T(2,128)S(1)}, f32[1,512,2,1024]{3,2,1,0:T(2,128)}, u32[]{:S(2)}) copy-start(f32[1,512,2,1024]{3,2,1,0:T(2,128)} %get-tuple-element.18) | copy-start | bytes 12582916
  714.6 17.9 %copy-start.4 = (f32[2,1024]{1,0:T(2,128)S(1)}, f32[2,1024]{1,0:T(2,128)}, u32[]{:S(2)}) copy-start(f32[2,1024]{1,0:T(2,128)} %copy-done.3) | copy-start | bytes 24580
  714.6 17.9 %copy-start.6 = (f32[2,1024]{1,0:T(2,128)S(1)}, f32[2,1024]{1,0:T(2,128)}, u32[]{:S(2)}) copy-start(f32[2,1024]{1,0:T(2,128)} %copy-done.5) | copy-start | bytes 24580
  732.5 21.4 %copy-start.8 = (s32[2]{0:T(128)S(1)}, s32[2]{0:T(128)}, u32[]{:S(2)}) copy-start(s32[2]{0:T(128)} %copy-done.7) | copy-start | bytes 28
  895.9 67.9 %copy-start.10 = (f32[512]{0:T(512)S(1)}, f32[512]{0:T(512)}, u32[]{:S(2)}) copy-start(f32[512]{0:T(512)} %param.10) | copy-start | bytes 6148
  895.9 225.2 %reduce-scatter.5.cloned.1.call-start = ((), (), s32[]{:S(2)}) async-start(), calls=%async_computation.6 | async-start | bytes 10485760 | tf_op jit(solution)/shard_map/reduce_scatter | solution.py:112
Sparse Core Ops, SparseCore 0:
  8.9 152.3 all-gather.1
  896.0 67.6 reduce-scatter.2
  976.6 144.4 reduce-scatter.4
where the time goes:
time: 1130 us
  matrix products  522 us (46%)
  waiting for transfers between devices  407 us (36%)
  other arithmetic  115 us (10%)
  local copies, waits for them, and re-layouts  38.7 us (3%)
  blocking collectives  24.8 us (2%)
  between operations  13.7 us (1%)
    dot_general x12, matrix products, three_pass(): jnp.einsum(form, left_high, right_low, preferred_element_type=jnp.float32)  174 us
    dot_general x12, matrix products, three_pass(): jnp.einsum(form, left_low, right_high, preferred_element_type=jnp.float32)  159 us
    dot_general x12, matrix products, three_pass(): jnp.einsum(form, left_high, right_high, preferred_element_type=jnp.float32)  158 us
    all_gather x1, waiting for transfers between devices, shards(): lax.all_gather(tokens, 'chan', axis=1, tiled=True)  154 us
    reduce_scatter x1, waiting for transfers between devices, shards(): lax.psum_scatter(partial_terms.astype(jnp.bfloat16), 'chan', scatter_dime...  145 us
    convert_element_type x1, other arithmetic, shards(): (partial_terms * norm_factor).astype(jnp.bfloat16)  95.7 us
    reduce_scatter x1, waiting for transfers between devices, shards(): lax.psum_scatter((partial_terms * norm_factor).astype(jnp.bfloat16), 'seq...  67.8 us
    all_to_all x1, waiting for transfers between devices, shards(): lax.all_to_all(stacked.astype(jnp.bfloat16), 'seq', split_axis=2, concat_...  38.8 us
  transfers between devices with their start and end apart: 5, of which 5 were waited for; matrix products, arithmetic and copies ran while one was open for 1% of the time, Pallas kernels for 0%

commit v1 on v0

v1 whole, which is shorter than its diff:
```python
import math

import jax
import jax.numpy as jnp
import numpy as np
from jax import lax
from jax.experimental import pallas as pl
from jax.experimental.pallas import tpu as pltpu
from jax.sharding import PartitionSpec as P

TAPS = 3
LANES = 128
CHAN_BLOCK = 8


def from_behind(value, axis, by):
    size = lax.axis_size(axis)
    pairs = [(i, i + by) for i in range(size) if 0 <= i + by < size]
    return lax.ppermute(value, axis, pairs)


def gather_by_doubling(value, axis):
    size = lax.axis_size(axis)
    index = lax.axis_index(axis)
    held = value[None]
    bit = 1
    while bit < size:
        other = lax.ppermute(held, axis, [(i, i ^ bit) for i in range(size)])
        upper = (index // bit) % 2 == 1
        first = jnp.where(upper, other, held)
        second = jnp.where(upper, held, other)
        held = jnp.concatenate([first, second], axis=0)
        bit *= 2
    return held


def transform_tables(seq_count, tok_rows):
    runs = tok_rows // LANES
    wide = 2 * seq_count * runs
    fft_len = wide * LANES
    k1 = np.arange(seq_count + 1)[:, None]
    k2a = np.arange(runs)[None, :]
    ka = (k1 + 2 * seq_count * k2a).reshape(-1)
    a = np.arange(seq_count * runs)
    b = np.arange(LANES)
    outer = 2.0 * np.pi * ((ka[:, None] * a[None, :]) % wide) / wide
    first = np.concatenate([np.cos(outer), -np.sin(outer)], axis=0)
    last = first.T / fft_len
    turn = 2.0 * np.pi * ((ka[:, None] * b[None, :]) % fft_len) / fft_len
    inner = 2.0 * np.pi * ((b[:, None] * b[None, :]) % LANES) / LANES
    cos, sin = np.cos(inner), np.sin(inner)
    forward = np.block([[cos, -sin], [sin, cos]])
    backward = np.block([[cos, sin], [-sin, cos]])
    half = lambda table: jnp.asarray(table, jnp.bfloat16)
    full = lambda table: jnp.asarray(table, jnp.float32)
    return half(first), half(last), full(np.cos(turn)), full(np.sin(turn)), half(forward), half(backward)


def conv_kernel(signal_ref, resp_ref, first_ref, last_ref, cos_ref, sin_ref, fwd_ref, bwd_ref, out_ref, held):
    seq_count, block, tok_rows = signal_ref.shape
    runs = tok_rows // LANES
    span = seq_count * runs
    rows = cos_ref.shape[0]
    for s in range(seq_count):
        for r in range(runs):
            piece = signal_ref[s, :, r * LANES : (r + 1) * LANES].astype(jnp.float32)
            held[pl.ds(s * runs + r, block, stride=span), :] = piece
    cos, sin = cos_ref[...], sin_ref[...]
    for c in range(block):
        x = held[c * span : (c + 1) * span, :].astype(jnp.bfloat16)
        y = jnp.dot(first_ref[...], x, preferred_element_type=jnp.float32)
        re, im = y[:rows], y[rows:]
        z = jnp.concatenate([re * cos + im * sin, im * cos - re * sin], axis=1)
        f = jnp.dot(z.astype(jnp.bfloat16), fwd_ref[...], preferred_element_type=jnp.float32)
        re, im = f[:, :LANES], f[:, LANES:]
        hr = resp_ref[0, c].astype(jnp.float32)
        hi = resp_ref[1, c].astype(jnp.float32)
        p = jnp.concatenate([re * hr - im * hi, re * hi + im * hr], axis=1)
        q = jnp.dot(p.astype(jnp.bfloat16), bwd_ref[...], preferred_element_type=jnp.float32)
        re, im = q[:, :LANES], q[:, LANES:]
        w = jnp.concatenate([re * cos - im * sin, im * cos + re * sin], axis=0)
        held[c * span : (c + 1) * span, :] = jnp.dot(
            last_ref[...], w.astype(jnp.bfloat16), preferred_element_type=jnp.float32
        )
    for s in range(seq_count):
        for r in range(runs):
            piece = held[pl.ds(s * runs + r, block, stride=span), :]
            out_ref[s, :, r * LANES : (r + 1) * LANES] = piece.astype(out_ref.dtype)


def long_conv(values, response):
    seq_count, chans, tok_rows = values.shape
    rows = response.shape[2]
    block = min(CHAN_BLOCK, chans)
    tables = transform_tables(seq_count, tok_rows)
    fixed = [pl.BlockSpec(t.shape, lambda i: (0, 0)) for t in tables]
    span = seq_count * tok_rows // LANES
    flops = chans * 2 * (2 * 2 * rows * span * LANES + 2 * rows * 4 * LANES * LANES)
    return pl.pallas_call(
        conv_kernel,
        grid=(chans // block,),
        in_specs=[
            pl.BlockSpec((seq_count, block, tok_rows), lambda i: (0, i, 0)),
            pl.BlockSpec((2, block, rows, LANES), lambda i: (0, i, 0, 0)),
            *fixed,
        ],
        out_specs=pl.BlockSpec((seq_count, block, tok_rows), lambda i: (0, i, 0)),
        out_shape=jax.ShapeDtypeStruct((seq_count, chans, tok_rows), jnp.bfloat16),
        scratch_shapes=[pltpu.VMEM((block * span, LANES), jnp.float32)],
        compiler_params=pltpu.CompilerParams(vmem_limit_bytes=48 * 1024 * 1024),
        cost_estimate=pl.CostEstimate(flops=flops, bytes_accessed=8 * 2**20, transcendentals=0),
    )(values, response, *tables)


def folded_response(spectrum, seq_count):
    parts, chans, own, tok_rows = spectrum.shape
    runs = tok_rows // LANES
    each = chans // seq_count
    sent = spectrum.astype(jnp.bfloat16).reshape(parts, seq_count, each, own, LANES, runs)
    sent = sent.transpose(1, 0, 2, 3, 5, 4)
    got = lax.all_to_all(sent, "seq", split_axis=0, concat_axis=0, tiled=True)
    got = got.transpose(1, 2, 0, 3, 4, 5).reshape(parts, each, own * seq_count, runs, LANES)
    kept = got[:, :, : seq_count + 1].astype(jnp.float32)
    mirror = got[:, :, seq_count + 1 :][:, :, ::-1, ::-1, ::-1].astype(jnp.float32)
    mirror = jnp.stack([mirror[0], -mirror[1]])
    mirror = jnp.pad(mirror, ((0, 0), (0, 0), (1, 1), (0, 0), (0, 0)))
    return (kept + mirror).astype(jnp.bfloat16).reshape(parts, each, (seq_count + 1) * runs, LANES)


def feature_slice(out_weight, seq_count):
    group = out_weight.shape[0]
    each = group // seq_count
    own = lax.dynamic_slice_in_dim(out_weight, lax.axis_index("seq") * each, each, axis=0)
    own = lax.all_to_all(own, "chan", split_axis=1, concat_axis=0, tiled=True)
    chan_count = lax.axis_size("chan")
    whole = gather_by_doubling(own.reshape(chan_count, each, own.shape[1]), "seq")
    return whole.transpose(1, 0, 2, 3).reshape(chan_count * group, own.shape[1])


def shards(tokens, in_weight, conv_weight, spectrum, skip, out_weight):
    tok_rows = tokens.shape[0]
    seq_count = lax.axis_size("seq")
    gathered = lax.all_gather(tokens, "chan", axis=1, tiled=True)
    response = folded_response(spectrum, seq_count)
    weight_slice = feature_slice(out_weight, seq_count)
    projected = jnp.einsum(
        "td,pdc->pct", gathered, in_weight, preferred_element_type=jnp.float32
    ).astype(jnp.bfloat16)
    margin = TAPS - 1
    earlier = from_behind(projected[:, :, tok_rows - margin :], "seq", 1)
    extended = jnp.concatenate([earlier, projected], axis=2).astype(jnp.float32)
    filtered = conv_weight[0][:, :, None] * extended[:, :, margin : margin + tok_rows]
    for tap_index in range(1, TAPS):
        filtered = (
            filtered
            + conv_weight[tap_index][:, :, None]
            * extended[:, :, margin - tap_index : margin - tap_index + tok_rows]
        )
    query_rows = filtered[0]
    signal = (filtered[1] * filtered[2]).astype(jnp.bfloat16)
    chans = signal.shape[0]
    values = signal.reshape(seq_count, chans // seq_count, tok_rows)
    values = lax.all_to_all(values, "seq", split_axis=0, concat_axis=0, tiled=True)
    longconv = lax.all_to_all(
        long_conv(values, response), "seq", split_axis=0, concat_axis=0, tiled=True
    ).reshape(chans, tok_rows).astype(jnp.float32)
    gated = (query_rows * (longconv + skip[:, None] * signal.astype(jnp.float32))).astype(
        jnp.bfloat16
    )
    gated = lax.all_gather(gated, "chan", axis=0, tiled=True)
    return lax.dot_general(
        gated, weight_slice, (((0,), (0,)), ((), ())), preferred_element_type=jnp.float32
    ).astype(jnp.bfloat16)


def solution(mesh):
    placed = (
        P("seq", "chan"),
        P(None, None, "chan"),
        P(None, None, "chan"),
        P(None, "chan", "seq", None),
        P("chan"),
        P("chan", None),
    )
    return jax.shard_map(
        shards, mesh=mesh, in_specs=placed, out_specs=P("seq", "chan"), check_vma=False
    )
```

time: 1130 us -> 406 us (0.36)
  matrix products: 522 us -> 27.7 us
  waiting for transfers between devices: 407 us -> 195 us
  other arithmetic: 115 us -> 29.3 us
  Pallas kernels: 0 us -> 28.5 us
  local copies, waits for them, and re-layouts: 38.7 us -> 57.9 us
  starting transfers between devices: 6.85 us -> 23.7 us
    dot_general x38 -> x2, matrix products: 522 us -> 27.7 us  [the longest x1 18.3 us: shards(): jnp.einsum('td,pdc->pct', gathered, in_weight, preferred_element_type=jnp...]
    reduce_scatter x2 -> x0, waiting for transfers between devices: 212 us -> none  [the longest x1 145 us: shards(): lax.psum_scatter(partial_terms.astype(jnp.bfloat16), 'chan', scatter_dime...]
    convert_element_type x2 -> x3, other arithmetic: 100 us -> 12.8 us  [the longest x1 8.25 us: folded_response(): spectrum.astype(jnp.bfloat16)]
    ppermute x0 -> x3, waiting for transfers between devices: none -> 72.9 us  [gather_by_doubling(): other = lax.ppermute(held, axis, [(i, i ^ bit) for i in range(size)])]
    all_gather x1 -> x2, waiting for transfers between devices: 154 us -> 104 us  [the longest x1 104 us: shards(): gathered = lax.all_gather(tokens, 'chan', axis=1, tiled=True)]
    pallas_call x0 -> x1, Pallas kernels: none -> 28.5 us  [long_conv(): pl.pallas_call(conv_kernel, grid=(chans // block,), in_specs=[pl.BlockSpe...]
    all_to_all x1 -> x3, waiting for transfers between devices: 38.8 us -> 16.2 us  [the longest x1 15.4 us: shards(): lax.all_to_all(long_conv(values, response), 'seq', split_axis=0, concat_a...]
    transpose x0 -> x1, local copies, waits for them, and re-layouts: none -> 13.8 us  [folded_response(): sent = sent.transpose(1, 0, 2, 3, 5, 4)]
  transfers between devices with their start and end apart: 5 -> 9, of which waited for: 5 -> 7; matrix products, arithmetic and copies ran while one was open for 1% -> 22% of each run, Pallas kernels for 0% -> 0%
where the time goes in v1:
time: 406 us; the launch traced here: 404 us
  waiting for transfers between devices  195 us (48%)
  local copies, waits for them, and re-layouts  57.9 us (14%)
  other arithmetic  29.3 us (7%)
  Pallas kernels  28.5 us (7%)
  blocking collectives  28.2 us (7%)
  matrix products  27.7 us (7%)
  starting transfers between devices  23.7 us (6%)
  between operations  13.6 us (3%)
    all_gather x1, waiting for transfers between devices, shards(): gathered = lax.all_gather(tokens, 'chan', axis=1, tiled=True)  104 us
    ppermute x3, waiting for transfers between devices, gather_by_doubling(): other = lax.ppermute(held, axis, [(i, i ^ bit) for i in range(size)])  72.9 us
    pallas_call x1, Pallas kernels, long_conv(): pl.pallas_call(conv_kernel, grid=(chans // block,), in_specs=[pl.BlockSpe...  28.5 us
    all_to_all x1, blocking collectives, feature_slice(): own = lax.all_to_all(own, 'chan', split_axis=1, concat_axis=0, tiled=True)  28.2 us
    dot_general x1, matrix products, shards(): jnp.einsum('td,pdc->pct', gathered, in_weight, preferred_element_type=jnp...  18.3 us
    all_to_all x1, waiting for transfers between devices, shards(): lax.all_to_all(long_conv(values, response), 'seq', split_axis=0, concat_a...  15.4 us
    transpose x1, local copies, waits for them, and re-layouts, folded_response(): sent = sent.transpose(1, 0, 2, 3, 5, 4)  13.8 us
    convert_element_type x1, local copies, waits for them, and re-layouts, folded_response(): spectrum.astype(jnp.bfloat16)  11.4 us
  transfers between devices with their start and end apart: 9, of which 7 were waited for; matrix products, arithmetic and copies ran while one was open for 22% of the time, Pallas kernels for 0%

profile of v1, /device:TPU:0, one launch (start us, length us, event | category | flops | bytes accessed | tf_op | source)
XLA Modules:
  0.0 404.2 jit_solution(9577638355475836248)
XLA Ops:
  6.5 0.0 all-gather.3.cloned.1.call-start
  6.5 0.7 all-gather.3.cloned.1.call-update
  7.3 8.3 %convert_element_type.50 = bf16[2,512,2,1024]{3,2,1,0:T(2,128)(2,1)} convert(f32[2,512,2,1024]{3,2,1,0:T(2,128)} %param.15) | non-fusion elementwise | flops 2097152 | bytes 12582912 | tf_op jit(solution)/shard_map/convert_element_type | solution.py:119
  15.5 11.4 %copy.22 = bf16[2,512,2,1024]{1,3,2,0:T(8,128)(2,1)} copy(bf16[2,512,2,1024]{3,2,1,0:T(2,128)(2,1)} %convert_element_type.50) | data formatting | bytes 8388608 | tf_op jit(solution)/shard_map/convert_element_type | solution.py:119
  26.9 11.2 %reshape.32 = bf16[2,8,64,2,128,8]{2,1,5,4,3,0:T(8,128)(2,1)} reshape(bf16[2,512,2,1024]{1,3,2,0:T(8,128)(2,1)} %copy.22) | data formatting | bytes 8388608 | tf_op jit(solution)/shard_map/reshape | solution.py:119
  38.1 13.8 %copy.23 = bf16[8,2,64,2,8,128]{5,4,3,2,1,0:T(8,128)(2,1)} copy(bf16[8,2,64,2,8,128]{2,0,4,5,3,1:T(8,128)(2,1)} %bitcast.49) | data formatting | bytes 8388608 | tf_op jit(solution)/shard_map/transpose | solution.py:120
  51.9 5.2 %all-to-all-start.1 = ((bf16[8,2,64,2,8,128]{5,4,3,2,1,0:T(8,128)(2,1)}), bf16[8,2,64,2,8,128]{5,4,3,2,1,0:T(8,128)(2,1)}, u32[]{:S(2)}, u32[]{:S(2)}) async-start(bf16[8,2,64,2,8,128]{5,4,3,2,1,0:T(8,128)(2,1)} %copy.23), calls=%async_computation.1 | async-start | bytes 8388608 | tf_op jit(solution)/shard_map/all_to_all | solution.py:121
  57.1 0.0 copy-start.9
  57.1 104.2 %all-gather.3.cloned.1.call-done = bf16[1024,4096]{1,0:T(8,128)(2,1)} async-done(((bf16[1024,1024]{1,0:T(8,128)(2,1)}), bf16[1024,4096]{1,0:T(8,128)(2,1)}) %all-gather.3.cloned.1.call-update) | async-done | bytes 8388624 | tf_op jit(solution)/shard_map/all_gather | solution.py:143
  161.3 18.3 %fusion.8 = bf16[3,512,1024]{2,1,0:T(8,128)(2,1)S(1)} fusion(bf16[3,4096,512]{2,1,0:T(8,128)(2,1)} %param.13, bf16[1024,4096]{1,0:T(8,128)(2,1)} %all-gather.3.cloned.1.call-done), kind=kOutput, calls=%fused_computation.16 | convolution fusion | flops 12886474752 | bytes 24117248 | tf_op jit(solution)/shard_map/td,pdc->pct/dot_general | solution.py:146
  179.6 0.2 slice.56
  179.8 2.0 collective-permute-start
  181.8 0.0 copy-done.9
  181.8 1.3 collective-permute-done
  183.1 2.0 maximum_convert_fusion
  185.2 5.1 %fusion.2 = f32[3,512,1024]{2,1,0:T(8,128)S(1)} fusion(f32[3,512,1026]{2,1,0:T(8,128)S(1)} %maximum_convert_fusion, f32[3,512]{1,0:T(4,128)S(1)} %get-tuple-element.12, f32[3,512]{1,0:T(4,128)S(1)} %get-tuple-element.13, f32[3,512]{1,0:T(4,128)S(1)} %get-tuple-element.11), kind=kLoop, calls=%fused_computation.5 | loop fusion | flops 7864320 | bytes 25184256 | tf_op jit(solution)/shard_map/add | solution.py:155
  190.2 0.0 copy-start.6
  190.2 2.6 copy-done.6
  192.9 1.3 fusion.11
  194.2 0.0 all-to-all-done.1
  194.2 9.5 %all-to-all-start = ((bf16[8,64,1024]{2,1,0:T(8,128)(2,1)}), bf16[8,64,1024]{2,1,0:T(8,128)(2,1)S(1)}, u32[]{:S(2)}, u32[]{:S(2)}) async-start(bf16[8,64,1024]{2,1,0:T(8,128)(2,1)} %bitcast.5), calls=%async_computation | async-start | bytes 2097152 | tf_op jit(solution)/shard_map/all_to_all | solution.py:163
  203.7 3.4 copy.24
  207.1 0.0 copy-start.7
  207.1 2.1 copy-done.7
  209.2 1.4 slice.64
  210.6 4.5 %rev.3 = bf16[2,64,7,8,128]{4,3,2,1,0:T(8,128)(2,1)S(1)} reverse(bf16[2,64,7,8,128]{4,3,2,1,0:T(8,128)(2,1)} %slice.64), dimensions={2,3,4} | reverse | bytes 3670016 | tf_op jit(solution)/shard_map/rev | solution.py:124
  215.2 0.2 convert_element_type.52
  215.4 0.0 copy-start.8
  215.4 0.1 slice.65
  215.5 0.1 slice_negate_fusion
  215.7 1.9 copy-done.8
  217.6 0.0 copy-start
  217.6 0.6 fusion.7.resp_ref
  218.2 0.9 all-to-all-done.signal_ref
  219.1 0.0 copy-done
  219.1 0.0 copy-start.1
  219.1 0.9 copy-done.1
  220.0 0.0 copy-start.2
  220.0 0.8 copy-done.2
  220.7 0.8 copy-done.3
  221.5 0.8 copy-done.4
  222.3 0.8 copy-done.5
  223.0 28.5 %shard_map.118 = bf16[8,64,1024]{2,1,0:T(8,128)(2,1)} custom-call(bf16[8,64,1024]{2,1,0:T(8,128)(2,1)S(1)} %all-to-all-done.signal_ref, bf16[2,64,72,128]{3,2,1,0:T(8,128)(2,1)S(1)} %fusion.7.resp_ref, bf16[144,64]{1,0:T(8,128)(2,1)S(1)} %copy-done.2, bf16[64,144]{1,0:T(8,128)(2,1)S(1)} %copy-done.5, f32[72,128]{1,0:T(8,128)S(1)} %copy-done.3, ...), custom_call_target="tpu_custom_call" | custom-call | flops 1509949440 | bytes 8388608 | tf_op jit(solution)/shard_map/pallas_call | solution.py:99
  251.6 3.6 all-to-all-start.2
  255.2 0.0 all-gather.5.cloned.1.call-start
  255.3 15.4 %all-to-all-done.2 = bf16[8,64,1024]{2,1,0:T(8,128)(2,1)S(1)} async-done(((bf16[8,64,1024]{2,1,0:T(8,128)(2,1)}), bf16[8,64,1024]{2,1,0:T(8,128)(2,1)S(1)}, u32[]{:S(2)}, u32[]{:S(2)}) %all-to-all-start.2) | async-done | bytes 1048608 | tf_op jit(solution)/shard_map/all_to_all | solution.py:164
  270.6 0.0 copy-done.10
  270.6 4.3 %fusion.13 = bf16[512,1024]{1,0:T(8,128)(2,1)} fusion(f32[3,512,1024]{2,1,0:T(8,128)} %copy-done.6, bf16[8,64,1024]{2,1,0:T(8,128)(2,1)S(1)} %all-to-all-done.2, f32[512]{0:T(512)S(1)} %copy-done.10), kind=kLoop, calls=%fused_computation.21 | loop fusion | flops 4194304 | bytes 8390656 | tf_op jit(solution)/shard_map/convert_element_type | solution.py:167
  275.0 0.0 all-gather.5.cloned.1.call-update
  275.0 1.1 constant_dynamic-slice_fusion
  276.1 28.2 %all_to_all.31 = bf16[64,4,1024]{2,0,1:T(8,128)(2,1)S(1)} all-to-all(bf16[64,4,1024]{2,0,1:T(8,128)(2,1)S(1)} %bitcast.55), channel_id=1, replica_groups=mesh['seq'=8,'chan'=4] {'chan'}, dimensions={1} | all-to-all | bytes 1048576 | tf_op jit(solution)/shard_map/all_to_all | solution.py:134
  304.3 0.0 collective-permute-start.1
  304.3 1.9 collective-permute-done.1
  306.2 0.1 broadcast_select_fusion.5
  306.3 0.1 pad_maximum_fusion.2
  306.4 3.4 collective-permute-start.2
  309.8 23.6 %collective-permute-done.2 = bf16[2,4,64,1024]{3,2,0,1:T(8,128)(2,1)} collective-permute-done((bf16[2,4,64,1024]{3,2,0,1:T(8,128)(2,1)S(1)}, bf16[2,4,64,1024]{3,2,0,1:T(8,128)(2,1)}, u32[]{:S(2)}, u32[]{:S(2)}) %collective-permute-start.2) | collective-permute-done | bytes 1048608 | tf_op jit(solution)/shard_map/ppermute | solution.py:28
  333.4 1.4 broadcast_select_fusion.3
  334.7 1.5 pad_maximum_fusion.1
  336.2 0.0 collective-permute-start.3
  336.3 47.5 %collective-permute-done.3 = bf16[4,4,64,1024]{3,2,0,1:T(8,128)(2,1)} collective-permute-done((bf16[4,4,64,1024]{3,2,0,1:T(8,128)(2,1)}, bf16[4,4,64,1024]{3,2,0,1:T(8,128)(2,1)}, u32[]{:S(2)}, u32[]{:S(2)}) %collective-permute-start.3) | collective-permute-done | bytes 2097184 | tf_op jit(solution)/shard_map/ppermute | solution.py:28
  383.7 1.9 broadcast_select_fusion.1
  385.6 2.4 pad_maximum_fusion
  388.0 9.4 %convolution_convert_fusion = bf16[1024,1024]{1,0:T(8,128)(2,1)} fusion(bf16[2048,1024]{1,0:T(8,128)(2,1)} %all-gather.5.cloned.1.call-done, bf16[2048,1024]{1,0:T(8,128)(2,1)} %bitcast.52), kind=kOutput, calls=%fused_computation.27 | convolution fusion | flops 4296015872 | bytes 10485760 | tf_op jit(solution)/shard_map/dot_general | solution.py:171
  (7 shorter events, 0.0 us)
Async XLA Ops:
  6.5 154.8 %all-gather.3.cloned.1.call-start = ((), (), s32[]{:S(2)}) async-start(), calls=%async_computation.4 | async-start | bytes 10485760 | tf_op jit(solution)/shard_map/all_gather | solution.py:143
  51.9 142.3 %all-to-all-start.1 = ((bf16[8,2,64,2,8,128]{5,4,3,2,1,0:T(8,128)(2,1)}), bf16[8,2,64,2,8,128]{5,4,3,2,1,0:T(8,128)(2,1)}, u32[]{:S(2)}, u32[]{:S(2)}) async-start(bf16[8,2,64,2,8,128]{5,4,3,2,1,0:T(8,128)(2,1)} %copy.23), calls=%async_computation.1 | async-start | bytes 8388608 | tf_op jit(solution)/shard_map/all_to_all | solution.py:121
  57.1 124.7 %copy-start.9 = (f32[3,3,512]{2,1,0:T(4,128)S(1)}, f32[3,3,512]{2,1,0:T(4,128)}, u32[]{:S(2)}) copy-start(f32[3,3,512]{2,1,0:T(4,128)} %param.14) | copy-start | bytes 55300
  179.8 3.3 collective-permute-start
  190.2 2.6 copy-start.6
  194.2 24.9 %all-to-all-start = ((bf16[8,64,1024]{2,1,0:T(8,128)(2,1)}), bf16[8,64,1024]{2,1,0:T(8,128)(2,1)S(1)}, u32[]{:S(2)}, u32[]{:S(2)}) async-start(bf16[8,64,1024]{2,1,0:T(8,128)(2,1)} %bitcast.5), calls=%async_computation | async-start | bytes 2097152 | tf_op jit(solution)/shard_map/all_to_all | solution.py:163
  207.1 2.1 copy-start.7
  215.4 2.2 copy-start.8
  217.6 1.5 copy-start
  219.1 0.9 copy-start.1
  220.0 0.8 copy-start.2
  220.7 0.8 copy-start.3
  221.5 0.8 copy-start.4
  222.3 0.8 copy-start.5
  223.0 47.6 %copy-start.10 = (f32[512]{0:T(512)S(1)}, f32[512]{0:T(512)}, u32[]{:S(2)}) copy-start(f32[512]{0:T(512)} %param.16) | copy-start | bytes 6148
  251.6 19.0 %all-to-all-start.2 = ((bf16[8,64,1024]{2,1,0:T(8,128)(2,1)}), bf16[8,64,1024]{2,1,0:T(8,128)(2,1)S(1)}, u32[]{:S(2)}, u32[]{:S(2)}) async-start(bf16[8,64,1024]{2,1,0:T(8,128)(2,1)} %shard_map.118), calls=%async_computation.2 | async-start | bytes 2097152 | tf_op jit(solution)/shard_map/all_to_all | solution.py:164
  255.2 132.7 %all-gather.5.cloned.1.call-start = ((), (), s32[]{:S(2)}) async-start(), calls=%async_computation.5 | async-start | bytes 5242880 | tf_op jit(solution)/shard_map/all_gather | solution.py:170
  304.3 1.9 collective-permute-start.1
  306.4 26.9 %collective-permute-start.2 = (bf16[2,4,64,1024]{3,2,0,1:T(8,128)(2,1)S(1)}, bf16[2,4,64,1024]{3,2,0,1:T(8,128)(2,1)}, u32[]{:S(2)}, u32[]{:S(2)}) collective-permute-start(bf16[2,4,64,1024]{3,2,0,1:T(8,128)(2,1)S(1)} %pad_maximum_fusion.2), channel_id=1, source_target_pairs={{0,8},{4,12},{8,0},{12,4},{16,24},{20,28},{24,16},{28,20},{1,9},{5... | collective-permute-start | bytes 3145736 | tf_op jit(solution)/shard_map/ppermute | solution.py:28
  336.2 47.5 %collective-permute-start.3 = (bf16[4,4,64,1024]{3,2,0,1:T(8,128)(2,1)}, bf16[4,4,64,1024]{3,2,0,1:T(8,128)(2,1)}, u32[]{:S(2)}, u32[]{:S(2)}) collective-permute-start(bf16[4,4,64,1024]{3,2,0,1:T(8,128)(2,1)} %pad_maximum_fusion.1), channel_id=1, source_target_pairs={{0,16},{4,20},{8,24},{12,28},{16,0},{20,4},{24,8},{28,12},{1,17},{... | collective-permute-start | bytes 6291464 | tf_op jit(solution)/shard_map/ppermute | solution.py:28
Sparse Core Ops, SparseCore 0:
  8.9 152.3 all-gather.2
  275.1 83.4 all-gather.4

commit v2 on v1

v2 whole, which is shorter than its diff:
```python
import jax
import jax.numpy as jnp
import numpy as np
from jax import lax
from jax.experimental import pallas as pl
from jax.experimental.pallas import tpu as pltpu
from jax.sharding import PartitionSpec as P

TAPS = 3
LANES = 128
HALO = 16
CHAN_BLOCK = 16
CHUNK_QUARTERS = (1, 1, 2)
VMEM_BYTES = 48 * 1024 * 1024


def from_behind(value, axis, by):
    size = lax.axis_size(axis)
    pairs = [(i, i + by) for i in range(size) if 0 <= i + by < size]
    return lax.ppermute(value, axis, pairs)


def gather_by_doubling(value, axis):
    size = lax.axis_size(axis)
    index = lax.axis_index(axis)
    held = value[None]
    bit = size // 2
    while bit >= 1:
        other = lax.ppermute(held, axis, [(i, i ^ bit) for i in range(size)])
        upper = (index // bit) % 2 == 1
        first = jnp.where(upper, other, held)
        second = jnp.where(upper, held, other)
        held = jnp.stack([first, second], axis=1).reshape((2 * held.shape[0],) + held.shape[1:])
        bit //= 2
    return held


def chunk_ranges(chans, seq_count):
    quarter = chans // sum(CHUNK_QUARTERS)
    if quarter % LANES or (quarter // seq_count) % CHAN_BLOCK:
        return [(0, chans)]
    ends = np.cumsum(CHUNK_QUARTERS) * quarter
    return [(int(end) - size * quarter, int(end)) for end, size in zip(ends, CHUNK_QUARTERS)]


def project_kernel(extras, tok_ref, w_ref, taps_ref, *rest):
    signal_ref, signal_t_ref, query_t_ref, acc = rest[extras:]
    step = pl.program_id(1)
    rows = signal_t_ref.shape[0]
    for p in range(3):
        part = jnp.dot(tok_ref[0], w_ref[p], preferred_element_type=jnp.float32)
        acc[p] = part + jnp.where(step == 0, 0.0, acc[p])

    @pl.when(step == pl.num_programs(1) - 1)
    def _():
        for p in range(3):
            acc[p] = acc[p].astype(jnp.bfloat16).astype(jnp.float32)
        tile = min(LANES, rows)
        for r in range(0, rows, tile):
            streams = []
            for p in range(3):
                total = taps_ref[0, p][None, :] * acc[p, pl.ds(HALO + r, tile), :]
                for j in range(1, TAPS):
                    total = total + taps_ref[j, p][None, :] * acc[p, pl.ds(HALO + r - j, tile), :]
                streams.append(total)
            signal = streams[1] * streams[2]
            query_t_ref[r : r + tile, :] = streams[0].astype(query_t_ref.dtype)
            signal_t_ref[r : r + tile, :] = signal.astype(signal_t_ref.dtype)
            signal_ref[:, r : r + tile] = signal.T.astype(signal_ref.dtype)


def project(gathered, in_weight, conv_weight, *after):
    parts, held_rows, depth = gathered.shape
    rows = held_rows - HALO
    chans = in_weight.shape[2]
    tile = 2 * LANES if chans % (2 * LANES) == 0 else chans
    flat = jax.ShapeDtypeStruct((rows, chans), jnp.bfloat16)
    return pl.pallas_call(
        lambda *refs: project_kernel(len(after), *refs),
        grid=(chans // tile, parts),
        in_specs=[
            pl.BlockSpec((1, held_rows, depth), lambda i, z: (z, 0, 0)),
            pl.BlockSpec((3, depth, tile), lambda i, z: (0, z, i)),
            pl.BlockSpec((TAPS, 3, tile), lambda i, z: (0, 0, i)),
            *[pl.BlockSpec(memory_space=pl.ANY) for _ in after],
        ],
        out_specs=[
            pl.BlockSpec((tile, rows), lambda i, z: (i, 0)),
            pl.BlockSpec((rows, tile), lambda i, z: (0, i)),
            pl.BlockSpec((rows, tile), lambda i, z: (0, i)),
        ],
        out_shape=[jax.ShapeDtypeStruct((chans, rows), jnp.bfloat16), flat, flat],
        scratch_shapes=[pltpu.VMEM((3, held_rows, tile), jnp.float32)],
        compiler_params=pltpu.CompilerParams(vmem_limit_bytes=VMEM_BYTES),
        cost_estimate=pl.CostEstimate(
            flops=2 * 3 * held_rows * depth * parts * chans,
            bytes_accessed=2 * depth * parts * (3 * chans + 2 * held_rows),
            transcendentals=0,
        ),
    )(gathered, in_weight, conv_weight, *after)


def transform_tables(seq_count, tok_rows):
    runs = tok_rows // LANES
    wide = 2 * seq_count * runs
    fft_len = wide * LANES
    k1 = np.arange(seq_count + 1)[:, None]
    k2a = np.arange(runs)[None, :]
    ka = (k1 + 2 * seq_count * k2a).reshape(-1)
    a = np.arange(seq_count * runs)
    b = np.arange(LANES)
    outer = 2.0 * np.pi * ((ka[:, None] * a[None, :]) % wide) / wide
    first = np.concatenate([np.cos(outer), -np.sin(outer)], axis=0)
    last = first.T / fft_len
    turn = 2.0 * np.pi * ((ka[:, None] * b[None, :]) % fft_len) / fft_len
    inner = 2.0 * np.pi * ((b[:, None] * b[None, :]) % LANES) / LANES
    cos, sin = np.cos(inner), np.sin(inner)
    forward = np.block([[cos, -sin], [sin, cos]])
    backward = np.block([[cos, sin], [-sin, cos]])
    half = lambda table: jnp.asarray(table, jnp.bfloat16)
    full = lambda table: jnp.asarray(table, jnp.float32)
    return half(first), half(last), full(np.cos(turn)), full(np.sin(turn)), half(forward), half(backward)


def conv_kernel(signal_ref, resp_ref, first_ref, last_ref, cos_ref, sin_ref, fwd_ref, bwd_ref, out_ref, held, low, high):
    seq_count, block, tok_rows = signal_ref.shape
    runs = tok_rows // LANES
    span = seq_count * runs
    rows = cos_ref.shape[0]
    pair = 2 * rows
    for s in range(seq_count):
        for r in range(runs):
            piece = signal_ref[s, :, r * LANES : (r + 1) * LANES].astype(jnp.float32)
            held[pl.ds(s * runs + r, block, stride=span), :] = piece
    cos, sin = cos_ref[...], sin_ref[...]
    for c in range(0, block, 2):
        x = jnp.concatenate([held[c * span : (c + 1) * span, :], held[(c + 1) * span : (c + 2) * span, :]], axis=1)
        y = jnp.dot(first_ref[...], x.astype(jnp.bfloat16), preferred_element_type=jnp.float32)
        turned = []
        for half in (slice(0, LANES), slice(LANES, 2 * LANES)):
            re, im = y[:rows, half], y[rows:, half]
            turned.append(jnp.concatenate([re * cos + im * sin, im * cos - re * sin], axis=1))
        low[c * rows : c * rows + pair, :] = jnp.concatenate(turned, axis=0).astype(jnp.bfloat16)
    high[...] = jnp.dot(low[...], fwd_ref[...], preferred_element_type=jnp.float32)
    for c in range(0, block, 2):
        done = []
        for d in (c, c + 1):
            re = high[d * rows : (d + 1) * rows, :LANES]
            im = high[d * rows : (d + 1) * rows, LANES:]
            hr = resp_ref[0, d].astype(jnp.float32)
            hi = resp_ref[1, d].astype(jnp.float32)
            done.append(jnp.concatenate([re * hr - im * hi, re * hi + im * hr], axis=1))
        low[c * rows : c * rows + pair, :] = jnp.concatenate(done, axis=0).astype(jnp.bfloat16)
    high[...] = jnp.dot(low[...], bwd_ref[...], preferred_element_type=jnp.float32)
    for c in range(0, block, 2):
        turned = []
        for d in (c, c + 1):
            re = high[d * rows : (d + 1) * rows, :LANES]
            im = high[d * rows : (d + 1) * rows, LANES:]
            turned.append(jnp.concatenate([re * cos - im * sin, im * cos + re * sin], axis=0))
        w = jnp.concatenate(turned, axis=1).astype(jnp.bfloat16)
        y = jnp.dot(last_ref[...], w, preferred_element_type=jnp.float32)
        held[c * span : (c + 1) * span, :] = y[:, :LANES]
        held[(c + 1) * span : (c + 2) * span, :] = y[:, LANES:]
    for s in range(seq_count):
        for r in range(runs):
            piece = held[pl.ds(s * runs + r, block, stride=span), :]
            out_ref[s, :, r * LANES : (r + 1) * LANES] = piece.astype(out_ref.dtype)


def long_conv(values, response, start=0):
    seq_count, chans, tok_rows = values.shape
    rows = response.shape[2]
    block = min(CHAN_BLOCK, chans)
    tables = transform_tables(seq_count, tok_rows)
    fixed = [pl.BlockSpec(t.shape, lambda i: (0, 0)) for t in tables]
    span = seq_count * tok_rows // LANES
    flops = chans * 2 * (2 * 2 * rows * span * LANES + 2 * rows * 4 * LANES * LANES)
    moved = 2 * (2 * values.size + 2 * chans * rows * LANES)
    return pl.pallas_call(
        conv_kernel,
        grid=(chans // block,),
        in_specs=[
            pl.BlockSpec((seq_count, block, tok_rows), lambda i: (0, i, 0)),
            pl.BlockSpec((2, block, rows, LANES), lambda i: (0, start // block + i, 0, 0)),
            *fixed,
        ],
        out_specs=pl.BlockSpec((seq_count, block, tok_rows), lambda i: (0, i, 0)),
        out_shape=jax.ShapeDtypeStruct((seq_count, chans, tok_rows), jnp.bfloat16),
        scratch_shapes=[
            pltpu.VMEM((block * span, LANES), jnp.float32),
            pltpu.VMEM((block * rows, 2 * LANES), jnp.bfloat16),
            pltpu.VMEM((block * rows, 2 * LANES), jnp.float32),
        ],
        compiler_params=pltpu.CompilerParams(vmem_limit_bytes=VMEM_BYTES),
        cost_estimate=pl.CostEstimate(flops=flops, bytes_accessed=moved, transcendentals=0),
    )(values, response, *tables)


def gate_kernel(conv_ref, skip_ref, *refs):
    out_ref = refs[-1]
    conv = conv_ref[...].astype(jnp.float32).T
    skip = skip_ref[...]
    at = 0
    for signal_ref, query_ref in zip(refs[0:-1:2], refs[1:-1:2]):
        rows = signal_ref.shape[0]
        inner = conv[at : at + rows] + skip * signal_ref[...].astype(jnp.float32)
        out_ref[at : at + rows, :] = (query_ref[...].astype(jnp.float32) * inner).astype(out_ref.dtype)
        at += rows


def gate(longconv, skip, start, pieces):
    chans, tok_rows = longconv.shape
    first = start // LANES
    given, specs = [], []
    for piece in pieces:
        for array in piece:
            given.append(array)
            specs.append(pl.BlockSpec((array.shape[0], LANES), lambda i: (0, first + i)))
    return pl.pallas_call(
        gate_kernel,
        grid=(chans // LANES,),
        in_specs=[
            pl.BlockSpec((LANES, tok_rows), lambda i: (i, 0)),
            pl.BlockSpec((1, LANES), lambda i: (0, first + i)),
            *specs,
        ],
        out_specs=pl.BlockSpec((tok_rows, LANES), lambda i: (0, i)),
        out_shape=jax.ShapeDtypeStruct((tok_rows, chans), jnp.bfloat16),
        compiler_params=pltpu.CompilerParams(vmem_limit_bytes=VMEM_BYTES),
        cost_estimate=pl.CostEstimate(flops=4 * chans * tok_rows, bytes_accessed=8 * chans * tok_rows, transcendentals=0),
    )(longconv, skip[None, :], *given)


def folded_response(spectrum, seq_count, ranges):
    parts, chans, own, tok_rows = spectrum.shape
    runs = tok_rows // LANES
    each = chans // seq_count
    sent = spectrum.astype(jnp.bfloat16)
    sent = jnp.concatenate(
        [sent[:, lo:hi].reshape(parts, seq_count, (hi - lo) // seq_count, own, LANES, runs) for lo, hi in ranges],
        axis=2,
    )
    sent = sent.transpose(1, 0, 2, 3, 5, 4)
    got = lax.all_to_all(sent, "seq", split_axis=0, concat_axis=0, tiled=True)
    got = got.transpose(1, 2, 0, 3, 4, 5).reshape(parts, each, own * seq_count, runs, LANES)
    kept = got[:, :, : seq_count + 1].astype(jnp.float32)
    mirror = got[:, :, seq_count + 1 :][:, :, ::-1, ::-1, ::-1].astype(jnp.float32)
    mirror = jnp.stack([mirror[0], -mirror[1]])
    mirror = jnp.pad(mirror, ((0, 0), (0, 0), (1, 1), (0, 0), (0, 0)))
    return (kept + mirror).astype(jnp.bfloat16).reshape(parts, each, (seq_count + 1) * runs, LANES)


def feature_slice(out_weight, seq_count):
    group = out_weight.shape[0]
    each = group // seq_count
    own = lax.dynamic_slice_in_dim(out_weight, lax.axis_index("seq") * each, each, axis=0)
    own = lax.all_to_all(own, "chan", split_axis=1, concat_axis=0, tiled=True)
    chan_count = lax.axis_size("chan")
    whole = gather_by_doubling(own.reshape(chan_count, each, own.shape[1]), "seq")
    return whole.transpose(1, 0, 2, 3).reshape(chan_count, group, own.shape[1])


def shards(tokens, in_weight, conv_weight, spectrum, skip, out_weight):
    tok_rows = tokens.shape[0]
    seq_count = lax.axis_size("seq")
    chans = in_weight.shape[2]
    ranges = chunk_ranges(chans, seq_count)
    cut = tok_rows // 4
    later = lax.all_gather(tokens[cut - HALO :], "chan")
    halo = from_behind(tokens[tok_rows - HALO :], "seq", 1)
    earlier = lax.all_gather(jnp.concatenate([halo, tokens[:cut]], axis=0), "chan")
    response = folded_response(spectrum, seq_count, ranges)
    weight_slice = feature_slice(out_weight, seq_count)
    signal_b, signal_bt, query_bt = project(later, in_weight, conv_weight)
    signal_a, signal_at, query_at = project(earlier, in_weight, conv_weight, response, weight_slice)
    signal = jnp.concatenate([signal_a, signal_b], axis=1)
    pieces = ((signal_at, query_at), (signal_bt, query_bt))
    total = None
    for lo, hi in ranges:
        values = signal[lo:hi].reshape(seq_count, (hi - lo) // seq_count, tok_rows)
        values = lax.all_to_all(values, "seq", split_axis=0, concat_axis=0, tiled=True)
        longconv = lax.all_to_all(
            long_conv(values, response, lo // seq_count), "seq", split_axis=0, concat_axis=0, tiled=True
        ).reshape(hi - lo, tok_rows)
        gated = lax.all_gather(gate(longconv, skip, lo, pieces), "chan", axis=1, tiled=True)
        weight = weight_slice[:, lo:hi].reshape(gated.shape[1], weight_slice.shape[2])
        term = jnp.dot(gated, weight, preferred_element_type=jnp.float32)
        total = term if total is None else total + term
    return total.astype(jnp.bfloat16)


def solution(mesh):
    placed = (
        P("seq", "chan"),
        P(None, None, "chan"),
        P(None, None, "chan"),
        P(None, "chan", "seq", None),
        P("chan"),
        P("chan", None),
    )
    return jax.shard_map(
        shards, mesh=mesh, in_specs=placed, out_specs=P("seq", "chan"), check_vma=False
    )
```

time: 406 us -> 374 us (0.921)
  waiting for transfers between devices: 195 us -> 103 us
  blocking collectives: 28.2 us -> 63 us
  local copies, waits for them, and re-layouts: 57.9 us -> 92.5 us
  matrix products: 27.7 us -> 17.1 us
  Pallas kernels: 28.5 us -> 34.8 us
  starting transfers between devices: 23.7 us -> 19.2 us
    all_gather x2 -> x5, waiting for transfers between devices: 104 us -> 35.1 us  [the longest x3 35.1 us: shards(): lax.all_gather(gate(longconv, skip, lo, pieces), 'chan', axis=1, tiled=True)]
    all_to_all x1 -> x6, blocking collectives: 28.2 us -> 63 us  [the longest x3 32.2 us: shards(): lax.all_to_all(values, 'seq', split_axis=0, concat_axis=0, tiled=True)]
    pallas_call x0 -> x5, Pallas kernels: none -> 29.1 us  [the longest x2 27.4 us: project(): pl.pallas_call(lambda *refs: project_kernel(len(after), *refs), grid=(cha...]
    pallas_call x1 -> x3, Pallas kernels: 28.5 us -> 5.68 us  [long_conv(): pl.pallas_call(conv_kernel, grid=(chans // block,), in_specs=[pl.BlockSpe...]
    slice x1 -> x13, local copies, waits for them, and re-layouts: 0.18 us -> 20 us  [the longest x6 10.4 us: folded_response(): sent[:, lo:hi]]
    all_to_all x2 -> x1, waiting for transfers between devices: 16.2 us -> 0.01 us  [feature_slice(): own = lax.all_to_all(own, 'chan', split_axis=1, concat_axis=0, tiled=True)]
    transpose x0 -> x1, other arithmetic: none -> 14.5 us  [folded_response(): sent = sent.transpose(1, 0, 2, 3, 5, 4)]
    reshape x1 -> x3, local copies, waits for them, and re-layouts: 11.2 us -> 24.8 us  [folded_response(): sent[:, lo:hi]]
  transfers between devices with their start and end apart: 9 -> 11, of which waited for: 7 -> 3; matrix products, arithmetic and copies ran while one was open for 22% -> 30% of each run, Pallas kernels for 0% -> 4%
where the time goes in v2:
time: 374 us; the launch traced here: 372 us
  waiting for transfers between devices  103 us (28%)
  local copies, waits for them, and re-layouts  92.5 us (25%)
  blocking collectives  63 us (17%)
  Pallas kernels  34.8 us (9%)
  other arithmetic  29.6 us (8%)
  starting transfers between devices  19.2 us (5%)
  matrix products  17.1 us (5%)
  between operations  13.6 us (4%)
    ppermute x3, waiting for transfers between devices, gather_by_doubling(): other = lax.ppermute(held, axis, [(i, i ^ bit) for i in range(size)])  67.4 us
    all_gather x3, waiting for transfers between devices, shards(): lax.all_gather(gate(longconv, skip, lo, pieces), 'chan', axis=1, tiled=True)  35.1 us
    all_to_all x3, blocking collectives, shards(): lax.all_to_all(values, 'seq', split_axis=0, concat_axis=0, tiled=True)  32.2 us
    all_to_all x3, blocking collectives, shards(): lax.all_to_all(long_conv(values, response, lo // seq_count), 'seq', split...  30.9 us
    pallas_call x2, Pallas kernels, project(): pl.pallas_call(lambda *refs: project_kernel(len(after), *refs), grid=(cha...  27.4 us
    reshape x3, local copies, waits for them, and re-layouts, folded_response(): sent[:, lo:hi]  24.8 us
    unnamed x69, local copies, waits for them, and re-layouts  17.4 us
    dot_general x3, matrix products, shards(): term = jnp.dot(gated, weight, preferred_element_type=jnp.float32)  17.1 us
  transfers between devices with their start and end apart: 11, of which 3 were waited for; matrix products, arithmetic and copies ran while one was open for 30% of the time, Pallas kernels for 4%

profile of v2, /device:TPU:0, one launch (start us, length us, event | category | flops | bytes accessed | tf_op | source)
XLA Modules:
  0.0 372.3 jit_solution(16938258970077070906)
XLA Ops:
  7.3 2.3 collective-permute-start
  9.7 1.1 slice.49
  10.7 0.8 pad_maximum_fusion.2
  11.7 2.7 slice.57
  14.4 1.1 constant_dynamic-slice_fusion
  15.5 0.8 copy.59
  16.3 5.7 %all-to-all-start.1 = ((bf16[64,4,1024]{2,0,1:T(8,128)(2,1)}), bf16[64,4,1024]{2,0,1:T(8,128)(2,1)}, u32[]{:S(2)}, u32[]{:S(2)}) async-start(bf16[64,4,1024]{2,0,1:T(8,128)(2,1)} %bitcast.70), calls=%async_computation.1 | async-start | bytes 1048576 | tf_op jit(solution)/shard_map/all_to_all | solution.py:258
  22.0 8.8 %convert_element_type.17 = bf16[2,512,2,1024]{3,2,1,0:T(2,128)(2,1)} convert(f32[2,512,2,1024]{3,2,1,0:T(2,128)} %param.27) | non-fusion elementwise | flops 2097152 | bytes 12582912 | tf_op jit(solution)/shard_map/convert_element_type | solution.py:239
  30.9 1.6 slice-done
  32.4 4.1 %copy.50 = bf16[2,256,2,1024]{1,3,2,0:T(8,128)(2,1)} copy(bf16[2,256,2,1024]{3,2,1,0:T(2,128)(2,1)S(1)} %slice-done) | data formatting | bytes 4194304 | tf_op jit(solution)/shard_map/slice | solution.py:241
  36.5 10.1 %reshape.60 = bf16[2,8,32,2,128,8]{2,1,5,4,3,0:T(8,128)(2,1)} reshape(bf16[2,256,2,1024]{1,3,2,0:T(8,128)(2,1)} %copy.50) | data formatting | bytes 4194304 | tf_op jit(solution)/shard_map/reshape | solution.py:241
  46.6 2.7 fusion.5
  49.3 1.1 copy.49
  50.4 7.3 %reshape.59 = bf16[2,8,16,2,128,8]{2,1,5,4,3,0:T(8,128)(2,1)} reshape(bf16[2,128,2,1024]{1,3,2,0:T(8,128)(2,1)S(1)} %copy.49) | data formatting | bytes 2097152 | tf_op jit(solution)/shard_map/reshape | solution.py:241
  57.7 1.0 copy.48
  58.8 7.4 %reshape.58 = bf16[2,8,16,2,128,8]{2,1,5,4,3,0:T(8,128)(2,1)} reshape(bf16[2,128,2,1024]{1,3,2,0:T(8,128)(2,1)S(1)} %copy.48) | data formatting | bytes 2097152 | tf_op jit(solution)/shard_map/reshape | solution.py:241
  66.1 4.3 %collective-permute-start.1 = (bf16[1,4,64,1024]{3,2,1,0:T(8,128)(2,1)}, bf16[1,4,64,1024]{3,2,1,0:T(8,128)(2,1)S(1)}, u32[]{:S(2)}, u32[]{:S(2)}) collective-permute-start(bf16[1,4,64,1024]{3,2,1,0:T(8,128)(2,1)} %bitcast.7), channel_id=1, source_target_pairs={{0,16},{4,20},{8,24},{12,28},{16,0},{20,4},{24,8},{28,12},{1,17},{... | collective-permute-start | bytes 1572872 | tf_op jit(solution)/shard_map/ppermute | solution.py:29
  70.5 14.5 %maximum_bitcast_fusion = bf16[8,2,64,2,8,128]{2,0,4,5,3,1:T(8,128)(2,1)} fusion(bf16[2,8,32,2,128,8]{2,1,5,4,3,0:T(8,128)(2,1)} %reshape.60, bf16[2,8,16,2,128,8]{2,1,5,4,3,0:T(8,128)(2,1)} %reshape.59, bf16[2,8,16,2,128,8]{2,1,5,4,3,0:T(8,128)(2,1)} %reshape.58), kind=kLoop, calls=%fused_computation | loop fusion | flops 12582912 | bytes 8388608 | tf_op jit(solution)/shard_map/transpose | solution.py:244
  85.0 14.0 %copy.51 = bf16[8,2,64,2,8,128]{5,4,3,2,1,0:T(8,128)(2,1)} copy(bf16[8,2,64,2,8,128]{2,0,4,5,3,1:T(8,128)(2,1)} %maximum_bitcast_fusion) | data formatting | bytes 8388608 | tf_op jit(solution)/shard_map/transpose | solution.py:244
  99.0 4.8 %all-to-all-start = ((bf16[8,2,64,2,8,128]{5,4,3,2,1,0:T(8,128)(2,1)}), bf16[8,2,64,2,8,128]{5,4,3,2,1,0:T(8,128)(2,1)}, u32[]{:S(2)}, u32[]{:S(2)}) async-start(bf16[8,2,64,2,8,128]{5,4,3,2,1,0:T(8,128)(2,1)} %copy.51), calls=%async_computation | async-start | bytes 8388608 | tf_op jit(solution)/shard_map/all_to_all | solution.py:245
  103.9 1.1 select_bitcast_fusion.5
  105.1 1.9 collective-permute-start.2
  107.0 67.4 %collective-permute-done.2 = bf16[2,4,64,1024]{3,2,1,0:T(8,128)(2,1)S(1)} collective-permute-done((bf16[2,4,64,1024]{3,2,1,0:T(8,128)(2,1)S(1)}, bf16[2,4,64,1024]{3,2,1,0:T(8,128)(2,1)S(1)}, u32[]{:S(2)}, u32[]{:S(2)}) %collective-permute-start.2) | collective-permute-done | bytes 1048608 | tf_op jit(solution)/shard_map/ppermute | solution.py:29
  174.7 1.5 copy.54
  176.2 3.4 copy.52
  179.6 2.0 copy-done.30
  181.6 1.5 slice.68
  183.1 4.5 %rev.3 = bf16[2,64,7,8,128]{4,3,2,1,0:T(8,128)(2,1)S(1)} reverse(bf16[2,64,7,8,128]{4,3,2,1,0:T(8,128)(2,1)} %slice.68), dimensions={2,3,4} | reverse | bytes 3670016 | tf_op jit(solution)/shard_map/rev | solution.py:248
  188.2 1.9 copy-done.31
  190.7 2.5 select_bitcast_fusion.1
  194.3 2.4 copy.56
  196.8 1.6 copy-done.7
  198.4 10.0 %shard_map.226 = (bf16[512,256]{1,0:T(8,128)(2,1)S(1)}, bf16[256,512]{1,0:T(8,128)(2,1)S(1)}, bf16[256,512]{1,0:T(8,128)(2,1)S(1)}) custom-call(bf16[4,272,1024]{2,1,0:T(8,128)(2,1)S(1)} %bitcast.71, bf16[3,4096,512]{2,1,0:T(8,128)(2,1)} %refs_1_.3, f32[3,3,512]{2,1,0:T(4,128)S(1)} %copy-done.26, bf16[2,64,72,128]{3,2,1,0:T(8,128)(2,1)S(1)} %fusion.3.refs_3_.resp_ref, ...), custom_call_target="tpu_custom_call" | custom-call | flops 3422552064 | bytes 17039360 | tf_op jit(solution)/shard_map/pallas_call | solution.py:78
  208.4 0.8 constant_dynamic-update-slice_fusion.1
  210.0 17.4 %shard_map.227 = (bf16[512,768]{1,0:T(8,128)(2,1)S(1)}, bf16[768,512]{1,0:T(8,128)(2,1)S(1)}, bf16[768,512]{1,0:T(8,128)(2,1)S(1)}) custom-call(bf16[4,784,1024]{2,1,0:T(8,128)(2,1)} %bitcast.91, bf16[3,4096,512]{2,1,0:T(8,128)(2,1)} %refs_1_.3, f32[3,3,512]{2,1,0:T(4,128)S(1)} %copy-done.27), custom_call_target="tpu_custom_call" | custom-call | flops 9865003008 | bytes 25427968 | tf_op jit(solution)/shard_map/pallas_call | solution.py:78
  227.6 0.8 fusion.6
  228.3 9.6 %all_to_all.51.signal_ref = bf16[8,16,1024]{2,1,0:T(8,128)(2,1)S(1)} all-to-all(bf16[8,16,1024]{2,1,0:T(8,128)(2,1)S(1)} %bitcast.89), channel_id=1, replica_groups=mesh['seq'=8,'chan'=4] {'seq'}, dimensions={0} | all-to-all | bytes 524288 | tf_op jit(solution)/shard_map/all_to_all | solution.py:282
  238.0 1.4 shard_map.228
  239.4 9.3 %all_to_all.52 = bf16[8,16,1024]{2,1,0:T(8,128)(2,1)S(1)} all-to-all(bf16[8,16,1024]{2,1,0:T(8,128)(2,1)S(1)} %shard_map.228), channel_id=1, replica_groups=mesh['seq'=8,'chan'=4] {'seq'}, dimensions={0} | all-to-all | bytes 524288 | tf_op jit(solution)/shard_map/all_to_all | solution.py:283
  249.7 1.2 slice.75
  250.9 12.2 %all_to_all.53.signal_ref = bf16[8,32,1024]{2,1,0:T(8,128)(2,1)S(1)} all-to-all(bf16[8,32,1024]{2,1,0:T(8,128)(2,1)S(1)} %bitcast.87), channel_id=1, replica_groups=mesh['seq'=8,'chan'=4] {'seq'}, dimensions={0} | all-to-all | bytes 1048576 | tf_op jit(solution)/shard_map/all_to_all | solution.py:282
  263.1 0.9 copy-done.11
  264.0 0.8 copy-done.15
  264.7 0.8 copy-done.18
  265.5 0.8 copy-done.21
  267.0 2.9 shard_map.232
  270.0 12.2 %all_to_all.54 = bf16[8,32,1024]{2,1,0:T(8,128)(2,1)S(1)} all-to-all(bf16[8,32,1024]{2,1,0:T(8,128)(2,1)S(1)} %shard_map.232), channel_id=1, replica_groups=mesh['seq'=8,'chan'=4] {'seq'}, dimensions={0} | all-to-all | bytes 1048576 | tf_op jit(solution)/shard_map/all_to_all | solution.py:283
  282.8 0.8 copy-done.8
  283.7 10.4 %all_to_all.55.signal_ref = bf16[8,16,1024]{2,1,0:T(8,128)(2,1)S(1)} all-to-all(bf16[8,16,1024]{2,1,0:T(8,128)(2,1)} %bitcast.88), channel_id=1, replica_groups=mesh['seq'=8,'chan'=4] {'seq'}, dimensions={0} | all-to-all | bytes 524288 | tf_op jit(solution)/shard_map/all_to_all | solution.py:282
  294.1 0.9 copy-done.12
  295.0 0.8 copy-done.16
  295.7 0.8 copy-done.19
  296.5 0.8 copy-done.22
  298.0 1.4 shard_map.230
  299.4 9.3 %all_to_all.56 = bf16[8,16,1024]{2,1,0:T(8,128)(2,1)S(1)} all-to-all(bf16[8,16,1024]{2,1,0:T(8,128)(2,1)S(1)} %shard_map.230), channel_id=1, replica_groups=mesh['seq'=8,'chan'=4] {'seq'}, dimensions={0} | all-to-all | bytes 524288 | tf_op jit(solution)/shard_map/all_to_all | solution.py:283
  308.7 0.9 shard_map.231
  309.7 1.9 slice.76
  311.6 0.9 copy-done.29
  312.5 1.1 fusion.4
  313.6 4.8 %fusion.7 = f32[1024,1024]{1,0:T(8,128)} fusion(bf16[1024,512]{1,0:T(8,128)(2,1)} %all-gather.8.cloned.1.call-done, bf16[512,1024]{1,0:T(8,128)(2,1)} %bitcast.90), kind=kOutput, calls=%fused_computation.27 | convolution fusion | flops 1073741824 | bytes 6291456 | tf_op jit(solution)/shard_map/dot_general | solution.py:288
  318.4 11.2 %all-gather.12.cloned.1.call-done = bf16[1024,1024]{1,0:T(8,128)(2,1)} async-done(((bf16[1024,256]{1,0:T(8,128)(2,1)}), bf16[1024,1024]{1,0:T(8,128)(2,1)}) %all-gather.12.cloned.1.call-update) | async-done | bytes 2097168 | tf_op jit(solution)/shard_map/all_gather | solution.py:286
  329.6 5.9 %fusion.8 = f32[1024,1024]{1,0:T(8,128)} fusion(bf16[1024,1024]{1,0:T(8,128)(2,1)} %all-gather.12.cloned.1.call-done, bf16[1024,1024]{1,0:T(8,128)(2,1)S(1)} %bitcast.85), kind=kOutput, calls=%fused_computation.28 | convolution fusion | flops 2147483648 | bytes 8388608 | tf_op jit(solution)/shard_map/dot_general | solution.py:288
  335.5 23.9 %all-gather.10.cloned.1.call-done = bf16[1024,512]{1,0:T(8,128)(2,1)} async-done(((bf16[1024,128]{1,0:T(8,128)(2,1)}), bf16[1024,512]{1,0:T(8,128)(2,1)}) %all-gather.10.cloned.1.call-update) | async-done | bytes 1048592 | tf_op jit(solution)/shard_map/all_gather | solution.py:286
  359.5 6.4 %add_convert_fusion = bf16[1024,1024]{1,0:T(8,128)(2,1)} fusion(f32[1024,1024]{1,0:T(8,128)} %fusion.8, f32[1024,1024]{1,0:T(8,128)} %fusion.7, bf16[1024,512]{1,0:T(8,128)(2,1)} %all-gather.10.cloned.1.call-done, bf16[512,1024]{1,0:T(8,128)(2,1)S(1)} %bitcast.84), kind=kOutput, calls=%fused_computation.8 | convolution fusion | flops 1076887552 | bytes 12582912 | tf_op jit(solution)/shard_map/dot_general | solution.py:288
  (88 shorter events, 7.6 us)
Async XLA Ops:
  6.5 190.2 %all-gather.14.cloned.1.call-start = ((), (), s32[]{:S(2)}) async-start(), calls=%async_computation.11 | async-start | bytes 2785280 | tf_op jit(solution)/shard_map/all_gather | solution.py:272
  7.3 3.4 collective-permute-start
  11.6 197.5 %all-gather.16.cloned.1.call-start = ((), (), s32[]{:S(2)}) async-start(), calls=%async_computation.12 | async-start | bytes 8028160 | tf_op jit(solution)/shard_map/all_gather | solution.py:270
  16.3 49.8 %all-to-all-start.1 = ((bf16[64,4,1024]{2,0,1:T(8,128)(2,1)}), bf16[64,4,1024]{2,0,1:T(8,128)(2,1)}, u32[]{:S(2)}, u32[]{:S(2)}) async-start(bf16[64,4,1024]{2,0,1:T(8,128)(2,1)} %bitcast.70), calls=%async_computation.1 | async-start | bytes 1048576 | tf_op jit(solution)/shard_map/all_to_all | solution.py:258
  30.8 1.6 slice-start
  66.1 37.7 %collective-permute-start.1 = (bf16[1,4,64,1024]{3,2,1,0:T(8,128)(2,1)}, bf16[1,4,64,1024]{3,2,1,0:T(8,128)(2,1)S(1)}, u32[]{:S(2)}, u32[]{:S(2)}) collective-permute-start(bf16[1,4,64,1024]{3,2,1,0:T(8,128)(2,1)} %bitcast.7), channel_id=1, source_target_pairs={{0,16},{4,20},{8,24},{12,28},{16,0},{20,4},{24,8},{28,12},{1,17},{... | collective-permute-start | bytes 1572872 | tf_op jit(solution)/shard_map/ppermute | solution.py:29
  99.0 77.2 %all-to-all-start = ((bf16[8,2,64,2,8,128]{5,4,3,2,1,0:T(8,128)(2,1)}), bf16[8,2,64,2,8,128]{5,4,3,2,1,0:T(8,128)(2,1)}, u32[]{:S(2)}, u32[]{:S(2)}) async-start(bf16[8,2,64,2,8,128]{5,4,3,2,1,0:T(8,128)(2,1)} %copy.51), calls=%async_computation | async-start | bytes 8388608 | tf_op jit(solution)/shard_map/all_to_all | solution.py:245
  103.8 209.9 %all-gather.8.cloned.1.call-start = ((), (), s32[]{:S(2)}) async-start(), calls=%async_computation.8 | async-start | bytes 1310720 | tf_op jit(solution)/shard_map/all_gather | solution.py:286
  105.1 69.2 %collective-permute-start.2 = (bf16[2,4,64,1024]{3,2,1,0:T(8,128)(2,1)S(1)}, bf16[2,4,64,1024]{3,2,1,0:T(8,128)(2,1)S(1)}, u32[]{:S(2)}, u32[]{:S(2)}) collective-permute-start(bf16[2,4,64,1024]{3,2,1,0:T(8,128)(2,1)S(1)} %maximum_bitcast_fusion.1), channel_id=1, source_target_pairs={{0,8},{4,12},{8,0},{12,4},{16,24},{20,28},{24,16},{28,20},{1,9},{5... | collective-permute-start | bytes 3145736 | tf_op jit(solution)/shard_map/ppermute | solution.py:29
  176.2 14.5 %collective-permute-start.3 = (bf16[4,4,64,1024]{3,2,1,0:T(8,128)(2,1)}, bf16[4,4,64,1024]{3,2,1,0:T(8,128)(2,1)}, u32[]{:S(2)}, u32[]{:S(2)}) collective-permute-start(bf16[4,4,64,1024]{3,2,1,0:T(8,128)(2,1)} %bitcast.14), channel_id=1, source_target_pairs={{0,4},{4,0},{8,12},{12,8},{16,20},{20,16},{24,28},{28,24},{1,5},{5... | collective-permute-start | bytes 6291464 | tf_op jit(solution)/shard_map/ppermute | solution.py:29
  179.6 2.0 copy-start.30
  187.9 2.2 copy-start.31
  194.3 2.4 copy-start.26
  196.8 1.6 copy-start.7
  208.4 0.8 copy-start.3
  209.2 0.7 copy-start.27
  209.9 17.5 %copy-start.32 = (bf16[512,1024]{1,0:T(8,128)(2,1)S(1)}, bf16[512,1024]{1,0:T(8,128)(2,1)}, u32[]{:S(2)}) copy-start(bf16[512,1024]{1,0:T(8,128)(2,1)} %constant_dynamic-update-slice_fusion.1) | copy-start | bytes 3145732
  209.9 28.0 %copy-start.9 = (bf16[256,256]{1,0:T(8,128)(2,1)S(1)}, bf16[256,256]{1,0:T(8,128)(2,1)}, u32[]{:S(2)}) copy-start(bf16[256,256]{1,0:T(8,128)(2,1)} %constant.80.clone.fwd_ref) | copy-start | bytes 393220
  209.9 28.0 %copy-start.10 = (bf16[256,256]{1,0:T(8,128)(2,1)S(1)}, bf16[256,256]{1,0:T(8,128)(2,1)}, u32[]{:S(2)}) copy-start(bf16[256,256]{1,0:T(8,128)(2,1)} %constant.81.clone.bwd_ref) | copy-start | bytes 393220
  209.9 28.0 %copy-start.14 = (bf16[144,64]{1,0:T(8,128)(2,1)S(1)}, bf16[144,64]{1,0:T(8,128)(2,1)}, u32[]{:S(2)}) copy-start(bf16[144,64]{1,0:T(8,128)(2,1)} %constant.76.clone.first_ref) | copy-start | bytes 55300
  209.9 28.0 %copy-start.17 = (f32[72,128]{1,0:T(8,128)S(1)}, f32[72,128]{1,0:T(8,128)}, u32[]{:S(2)}) copy-start(f32[72,128]{1,0:T(8,128)} %constant.78.clone.cos_ref) | copy-start | bytes 110596
  209.9 28.0 %copy-start.20 = (f32[72,128]{1,0:T(8,128)S(1)}, f32[72,128]{1,0:T(8,128)}, u32[]{:S(2)}) copy-start(f32[72,128]{1,0:T(8,128)} %constant.79.clone.sin_ref) | copy-start | bytes 110596
  210.0 28.0 %copy-start.23 = (bf16[64,144]{1,0:T(8,128)(2,1)S(1)}, bf16[64,144]{1,0:T(8,128)(2,1)}, u32[]{:S(2)}) copy-start(bf16[64,144]{1,0:T(8,128)(2,1)} %constant.77.clone.last_ref) | copy-start | bytes 55300
  227.4 21.3 %copy-start = (bf16[768,512]{1,0:T(8,128)(2,1)}, bf16[768,512]{1,0:T(8,128)(2,1)S(1)}, u32[]{:S(2)}) copy-start(bf16[768,512]{1,0:T(8,128)(2,1)S(1)} %get-tuple-element.16.refs_3_) | copy-start | bytes 2359300
  227.4 21.3 %copy-start.4 = (bf16[256,512]{1,0:T(8,128)(2,1)S(1)}, bf16[256,512]{1,0:T(8,128)(2,1)}, u32[]{:S(2)}) copy-start(bf16[256,512]{1,0:T(8,128)(2,1)} %copy-done.3) | copy-start | bytes 786436
  227.4 21.3 %copy-start.28 = (f32[512]{0:T(512)S(1)}, f32[512]{0:T(512)}, u32[]{:S(2)}) copy-start(f32[512]{0:T(512)} %param.28) | copy-start | bytes 6148
  227.5 21.2 %copy-start.33 = (bf16[512,1024]{1,0:T(8,128)(2,1)}, bf16[512,1024]{1,0:T(8,128)(2,1)S(1)}, u32[]{:S(2)}) copy-start(bf16[512,1024]{1,0:T(8,128)(2,1)S(1)} %constant_dynamic-update-slice_fusion) | copy-start | bytes 3145732
  248.9 0.7 copy-start.13
  249.7 79.9 %all-gather.12.cloned.1.call-start = ((), (), s32[]{:S(2)}) async-start(), calls=%async_computation.10 | async-start | bytes 2621440 | tf_op jit(solution)/shard_map/all_gather | solution.py:286
  249.7 32.4 %copy-start.1 = (bf16[768,512]{1,0:T(8,128)(2,1)S(1)}, bf16[768,512]{1,0:T(8,128)(2,1)}, u32[]{:S(2)}) copy-start(bf16[768,512]{1,0:T(8,128)(2,1)} %copy-done) | copy-start | bytes 2359300
  249.7 32.4 %copy-start.5 = (bf16[256,512]{1,0:T(8,128)(2,1)S(1)}, bf16[256,512]{1,0:T(8,128)(2,1)}, u32[]{:S(2)}) copy-start(bf16[256,512]{1,0:T(8,128)(2,1)} %copy-done.3) | copy-start | bytes 786436
  263.1 0.9 copy-start.11
  264.0 0.8 copy-start.15
  264.7 0.8 copy-start.18
  265.5 0.8 copy-start.21
  266.3 0.8 copy-start.24
  282.8 0.8 copy-start.8
  283.6 75.9 %all-gather.10.cloned.1.call-start = ((), (), s32[]{:S(2)}) async-start(), calls=%async_computation.9 | async-start | bytes 1310720 | tf_op jit(solution)/shard_map/all_gather | solution.py:286
  283.6 25.1 %copy-start.2 = (bf16[768,512]{1,0:T(8,128)(2,1)S(1)}, bf16[768,512]{1,0:T(8,128)(2,1)}, u32[]{:S(2)}) copy-start(bf16[768,512]{1,0:T(8,128)(2,1)} %copy-done) | copy-start | bytes 2359300
  283.6 25.1 %copy-start.6 = (bf16[256,512]{1,0:T(8,128)(2,1)S(1)}, bf16[256,512]{1,0:T(8,128)(2,1)}, u32[]{:S(2)}) copy-start(bf16[256,512]{1,0:T(8,128)(2,1)} %copy-done.3) | copy-start | bytes 786436
  294.1 0.9 copy-start.12
  295.0 0.8 copy-start.16
  295.7 0.8 copy-start.19
  296.5 0.8 copy-start.22
  297.3 0.8 copy-start.25
  309.7 2.8 copy-start.29
Sparse Core Ops, SparseCore 0:
  11.7 62.6 all-gather.13
  76.0 116.1 all-gather.15
  249.8 29.7 all-gather.7
  283.7 45.8 all-gather.11
  331.0 28.4 all-gather.9

commit v3 on v2

--- a/solution.py
+++ b/solution.py
@@ -10,7 +10,7 @@
 LANES = 128
 HALO = 16
 CHAN_BLOCK = 16
-CHUNK_QUARTERS = (1, 1, 2)
+CHUNKS = 2
 VMEM_BYTES = 48 * 1024 * 1024
 
 
@@ -35,69 +35,91 @@
     return held
 
 
-def chunk_ranges(chans, seq_count):
-    quarter = chans // sum(CHUNK_QUARTERS)
-    if quarter % LANES or (quarter // seq_count) % CHAN_BLOCK:
-        return [(0, chans)]
-    ends = np.cumsum(CHUNK_QUARTERS) * quarter
-    return [(int(end) - size * quarter, int(end)) for end, size in zip(ends, CHUNK_QUARTERS)]
-
-
-def project_kernel(extras, tok_ref, w_ref, taps_ref, *rest):
-    signal_ref, signal_t_ref, query_t_ref, acc = rest[extras:]
-    step = pl.program_id(1)
-    rows = signal_t_ref.shape[0]
-    for p in range(3):
-        part = jnp.dot(tok_ref[0], w_ref[p], preferred_element_type=jnp.float32)
-        acc[p] = part + jnp.where(step == 0, 0.0, acc[p])
-
-    @pl.when(step == pl.num_programs(1) - 1)
+def chunk_count(chans, seq_count):
+    size = chans // CHUNKS
+    return 1 if size % LANES or (size // seq_count) % CHAN_BLOCK else CHUNKS
+
+
+def project_kernel(extras, tok_ref, w_ref, taps_ref, halo_ref, *rest):
+    signal_ref, signal_t_ref, query_t_ref, tok, held, keys, sems = rest[extras:]
+    rows = tok.shape[0]
+    tile = rows // sems.shape[0]
+    stream = pl.program_id(1)
+    first = jnp.logical_and(pl.program_id(0) == 0, stream == 0)
+    pieces = [pl.ds(r, tile) for r in range(0, rows, tile)]
+    copies = [pltpu.make_async_copy(tok_ref.at[p], tok.at[p], sems.at[i]) for i, p in enumerate(pieces)]
+
+    @pl.when(first)
     def _():
-        for p in range(3):
-            acc[p] = acc[p].astype(jnp.bfloat16).astype(jnp.float32)
-        tile = min(LANES, rows)
-        for r in range(0, rows, tile):
-            streams = []
-            for p in range(3):
-                total = taps_ref[0, p][None, :] * acc[p, pl.ds(HALO + r, tile), :]
-                for j in range(1, TAPS):
-                    total = total + taps_ref[j, p][None, :] * acc[p, pl.ds(HALO + r - j, tile), :]
-                streams.append(total)
-            signal = streams[1] * streams[2]
-            query_t_ref[r : r + tile, :] = streams[0].astype(query_t_ref.dtype)
-            signal_t_ref[r : r + tile, :] = signal.astype(signal_t_ref.dtype)
-            signal_ref[:, r : r + tile] = signal.T.astype(signal_ref.dtype)
-
-
-def project(gathered, in_weight, conv_weight, *after):
-    parts, held_rows, depth = gathered.shape
-    rows = held_rows - HALO
+        for copy in copies:
+            copy.start()
+
+    held[0:HALO, :] = halo_ref[0].astype(jnp.float32)
+    for r, copy in zip(range(0, rows, tile), copies):
+        pl.when(first)(copy.wait)
+        part = jnp.dot(tok[r : r + tile, :], w_ref[0], preferred_element_type=jnp.float32)
+        held[HALO + r : HALO + r + tile, :] = part.astype(jnp.bfloat16).astype(jnp.float32)
+
+    def filtered(r, size):
+        total = taps_ref[0, 0] * held[pl.ds(HALO + r, size), :]
+        for j in range(1, TAPS):
+            total = total + taps_ref[0, j] * held[pl.ds(HALO + r - j, size), :]
+        return total
+
+    @pl.when(stream == 0)
+    def _():
+        for r in range(0, rows, LANES):
+            query_t_ref[r : r + LANES, :] = filtered(r, LANES).astype(query_t_ref.dtype)
+
+    @pl.when(stream == 1)
+    def _():
+        for r in range(0, rows, LANES):
+            keys[r : r + LANES, :] = filtered(r, LANES)
+
+    @pl.when(stream == 2)
+    def _():
+        for r in range(0, rows, LANES):
+            signal = keys[r : r + LANES, :] * filtered(r, LANES)
+            signal_t_ref[r : r + LANES, :] = signal.astype(signal_t_ref.dtype)
+            signal_ref[:, r : r + LANES] = signal.T.astype(signal_ref.dtype)
+
+
+def project(gathered, in_weight, conv_weight, halo, *after):
+    rows, depth = gathered.shape
     chans = in_weight.shape[2]
     tile = 2 * LANES if chans % (2 * LANES) == 0 else chans
+    pieces = 4
     flat = jax.ShapeDtypeStruct((rows, chans), jnp.bfloat16)
+    taps = conv_weight.transpose(1, 0, 2)[:, :, None, :]
     return pl.pallas_call(
         lambda *refs: project_kernel(len(after), *refs),
-        grid=(chans // tile, parts),
+        grid=(chans // tile, 3),
         in_specs=[
-            pl.BlockSpec((1, held_rows, depth), lambda i, z: (z, 0, 0)),
-            pl.BlockSpec((3, depth, tile), lambda i, z: (0, z, i)),
-            pl.BlockSpec((TAPS, 3, tile), lambda i, z: (0, 0, i)),
+            pl.BlockSpec(memory_space=pl.ANY),
+            pl.BlockSpec((1, depth, tile), lambda i, p: (p, 0, i)),
+            pl.BlockSpec((1, TAPS, 1, tile), lambda i, p: (p, 0, 0, i)),
+            pl.BlockSpec((1, HALO, tile), lambda i, p: (p, 0, i)),
             *[pl.BlockSpec(memory_space=pl.ANY) for _ in after],
         ],
         out_specs=[
-            pl.BlockSpec((tile, rows), lambda i, z: (i, 0)),
-            pl.BlockSpec((rows, tile), lambda i, z: (0, i)),
-            pl.BlockSpec((rows, tile), lambda i, z: (0, i)),
+            pl.BlockSpec((tile, rows), lambda i, p: (i, 0)),
+            pl.BlockSpec((rows, tile), lambda i, p: (0, i)),
+            pl.BlockSpec((rows, tile), lambda i, p: (0, i)),
         ],
         out_shape=[jax.ShapeDtypeStruct((chans, rows), jnp.bfloat16), flat, flat],
-        scratch_shapes=[pltpu.VMEM((3, held_rows, tile), jnp.float32)],
+        scratch_shapes=[
+            pltpu.VMEM((rows, depth), jnp.bfloat16),
+            pltpu.VMEM((HALO + rows, tile), jnp.float32),
+            pltpu.VMEM((rows, tile), jnp.float32),
+            pltpu.SemaphoreType.DMA((pieces,)),
+        ],
         compiler_params=pltpu.CompilerParams(vmem_limit_bytes=VMEM_BYTES),
         cost_estimate=pl.CostEstimate(
-            flops=2 * 3 * held_rows * depth * parts * chans,
-            bytes_accessed=2 * depth * parts * (3 * chans + 2 * held_rows),
+            flops=2 * 3 * rows * depth * chans,
+            bytes_accessed=2 * depth * (3 * chans + rows),
             transcendentals=0,
         ),
-    )(gathered, in_weight, conv_weight, *after)
+    )(gathered, in_weight, taps, halo, *after)
 
 
 def transform_tables(seq_count, tok_rows):
@@ -232,23 +254,79 @@
     )(longconv, skip[None, :], *given)
 
 
-def folded_response(spectrum, seq_count, ranges):
+def reorder_kernel(spec_ref, order_ref, out_ref):
+    each = out_ref.shape[3]
+    x = spec_ref[0].astype(jnp.bfloat16)
+    y = jnp.dot(x, order_ref[...], preferred_element_type=jnp.float32).astype(jnp.bfloat16)
+    for d in range(out_ref.shape[0]):
+        out_ref[d, 0, 0] = y[d * each : (d + 1) * each]
+
+
+def fold_kernel(got_ref, out_ref, came, held):
+    seq_count, pairs, tok_rows = got_ref.shape[0], got_ref.shape[3], got_ref.shape[4]
+    chans = pairs // 2
+    runs = tok_rows // LANES
+    rows = (seq_count + 1) * runs
+    for part in range(2):
+        sign = 1.0 if part == 0 else -1.0
+        for s in range(seq_count):
+            for r in range(runs):
+                at = (s * runs + r) * pairs
+                lanes = slice(r * LANES, (r + 1) * LANES)
+                came[at : at + pairs, :] = got_ref[s, part, 0, :, lanes].astype(jnp.float32)
+        for k1 in range(seq_count + 1):
+            other = 2 * seq_count - k1
+            for r in range(runs):
+                value = came[pl.ds((k1 // 2 * runs + r) * pairs + k1 % 2, chans, stride=2), :]
+                if k1 == seq_count:
+                    value = sign * value
+                elif k1 > 0:
+                    value = value + sign * came[pl.ds((other // 2 * runs + r) * pairs + other % 2, chans, stride=2), :]
+                held[pl.ds(k1 * runs + r, chans, stride=rows), :] = value
+        out_ref[part] = held[...].reshape(chans, rows, LANES).astype(out_ref.dtype)
+
+
+def folded_response(spectrum, seq_count, chunks):
     parts, chans, own, tok_rows = spectrum.shape
     runs = tok_rows // LANES
-    each = chans // seq_count
-    sent = spectrum.astype(jnp.bfloat16)
-    sent = jnp.concatenate(
-        [sent[:, lo:hi].reshape(parts, seq_count, (hi - lo) // seq_count, own, LANES, runs) for lo, hi in ranges],
-        axis=2,
-    )
-    sent = sent.transpose(1, 0, 2, 3, 5, 4)
+    size = chans // chunks
+    each = size // seq_count
+    col = lax.broadcasted_iota(jnp.int32, (tok_rows, tok_rows), 1)
+    row = lax.broadcasted_iota(jnp.int32, (tok_rows, tok_rows), 0)
+    wanted = col // LANES + runs * (col % LANES)
+    wanted = jnp.where(lax.axis_index("seq") >= seq_count // 2, tok_rows - 1 - wanted, wanted)
+    order = (row == wanted).astype(jnp.bfloat16)
+    shape = (seq_count, parts, chunks, own * each, tok_rows)
+    sent = pl.pallas_call(
+        reorder_kernel,
+        grid=(parts, chunks),
+        in_specs=[
+            pl.BlockSpec((1, own * size, tok_rows), lambda p, j: (p, j, 0)),
+            pl.BlockSpec((tok_rows, tok_rows), lambda p, j: (0, 0)),
+        ],
+        out_specs=pl.BlockSpec((seq_count, 1, 1, own * each, tok_rows), lambda p, j: (0, p, j, 0, 0)),
+        out_shape=jax.ShapeDtypeStruct(shape, jnp.bfloat16),
+        compiler_params=pltpu.CompilerParams(vmem_limit_bytes=VMEM_BYTES),
+        cost_estimate=pl.CostEstimate(
+            flops=2 * spectrum.size * tok_rows, bytes_accessed=6 * spectrum.size, transcendentals=0
+        ),
+    )(spectrum.reshape(parts, chans * own, tok_rows), order)
     got = lax.all_to_all(sent, "seq", split_axis=0, concat_axis=0, tiled=True)
-    got = got.transpose(1, 2, 0, 3, 4, 5).reshape(parts, each, own * seq_count, runs, LANES)
-    kept = got[:, :, : seq_count + 1].astype(jnp.float32)
-    mirror = got[:, :, seq_count + 1 :][:, :, ::-1, ::-1, ::-1].astype(jnp.float32)
-    mirror = jnp.stack([mirror[0], -mirror[1]])
-    mirror = jnp.pad(mirror, ((0, 0), (0, 0), (1, 1), (0, 0), (0, 0)))
-    return (kept + mirror).astype(jnp.bfloat16).reshape(parts, each, (seq_count + 1) * runs, LANES)
+    block = min(CHAN_BLOCK, each)
+    rows = (seq_count + 1) * runs
+    return pl.pallas_call(
+        fold_kernel,
+        grid=(chunks, each // block),
+        in_specs=[pl.BlockSpec((seq_count, parts, 1, own * block, tok_rows), lambda j, i: (0, 0, j, i, 0))],
+        out_specs=pl.BlockSpec((parts, block, rows, LANES), lambda j, i: (0, j * (each // block) + i, 0, 0)),
+        out_shape=jax.ShapeDtypeStruct((parts, chans // seq_count, rows, LANES), jnp.bfloat16),
+        scratch_shapes=[
+            pltpu.VMEM((seq_count * runs * own * block, LANES), jnp.float32),
+            pltpu.VMEM((block * rows, LANES), jnp.float32),
+        ],
+        compiler_params=pltpu.CompilerParams(vmem_limit_bytes=VMEM_BYTES),
+        cost_estimate=pl.CostEstimate(flops=spectrum.size, bytes_accessed=3 * spectrum.size, transcendentals=0),
+    )(got)
 
 
 def feature_slice(out_weight, seq_count):
@@ -262,29 +340,34 @@
 
 
 def shards(tokens, in_weight, conv_weight, spectrum, skip, out_weight):
-    tok_rows = tokens.shape[0]
+    tok_rows, depth = tokens.shape
     seq_count = lax.axis_size("seq")
+    chan_count = lax.axis_size("chan")
     chans = in_weight.shape[2]
-    ranges = chunk_ranges(chans, seq_count)
-    cut = tok_rows // 4
-    later = lax.all_gather(tokens[cut - HALO :], "chan")
-    halo = from_behind(tokens[tok_rows - HALO :], "seq", 1)
-    earlier = lax.all_gather(jnp.concatenate([halo, tokens[:cut]], axis=0), "chan")
-    response = folded_response(spectrum, seq_count, ranges)
+    chunks = chunk_count(chans, seq_count)
+    size = chans // chunks
+    gathered = lax.all_gather(tokens, "chan", axis=1, tiled=True)
+    halo = gather_by_doubling(from_behind(tokens[tok_rows - HALO :], "seq", 1), "chan")
+    halo = jnp.einsum(
+        "ztd,pzdc->ptc",
+        halo,
+        in_weight.reshape(3, chan_count, depth, chans),
+        preferred_element_type=jnp.float32,
+    ).astype(jnp.bfloat16)
+    response = folded_response(spectrum, seq_count, chunks)
     weight_slice = feature_slice(out_weight, seq_count)
-    signal_b, signal_bt, query_bt = project(later, in_weight, conv_weight)
-    signal_a, signal_at, query_at = project(earlier, in_weight, conv_weight, response, weight_slice)
-    signal = jnp.concatenate([signal_a, signal_b], axis=1)
-    pieces = ((signal_at, query_at), (signal_bt, query_bt))
+    signal, signal_t, query_t = project(gathered, in_weight, conv_weight, halo, response, weight_slice)
     total = None
-    for lo, hi in ranges:
-        values = signal[lo:hi].reshape(seq_count, (hi - lo) // seq_count, tok_rows)
+    for lo in range(0, chans, size):
+        values = signal[lo : lo + size].reshape(seq_count, size // seq_count, tok_rows)
         values = lax.all_to_all(values, "seq", split_axis=0, concat_axis=0, tiled=True)
         longconv = lax.all_to_all(
             long_conv(values, response, lo // seq_count), "seq", split_axis=0, concat_axis=0, tiled=True
-        ).reshape(hi - lo, tok_rows)
-        gated = lax.all_gather(gate(longconv, skip, lo, pieces), "chan", axis=1, tiled=True)
-        weight = weight_slice[:, lo:hi].reshape(gated.shape[1], weight_slice.shape[2])
+        ).reshape(size, tok_rows)
+        gated = lax.all_gather(
+            gate(longconv, skip, lo, ((signal_t, query_t),)), "chan", axis=1, tiled=True
+        )
+        weight = weight_slice[:, lo : lo + size].reshape(gated.shape[1], weight_slice.shape[2])
         term = jnp.dot(gated, weight, preferred_element_type=jnp.float32)
         total = term if total is None else total + term
     return total.astype(jnp.bfloat16)

time: 374 us -> 355 us (0.949)
  local copies, waits for them, and re-layouts: 92.5 us -> 28.1 us
  waiting for transfers between devices: 103 us -> 157 us
  other arithmetic: 29.6 us -> 4.17 us
  Pallas kernels: 34.8 us -> 55.8 us
  blocking collectives: 63 us -> 49.8 us
  starting transfers between devices: 19.2 us -> 26.2 us
    all_to_all x1, waiting for transfers between devices: 0.01 us -> 23.3 us  [feature_slice(): own = lax.all_to_all(own, 'chan', split_axis=1, concat_axis=0, tiled=True)]
    ppermute x3 -> x5, waiting for transfers between devices: 67.4 us -> 85.5 us  [gather_by_doubling(): other = lax.ppermute(held, axis, [(i, i ^ bit) for i in range(size)])]
    slice x15 -> x3, local copies, waits for them, and re-layouts: 21.6 us -> 5.82 us  [the longest x1 4.2 us: shards(): weight_slice[:, lo:lo + size].reshape(gated.shape[1], weight_slice.shape[2])]
    transpose x1 -> x0, other arithmetic: 14.5 us -> none  [folded_response(): sent = sent.transpose(1, 0, 2, 3, 5, 4)]
    transpose x1 -> x0, local copies, waits for them, and re-layouts: 14 us -> none  [folded_response(): sent = sent.transpose(1, 0, 2, 3, 5, 4)]
    reshape x3 -> x1, local copies, waits for them, and re-layouts: 24.8 us -> 10.9 us  [folded_response(): spectrum.reshape(parts, chans * own, tok_rows)]
    unnamed x69 -> x33, local copies, waits for them, and re-layouts: 17.4 us -> 4.82 us
    pallas_call x0 -> x2, Pallas kernels: none -> 12.5 us  [the longest x1 8.47 us: folded_response(): pl.pallas_call(reorder_kernel, grid=(parts, chunks), in_specs=[pl.BlockSp...]
  transfers between devices with their start and end apart: 11 -> 11, of which waited for: 3 -> 7; matrix products, arithmetic and copies ran while one was open for 30% -> 11% of each run, Pallas kernels for 4% -> 5%
where the time goes in v3:
time: 355 us; the launch traced here: 354 us
  waiting for transfers between devices  157 us (44%)
  Pallas kernels  55.8 us (16%)
  blocking collectives  49.8 us (14%)
  local copies, waits for them, and re-layouts  28.1 us (8%)
  starting transfers between devices  26.2 us (7%)
  matrix products  19.3 us (5%)
  between operations  13.5 us (4%)
  other arithmetic  4.17 us (1%)
    ppermute x5, waiting for transfers between devices, gather_by_doubling(): other = lax.ppermute(held, axis, [(i, i ^ bit) for i in range(size)])  85.5 us
    all_gather x2, waiting for transfers between devices, shards(): lax.all_gather(gate(longconv, skip, lo, ((signal_t, query_t),)), 'chan',...  46.3 us
    pallas_call x1, Pallas kernels, project(): pl.pallas_call(lambda *refs: project_kernel(len(after), *refs), grid=(cha...  35.6 us
    all_to_all x2, blocking collectives, shards(): lax.all_to_all(values, 'seq', split_axis=0, concat_axis=0, tiled=True)  25.5 us
    all_to_all x2, blocking collectives, shards(): lax.all_to_all(long_conv(values, response, lo // seq_count), 'seq', split...  24.3 us
    all_to_all x1, waiting for transfers between devices, feature_slice(): own = lax.all_to_all(own, 'chan', split_axis=1, concat_axis=0, tiled=True)  23.3 us
    dot_general x2, matrix products, shards(): term = jnp.dot(gated, weight, preferred_element_type=jnp.float32)  13 us
    ppermute x5, starting transfers between devices, gather_by_doubling(): other = lax.ppermute(held, axis, [(i, i ^ bit) for i in range(size)])  12.8 us
  transfers between devices with their start and end apart: 11, of which 7 were waited for; matrix products, arithmetic and copies ran while one was open for 11% of the time, Pallas kernels for 5%

profile of v3, /device:TPU:0, one launch (start us, length us, event | category | flops | bytes accessed | tf_op | source)
XLA Modules:
  0.0 353.6 jit_solution(7504734567723548301)
XLA Ops:
  6.5 0.7 all-gather.4.cloned.1.call-update
  7.3 1.1 constant_dynamic-slice_fusion
  8.3 0.8 copy.48
  9.2 6.3 %all-to-all-start.1 = ((bf16[64,4,1024]{2,0,1:T(8,128)(2,1)}), bf16[64,4,1024]{2,0,1:T(8,128)(2,1)S(1)}, u32[]{:S(2)}, u32[]{:S(2)}) async-start(bf16[64,4,1024]{2,0,1:T(8,128)(2,1)} %bitcast.78), calls=%async_computation.1 | async-start | bytes 1048576 | tf_op jit(solution)/shard_map/all_to_all | solution.py:336
  15.5 23.3 %all-to-all-done.1 = bf16[64,4,1024]{2,0,1:T(8,128)(2,1)S(1)} async-done(((bf16[64,4,1024]{2,0,1:T(8,128)(2,1)}), bf16[64,4,1024]{2,0,1:T(8,128)(2,1)S(1)}, u32[]{:S(2)}, u32[]{:S(2)}) %all-to-all-start.1) | async-done | bytes 524320 | tf_op jit(solution)/shard_map/all_to_all | solution.py:336
  38.9 1.5 collective-permute-start.3
  40.4 0.7 fusion.1.order_ref
  41.1 10.9 %reshape.49.spec_ref = f32[2,1024,1024]{2,1,0:T(8,128)} reshape(f32[2,512,2,1024]{3,2,1,0:T(2,128)} %param.21) | data formatting | bytes 16777216 | tf_op jit(solution)/shard_map/reshape | solution.py:313
  52.0 8.5 %shard_map.172 = bf16[8,2,2,64,1024]{4,3,2,1,0:T(8,128)(2,1)} custom-call(f32[2,1024,1024]{2,1,0:T(8,128)} %reshape.49.spec_ref, bf16[1024,1024]{1,0:T(8,128)(2,1)S(1)} %fusion.1.order_ref), custom_call_target="tpu_custom_call" | custom-call | flops 4294967296 | bytes 12582912 | tf_op jit(solution)/shard_map/pallas_call | solution.py:300
  60.5 4.6 %all-to-all-start = ((bf16[8,2,2,64,1024]{4,3,2,1,0:T(8,128)(2,1)}), bf16[8,2,2,64,1024]{4,3,2,1,0:T(8,128)(2,1)}, u32[]{:S(2)}, u32[]{:S(2)}) async-start(bf16[8,2,2,64,1024]{4,3,2,1,0:T(8,128)(2,1)} %shard_map.172), calls=%async_computation | async-start | bytes 8388608 | tf_op jit(solution)/shard_map/all_to_all | solution.py:314
  65.1 0.0 all-gather.6.cloned.1.call-start
  65.2 0.0 collective-permute-done.3
  65.2 0.1 select_bitcast_fusion.5
  65.3 0.1 maximum_bitcast_fusion
  65.4 1.9 collective-permute-start.4
  67.3 68.4 %collective-permute-done.4 = bf16[2,4,64,1024]{3,2,1,0:T(8,128)(2,1)S(1)} collective-permute-done((bf16[2,4,64,1024]{3,2,1,0:T(8,128)(2,1)S(1)}, bf16[2,4,64,1024]{3,2,1,0:T(8,128)(2,1)S(1)}, u32[]{:S(2)}, u32[]{:S(2)}) %collective-permute-start.4) | collective-permute-done | bytes 1048608 | tf_op jit(solution)/shard_map/ppermute | solution.py:29
  135.7 0.1 select_bitcast_fusion.3
  135.8 0.2 pad_maximum_fusion.1
  136.0 0.0 copy-start.15
  136.0 1.5 copy.41
  137.5 0.8 slice.15
  138.3 2.4 collective-permute-start
  140.7 0.8 collective-permute-done
  141.5 6.5 %collective-permute-done.1 = bf16[1,16,1024]{2,1,0:T(8,128)(2,1)S(1)} collective-permute-done((bf16[1,16,1024]{2,1,0:T(8,128)(2,1)S(1)}, bf16[1,16,1024]{2,1,0:T(8,128)(2,1)S(1)}, u32[]{:S(2)}, u32[]{:S(2)}) %collective-permute-start.1) | collective-permute-done | bytes 32800 | tf_op jit(solution)/shard_map/ppermute | solution.py:29
  148.1 9.4 %collective-permute-start.2 = (bf16[2,16,1024]{2,1,0:T(8,128)(2,1)S(1)}, bf16[2,16,1024]{2,1,0:T(8,128)(2,1)S(1)}, u32[]{:S(2)}, u32[]{:S(2)}) collective-permute-start(bf16[2,16,1024]{2,1,0:T(8,128)(2,1)S(1)} %maximum_bitcast_fusion.1), channel_id=1, source_target_pairs={{0,1},{1,0},{2,3},{3,2},{4,5},{5,4},{6,7},{7,6},{8,9},{9,8},{10,11... | collective-permute-start | bytes 196616 | tf_op jit(solution)/shard_map/ppermute | solution.py:29
  157.5 10.5 %collective-permute-done.2 = bf16[2,16,1024]{2,1,0:T(8,128)(2,1)S(1)} collective-permute-done((bf16[2,16,1024]{2,1,0:T(8,128)(2,1)S(1)}, bf16[2,16,1024]{2,1,0:T(8,128)(2,1)S(1)}, u32[]{:S(2)}, u32[]{:S(2)}) %collective-permute-start.2) | collective-permute-done | bytes 65568 | tf_op jit(solution)/shard_map/ppermute | solution.py:29
  168.1 6.3 %fusion.3.refs_3_ = bf16[3,16,512]{2,1,0:T(8,128)(2,1)S(1)} fusion(bf16[4,16,1024,1]{2,1,0,3:T(8,128)(2,1)S(1)} %bitcast.94, bf16[3,4,1024,512]{3,2,1,0:T(8,128)(2,1)} %bitcast.87), kind=kOutput, calls=%fused_computation.10 | convolution fusion | flops 201351168 | bytes 12763136 | tf_op jit(solution)/shard_map/ztd,pzdc->ptc/dot_general | solution.py:351
  174.4 4.1 %shard_map.173.refs_4_.resp_ref = bf16[2,64,72,128]{3,2,1,0:T(8,128)(2,1)S(1)} custom-call(bf16[8,2,2,64,1024]{4,3,2,1,0:T(8,128)(2,1)} %all-to-all-done.got_ref), custom_call_target="tpu_custom_call" | custom-call | flops 2097152 | bytes 6291456 | tf_op jit(solution)/shard_map/pallas_call | solution.py:317
  178.5 2.5 select_bitcast_fusion.1
  181.0 0.4 pad_maximum_fusion
  181.4 0.7 copy.42
  182.1 2.5 copy.43
  184.6 35.6 %shard_map.174 = (bf16[512,1024]{1,0:T(8,128)(2,1)S(1)}, bf16[1024,512]{1,0:T(8,128)(2,1)S(1)}, bf16[1024,512]{1,0:T(8,128)(2,1)S(1)}) custom-call(bf16[1024,4096]{1,0:T(8,128)(2,1)} %all-gather.4.cloned.1.call-done.refs_0_, bf16[3,4096,512]{2,1,0:T(8,128)(2,1)} %refs_1_.1, f32[3,3,1,512]{3,2,1,0:T(1,128)S(1)} %broadcast_in_dim.10.refs_2_, ...), custom_call_target="tpu_custom_call" | custom-call | flops 12884901888 | bytes 20971520 | tf_op jit(solution)/shard_map/pallas_call | solution.py:94
  220.1 0.0 copy-start
  220.2 0.0 copy-start.3
  220.2 0.0 copy-start.4
  220.2 0.0 copy-start.6
  220.2 0.0 copy-start.8
  220.2 0.0 copy-start.10
  220.2 0.0 copy-start.12
  220.2 0.9 fusion.11
  221.1 12.3 %all_to_all.41.signal_ref = bf16[8,32,1024]{2,1,0:T(8,128)(2,1)S(1)} all-to-all(bf16[8,32,1024]{2,1,0:T(8,128)(2,1)S(1)} %bitcast.91), channel_id=1, replica_groups=mesh['seq'=8,'chan'=4] {'seq'}, dimensions={0} | all-to-all | bytes 1048576 | tf_op jit(solution)/shard_map/all_to_all | solution.py:363
  233.4 0.0 copy-start.14
  233.4 3.0 shard_map.175
  236.4 12.2 %all_to_all.42 = bf16[8,32,1024]{2,1,0:T(8,128)(2,1)S(1)} all-to-all(bf16[8,32,1024]{2,1,0:T(8,128)(2,1)S(1)} %shard_map.175), channel_id=1, replica_groups=mesh['seq'=8,'chan'=4] {'seq'}, dimensions={0} | all-to-all | bytes 1048576 | tf_op jit(solution)/shard_map/all_to_all | solution.py:364
  248.6 0.6 shard_map.176
  249.2 0.8 copy-done.2
  250.0 0.0 all-gather.6.cloned.1.call-update
  250.0 0.0 all-gather.8.cloned.1.call-start
  250.0 13.2 %all_to_all.43.signal_ref = bf16[8,32,1024]{2,1,0:T(8,128)(2,1)S(1)} all-to-all(bf16[8,32,1024]{2,1,0:T(8,128)(2,1)} %bitcast.90), channel_id=1, replica_groups=mesh['seq'=8,'chan'=4] {'seq'}, dimensions={0} | all-to-all | bytes 1048576 | tf_op jit(solution)/shard_map/all_to_all | solution.py:363
  263.2 0.9 copy-done.5
  264.1 0.8 copy-done.7
  264.9 0.8 copy-done.9
  265.6 0.8 copy-done.11
  266.4 0.8 copy-done.13
  267.2 2.9 shard_map.177
  270.1 12.2 %all_to_all.44 = bf16[8,32,1024]{2,1,0:T(8,128)(2,1)S(1)} all-to-all(bf16[8,32,1024]{2,1,0:T(8,128)(2,1)S(1)} %shard_map.177), channel_id=1, replica_groups=mesh['seq'=8,'chan'=4] {'seq'}, dimensions={0} | all-to-all | bytes 1048576 | tf_op jit(solution)/shard_map/all_to_all | solution.py:364
  282.3 1.2 shard_map.178
  283.5 0.0 all-gather.8.cloned.1.call-update
  283.5 4.2 %fusion.10 = (bf16[4,256,1024]{2,1,0:T(8,128)(2,1)S(1)}, bf16[4,256,1024]{2,1,0:T(8,128)(2,1)}) fusion(bf16[4,512,1024]{2,1,0:T(8,128)(2,1)} %bitcast.85), kind=kLoop, calls=%fused_computation.35 | loop fusion | bytes 8388608 | tf_op jit(solution)/shard_map/slice | solution.py:370
  287.7 6.8 %all-gather.6.cloned.1.call-done = bf16[1024,1024]{1,0:T(8,128)(2,1)} async-done(((bf16[1024,256]{1,0:T(8,128)(2,1)}), bf16[1024,1024]{1,0:T(8,128)(2,1)}) %all-gather.6.cloned.1.call-update) | async-done | bytes 2097168 | tf_op jit(solution)/shard_map/all_gather | solution.py:367
  294.5 6.5 %fusion.12 = f32[1024,1024]{1,0:T(8,128)} fusion(bf16[1024,1024]{1,0:T(8,128)(2,1)} %all-gather.6.cloned.1.call-done, bf16[1024,1024]{1,0:T(8,128)(2,1)} %bitcast.93), kind=kOutput, calls=%fused_computation.37 | convolution fusion | flops 2147483648 | bytes 8388608 | tf_op jit(solution)/shard_map/dot_general | solution.py:371
  301.1 39.6 %all-gather.8.cloned.1.call-done = bf16[1024,1024]{1,0:T(8,128)(2,1)} async-done(((bf16[1024,256]{1,0:T(8,128)(2,1)}), bf16[1024,1024]{1,0:T(8,128)(2,1)}) %all-gather.8.cloned.1.call-update) | async-done | bytes 2097168 | tf_op jit(solution)/shard_map/all_gather | solution.py:367
  340.6 6.5 %add_convert_fusion = bf16[1024,1024]{1,0:T(8,128)(2,1)} fusion(f32[1024,1024]{1,0:T(8,128)} %fusion.12, bf16[1024,1024]{1,0:T(8,128)(2,1)} %all-gather.8.cloned.1.call-done, bf16[1024,1024]{1,0:T(8,128)(2,1)S(1)} %bitcast.92), kind=kOutput, calls=%fused_computation.3 | convolution fusion | flops 2149580800 | bytes 10485760 | tf_op jit(solution)/shard_map/dot_general | solution.py:371
  (33 shorter events, 0.1 us)
Async XLA Ops:
  6.5 178.0 %all-gather.4.cloned.1.call-start = ((), (), s32[]{:S(2)}) async-start(), calls=%async_computation.6 | async-start | bytes 10485760 | tf_op jit(solution)/shard_map/all_gather | solution.py:349
  9.2 29.7 %all-to-all-start.1 = ((bf16[64,4,1024]{2,0,1:T(8,128)(2,1)}), bf16[64,4,1024]{2,0,1:T(8,128)(2,1)S(1)}, u32[]{:S(2)}, u32[]{:S(2)}) async-start(bf16[64,4,1024]{2,0,1:T(8,128)(2,1)} %bitcast.78), calls=%async_computation.1 | async-start | bytes 1048576 | tf_op jit(solution)/shard_map/all_to_all | solution.py:336
  38.9 26.3 %collective-permute-start.3 = (bf16[1,4,64,1024]{3,2,1,0:T(8,128)(2,1)S(1)}, bf16[1,4,64,1024]{3,2,1,0:T(8,128)(2,1)S(1)}, u32[]{:S(2)}, u32[]{:S(2)}) collective-permute-start(bf16[1,4,64,1024]{3,2,1,0:T(8,128)(2,1)S(1)} %bitcast.88), channel_id=1, source_target_pairs={{0,16},{4,20},{8,24},{12,28},{16,0},{20,4},{24,8},{28,12},{1,17},{... | collective-permute-start | bytes 1572872 | tf_op jit(solution)/shard_map/ppermute | solution.py:29
  60.5 113.9 %all-to-all-start = ((bf16[8,2,2,64,1024]{4,3,2,1,0:T(8,128)(2,1)}), bf16[8,2,2,64,1024]{4,3,2,1,0:T(8,128)(2,1)}, u32[]{:S(2)}, u32[]{:S(2)}) async-start(bf16[8,2,2,64,1024]{4,3,2,1,0:T(8,128)(2,1)} %shard_map.172), calls=%async_computation | async-start | bytes 8388608 | tf_op jit(solution)/shard_map/all_to_all | solution.py:314
  65.1 229.4 %all-gather.6.cloned.1.call-start = ((), (), s32[]{:S(2)}) async-start(), calls=%async_computation.7 | async-start | bytes 2621440 | tf_op jit(solution)/shard_map/all_gather | solution.py:367
  65.4 70.3 %collective-permute-start.4 = (bf16[2,4,64,1024]{3,2,1,0:T(8,128)(2,1)S(1)}, bf16[2,4,64,1024]{3,2,1,0:T(8,128)(2,1)S(1)}, u32[]{:S(2)}, u32[]{:S(2)}) collective-permute-start(bf16[2,4,64,1024]{3,2,1,0:T(8,128)(2,1)S(1)} %maximum_bitcast_fusion), channel_id=1, source_target_pairs={{0,8},{4,12},{8,0},{12,4},{16,24},{20,28},{24,16},{28,20},{1,9},{5... | collective-permute-start | bytes 3145736 | tf_op jit(solution)/shard_map/ppermute | solution.py:29
  136.0 21.5 %copy-start.15 = (f32[3,3,512]{2,1,0:T(4,128)S(1)}, f32[3,3,512]{2,1,0:T(4,128)}, u32[]{:S(2)}) copy-start(f32[3,3,512]{2,1,0:T(4,128)} %param.20) | copy-start | bytes 55300
  137.5 41.0 %collective-permute-start.5 = (bf16[4,4,64,1024]{3,2,1,0:T(8,128)(2,1)}, bf16[4,4,64,1024]{3,2,1,0:T(8,128)(2,1)}, u32[]{:S(2)}, u32[]{:S(2)}) collective-permute-start(bf16[4,4,64,1024]{3,2,1,0:T(8,128)(2,1)} %bitcast.21), channel_id=1, source_target_pairs={{0,4},{4,0},{8,12},{12,8},{16,20},{20,16},{24,28},{28,24},{1,5},{5... | collective-permute-start | bytes 6291464 | tf_op jit(solution)/shard_map/ppermute | solution.py:29
  138.3 3.2 collective-permute-start
  141.5 6.5 %collective-permute-start.1 = (bf16[1,16,1024]{2,1,0:T(8,128)(2,1)S(1)}, bf16[1,16,1024]{2,1,0:T(8,128)(2,1)S(1)}, u32[]{:S(2)}, u32[]{:S(2)}) collective-permute-start(bf16[1,16,1024]{2,1,0:T(8,128)(2,1)S(1)} %bitcast.96), channel_id=1, source_target_pairs={{0,2},{1,3},{2,0},{3,1},{4,6},{5,7},{6,4},{7,5},{8,10},{9,11},{10,... | collective-permute-start | bytes 98312 | tf_op jit(solution)/shard_map/ppermute | solution.py:29
  148.1 20.0 %collective-permute-start.2 = (bf16[2,16,1024]{2,1,0:T(8,128)(2,1)S(1)}, bf16[2,16,1024]{2,1,0:T(8,128)(2,1)S(1)}, u32[]{:S(2)}, u32[]{:S(2)}) collective-permute-start(bf16[2,16,1024]{2,1,0:T(8,128)(2,1)S(1)} %maximum_bitcast_fusion.1), channel_id=1, source_target_pairs={{0,1},{1,0},{2,3},{3,2},{4,5},{5,4},{6,7},{7,6},{8,9},{9,8},{10,11... | collective-permute-start | bytes 196616 | tf_op jit(solution)/shard_map/ppermute | solution.py:29
  220.1 28.4 %copy-start = (bf16[1024,512]{1,0:T(8,128)(2,1)}, bf16[1024,512]{1,0:T(8,128)(2,1)S(1)}, u32[]{:S(2)}) copy-start(bf16[1024,512]{1,0:T(8,128)(2,1)S(1)} %get-tuple-element.10.refs_1_) | copy-start | bytes 3145732
  220.2 13.2 %copy-start.3 = (bf16[256,256]{1,0:T(8,128)(2,1)S(1)}, bf16[256,256]{1,0:T(8,128)(2,1)}, u32[]{:S(2)}) copy-start(bf16[256,256]{1,0:T(8,128)(2,1)} %constant.138.clone.fwd_ref) | copy-start | bytes 393220
  220.2 13.2 %copy-start.4 = (bf16[256,256]{1,0:T(8,128)(2,1)S(1)}, bf16[256,256]{1,0:T(8,128)(2,1)}, u32[]{:S(2)}) copy-start(bf16[256,256]{1,0:T(8,128)(2,1)} %constant.139.clone.bwd_ref) | copy-start | bytes 393220
  220.2 13.2 %copy-start.6 = (bf16[144,64]{1,0:T(8,128)(2,1)S(1)}, bf16[144,64]{1,0:T(8,128)(2,1)}, u32[]{:S(2)}) copy-start(bf16[144,64]{1,0:T(8,128)(2,1)} %constant.134.clone.first_ref) | copy-start | bytes 55300
  220.2 13.2 %copy-start.8 = (f32[72,128]{1,0:T(8,128)S(1)}, f32[72,128]{1,0:T(8,128)}, u32[]{:S(2)}) copy-start(f32[72,128]{1,0:T(8,128)} %constant.136.clone.cos_ref) | copy-start | bytes 110596
  220.2 13.2 %copy-start.10 = (f32[72,128]{1,0:T(8,128)S(1)}, f32[72,128]{1,0:T(8,128)}, u32[]{:S(2)}) copy-start(f32[72,128]{1,0:T(8,128)} %constant.137.clone.sin_ref) | copy-start | bytes 110596
  220.2 13.2 %copy-start.12 = (bf16[64,144]{1,0:T(8,128)(2,1)S(1)}, bf16[64,144]{1,0:T(8,128)(2,1)}, u32[]{:S(2)}) copy-start(bf16[64,144]{1,0:T(8,128)(2,1)} %constant.135.clone.last_ref) | copy-start | bytes 55300
  233.4 15.1 %copy-start.14 = (f32[512]{0:T(512)S(1)}, f32[512]{0:T(512)}, u32[]{:S(2)}) copy-start(f32[512]{0:T(512)} %param.22) | copy-start | bytes 6148
  249.2 0.8 copy-start.2
  250.0 90.6 %all-gather.8.cloned.1.call-start = ((), (), s32[]{:S(2)}) async-start(), calls=%async_computation.8 | async-start | bytes 2621440 | tf_op jit(solution)/shard_map/all_gather | solution.py:367
  263.2 0.9 copy-start.5
  264.1 0.8 copy-start.7
  264.9 0.8 copy-start.9
  265.6 0.8 copy-start.11
  266.4 0.8 copy-start.13
  267.2 15.1 %copy-start.1 = (bf16[1024,512]{1,0:T(8,128)(2,1)S(1)}, bf16[1024,512]{1,0:T(8,128)(2,1)}, u32[]{:S(2)}) copy-start(bf16[1024,512]{1,0:T(8,128)(2,1)} %copy-done) | copy-start | bytes 3145732
Sparse Core Ops, SparseCore 0:
  8.9 158.1 all-gather.3
  250.1 44.3 all-gather.5
  296.1 44.4 all-gather.7

commit v4 on v3

--- a/solution.py
+++ b/solution.py
@@ -18,6 +18,15 @@
     size = lax.axis_size(axis)
     pairs = [(i, i + by) for i in range(size) if 0 <= i + by < size]
     return lax.ppermute(value, axis, pairs)
+
+
+def shifted(value, axis, by):
+    size = lax.axis_size(axis)
+    return lax.ppermute(value, axis, [(i, (i + by) % size) for i in range(size)])
+
+
+def slots_of(value, axis):
+    return [value] + [shifted(value, axis, by) for by in range(1, lax.axis_size(axis))]
 
 
 def gather_by_doubling(value, axis):
@@ -40,86 +49,79 @@
     return 1 if size % LANES or (size // seq_count) % CHAN_BLOCK else CHUNKS
 
 
-def project_kernel(extras, tok_ref, w_ref, taps_ref, halo_ref, *rest):
-    signal_ref, signal_t_ref, query_t_ref, tok, held, keys, sems = rest[extras:]
-    rows = tok.shape[0]
-    tile = rows // sems.shape[0]
-    stream = pl.program_id(1)
-    first = jnp.logical_and(pl.program_id(0) == 0, stream == 0)
-    pieces = [pl.ds(r, tile) for r in range(0, rows, tile)]
-    copies = [pltpu.make_async_copy(tok_ref.at[p], tok.at[p], sems.at[i]) for i, p in enumerate(pieces)]
-
-    @pl.when(first)
+def project_kernel(slots, extras, me_ref, *refs):
+    tok_refs = refs[:slots]
+    w_ref, taps_ref, halo_ref = refs[slots : slots + 3]
+    signal_ref, signal_t_ref, query_t_ref, tail_ref, acc = refs[slots + 3 + extras :]
+    step = pl.program_id(1)
+    rows = signal_t_ref.shape[0]
+    for z, tok_ref in enumerate(tok_refs):
+
+        @pl.when(step == z)
+        def _():
+            for p in range(3):
+                part = jnp.dot(tok_ref[...], w_ref[p], preferred_element_type=jnp.float32)
+                acc[p, HALO:, :] = part if z == 0 else part + acc[p, HALO:, :]
+
+    @pl.when(step == slots - 1)
     def _():
-        for copy in copies:
-            copy.start()
-
-    held[0:HALO, :] = halo_ref[0].astype(jnp.float32)
-    for r, copy in zip(range(0, rows, tile), copies):
-        pl.when(first)(copy.wait)
-        part = jnp.dot(tok[r : r + tile, :], w_ref[0], preferred_element_type=jnp.float32)
-        held[HALO + r : HALO + r + tile, :] = part.astype(jnp.bfloat16).astype(jnp.float32)
-
-    def filtered(r, size):
-        total = taps_ref[0, 0] * held[pl.ds(HALO + r, size), :]
-        for j in range(1, TAPS):
-            total = total + taps_ref[0, j] * held[pl.ds(HALO + r - j, size), :]
-        return total
-
-    @pl.when(stream == 0)
-    def _():
+        for p in range(3):
+            acc[p, :HALO, :] = halo_ref[p].astype(jnp.float32)
+            acc[p, HALO:, :] = acc[p, HALO:, :].astype(jnp.bfloat16).astype(jnp.float32)
+            tail_ref[p] = acc[p, rows:, :].astype(tail_ref.dtype)
         for r in range(0, rows, LANES):
-            query_t_ref[r : r + LANES, :] = filtered(r, LANES).astype(query_t_ref.dtype)
-
-    @pl.when(stream == 1)
-    def _():
-        for r in range(0, rows, LANES):
-            keys[r : r + LANES, :] = filtered(r, LANES)
-
-    @pl.when(stream == 2)
-    def _():
-        for r in range(0, rows, LANES):
-            signal = keys[r : r + LANES, :] * filtered(r, LANES)
+            streams = []
+            for p in range(3):
+                total = taps_ref[0, p][None, :] * acc[p, pl.ds(HALO + r, LANES), :]
+                for j in range(1, TAPS):
+                    total = total + taps_ref[j, p][None, :] * acc[p, pl.ds(HALO + r - j, LANES), :]
+                streams.append(total)
+            signal = streams[1] * streams[2]
+            query_t_ref[r : r + LANES, :] = streams[0].astype(query_t_ref.dtype)
             signal_t_ref[r : r + LANES, :] = signal.astype(signal_t_ref.dtype)
             signal_ref[:, r : r + LANES] = signal.T.astype(signal_ref.dtype)
 
 
-def project(gathered, in_weight, conv_weight, halo, *after):
-    rows, depth = gathered.shape
+def project(slots, in_weight, conv_weight, halo, *after):
+    rows, depth = slots[0].shape
+    count = len(slots)
     chans = in_weight.shape[2]
     tile = 2 * LANES if chans % (2 * LANES) == 0 else chans
-    pieces = 4
     flat = jax.ShapeDtypeStruct((rows, chans), jnp.bfloat16)
-    taps = conv_weight.transpose(1, 0, 2)[:, :, None, :]
+    me = lax.axis_index("chan").astype(jnp.int32).reshape(1)
     return pl.pallas_call(
-        lambda *refs: project_kernel(len(after), *refs),
-        grid=(chans // tile, 3),
-        in_specs=[
-            pl.BlockSpec(memory_space=pl.ANY),
-            pl.BlockSpec((1, depth, tile), lambda i, p: (p, 0, i)),
-            pl.BlockSpec((1, TAPS, 1, tile), lambda i, p: (p, 0, 0, i)),
-            pl.BlockSpec((1, HALO, tile), lambda i, p: (p, 0, i)),
-            *[pl.BlockSpec(memory_space=pl.ANY) for _ in after],
-        ],
-        out_specs=[
-            pl.BlockSpec((tile, rows), lambda i, p: (i, 0)),
-            pl.BlockSpec((rows, tile), lambda i, p: (0, i)),
-            pl.BlockSpec((rows, tile), lambda i, p: (0, i)),
-        ],
-        out_shape=[jax.ShapeDtypeStruct((chans, rows), jnp.bfloat16), flat, flat],
-        scratch_shapes=[
-            pltpu.VMEM((rows, depth), jnp.bfloat16),
-            pltpu.VMEM((HALO + rows, tile), jnp.float32),
-            pltpu.VMEM((rows, tile), jnp.float32),
-            pltpu.SemaphoreType.DMA((pieces,)),
+        lambda *refs: project_kernel(count, len(after), *refs),
+        grid_spec=pltpu.PrefetchScalarGridSpec(
+            num_scalar_prefetch=1,
+            grid=(chans // tile, count),
+            in_specs=[
+                *[pl.BlockSpec((rows, depth), lambda i, z, me: (0, 0)) for _ in slots],
+                pl.BlockSpec((3, depth, tile), lambda i, z, me: (0, lax.rem(me[0] - z + count, count), i)),
+                pl.BlockSpec((TAPS, 3, tile), lambda i, z, me: (0, 0, i)),
+                pl.BlockSpec((3, HALO, tile), lambda i, z, me: (0, 0, i)),
+                *[pl.BlockSpec(memory_space=pl.ANY) for _ in after],
+            ],
+            out_specs=[
+                pl.BlockSpec((tile, rows), lambda i, z, me: (i, 0)),
+                pl.BlockSpec((rows, tile), lambda i, z, me: (0, i)),
+                pl.BlockSpec((rows, tile), lambda i, z, me: (0, i)),
+                pl.BlockSpec((3, HALO, tile), lambda i, z, me: (0, 0, i)),
+            ],
+            scratch_shapes=[pltpu.VMEM((3, HALO + rows, tile), jnp.float32)],
+        ),
+        out_shape=[
+            jax.ShapeDtypeStruct((chans, rows), jnp.bfloat16),
+            flat,
+            flat,
+            jax.ShapeDtypeStruct((3, HALO, chans), jnp.bfloat16),
         ],
         compiler_params=pltpu.CompilerParams(vmem_limit_bytes=VMEM_BYTES),
         cost_estimate=pl.CostEstimate(
-            flops=2 * 3 * rows * depth * chans,
-            bytes_accessed=2 * depth * (3 * chans + rows),
+            flops=2 * 3 * rows * depth * count * chans,
+            bytes_accessed=2 * depth * count * (3 * chans + rows),
             transcendentals=0,
         ),
-    )(gathered, in_weight, taps, halo, *after)
+    )(me, *slots, in_weight, conv_weight, halo, *after)
 
 
 def transform_tables(seq_count, tok_rows):
@@ -329,14 +331,55 @@
     )(got)
 
 
-def feature_slice(out_weight, seq_count):
-    group = out_weight.shape[0]
-    each = group // seq_count
+def feature_rows(out_weight, seq_count):
+    each = out_weight.shape[0] // seq_count
     own = lax.dynamic_slice_in_dim(out_weight, lax.axis_index("seq") * each, each, axis=0)
-    own = lax.all_to_all(own, "chan", split_axis=1, concat_axis=0, tiled=True)
-    chan_count = lax.axis_size("chan")
-    whole = gather_by_doubling(own.reshape(chan_count, each, own.shape[1]), "seq")
-    return whole.transpose(1, 0, 2, 3).reshape(chan_count, group, own.shape[1])
+    count = lax.axis_size("chan")
+    me = lax.axis_index("chan")
+    wide = out_weight.shape[1] // count
+    pieces = []
+    for by in range(count):
+        piece = lax.dynamic_slice_in_dim(own, lax.rem(me + by, count) * wide, wide, axis=1)
+        pieces.append(shifted(piece, "chan", by) if by else piece)
+    return jnp.stack(pieces)
+
+
+def combine_kernel(slots, *refs):
+    total_ref = refs[slots + 1] if len(refs) == slots + 3 else None
+    w_ref, out_ref = refs[slots], refs[-1]
+    total = None if total_ref is None else total_ref[...]
+    for z in range(slots):
+        weight = w_ref[:, z].reshape(refs[z].shape[1], out_ref.shape[1])
+        term = jnp.dot(refs[z][...], weight, preferred_element_type=jnp.float32)
+        total = term if total is None else total + term
+    out_ref[...] = total.astype(out_ref.dtype)
+
+
+def combine(slots, weight, start, total, dtype):
+    tok_rows, size = slots[0].shape
+    _, count, each, features = weight.shape
+    per = size // each
+    first = start // size
+    tile = min(2 * LANES, features)
+    block = pl.BlockSpec((tok_rows, tile), lambda i: (0, i))
+    given = [] if total is None else [total]
+    return pl.pallas_call(
+        lambda *refs: combine_kernel(count, *refs),
+        grid=(features // tile,),
+        in_specs=[
+            *[pl.BlockSpec((tok_rows, size), lambda i: (0, 0)) for _ in slots],
+            pl.BlockSpec((per, count, each, tile), lambda i: (first, 0, 0, i)),
+            *[block for _ in given],
+        ],
+        out_specs=block,
+        out_shape=jax.ShapeDtypeStruct((tok_rows, features), dtype),
+        compiler_params=pltpu.CompilerParams(vmem_limit_bytes=VMEM_BYTES),
+        cost_estimate=pl.CostEstimate(
+            flops=2 * tok_rows * size * count * features,
+            bytes_accessed=2 * count * size * (tok_rows + features) + 6 * tok_rows * features,
+            transcendentals=0,
+        ),
+    )(*slots, weight, *given)
 
 
 def shards(tokens, in_weight, conv_weight, spectrum, skip, out_weight):
@@ -346,8 +389,11 @@
     chans = in_weight.shape[2]
     chunks = chunk_count(chans, seq_count)
     size = chans // chunks
-    gathered = lax.all_gather(tokens, "chan", axis=1, tiled=True)
+    cut = tok_rows * 3 // 4
+    early = slots_of(tokens[:cut], "chan")
     halo = gather_by_doubling(from_behind(tokens[tok_rows - HALO :], "seq", 1), "chan")
+    late, *early[1:] = lax.optimization_barrier((tokens[cut:], *early[1:]))
+    late = slots_of(late, "chan")
     halo = jnp.einsum(
         "ztd,pzdc->ptc",
         halo,
@@ -355,22 +401,28 @@
         preferred_element_type=jnp.float32,
     ).astype(jnp.bfloat16)
     response = folded_response(spectrum, seq_count, chunks)
-    weight_slice = feature_slice(out_weight, seq_count)
-    signal, signal_t, query_t = project(gathered, in_weight, conv_weight, halo, response, weight_slice)
-    total = None
+    signal_a, *piece_a, tail = project(early, in_weight, conv_weight, halo)
+    signal_b, *piece_b, _ = project(late, in_weight, conv_weight, tail, response)
+    signal = jnp.concatenate([signal_a, signal_b], axis=1)
+    signal, out_weight = lax.optimization_barrier((signal, out_weight))
+    weight = feature_rows(out_weight, seq_count)
+    gated = []
     for lo in range(0, chans, size):
         values = signal[lo : lo + size].reshape(seq_count, size // seq_count, tok_rows)
         values = lax.all_to_all(values, "seq", split_axis=0, concat_axis=0, tiled=True)
         longconv = lax.all_to_all(
             long_conv(values, response, lo // seq_count), "seq", split_axis=0, concat_axis=0, tiled=True
         ).reshape(size, tok_rows)
-        gated = lax.all_gather(
-            gate(longconv, skip, lo, ((signal_t, query_t),)), "chan", axis=1, tiled=True
-        )
-        weight = weight_slice[:, lo : lo + size].reshape(gated.shape[1], weight_slice.shape[2])
-        term = jnp.dot(gated, weight, preferred_element_type=jnp.float32)
-        total = term if total is None else total + term
-    return total.astype(jnp.bfloat16)
+        gated.append(gate(longconv, skip, lo, (piece_a, piece_b)))
+        if lo == 0:
+            gated[0], weight = lax.optimization_barrier((gated[0], weight))
+    slots = [slots_of(value, "chan") for value in gated]
+    weight = gather_by_doubling(weight, "seq")
+    total = None
+    for j, lo in enumerate(range(0, chans, size)):
+        dtype = jnp.bfloat16 if lo + size == chans else jnp.float32
+        total = combine(slots[j], weight, lo, total, dtype)
+    return total
 
 
 def solution(mesh):

time: 355 us -> 474 us (1.34)
  the two profiles are of different devices: /device:TPU:0 before, /device:TPU:19 now
where the time goes in v4:
time: 474 us; the launch traced here: 472 us
  waiting for transfers between devices  298 us (63%)
  Pallas kernels  60.6 us (13%)
  starting transfers between devices  46.8 us (10%)
  local copies, waits for them, and re-layouts  38.9 us (8%)
  blocking collectives  11.4 us (2%)
  other arithmetic  10.1 us (2%)
  matrix products  6.3 us (1%)
    ppermute x5, waiting for transfers between devices, gather_by_doubling(): other = lax.ppermute(held, axis, [(i, i ^ bit) for i in range(size)])  134 us
    ppermute x15, waiting for transfers between devices, shifted(): lax.ppermute(value, axis, [(i, (i + by) % size) for i in range(size)])  108 us
    ppermute x1, waiting for transfers between devices, from_behind(): return lax.ppermute(value, axis, pairs)  41.8 us
    pallas_call x2, Pallas kernels, project(): pl.pallas_call(lambda *refs: project_kernel(count, len(after), *refs), gr...  27.1 us
    ppermute x15, starting transfers between devices, shifted(): lax.ppermute(value, axis, [(i, (i + by) % size) for i in range(size)])  19.4 us
    unnamed x66, local copies, waits for them, and re-layouts  19 us
    pallas_call x2, Pallas kernels, combine(): pl.pallas_call(lambda *refs: combine_kernel(count, *refs), grid=(features...  12.2 us
    all_to_all x1, blocking collectives, shards(): lax.all_to_all(values, 'seq', split_axis=0, concat_axis=0, tiled=True)  11.4 us
  transfers between devices with their start and end apart: 25, of which 17 were waited for; matrix products, arithmetic and copies ran while one was open for 4% of the time, Pallas kernels for 6%

profile of v4, /device:TPU:19, one launch (start us, length us, event | category | flops | bytes accessed | tf_op | source)
XLA Modules:
  0.0 472.4 jit_solution(1541513405653592053)
XLA Ops:
  0.0 10.9 %reshape.41.spec_ref = f32[2,1024,1024]{2,1,0:T(8,128)} reshape(f32[2,512,2,1024]{3,2,1,0:T(2,128)} %param.21) | data formatting | bytes 16777216 | tf_op jit(solution)/shard_map/reshape | solution.py:315
  11.7 8.5 %shard_map.173 = bf16[8,2,2,64,1024]{4,3,2,1,0:T(8,128)(2,1)} custom-call(f32[2,1024,1024]{2,1,0:T(8,128)} %reshape.41.spec_ref, bf16[1024,1024]{1,0:T(8,128)(2,1)S(1)} %fusion.1.order_ref), custom_call_target="tpu_custom_call" | custom-call | flops 4294967296 | bytes 12582912 | tf_op jit(solution)/shard_map/pallas_call | solution.py:302
  20.2 5.3 %all-to-all-start = ((bf16[8,2,2,64,1024]{4,3,2,1,0:T(8,128)(2,1)}), bf16[8,2,2,64,1024]{4,3,2,1,0:T(8,128)(2,1)}, u32[]{:S(2)}, u32[]{:S(2)}) async-start(bf16[8,2,2,64,1024]{4,3,2,1,0:T(8,128)(2,1)} %shard_map.173), calls=%async_computation | async-start | bytes 8388608 | tf_op jit(solution)/shard_map/all_to_all | solution.py:316
  26.3 3.3 collective-permute-start.3
  29.6 41.8 %collective-permute-done.3 = bf16[16,1024]{1,0:T(8,128)(2,1)S(1)} collective-permute-done((bf16[16,1024]{1,0:T(8,128)(2,1)S(1)}, bf16[16,1024]{1,0:T(8,128)(2,1)S(1)}, u32[]{:S(2)}, u32[]{:S(2)}) %collective-permute-start.3) | collective-permute-done | bytes 32800 | tf_op jit(solution)/shard_map/ppermute | solution.py:20
  71.5 1.5 slice.15.refs_1_
  73.0 1.4 collective-permute-start
  74.4 2.3 collective-permute-start.1
  76.7 1.1 collective-permute-start.2
  78.3 1.9 slice.16.refs_1_
  80.2 98.2 %collective-permute-done.5 = bf16[2,16,1024]{2,1,0:T(8,128)(2,1)S(1)} collective-permute-done((bf16[2,16,1024]{2,1,0:T(8,128)(2,1)S(1)}, bf16[2,16,1024]{2,1,0:T(8,128)(2,1)S(1)}, u32[]{:S(2)}, u32[]{:S(2)}) %collective-permute-start.5) | collective-permute-done | bytes 65568 | tf_op jit(solution)/shard_map/ppermute | solution.py:38
  178.5 6.3 %fusion.3.refs_7_ = bf16[3,16,512]{2,1,0:T(8,128)(2,1)S(1)} fusion(bf16[4,16,1024,1]{2,1,0,3:T(8,128)(2,1)S(1)} %bitcast.79, bf16[3,4,1024,512]{3,2,1,0:T(8,128)(2,1)} %bitcast.73), kind=kOutput, calls=%fused_computation.9 | convolution fusion | flops 201351168 | bytes 12763136 | tf_op jit(solution)/shard_map/ztd,pzdc->ptc/dot_general | solution.py:397
  184.8 1.2 copy-done.29
  186.0 25.7 %collective-permute-done.2.refs_4_ = bf16[768,1024]{1,0:T(8,128)(2,1)} collective-permute-done((bf16[768,1024]{1,0:T(8,128)(2,1)S(1)}, bf16[768,1024]{1,0:T(8,128)(2,1)}, u32[]{:S(2)}, u32[]{:S(2)}) %collective-permute-start.2) | collective-permute-done | bytes 1572896 | tf_op jit(solution)/shard_map/ppermute | solution.py:25
  212.4 2.7 collective-permute-start.7
  215.2 1.4 copy-done.10
  216.6 1.4 copy-done.30
  218.0 15.9 %shard_map.172 = (bf16[512,768]{1,0:T(8,128)(2,1)S(1)}, bf16[768,512]{1,0:T(8,128)(2,1)S(1)}, bf16[768,512]{1,0:T(8,128)(2,1)S(1)}, bf16[3,16,512]{2,1,0:T(8,128)(2,1)S(1)}) custom-call(s32[1]{0:T(128)} %bitcast.refs_0_, bf16[768,1024]{1,0:T(8,128)(2,1)S(1)} %copy-done.10, bf16[768,1024]{1,0:T(8,128)(2,1)S(1)} %copy-done.30, ...), custom_call_target="tpu_custom_call" | custom-call | flops 9663676416 | bytes 18874368 | tf_op jit(solution)/shard_map/pallas_call | solution.py:92
  233.9 0.9 copy-done
  235.7 4.0 shard_map.174.refs_8_.resp_ref
  239.7 6.9 %collective-permute-done.7.refs_3_ = bf16[256,1024]{1,0:T(8,128)(2,1)} collective-permute-done((bf16[256,1024]{1,0:T(8,128)(2,1)}, bf16[256,1024]{1,0:T(8,128)(2,1)}, u32[]{:S(2)}, u32[]{:S(2)}) %collective-permute-start.7) | collective-permute-done | bytes 524320 | tf_op jit(solution)/shard_map/ppermute | solution.py:25
  246.6 11.2 %collective-permute-done.8.refs_4_ = bf16[256,1024]{1,0:T(8,128)(2,1)} collective-permute-done((bf16[256,1024]{1,0:T(8,128)(2,1)}, bf16[256,1024]{1,0:T(8,128)(2,1)}, u32[]{:S(2)}, u32[]{:S(2)}) %collective-permute-start.8) | collective-permute-done | bytes 524320 | tf_op jit(solution)/shard_map/ppermute | solution.py:25
  257.9 11.2 %shard_map.175 = (bf16[512,256]{1,0:T(8,128)(2,1)S(1)}, bf16[256,512]{1,0:T(8,128)(2,1)S(1)}, bf16[256,512]{1,0:T(8,128)(2,1)S(1)}, bf16[3,16,512]{2,1,0:T(8,128)(2,1)}) custom-call(s32[1]{0:T(128)} %bitcast.refs_0_, bf16[256,1024]{1,0:T(8,128)(2,1)} %slice.16.refs_1_, bf16[256,1024]{1,0:T(8,128)(2,1)} %collective-permute-done.6.refs_2_, ...), custom_call_target="tpu_custom_call" | custom-call | flops 3221225472 | bytes 14680064 | tf_op jit(solution)/shard_map/pallas_call | solution.py:92
  270.1 11.4 %all_to_all.25.signal_ref = bf16[8,32,1024]{2,1,0:T(8,128)(2,1)S(1)} all-to-all(bf16[8,32,1024]{2,1,0:T(8,128)(2,1)S(1)} %bitcast.78), channel_id=1, replica_groups=mesh['seq'=8,'chan'=4] {'seq'}, dimensions={0} | all-to-all | bytes 1048576 | tf_op jit(solution)/shard_map/all_to_all | solution.py:412
  281.6 2.9 shard_map.178
  285.3 5.7 %all-to-all-start.4 = ((bf16[8,32,1024]{2,1,0:T(8,128)(2,1)}), bf16[8,32,1024]{2,1,0:T(8,128)(2,1)}, u32[]{:S(2)}, u32[]{:S(2)}) async-start(bf16[8,32,1024]{2,1,0:T(8,128)(2,1)} %copy-done.5), calls=%async_computation.4 | async-start | bytes 1048576 | tf_op jit(solution)/shard_map/all_to_all | solution.py:413
  291.0 1.4 dynamic-slice_bitcast_fusion
  292.5 3.8 collective-permute-start.12
  296.3 1.3 collective-permute-start.14
  297.6 2.5 collective-permute-done.12
  300.0 4.9 %collective-permute-done.13 = bf16[64,1024]{1,0:T(8,128)(2,1)S(1)} collective-permute-done((bf16[64,1024]{1,0:T(8,128)(2,1)S(1)}, bf16[64,1024]{1,0:T(8,128)(2,1)S(1)}, u32[]{:S(2)}, u32[]{:S(2)}) %collective-permute-start.13) | collective-permute-done | bytes 131104 | tf_op jit(solution)/shard_map/ppermute | solution.py:25
  304.9 2.8 collective-permute-done.14
  308.6 1.1 copy-done.1
  309.7 0.9 copy-done.12
  310.7 1.3 shard_map.179.refs_0_
  312.8 1.2 collective-permute-start.15
  314.0 12.1 %collective-permute-done.15 = bf16[1,4,64,1024]{3,2,1,0:T(8,128)(2,1)} collective-permute-done((bf16[1,4,64,1024]{3,2,1,0:T(8,128)(2,1)}, bf16[1,4,64,1024]{3,2,1,0:T(8,128)(2,1)}, u32[]{:S(2)}, u32[]{:S(2)}) %collective-permute-start.15) | collective-permute-done | bytes 524320 | tf_op jit(solution)/shard_map/ppermute | solution.py:38
  326.1 1.3 select_bitcast_fusion.5
  328.2 1.1 maximum_bitcast_fusion
  329.4 23.5 %collective-permute-done.16 = bf16[2,4,64,1024]{3,2,1,0:T(8,128)(2,1)} collective-permute-done((bf16[2,4,64,1024]{3,2,1,0:T(8,128)(2,1)}, bf16[2,4,64,1024]{3,2,1,0:T(8,128)(2,1)}, u32[]{:S(2)}, u32[]{:S(2)}) %collective-permute-start.16) | collective-permute-done | bytes 1048608 | tf_op jit(solution)/shard_map/ppermute | solution.py:38
  352.9 1.7 select_bitcast_fusion.3
  354.6 1.5 pad_maximum_fusion.1
  356.1 2.3 collective-permute-start.17
  358.3 4.1 all-to-all-start.1
  362.7 8.0 %all-to-all-done.1.signal_ref = bf16[8,32,1024]{2,1,0:T(8,128)(2,1)} async-done(((bf16[8,32,1024]{2,1,0:T(8,128)(2,1)}), bf16[8,32,1024]{2,1,0:T(8,128)(2,1)}, u32[]{:S(2)}, u32[]{:S(2)}) %all-to-all-start.1) | async-done | bytes 524320 | tf_op jit(solution)/shard_map/all_to_all | solution.py:412
  370.7 0.9 copy-done.18
  374.7 3.8 shard_map.176
  379.2 4.9 %all-to-all-start.2 = ((bf16[8,32,1024]{2,1,0:T(8,128)(2,1)}), bf16[8,32,1024]{2,1,0:T(8,128)(2,1)S(1)}, u32[]{:S(2)}, u32[]{:S(2)}) async-start(bf16[8,32,1024]{2,1,0:T(8,128)(2,1)} %copy-done.8), calls=%async_computation.2 | async-start | bytes 1048576 | tf_op jit(solution)/shard_map/all_to_all | solution.py:413
  384.5 2.0 collective-permute-start.20
  386.4 6.1 %all-to-all-done.2 = bf16[8,32,1024]{2,1,0:T(8,128)(2,1)S(1)} async-done(((bf16[8,32,1024]{2,1,0:T(8,128)(2,1)}), bf16[8,32,1024]{2,1,0:T(8,128)(2,1)S(1)}, u32[]{:S(2)}, u32[]{:S(2)}) %all-to-all-start.2) | async-done | bytes 524320 | tf_op jit(solution)/shard_map/all_to_all | solution.py:413
  393.3 1.1 copy-done.2
  394.4 1.0 copy-done.7
  395.5 0.9 copy-done.13
  397.4 2.1 collective-permute-start.11
  399.4 1.2 collective-permute-start.9
  400.6 2.5 select_bitcast_fusion.1
  403.5 2.4 copy.23
  406.0 1.1 collective-permute-done.19.refs_2_
  407.0 22.5 %collective-permute-done.20.refs_3_ = bf16[1024,256]{1,0:T(8,128)(2,1)} collective-permute-done((bf16[1024,256]{1,0:T(8,128)(2,1)}, bf16[1024,256]{1,0:T(8,128)(2,1)}, u32[]{:S(2)}, u32[]{:S(2)}) %collective-permute-start.20) | collective-permute-done | bytes 524320 | tf_op jit(solution)/shard_map/ppermute | solution.py:25
  429.5 6.2 %shard_map.180.refs_5_ = f32[1024,1024]{1,0:T(8,128)} custom-call(bf16[1024,256]{1,0:T(8,128)(2,1)S(1)} %copy-done.4, bf16[1024,256]{1,0:T(8,128)(2,1)} %collective-permute-done.18.refs_1_, bf16[1024,256]{1,0:T(8,128)(2,1)} %collective-permute-done.19.refs_2_, bf16[1024,256]{1,0:T(8,128)(2,1)} %collective-permute-done.20.refs_3_, ...), custom_call_target="tpu_custom_call" | custom-call | flops 2147483648 | bytes 10485760 | tf_op jit(solution)/shard_map/pallas_call | solution.py:366
  435.7 16.2 %collective-permute-done.10.refs_2_ = bf16[1024,256]{1,0:T(8,128)(2,1)S(1)} collective-permute-done((bf16[1024,256]{1,0:T(8,128)(2,1)S(1)}, bf16[1024,256]{1,0:T(8,128)(2,1)S(1)}, u32[]{:S(2)}, u32[]{:S(2)}) %collective-permute-start.10) | collective-permute-done | bytes 524320 | tf_op jit(solution)/shard_map/ppermute | solution.py:25
  451.9 11.2 %collective-permute-done.11.refs_3_ = bf16[1024,256]{1,0:T(8,128)(2,1)S(1)} collective-permute-done((bf16[1024,256]{1,0:T(8,128)(2,1)S(1)}, bf16[1024,256]{1,0:T(8,128)(2,1)S(1)}, u32[]{:S(2)}, u32[]{:S(2)}) %collective-permute-start.11) | collective-permute-done | bytes 524320 | tf_op jit(solution)/shard_map/ppermute | solution.py:25
  463.1 3.3 collective-permute-done.9.refs_1_
  466.4 6.1 %shard_map.181 = bf16[1024,1024]{1,0:T(8,128)(2,1)} custom-call(bf16[1024,256]{1,0:T(8,128)(2,1)S(1)} %shard_map.177.refs_0_, bf16[1024,256]{1,0:T(8,128)(2,1)S(1)} %collective-permute-done.9.refs_1_, bf16[1024,256]{1,0:T(8,128)(2,1)S(1)} %collective-permute-done.10.refs_2_, bf16[1024,256]{1,0:T(8,128)(2,1)S(1)} %collective-permute-done.11.refs_3_, ...), custom_call_target="tpu_custom_call" | custom-call | flops 2147483648 | bytes 10485760 | tf_op jit(solution)/shard_map/pallas_call | solution.py:366
  (88 shorter events, 14.6 us)
Async XLA Ops:
  20.2 215.4 %all-to-all-start = ((bf16[8,2,2,64,1024]{4,3,2,1,0:T(8,128)(2,1)}), bf16[8,2,2,64,1024]{4,3,2,1,0:T(8,128)(2,1)}, u32[]{:S(2)}, u32[]{:S(2)}) async-start(bf16[8,2,2,64,1024]{4,3,2,1,0:T(8,128)(2,1)} %shard_map.173), calls=%async_computation | async-start | bytes 8388608 | tf_op jit(solution)/shard_map/all_to_all | solution.py:316
  26.3 45.2 %collective-permute-start.3 = (bf16[16,1024]{1,0:T(8,128)(2,1)S(1)}, bf16[16,1024]{1,0:T(8,128)(2,1)S(1)}, u32[]{:S(2)}, u32[]{:S(2)}) collective-permute-start(bf16[16,1024]{1,0:T(8,128)(2,1)S(1)} %slice.17), channel_id=1, source_target_pairs={{0,4},{4,8},{8,12},{12,16},{16,20},{20,24},{24,28},{1,5},{5,9},{9,... | collective-permute-start | bytes 98312 | tf_op jit(solution)/shard_map/ppermute | solution.py:20
  71.5 6.3 %collective-permute-start.4 = (bf16[1,16,1024]{2,1,0:T(8,128)(2,1)S(1)}, bf16[1,16,1024]{2,1,0:T(8,128)(2,1)S(1)}, u32[]{:S(2)}, u32[]{:S(2)}) collective-permute-start(bf16[1,16,1024]{2,1,0:T(8,128)(2,1)S(1)} %bitcast.83), channel_id=1, source_target_pairs={{0,2},{1,3},{2,0},{3,1},{4,6},{5,7},{6,4},{7,5},{8,10},{9,11},{10,... | collective-permute-start | bytes 98312 | tf_op jit(solution)/shard_map/ppermute | solution.py:38
  73.0 111.8 %copy-start.9 = (bf16[768,1024]{1,0:T(8,128)(2,1)}, bf16[768,1024]{1,0:T(8,128)(2,1)S(1)}, u32[]{:S(2)}) copy-start(bf16[768,1024]{1,0:T(8,128)(2,1)S(1)} %slice.15.refs_1_) | copy-start | bytes 4718596
  73.0 111.8 %collective-permute-start = (bf16[768,1024]{1,0:T(8,128)(2,1)S(1)}, bf16[768,1024]{1,0:T(8,128)(2,1)S(1)}, u32[]{:S(2)}, u32[]{:S(2)}) collective-permute-start(bf16[768,1024]{1,0:T(8,128)(2,1)S(1)} %slice.15.refs_1_), channel_id=1, source_target_pairs={{0,1},{1,2},{2,3},{3,0},{4,5},{5,6},{6,7},{7,4},{8,9},{9,10},{10,1... | collective-permute-start | bytes 4718600 | tf_op jit(solution)/shard_map/ppermute | solution.py:25
  74.4 111.6 %collective-permute-start.1 = (bf16[768,1024]{1,0:T(8,128)(2,1)S(1)}, bf16[768,1024]{1,0:T(8,128)(2,1)}, u32[]{:S(2)}, u32[]{:S(2)}) collective-permute-start(bf16[768,1024]{1,0:T(8,128)(2,1)S(1)} %slice.15.refs_1_), channel_id=1, source_target_pairs={{0,2},{1,3},{2,0},{3,1},{4,6},{5,7},{6,4},{7,5},{8,10},{9,11},{10,... | collective-permute-start | bytes 4718600 | tf_op jit(solution)/shard_map/ppermute | solution.py:25
  76.7 134.9 %collective-permute-start.2 = (bf16[768,1024]{1,0:T(8,128)(2,1)S(1)}, bf16[768,1024]{1,0:T(8,128)(2,1)}, u32[]{:S(2)}, u32[]{:S(2)}) collective-permute-start(bf16[768,1024]{1,0:T(8,128)(2,1)S(1)} %slice.15.refs_1_), channel_id=1, source_target_pairs={{0,3},{1,0},{2,1},{3,2},{4,7},{5,4},{6,5},{7,6},{8,11},{9,8},{10,9... | collective-permute-start | bytes 4718600 | tf_op jit(solution)/shard_map/ppermute | solution.py:25
  77.8 100.6 %collective-permute-start.5 = (bf16[2,16,1024]{2,1,0:T(8,128)(2,1)S(1)}, bf16[2,16,1024]{2,1,0:T(8,128)(2,1)S(1)}, u32[]{:S(2)}, u32[]{:S(2)}) collective-permute-start(bf16[2,16,1024]{2,1,0:T(8,128)(2,1)S(1)} %maximum_bitcast_fusion.1), channel_id=1, source_target_pairs={{0,1},{1,0},{2,3},{3,2},{4,5},{5,4},{6,7},{7,6},{8,9},{9,8},{10,11... | collective-permute-start | bytes 196616 | tf_op jit(solution)/shard_map/ppermute | solution.py:38
  178.5 36.7 %copy-start.27 = (f32[3,3,512]{2,1,0:T(4,128)S(1)}, f32[3,3,512]{2,1,0:T(4,128)}, u32[]{:S(2)}) copy-start(f32[3,3,512]{2,1,0:T(4,128)} %refs_6_.3) | copy-start | bytes 55300
  184.8 1.2 copy-start.29
  211.7 28.1 %collective-permute-start.6 = (bf16[256,1024]{1,0:T(8,128)(2,1)}, bf16[256,1024]{1,0:T(8,128)(2,1)}, u32[]{:S(2)}, u32[]{:S(2)}) collective-permute-start(bf16[256,1024]{1,0:T(8,128)(2,1)} %slice.16.refs_1_), channel_id=1, source_target_pairs={{0,1},{1,2},{2,3},{3,0},{4,5},{5,6},{6,7},{7,4},{8,9},{9,10},{10,1... | collective-permute-start | bytes 1572872 | tf_op jit(solution)/shard_map/ppermute | solution.py:25
  212.4 34.2 %collective-permute-start.7 = (bf16[256,1024]{1,0:T(8,128)(2,1)}, bf16[256,1024]{1,0:T(8,128)(2,1)}, u32[]{:S(2)}, u32[]{:S(2)}) collective-permute-start(bf16[256,1024]{1,0:T(8,128)(2,1)} %slice.16.refs_1_), channel_id=1, source_target_pairs={{0,2},{1,3},{2,0},{3,1},{4,6},{5,7},{6,4},{7,5},{8,10},{9,11},{10,... | collective-permute-start | bytes 1572872 | tf_op jit(solution)/shard_map/ppermute | solution.py:25
  215.1 42.7 %collective-permute-start.8 = (bf16[256,1024]{1,0:T(8,128)(2,1)}, bf16[256,1024]{1,0:T(8,128)(2,1)}, u32[]{:S(2)}, u32[]{:S(2)}) collective-permute-start(bf16[256,1024]{1,0:T(8,128)(2,1)} %slice.16.refs_1_), channel_id=1, source_target_pairs={{0,3},{1,0},{2,1},{3,2},{4,7},{5,4},{6,5},{7,6},{8,11},{9,8},{10,9... | collective-permute-start | bytes 1572872 | tf_op jit(solution)/shard_map/ppermute | solution.py:25
  215.2 1.4 copy-start.10
  216.6 1.4 copy-start.30
  233.9 0.9 copy-start
  234.8 0.9 copy-start.14
  257.9 11.2 %copy-start.15 = (bf16[512,768]{1,0:T(8,128)(2,1)S(1)}, bf16[512,768]{1,0:T(8,128)(2,1)}, u32[]{:S(2)}) copy-start(bf16[512,768]{1,0:T(8,128)(2,1)} %copy-done.14) | copy-start | bytes 2359300
  269.0 1.1 copy-start.11
  269.0 12.5 %copy-start.16 = (bf16[256,256]{1,0:T(8,128)(2,1)S(1)}, bf16[256,256]{1,0:T(8,128)(2,1)}, u32[]{:S(2)}) copy-start(bf16[256,256]{1,0:T(8,128)(2,1)} %constant.193.clone.fwd_ref) | copy-start | bytes 393220
  269.0 12.5 %copy-start.17 = (bf16[256,256]{1,0:T(8,128)(2,1)S(1)}, bf16[256,256]{1,0:T(8,128)(2,1)}, u32[]{:S(2)}) copy-start(bf16[256,256]{1,0:T(8,128)(2,1)} %constant.194.clone.bwd_ref) | copy-start | bytes 393220
  269.0 12.5 %copy-start.19 = (bf16[144,64]{1,0:T(8,128)(2,1)S(1)}, bf16[144,64]{1,0:T(8,128)(2,1)}, u32[]{:S(2)}) copy-start(bf16[144,64]{1,0:T(8,128)(2,1)} %constant.189.clone.first_ref) | copy-start | bytes 55300
  269.1 12.5 %copy-start.21 = (f32[72,128]{1,0:T(8,128)S(1)}, f32[72,128]{1,0:T(8,128)}, u32[]{:S(2)}) copy-start(f32[72,128]{1,0:T(8,128)} %constant.191.clone.cos_ref) | copy-start | bytes 110596
  269.1 12.5 %copy-start.23 = (f32[72,128]{1,0:T(8,128)S(1)}, f32[72,128]{1,0:T(8,128)}, u32[]{:S(2)}) copy-start(f32[72,128]{1,0:T(8,128)} %constant.192.clone.sin_ref) | copy-start | bytes 110596
  269.1 12.5 %copy-start.25 = (bf16[64,144]{1,0:T(8,128)(2,1)S(1)}, bf16[64,144]{1,0:T(8,128)(2,1)}, u32[]{:S(2)}) copy-start(bf16[64,144]{1,0:T(8,128)(2,1)} %constant.190.clone.last_ref) | copy-start | bytes 55300
  270.1 38.5 %copy-start.28 = (f32[512]{0:T(512)S(1)}, f32[512]{0:T(512)}, u32[]{:S(2)}) copy-start(f32[512]{0:T(512)} %param.22) | copy-start | bytes 6148
  284.5 0.8 copy-start.5
  285.3 23.2 %all-to-all-start.4 = ((bf16[8,32,1024]{2,1,0:T(8,128)(2,1)}), bf16[8,32,1024]{2,1,0:T(8,128)(2,1)}, u32[]{:S(2)}, u32[]{:S(2)}) async-start(bf16[8,32,1024]{2,1,0:T(8,128)(2,1)} %copy-done.5), calls=%async_computation.4 | async-start | bytes 1048576 | tf_op jit(solution)/shard_map/all_to_all | solution.py:413
  292.5 7.6 %collective-permute-start.12 = (bf16[64,1024]{1,0:T(8,128)(2,1)S(1)}, bf16[64,1024]{1,0:T(8,128)(2,1)S(1)}, u32[]{:S(2)}, u32[]{:S(2)}) collective-permute-start(bf16[64,1024]{1,0:T(8,128)(2,1)S(1)} %get-tuple-element.40), channel_id=1, source_target_pairs={{0,1},{1,2},{2,3},{3,0},{4,5},{5,6},{6,7},{7,4},{8,9},{9,10},{10,1... | collective-permute-start | bytes 393224 | tf_op jit(solution)/shard_map/ppermute | solution.py:25
  296.3 8.6 %collective-permute-start.13 = (bf16[64,1024]{1,0:T(8,128)(2,1)S(1)}, bf16[64,1024]{1,0:T(8,128)(2,1)S(1)}, u32[]{:S(2)}, u32[]{:S(2)}) collective-permute-start(bf16[64,1024]{1,0:T(8,128)(2,1)S(1)} %get-tuple-element.39), channel_id=1, source_target_pairs={{0,2},{1,3},{2,0},{3,1},{4,6},{5,7},{6,4},{7,5},{8,10},{9,11},{10,... | collective-permute-start | bytes 393224 | tf_op jit(solution)/shard_map/ppermute | solution.py:25
  296.3 11.4 %collective-permute-start.14 = (bf16[64,1024]{1,0:T(8,128)(2,1)S(1)}, bf16[64,1024]{1,0:T(8,128)(2,1)S(1)}, u32[]{:S(2)}, u32[]{:S(2)}) collective-permute-start(bf16[64,1024]{1,0:T(8,128)(2,1)S(1)} %get-tuple-element.38), channel_id=1, source_target_pairs={{0,3},{1,0},{2,1},{3,2},{4,7},{5,4},{6,5},{7,6},{8,11},{9,8},{10,9... | collective-permute-start | bytes 393224 | tf_op jit(solution)/shard_map/ppermute | solution.py:25
  308.6 1.1 copy-start.1
  309.7 0.9 copy-start.12
  312.0 0.8 copy-start.3
  312.8 13.3 %collective-permute-start.15 = (bf16[1,4,64,1024]{3,2,1,0:T(8,128)(2,1)}, bf16[1,4,64,1024]{3,2,1,0:T(8,128)(2,1)}, u32[]{:S(2)}, u32[]{:S(2)}) collective-permute-start(bf16[1,4,64,1024]{3,2,1,0:T(8,128)(2,1)} %bitcast.76), channel_id=1, source_target_pairs={{0,16},{4,20},{8,24},{12,28},{16,0},{20,4},{24,8},{28,12},{1,17},{... | collective-permute-start | bytes 1572872 | tf_op jit(solution)/shard_map/ppermute | solution.py:38
  327.4 0.8 copy-start.31
  327.4 1.9 copy-start.32
  329.3 23.6 %collective-permute-start.16 = (bf16[2,4,64,1024]{3,2,1,0:T(8,128)(2,1)}, bf16[2,4,64,1024]{3,2,1,0:T(8,128)(2,1)}, u32[]{:S(2)}, u32[]{:S(2)}) collective-permute-start(bf16[2,4,64,1024]{3,2,1,0:T(8,128)(2,1)} %maximum_bitcast_fusion), channel_id=1, source_target_pairs={{0,8},{4,12},{8,0},{12,4},{16,24},{20,28},{24,16},{28,20},{1,9},{5... | collective-permute-start | bytes 3145736 | tf_op jit(solution)/shard_map/ppermute | solution.py:38
  356.1 43.4 %collective-permute-start.17 = (bf16[4,4,64,1024]{3,2,1,0:T(8,128)(2,1)}, bf16[4,4,64,1024]{3,2,1,0:T(8,128)(2,1)}, u32[]{:S(2)}, u32[]{:S(2)}) collective-permute-start(bf16[4,4,64,1024]{3,2,1,0:T(8,128)(2,1)} %bitcast.29), channel_id=1, source_target_pairs={{0,4},{4,0},{8,12},{12,8},{16,20},{20,16},{24,28},{28,24},{1,5},{5... | collective-permute-start | bytes 6291464 | tf_op jit(solution)/shard_map/ppermute | solution.py:38
  358.3 12.4 %all-to-all-start.1 = ((bf16[8,32,1024]{2,1,0:T(8,128)(2,1)}), bf16[8,32,1024]{2,1,0:T(8,128)(2,1)}, u32[]{:S(2)}, u32[]{:S(2)}) async-start(bf16[8,32,1024]{2,1,0:T(8,128)(2,1)} %bitcast.77), calls=%async_computation.1 | async-start | bytes 1048576 | tf_op jit(solution)/shard_map/all_to_all | solution.py:412
  362.4 35.0 %collective-permute-start.18 = (bf16[1024,256]{1,0:T(8,128)(2,1)}, bf16[1024,256]{1,0:T(8,128)(2,1)}, u32[]{:S(2)}, u32[]{:S(2)}) collective-permute-start(bf16[1024,256]{1,0:T(8,128)(2,1)} %copy-done.3), channel_id=1, source_target_pairs={{0,1},{1,2},{2,3},{3,0},{4,5},{5,6},{6,7},{7,4},{8,9},{9,10},{10,1... | collective-permute-start | bytes 1572872 | tf_op jit(solution)/shard_map/ppermute | solution.py:25
  370.7 0.9 copy-start.18
  371.6 0.8 copy-start.20
  372.4 0.8 copy-start.22
  373.1 0.8 copy-start.24
  373.9 0.8 copy-start.26
  378.5 0.8 copy-start.8
  379.2 13.3 %all-to-all-start.2 = ((bf16[8,32,1024]{2,1,0:T(8,128)(2,1)}), bf16[8,32,1024]{2,1,0:T(8,128)(2,1)S(1)}, u32[]{:S(2)}, u32[]{:S(2)}) async-start(bf16[8,32,1024]{2,1,0:T(8,128)(2,1)} %copy-done.8), calls=%async_computation.2 | async-start | bytes 1048576 | tf_op jit(solution)/shard_map/all_to_all | solution.py:413
  384.2 22.8 %collective-permute-start.19 = (bf16[1024,256]{1,0:T(8,128)(2,1)}, bf16[1024,256]{1,0:T(8,128)(2,1)}, u32[]{:S(2)}, u32[]{:S(2)}) collective-permute-start(bf16[1024,256]{1,0:T(8,128)(2,1)} %copy-done.3), channel_id=1, source_target_pairs={{0,2},{1,3},{2,0},{3,1},{4,6},{5,7},{6,4},{7,5},{8,10},{9,11},{10,... | collective-permute-start | bytes 1572872 | tf_op jit(solution)/shard_map/ppermute | solution.py:25
  384.5 45.0 %collective-permute-start.20 = (bf16[1024,256]{1,0:T(8,128)(2,1)}, bf16[1024,256]{1,0:T(8,128)(2,1)}, u32[]{:S(2)}, u32[]{:S(2)}) collective-permute-start(bf16[1024,256]{1,0:T(8,128)(2,1)} %copy-done.3), channel_id=1, source_target_pairs={{0,3},{1,0},{2,1},{3,2},{4,7},{5,4},{6,5},{7,6},{8,11},{9,8},{10,9... | collective-permute-start | bytes 1572872 | tf_op jit(solution)/shard_map/ppermute | solution.py:25
  392.5 0.8 copy-start.6
  393.3 1.1 copy-start.2
  394.4 1.0 copy-start.7
  395.5 0.9 copy-start.13
  397.1 54.8 %collective-permute-start.10 = (bf16[1024,256]{1,0:T(8,128)(2,1)S(1)}, bf16[1024,256]{1,0:T(8,128)(2,1)S(1)}, u32[]{:S(2)}, u32[]{:S(2)}) collective-permute-start(bf16[1024,256]{1,0:T(8,128)(2,1)S(1)} %shard_map.177.refs_0_), channel_id=1, source_target_pairs={{0,2},{1,3},{2,0},{3,1},{4,6},{5,7},{6,4},{7,5},{8,10},{9,11},{10,... | collective-permute-start | bytes 1572872 | tf_op jit(solution)/shard_map/ppermute | solution.py:25
  397.4 65.7 %collective-permute-start.11 = (bf16[1024,256]{1,0:T(8,128)(2,1)S(1)}, bf16[1024,256]{1,0:T(8,128)(2,1)S(1)}, u32[]{:S(2)}, u32[]{:S(2)}) collective-permute-start(bf16[1024,256]{1,0:T(8,128)(2,1)S(1)} %shard_map.177.refs_0_), channel_id=1, source_target_pairs={{0,3},{1,0},{2,1},{3,2},{4,7},{5,4},{6,5},{7,6},{8,11},{9,8},{10,9... | collective-permute-start | bytes 1572872 | tf_op jit(solution)/shard_map/ppermute | solution.py:25
  399.4 66.9 %collective-permute-start.9 = (bf16[1024,256]{1,0:T(8,128)(2,1)S(1)}, bf16[1024,256]{1,0:T(8,128)(2,1)S(1)}, u32[]{:S(2)}, u32[]{:S(2)}) collective-permute-start(bf16[1024,256]{1,0:T(8,128)(2,1)S(1)} %shard_map.177.refs_0_), channel_id=1, source_target_pairs={{0,1},{1,2},{2,3},{3,0},{4,5},{5,6},{6,7},{7,4},{8,9},{9,10},{10,1... | collective-permute-start | bytes 1572872 | tf_op jit(solution)/shard_map/ppermute | solution.py:25
  403.5 26.0 %copy-start.4 = (bf16[1024,256]{1,0:T(8,128)(2,1)S(1)}, bf16[1024,256]{1,0:T(8,128)(2,1)}, u32[]{:S(2)}) copy-start(bf16[1024,256]{1,0:T(8,128)(2,1)} %copy-done.3) | copy-start | bytes 1572868

commit v5 on v4

--- a/solution.py
+++ b/solution.py
@@ -9,6 +9,7 @@
 TAPS = 3
 LANES = 128
 HALO = 16
+DEPTH_STEP = 1024
 CHAN_BLOCK = 16
 CHUNKS = 2
 VMEM_BYTES = 48 * 1024 * 1024
@@ -23,10 +24,6 @@
 def shifted(value, axis, by):
     size = lax.axis_size(axis)
     return lax.ppermute(value, axis, [(i, (i + by) % size) for i in range(size)])
-
-
-def slots_of(value, axis):
-    return [value] + [shifted(value, axis, by) for by in range(1, lax.axis_size(axis))]
 
 
 def gather_by_doubling(value, axis):
@@ -49,26 +46,26 @@
     return 1 if size % LANES or (size // seq_count) % CHAN_BLOCK else CHUNKS
 
 
-def project_kernel(slots, extras, me_ref, *refs):
-    tok_refs = refs[:slots]
-    w_ref, taps_ref, halo_ref = refs[slots : slots + 3]
-    signal_ref, signal_t_ref, query_t_ref, tail_ref, acc = refs[slots + 3 + extras :]
-    step = pl.program_id(1)
+def project_kernel(extras, tok_ref, w_ref, taps_ref, halo_ref, *rest):
+    signal_ref, signal_t_ref, query_t_ref, acc = rest[extras:]
+    step = pl.program_id(0)
     rows = signal_t_ref.shape[0]
-    for z, tok_ref in enumerate(tok_refs):
-
-        @pl.when(step == z)
-        def _():
-            for p in range(3):
-                part = jnp.dot(tok_ref[...], w_ref[p], preferred_element_type=jnp.float32)
-                acc[p, HALO:, :] = part if z == 0 else part + acc[p, HALO:, :]
-
-    @pl.when(step == slots - 1)
+
+    @pl.when(step == 0)
+    def _():
+        for p in range(3):
+            acc[p, HALO:, :] = jnp.dot(tok_ref[...], w_ref[p], preferred_element_type=jnp.float32)
+
+    @pl.when(step > 0)
+    def _():
+        for p in range(3):
+            acc[p, HALO:, :] += jnp.dot(tok_ref[...], w_ref[p], preferred_element_type=jnp.float32)
+
+    @pl.when(step == pl.num_programs(0) - 1)
     def _():
         for p in range(3):
             acc[p, :HALO, :] = halo_ref[p].astype(jnp.float32)
             acc[p, HALO:, :] = acc[p, HALO:, :].astype(jnp.bfloat16).astype(jnp.float32)
-            tail_ref[p] = acc[p, rows:, :].astype(tail_ref.dtype)
         for r in range(0, rows, LANES):
             streams = []
             for p in range(3):
@@ -82,46 +79,35 @@
             signal_ref[:, r : r + LANES] = signal.T.astype(signal_ref.dtype)
 
 
-def project(slots, in_weight, conv_weight, halo, *after):
-    rows, depth = slots[0].shape
-    count = len(slots)
-    chans = in_weight.shape[2]
-    tile = 2 * LANES if chans % (2 * LANES) == 0 else chans
-    flat = jax.ShapeDtypeStruct((rows, chans), jnp.bfloat16)
-    me = lax.axis_index("chan").astype(jnp.int32).reshape(1)
-    return pl.pallas_call(
-        lambda *refs: project_kernel(count, len(after), *refs),
-        grid_spec=pltpu.PrefetchScalarGridSpec(
-            num_scalar_prefetch=1,
-            grid=(chans // tile, count),
-            in_specs=[
-                *[pl.BlockSpec((rows, depth), lambda i, z, me: (0, 0)) for _ in slots],
-                pl.BlockSpec((3, depth, tile), lambda i, z, me: (0, lax.rem(me[0] - z + count, count), i)),
-                pl.BlockSpec((TAPS, 3, tile), lambda i, z, me: (0, 0, i)),
-                pl.BlockSpec((3, HALO, tile), lambda i, z, me: (0, 0, i)),
-                *[pl.BlockSpec(memory_space=pl.ANY) for _ in after],
-            ],
-            out_specs=[
-                pl.BlockSpec((tile, rows), lambda i, z, me: (i, 0)),
-                pl.BlockSpec((rows, tile), lambda i, z, me: (0, i)),
-                pl.BlockSpec((rows, tile), lambda i, z, me: (0, i)),
-                pl.BlockSpec((3, HALO, tile), lambda i, z, me: (0, 0, i)),
-            ],
-            scratch_shapes=[pltpu.VMEM((3, HALO + rows, tile), jnp.float32)],
-        ),
-        out_shape=[
-            jax.ShapeDtypeStruct((chans, rows), jnp.bfloat16),
-            flat,
-            flat,
-            jax.ShapeDtypeStruct((3, HALO, chans), jnp.bfloat16),
-        ],
+def project(gathered, in_weight, conv_weight, halo, lo, size, *after):
+    rows, depth = gathered.shape
+    step = min(DEPTH_STEP, depth)
+    at = lo // size
+    flat = jax.ShapeDtypeStruct((rows, size), jnp.bfloat16)
+    return pl.pallas_call(
+        lambda *refs: project_kernel(len(after), *refs),
+        grid=(depth // step,),
+        in_specs=[
+            pl.BlockSpec((rows, step), lambda z: (0, z)),
+            pl.BlockSpec((3, step, size), lambda z: (0, z, at)),
+            pl.BlockSpec((TAPS, 3, size), lambda z: (0, 0, at)),
+            pl.BlockSpec((3, HALO, size), lambda z: (0, 0, at)),
+            *[pl.BlockSpec(memory_space=pl.ANY) for _ in after],
+        ],
+        out_specs=[
+            pl.BlockSpec((size, rows), lambda z: (0, 0)),
+            pl.BlockSpec((rows, size), lambda z: (0, 0)),
+            pl.BlockSpec((rows, size), lambda z: (0, 0)),
+        ],
+        out_shape=[jax.ShapeDtypeStruct((size, rows), jnp.bfloat16), flat, flat],
+        scratch_shapes=[pltpu.VMEM((3, HALO + rows, size), jnp.float32)],
         compiler_params=pltpu.CompilerParams(vmem_limit_bytes=VMEM_BYTES),
         cost_estimate=pl.CostEstimate(
-            flops=2 * 3 * rows * depth * count * chans,
-            bytes_accessed=2 * depth * count * (3 * chans + rows),
+            flops=2 * 3 * rows * depth * size,
+            bytes_accessed=2 * depth * (3 * size + rows),
             transcendentals=0,
         ),
-    )(me, *slots, in_weight, conv_weight, halo, *after)
+    )(gathered, in_weight, conv_weight, halo, *after)
 
 
 def transform_tables(seq_count, tok_rows):
@@ -221,39 +207,30 @@
     )(values, response, *tables)
 
 
-def gate_kernel(conv_ref, skip_ref, *refs):
-    out_ref = refs[-1]
+def gate_kernel(conv_ref, skip_ref, signal_ref, query_ref, out_ref):
     conv = conv_ref[...].astype(jnp.float32).T
-    skip = skip_ref[...]
-    at = 0
-    for signal_ref, query_ref in zip(refs[0:-1:2], refs[1:-1:2]):
-        rows = signal_ref.shape[0]
-        inner = conv[at : at + rows] + skip * signal_ref[...].astype(jnp.float32)
-        out_ref[at : at + rows, :] = (query_ref[...].astype(jnp.float32) * inner).astype(out_ref.dtype)
-        at += rows
-
-
-def gate(longconv, skip, start, pieces):
+    inner = conv + skip_ref[...] * signal_ref[...].astype(jnp.float32)
+    out_ref[...] = (query_ref[...].astype(jnp.float32) * inner).astype(out_ref.dtype)
+
+
+def gate(longconv, skip, lo, signal, query):
     chans, tok_rows = longconv.shape
-    first = start // LANES
-    given, specs = [], []
-    for piece in pieces:
-        for array in piece:
-            given.append(array)
-            specs.append(pl.BlockSpec((array.shape[0], LANES), lambda i: (0, first + i)))
+    first = lo // LANES
+    flat = pl.BlockSpec((tok_rows, LANES), lambda i: (0, i))
     return pl.pallas_call(
         gate_kernel,
         grid=(chans // LANES,),
         in_specs=[
             pl.BlockSpec((LANES, tok_rows), lambda i: (i, 0)),
             pl.BlockSpec((1, LANES), lambda i: (0, first + i)),
-            *specs,
-        ],
-        out_specs=pl.BlockSpec((tok_rows, LANES), lambda i: (0, i)),
+            flat,
+            flat,
+        ],
+        out_specs=flat,
         out_shape=jax.ShapeDtypeStruct((tok_rows, chans), jnp.bfloat16),
         compiler_params=pltpu.CompilerParams(vmem_limit_bytes=VMEM_BYTES),
         cost_estimate=pl.CostEstimate(flops=4 * chans * tok_rows, bytes_accessed=8 * chans * tok_rows, transcendentals=0),
-    )(longconv, skip[None, :], *given)
+    )(longconv, skip[None, :], signal, query)
 
 
 def reorder_kernel(spec_ref, order_ref, out_ref):
@@ -288,7 +265,7 @@
         out_ref[part] = held[...].reshape(chans, rows, LANES).astype(out_ref.dtype)
 
 
-def folded_response(spectrum, seq_count, chunks):
+def reordered_spectrum(spectrum, seq_count, chunks):
     parts, chans, own, tok_rows = spectrum.shape
     runs = tok_rows // LANES
     size = chans // chunks
@@ -299,7 +276,7 @@
     wanted = jnp.where(lax.axis_index("seq") >= seq_count // 2, tok_rows - 1 - wanted, wanted)
     order = (row == wanted).astype(jnp.bfloat16)
     shape = (seq_count, parts, chunks, own * each, tok_rows)
-    sent = pl.pallas_call(
+    return pl.pallas_call(
         reorder_kernel,
         grid=(parts, chunks),
         in_specs=[
@@ -313,6 +290,12 @@
             flops=2 * spectrum.size * tok_rows, bytes_accessed=6 * spectrum.size, transcendentals=0
         ),
     )(spectrum.reshape(parts, chans * own, tok_rows), order)
+
+
+def folded_response(sent, own):
+    seq_count, parts, chunks, pairs, tok_rows = sent.shape
+    runs = tok_rows // LANES
+    each = pairs // own
     got = lax.all_to_all(sent, "seq", split_axis=0, concat_axis=0, tiled=True)
     block = min(CHAN_BLOCK, each)
     rows = (seq_count + 1) * runs
@@ -321,13 +304,13 @@
         grid=(chunks, each // block),
         in_specs=[pl.BlockSpec((seq_count, parts, 1, own * block, tok_rows), lambda j, i: (0, 0, j, i, 0))],
         out_specs=pl.BlockSpec((parts, block, rows, LANES), lambda j, i: (0, j * (each // block) + i, 0, 0)),
-        out_shape=jax.ShapeDtypeStruct((parts, chans // seq_count, rows, LANES), jnp.bfloat16),
+        out_shape=jax.ShapeDtypeStruct((parts, chunks * each, rows, LANES), jnp.bfloat16),
         scratch_shapes=[
             pltpu.VMEM((seq_count * runs * own * block, LANES), jnp.float32),
             pltpu.VMEM((block * rows, LANES), jnp.float32),
         ],
         compiler_params=pltpu.CompilerParams(vmem_limit_bytes=VMEM_BYTES),
-        cost_estimate=pl.CostEstimate(flops=spectrum.size, bytes_accessed=3 * spectrum.size, transcendentals=0),
+        cost_estimate=pl.CostEstimate(flops=sent.size, bytes_accessed=3 * sent.size, transcendentals=0),
     )(got)
 
 
@@ -344,7 +327,7 @@
     return jnp.stack(pieces)
 
 
-def combine_kernel(slots, *refs):
+def combine_kernel(slots, me_ref, *refs):
     total_ref = refs[slots + 1] if len(refs) == slots + 3 else None
     w_ref, out_ref = refs[slots], refs[-1]
     total = None if total_ref is None else total_ref[...]
@@ -355,23 +338,32 @@
     out_ref[...] = total.astype(out_ref.dtype)
 
 
-def combine(slots, weight, start, total, dtype):
-    tok_rows, size = slots[0].shape
+def combine(gathered, weight, lo, total, dtype):
+    tok_rows = gathered.shape[0]
     _, count, each, features = weight.shape
+    size = gathered.shape[1] // count
     per = size // each
-    first = start // size
+    first = lo // size
     tile = min(2 * LANES, features)
-    block = pl.BlockSpec((tok_rows, tile), lambda i: (0, i))
+    block = pl.BlockSpec((tok_rows, tile), lambda i, me: (0, i))
     given = [] if total is None else [total]
+    me = lax.axis_index("chan").astype(jnp.int32).reshape(1)
+
+    def slot(k):
+        return pl.BlockSpec((tok_rows, size), lambda i, me: (0, lax.rem(me[0] - k + count, count)))
+
     return pl.pallas_call(
         lambda *refs: combine_kernel(count, *refs),
-        grid=(features // tile,),
-        in_specs=[
-            *[pl.BlockSpec((tok_rows, size), lambda i: (0, 0)) for _ in slots],
-            pl.BlockSpec((per, count, each, tile), lambda i: (first, 0, 0, i)),
-            *[block for _ in given],
-        ],
-        out_specs=block,
+        grid_spec=pltpu.PrefetchScalarGridSpec(
+            num_scalar_prefetch=1,
+            grid=(features // tile,),
+            in_specs=[
+                *[slot(k) for k in range(count)],
+                pl.BlockSpec((per, count, each, tile), lambda i, me: (first, 0, 0, i)),
+                *[block for _ in given],
+            ],
+            out_specs=block,
+        ),
         out_shape=jax.ShapeDtypeStruct((tok_rows, features), dtype),
         compiler_params=pltpu.CompilerParams(vmem_limit_bytes=VMEM_BYTES),
         cost_estimate=pl.CostEstimate(
@@ -379,7 +371,7 @@
             bytes_accessed=2 * count * size * (tok_rows + features) + 6 * tok_rows * features,
             transcendentals=0,
         ),
-    )(*slots, weight, *given)
+    )(me, *[gathered] * count, weight, *given)
 
 
 def shards(tokens, in_weight, conv_weight, spectrum, skip, out_weight):
@@ -389,39 +381,31 @@
     chans = in_weight.shape[2]
     chunks = chunk_count(chans, seq_count)
     size = chans // chunks
-    cut = tok_rows * 3 // 4
-    early = slots_of(tokens[:cut], "chan")
+    gathered = lax.all_gather(tokens, "chan", axis=1, tiled=True)
     halo = gather_by_doubling(from_behind(tokens[tok_rows - HALO :], "seq", 1), "chan")
-    late, *early[1:] = lax.optimization_barrier((tokens[cut:], *early[1:]))
-    late = slots_of(late, "chan")
+    sent = reordered_spectrum(spectrum, seq_count, chunks)
+    halo, sent, out_weight = lax.optimization_barrier((halo, sent, out_weight))
+    response = folded_response(sent, spectrum.shape[2])
+    weight = gather_by_doubling(feature_rows(out_weight, seq_count), "seq")
     halo = jnp.einsum(
         "ztd,pzdc->ptc",
         halo,
         in_weight.reshape(3, chan_count, depth, chans),
         preferred_element_type=jnp.float32,
     ).astype(jnp.bfloat16)
-    response = folded_response(spectrum, seq_count, chunks)
-    signal_a, *piece_a, tail = project(early, in_weight, conv_weight, halo)
-    signal_b, *piece_b, _ = project(late, in_weight, conv_weight, tail, response)
-    signal = jnp.concatenate([signal_a, signal_b], axis=1)
-    signal, out_weight = lax.optimization_barrier((signal, out_weight))
-    weight = feature_rows(out_weight, seq_count)
-    gated = []
+    total = None
     for lo in range(0, chans, size):
-        values = signal[lo : lo + size].reshape(seq_count, size // seq_count, tok_rows)
+        signal, signal_t, query_t = project(
+            gathered, in_weight, conv_weight, halo, lo, size, response, weight
+        )
+        values = signal.reshape(seq_count, size // seq_count, tok_rows)
         values = lax.all_to_all(values, "seq", split_axis=0, concat_axis=0, tiled=True)
         longconv = lax.all_to_all(
             long_conv(values, response, lo // seq_count), "seq", split_axis=0, concat_axis=0, tiled=True
         ).reshape(size, tok_rows)
-        gated.append(gate(longconv, skip, lo, (piece_a, piece_b)))
-        if lo == 0:
-            gated[0], weight = lax.optimization_barrier((gated[0], weight))
-    slots = [slots_of(value, "chan") for value in gated]
-    weight = gather_by_doubling(weight, "seq")
-    total = None
-    for j, lo in enumerate(range(0, chans, size)):
+        gated = lax.all_gather(gate(longconv, skip, lo, signal_t, query_t), "chan", axis=1, tiled=True)
         dtype = jnp.bfloat16 if lo + size == chans else jnp.float32
-        total = combine(slots[j], weight, lo, total, dtype)
+        total = combine(gated, weight, lo, total, dtype)
     return total
 
 

time: 474 us -> 317 us (0.67)
  the two profiles are of different devices: /device:TPU:19 before, /device:TPU:0 now
where the time goes in v5:
time: 317 us; the launch traced here: 316 us
  waiting for transfers between devices  134 us (42%)
  Pallas kernels  55.1 us (17%)
  blocking collectives  49.7 us (16%)
  starting transfers between devices  33.1 us (10%)
  local copies, waits for them, and re-layouts  19.2 us (6%)
  between operations  13.4 us (4%)
  matrix products  6.3 us (2%)
  other arithmetic  5.57 us (2%)
    ppermute x5, waiting for transfers between devices, gather_by_doubling(): other = lax.ppermute(held, axis, [(i, i ^ bit) for i in range(size)])  60 us
    all_gather x2, waiting for transfers between devices, shards(): lax.all_gather(gate(longconv, skip, lo, signal_t, query_t), 'chan', axis=...  41.7 us
    all_to_all x2, blocking collectives, shards(): lax.all_to_all(values, 'seq', split_axis=0, concat_axis=0, tiled=True)  25.4 us
    all_to_all x2, blocking collectives, shards(): lax.all_to_all(long_conv(values, response, lo // seq_count), 'seq', split...  24.3 us
    pallas_call x2, Pallas kernels, project(): pl.pallas_call(lambda *refs: project_kernel(len(after), *refs), grid=(dep...  22.4 us
    ppermute x5, starting transfers between devices, gather_by_doubling(): other = lax.ppermute(held, axis, [(i, i ^ bit) for i in range(size)])  22.2 us
    ppermute x3, waiting for transfers between devices, shifted(): lax.ppermute(value, axis, [(i, (i + by) % size) for i in range(size)])  16.4 us
    all_gather x1, waiting for transfers between devices, shards(): gathered = lax.all_gather(tokens, 'chan', axis=1, tiled=True)  14.3 us
  transfers between devices with their start and end apart: 13, of which 9 were waited for; matrix products, arithmetic and copies ran while one was open for 9% of the time, Pallas kernels for 11%

profile of v5, /device:TPU:0, one launch (start us, length us, event | category | flops | bytes accessed | tf_op | source)
XLA Modules:
  0.0 316.4 jit_solution(2522813557012882352)
XLA Ops:
  6.5 0.7 all-gather.4.cloned.1.call-update
  7.3 0.8 slice.3
  8.0 2.3 collective-permute-start
  10.4 0.8 collective-permute-done
  11.2 3.4 %collective-permute-start.1 = (bf16[1,16,1024]{2,1,0:T(8,128)(2,1)S(1)}, bf16[1,16,1024]{2,1,0:T(8,128)(2,1)S(1)}, u32[]{:S(2)}, u32[]{:S(2)}) collective-permute-start(bf16[1,16,1024]{2,1,0:T(8,128)(2,1)S(1)} %bitcast.93), channel_id=1, source_target_pairs={{0,2},{1,3},{2,0},{3,1},{4,6},{5,7},{6,4},{7,5},{8,10},{9,11},{10,... | collective-permute-start | bytes 98312 | tf_op jit(solution)/shard_map/ppermute | solution.py:35
  14.6 0.7 fusion.1.order_ref
  15.4 11.3 %reshape.40.spec_ref = f32[2,1024,1024]{2,1,0:T(8,128)} reshape(f32[2,512,2,1024]{3,2,1,0:T(2,128)} %param.21) | data formatting | bytes 16777216 | tf_op jit(solution)/shard_map/reshape | solution.py:292
  26.7 0.0 collective-permute-done.1
  26.7 1.7 collective-permute-start.2
  28.4 8.5 %shard_map.172 = bf16[8,2,2,64,1024]{4,3,2,1,0:T(8,128)(2,1)} custom-call(f32[2,1024,1024]{2,1,0:T(8,128)} %reshape.40.spec_ref, bf16[1024,1024]{1,0:T(8,128)(2,1)S(1)} %fusion.1.order_ref), custom_call_target="tpu_custom_call" | custom-call | flops 4294967296 | bytes 12582912 | tf_op jit(solution)/shard_map/pallas_call | solution.py:279
  36.9 3.0 collective-permute-done.2
  39.9 1.5 dynamic-slice_bitcast_fusion
  41.4 0.1 collective-permute-start.3
  41.4 2.0 collective-permute-start.4
  43.4 1.9 collective-permute-start.5
  45.3 7.1 %collective-permute-done.3 = bf16[64,1024]{1,0:T(8,128)(2,1)S(1)} collective-permute-done((bf16[64,1024]{1,0:T(8,128)(2,1)S(1)}, bf16[64,1024]{1,0:T(8,128)(2,1)S(1)}, u32[]{:S(2)}, u32[]{:S(2)}) %collective-permute-start.3) | collective-permute-done | bytes 131104 | tf_op jit(solution)/shard_map/ppermute | solution.py:26
  52.4 9.3 %collective-permute-done.4 = bf16[64,1024]{1,0:T(8,128)(2,1)S(1)} collective-permute-done((bf16[64,1024]{1,0:T(8,128)(2,1)S(1)}, bf16[64,1024]{1,0:T(8,128)(2,1)S(1)}, u32[]{:S(2)}, u32[]{:S(2)}) %collective-permute-start.4) | collective-permute-done | bytes 131104 | tf_op jit(solution)/shard_map/ppermute | solution.py:26
  61.6 0.0 collective-permute-done.5
  61.6 0.1 maximum_bitcast_fusion.1
  61.7 3.8 %collective-permute-start.6 = (bf16[1,4,64,1024]{3,2,1,0:T(8,128)(2,1)S(1)}, bf16[1,4,64,1024]{3,2,1,0:T(8,128)(2,1)S(1)}, u32[]{:S(2)}, u32[]{:S(2)}) collective-permute-start(bf16[1,4,64,1024]{3,2,1,0:T(8,128)(2,1)S(1)} %maximum_bitcast_fusion.1), channel_id=1, source_target_pairs={{0,16},{4,20},{8,24},{12,28},{16,0},{20,4},{24,8},{28,12},{1,17},{... | collective-permute-start | bytes 1572872 | tf_op jit(solution)/shard_map/ppermute | solution.py:35
  65.5 4.6 %all-to-all-start = ((bf16[8,2,2,64,1024]{4,3,2,1,0:T(8,128)(2,1)}), bf16[8,2,2,64,1024]{4,3,2,1,0:T(8,128)(2,1)}, u32[]{:S(2)}, u32[]{:S(2)}) async-start(bf16[8,2,2,64,1024]{4,3,2,1,0:T(8,128)(2,1)} %shard_map.172), calls=%async_computation | async-start | bytes 8388608 | tf_op jit(solution)/shard_map/all_to_all | solution.py:299
  70.2 0.0 all-gather.8.cloned.1.call-start
  70.2 8.2 %collective-permute-done.6 = bf16[1,4,64,1024]{3,2,1,0:T(8,128)(2,1)S(1)} collective-permute-done((bf16[1,4,64,1024]{3,2,1,0:T(8,128)(2,1)S(1)}, bf16[1,4,64,1024]{3,2,1,0:T(8,128)(2,1)S(1)}, u32[]{:S(2)}, u32[]{:S(2)}) %collective-permute-start.6) | collective-permute-done | bytes 524320 | tf_op jit(solution)/shard_map/ppermute | solution.py:35
  78.4 0.1 select_bitcast_fusion.5
  78.5 0.1 maximum_bitcast_fusion
  78.6 13.3 %collective-permute-start.7 = (bf16[2,4,64,1024]{3,2,1,0:T(8,128)(2,1)S(1)}, bf16[2,4,64,1024]{3,2,1,0:T(8,128)(2,1)S(1)}, u32[]{:S(2)}, u32[]{:S(2)}) collective-permute-start(bf16[2,4,64,1024]{3,2,1,0:T(8,128)(2,1)S(1)} %maximum_bitcast_fusion), channel_id=1, source_target_pairs={{0,8},{4,12},{8,0},{12,4},{16,24},{20,28},{24,16},{28,20},{1,9},{5... | collective-permute-start | bytes 3145736 | tf_op jit(solution)/shard_map/ppermute | solution.py:35
  91.9 48.9 %collective-permute-done.7 = bf16[2,4,64,1024]{3,2,1,0:T(8,128)(2,1)S(1)} collective-permute-done((bf16[2,4,64,1024]{3,2,1,0:T(8,128)(2,1)S(1)}, bf16[2,4,64,1024]{3,2,1,0:T(8,128)(2,1)S(1)}, u32[]{:S(2)}, u32[]{:S(2)}) %collective-permute-start.7) | collective-permute-done | bytes 1048608 | tf_op jit(solution)/shard_map/ppermute | solution.py:35
  140.8 0.1 select_bitcast_fusion.3
  140.9 1.5 pad_maximum_fusion.1
  142.4 0.0 collective-permute-start.8
  142.4 6.3 %fusion.3.refs_3_ = bf16[3,16,512]{2,1,0:T(8,128)(2,1)S(1)} fusion(bf16[3,4,1024,512]{3,2,1,0:T(8,128)(2,1)} %bitcast.81, bf16[4,16,1024]{2,1,0:T(8,128)(2,1)S(1)} %bitcast.86), kind=kOutput, calls=%fused_computation.9 | convolution fusion | flops 201351168 | bytes 12763136 | tf_op jit(solution)/shard_map/ztd,pzdc->ptc/dot_general | solution.py:390
  148.7 0.0 all-to-all-done.got_ref
  148.7 4.1 %shard_map.173.refs_4_.resp_ref = bf16[2,64,72,128]{3,2,1,0:T(8,128)(2,1)S(1)} custom-call(bf16[8,2,2,64,1024]{4,3,2,1,0:T(8,128)(2,1)} %all-to-all-done.got_ref), custom_call_target="tpu_custom_call" | custom-call | flops 2097152 | bytes 6291456 | tf_op jit(solution)/shard_map/pallas_call | solution.py:302
  152.8 0.0 collective-permute-done.8
  152.8 2.5 select_bitcast_fusion.1
  155.3 0.4 pad_maximum_fusion
  155.7 0.0 copy-start.8
  155.7 2.5 copy.22
  158.2 14.3 %all-gather.4.cloned.1.call-done.refs_0_ = bf16[1024,4096]{1,0:T(8,128)(2,1)} async-done(((bf16[1024,1024]{1,0:T(8,128)(2,1)}), bf16[1024,4096]{1,0:T(8,128)(2,1)}) %all-gather.4.cloned.1.call-update) | async-done | bytes 8388624 | tf_op jit(solution)/shard_map/all_gather | solution.py:384
  172.5 0.0 copy-start.5
  172.5 0.0 copy-start.6
  172.5 0.0 copy-start.7
  172.5 11.2 %shard_map.177 = (bf16[256,1024]{1,0:T(8,128)(2,1)S(1)}, bf16[1024,256]{1,0:T(8,128)(2,1)S(1)}, bf16[1024,256]{1,0:T(8,128)(2,1)S(1)}) custom-call(bf16[1024,4096]{1,0:T(8,128)(2,1)} %all-gather.4.cloned.1.call-done.refs_0_, bf16[3,4096,512]{2,1,0:T(8,128)(2,1)} %refs_1_.3, f32[3,3,512]{2,1,0:T(4,128)S(1)} %copy-done.8, ...), custom_call_target="tpu_custom_call" | custom-call | flops 6442450944 | bytes 14680064 | tf_op jit(solution)/shard_map/pallas_call | solution.py:87
  183.7 0.0 copy-start.9
  183.7 13.2 %all_to_all.25.signal_ref = bf16[8,32,1024]{2,1,0:T(8,128)(2,1)S(1)} all-to-all(bf16[8,32,1024]{2,1,0:T(8,128)(2,1)S(1)} %bitcast.78), channel_id=1, replica_groups=mesh['seq'=8,'chan'=4] {'seq'}, dimensions={0} | all-to-all | bytes 1048576 | tf_op jit(solution)/shard_map/all_to_all | solution.py:402
  197.0 0.0 copy-done.2
  197.0 0.0 copy-done.4
  197.0 3.0 shard_map.178
  200.0 12.2 %all_to_all.26 = bf16[8,32,1024]{2,1,0:T(8,128)(2,1)S(1)} all-to-all(bf16[8,32,1024]{2,1,0:T(8,128)(2,1)S(1)} %shard_map.178), channel_id=1, replica_groups=mesh['seq'=8,'chan'=4] {'seq'}, dimensions={0} | all-to-all | bytes 1048576 | tf_op jit(solution)/shard_map/all_to_all | solution.py:403
  212.2 1.2 shard_map.179
  213.4 0.0 all-gather.8.cloned.1.call-update
  213.4 0.0 all-gather.6.cloned.1.call-start
  213.5 11.2 %shard_map.174 = (bf16[256,1024]{1,0:T(8,128)(2,1)S(1)}, bf16[1024,256]{1,0:T(8,128)(2,1)S(1)}, bf16[1024,256]{1,0:T(8,128)(2,1)S(1)}) custom-call(bf16[1024,4096]{1,0:T(8,128)(2,1)} %all-gather.4.cloned.1.call-done.refs_0_, bf16[3,4096,512]{2,1,0:T(8,128)(2,1)} %refs_1_.3, f32[3,3,512]{2,1,0:T(4,128)S(1)} %copy-done.8, ...), custom_call_target="tpu_custom_call" | custom-call | flops 6442450944 | bytes 14680064 | tf_op jit(solution)/shard_map/pallas_call | solution.py:87
  224.7 12.2 %all_to_all.27.signal_ref = bf16[8,32,1024]{2,1,0:T(8,128)(2,1)S(1)} all-to-all(bf16[8,32,1024]{2,1,0:T(8,128)(2,1)S(1)} %bitcast.77), channel_id=1, replica_groups=mesh['seq'=8,'chan'=4] {'seq'}, dimensions={0} | all-to-all | bytes 1048576 | tf_op jit(solution)/shard_map/all_to_all | solution.py:402
  236.9 3.0 shard_map.175
  239.8 12.2 %all_to_all.28 = bf16[8,32,1024]{2,1,0:T(8,128)(2,1)S(1)} all-to-all(bf16[8,32,1024]{2,1,0:T(8,128)(2,1)S(1)} %shard_map.175), channel_id=1, replica_groups=mesh['seq'=8,'chan'=4] {'seq'}, dimensions={0} | all-to-all | bytes 1048576 | tf_op jit(solution)/shard_map/all_to_all | solution.py:403
  252.0 1.2 shard_map.176
  253.2 0.0 all-gather.6.cloned.1.call-update
  253.2 2.9 all-gather.8.cloned.1.call-done.refs_1_.refs_2_.refs_3_.refs_4_
  256.1 1.6 copy-done
  257.7 5.7 %shard_map.180.refs_6_ = f32[1024,1024]{1,0:T(8,128)} custom-call(s32[1]{0:T(128)} %bitcast.refs_0_, bf16[1024,1024]{1,0:T(8,128)(2,1)S(1)} %copy-done, bf16[1024,1024]{1,0:T(8,128)(2,1)S(1)} %copy-done, bf16[1024,1024]{1,0:T(8,128)(2,1)S(1)} %copy-done, bf16[1024,1024]{1,0:T(8,128)(2,1)S(1)} %copy-done, bf16[8,4,64,1024]{3,2,1,0:T(8,128)(2,1)} %bitcast.84), custom_call_target="tpu_custom_call" | custom-call | flops 2147483648 | bytes 10485760 | tf_op jit(solution)/shard_map/pallas_call | solution.py:355
  263.4 38.8 %all-gather.6.cloned.1.call-done.refs_1_.refs_2_.refs_3_.refs_4_ = bf16[1024,1024]{1,0:T(8,128)(2,1)} async-done(((bf16[1024,256]{1,0:T(8,128)(2,1)}), bf16[1024,1024]{1,0:T(8,128)(2,1)}) %all-gather.6.cloned.1.call-update) | async-done | bytes 2097168 | tf_op jit(solution)/shard_map/all_gather | solution.py:406
  302.2 1.6 copy-done.1
  303.8 6.1 %shard_map.181 = bf16[1024,1024]{1,0:T(8,128)(2,1)} custom-call(s32[1]{0:T(128)} %bitcast.refs_0_, bf16[1024,1024]{1,0:T(8,128)(2,1)S(1)} %copy-done.1, bf16[1024,1024]{1,0:T(8,128)(2,1)S(1)} %copy-done.1, bf16[1024,1024]{1,0:T(8,128)(2,1)S(1)} %copy-done.1, bf16[1024,1024]{1,0:T(8,128)(2,1)S(1)} %copy-done.1, bf16[8,4,64,1024]{3,2,1,0:T(8,128)(2,1)} %bitcast.85, ...), custom_call_target="tpu_custom_call" | custom-call | flops 2147483648 | bytes 10485760 | tf_op jit(solution)/shard_map/pallas_call | solution.py:355
  (19 shorter events, 0.1 us)
Async XLA Ops:
  6.5 165.9 %all-gather.4.cloned.1.call-start = ((), (), s32[]{:S(2)}) async-start(), calls=%async_computation.5 | async-start | bytes 10485760 | tf_op jit(solution)/shard_map/all_gather | solution.py:384
  8.0 3.2 %collective-permute-start = (bf16[16,1024]{1,0:T(8,128)(2,1)S(1)}, bf16[16,1024]{1,0:T(8,128)(2,1)S(1)}, u32[]{:S(2)}, u32[]{:S(2)}) collective-permute-start(bf16[16,1024]{1,0:T(8,128)(2,1)S(1)} %slice.3), channel_id=1, source_target_pairs={{0,4},{4,8},{8,12},{12,16},{16,20},{20,24},{24,28},{1,5},{5,9},{9,... | collective-permute-start | bytes 98312 | tf_op jit(solution)/shard_map/ppermute | solution.py:21
  11.2 15.5 %collective-permute-start.1 = (bf16[1,16,1024]{2,1,0:T(8,128)(2,1)S(1)}, bf16[1,16,1024]{2,1,0:T(8,128)(2,1)S(1)}, u32[]{:S(2)}, u32[]{:S(2)}) collective-permute-start(bf16[1,16,1024]{2,1,0:T(8,128)(2,1)S(1)} %bitcast.93), channel_id=1, source_target_pairs={{0,2},{1,3},{2,0},{3,1},{4,6},{5,7},{6,4},{7,5},{8,10},{9,11},{10,... | collective-permute-start | bytes 98312 | tf_op jit(solution)/shard_map/ppermute | solution.py:35
  26.7 13.1 %collective-permute-start.2 = (bf16[2,16,1024]{2,1,0:T(8,128)(2,1)S(1)}, bf16[2,16,1024]{2,1,0:T(8,128)(2,1)S(1)}, u32[]{:S(2)}, u32[]{:S(2)}) collective-permute-start(bf16[2,16,1024]{2,1,0:T(8,128)(2,1)S(1)} %maximum_bitcast_fusion.2), channel_id=1, source_target_pairs={{0,1},{1,0},{2,3},{3,2},{4,5},{5,4},{6,7},{7,6},{8,9},{9,8},{10,11... | collective-permute-start | bytes 196616 | tf_op jit(solution)/shard_map/ppermute | solution.py:35
  41.4 11.0 %collective-permute-start.3 = (bf16[64,1024]{1,0:T(8,128)(2,1)S(1)}, bf16[64,1024]{1,0:T(8,128)(2,1)S(1)}, u32[]{:S(2)}, u32[]{:S(2)}) collective-permute-start(bf16[64,1024]{1,0:T(8,128)(2,1)S(1)} %get-tuple-element.28), channel_id=1, source_target_pairs={{0,1},{1,2},{2,3},{3,0},{4,5},{5,6},{6,7},{7,4},{8,9},{9,10},{10,1... | collective-permute-start | bytes 393224 | tf_op jit(solution)/shard_map/ppermute | solution.py:26
  41.4 20.2 %collective-permute-start.4 = (bf16[64,1024]{1,0:T(8,128)(2,1)S(1)}, bf16[64,1024]{1,0:T(8,128)(2,1)S(1)}, u32[]{:S(2)}, u32[]{:S(2)}) collective-permute-start(bf16[64,1024]{1,0:T(8,128)(2,1)S(1)} %get-tuple-element.27), channel_id=1, source_target_pairs={{0,2},{1,3},{2,0},{3,1},{4,6},{5,7},{6,4},{7,5},{8,10},{9,11},{10,... | collective-permute-start | bytes 393224 | tf_op jit(solution)/shard_map/ppermute | solution.py:26
  43.4 18.2 %collective-permute-start.5 = (bf16[64,1024]{1,0:T(8,128)(2,1)S(1)}, bf16[64,1024]{1,0:T(8,128)(2,1)S(1)}, u32[]{:S(2)}, u32[]{:S(2)}) collective-permute-start(bf16[64,1024]{1,0:T(8,128)(2,1)S(1)} %get-tuple-element.26), channel_id=1, source_target_pairs={{0,3},{1,0},{2,1},{3,2},{4,7},{5,4},{6,5},{7,6},{8,11},{9,8},{10,9... | collective-permute-start | bytes 393224 | tf_op jit(solution)/shard_map/ppermute | solution.py:26
  61.7 16.7 %collective-permute-start.6 = (bf16[1,4,64,1024]{3,2,1,0:T(8,128)(2,1)S(1)}, bf16[1,4,64,1024]{3,2,1,0:T(8,128)(2,1)S(1)}, u32[]{:S(2)}, u32[]{:S(2)}) collective-permute-start(bf16[1,4,64,1024]{3,2,1,0:T(8,128)(2,1)S(1)} %maximum_bitcast_fusion.1), channel_id=1, source_target_pairs={{0,16},{4,20},{8,24},{12,28},{16,0},{20,4},{24,8},{28,12},{1,17},{... | collective-permute-start | bytes 1572872 | tf_op jit(solution)/shard_map/ppermute | solution.py:35
  65.5 83.2 %all-to-all-start = ((bf16[8,2,2,64,1024]{4,3,2,1,0:T(8,128)(2,1)}), bf16[8,2,2,64,1024]{4,3,2,1,0:T(8,128)(2,1)}, u32[]{:S(2)}, u32[]{:S(2)}) async-start(bf16[8,2,2,64,1024]{4,3,2,1,0:T(8,128)(2,1)} %shard_map.172), calls=%async_computation | async-start | bytes 8388608 | tf_op jit(solution)/shard_map/all_to_all | solution.py:299
  70.2 186.0 %all-gather.8.cloned.1.call-start = ((), (), s32[]{:S(2)}) async-start(), calls=%async_computation.7 | async-start | bytes 2621440 | tf_op jit(solution)/shard_map/all_gather | solution.py:406
  78.6 62.2 %collective-permute-start.7 = (bf16[2,4,64,1024]{3,2,1,0:T(8,128)(2,1)S(1)}, bf16[2,4,64,1024]{3,2,1,0:T(8,128)(2,1)S(1)}, u32[]{:S(2)}, u32[]{:S(2)}) collective-permute-start(bf16[2,4,64,1024]{3,2,1,0:T(8,128)(2,1)S(1)} %maximum_bitcast_fusion), channel_id=1, source_target_pairs={{0,8},{4,12},{8,0},{12,4},{16,24},{20,28},{24,16},{28,20},{1,9},{5... | collective-permute-start | bytes 3145736 | tf_op jit(solution)/shard_map/ppermute | solution.py:35
  142.4 10.4 %collective-permute-start.8 = (bf16[4,4,64,1024]{3,2,1,0:T(8,128)(2,1)}, bf16[4,4,64,1024]{3,2,1,0:T(8,128)(2,1)}, u32[]{:S(2)}, u32[]{:S(2)}) collective-permute-start(bf16[4,4,64,1024]{3,2,1,0:T(8,128)(2,1)} %bitcast.25), channel_id=1, source_target_pairs={{0,4},{4,0},{8,12},{12,8},{16,20},{20,16},{24,28},{28,24},{1,5},{5... | collective-permute-start | bytes 6291464 | tf_op jit(solution)/shard_map/ppermute | solution.py:35
  155.7 16.8 %copy-start.8 = (f32[3,3,512]{2,1,0:T(4,128)S(1)}, f32[3,3,512]{2,1,0:T(4,128)}, u32[]{:S(2)}) copy-start(f32[3,3,512]{2,1,0:T(4,128)} %refs_2_.3) | copy-start | bytes 55300
  172.4 24.5 %copy-start.2 = (bf16[256,256]{1,0:T(8,128)(2,1)S(1)}, bf16[256,256]{1,0:T(8,128)(2,1)}, u32[]{:S(2)}) copy-start(bf16[256,256]{1,0:T(8,128)(2,1)} %constant.193.clone.fwd_ref) | copy-start | bytes 393220
  172.4 24.5 %copy-start.3 = (bf16[256,256]{1,0:T(8,128)(2,1)S(1)}, bf16[256,256]{1,0:T(8,128)(2,1)}, u32[]{:S(2)}) copy-start(bf16[256,256]{1,0:T(8,128)(2,1)} %constant.194.clone.bwd_ref) | copy-start | bytes 393220
  172.5 24.5 %copy-start.4 = (bf16[144,64]{1,0:T(8,128)(2,1)S(1)}, bf16[144,64]{1,0:T(8,128)(2,1)}, u32[]{:S(2)}) copy-start(bf16[144,64]{1,0:T(8,128)(2,1)} %constant.189.clone.first_ref) | copy-start | bytes 55300
  172.5 24.5 %copy-start.5 = (f32[72,128]{1,0:T(8,128)S(1)}, f32[72,128]{1,0:T(8,128)}, u32[]{:S(2)}) copy-start(f32[72,128]{1,0:T(8,128)} %constant.191.clone.cos_ref) | copy-start | bytes 110596
  172.5 24.5 %copy-start.6 = (f32[72,128]{1,0:T(8,128)S(1)}, f32[72,128]{1,0:T(8,128)}, u32[]{:S(2)}) copy-start(f32[72,128]{1,0:T(8,128)} %constant.192.clone.sin_ref) | copy-start | bytes 110596
  172.5 24.5 %copy-start.7 = (bf16[64,144]{1,0:T(8,128)(2,1)S(1)}, bf16[64,144]{1,0:T(8,128)(2,1)}, u32[]{:S(2)}) copy-start(bf16[64,144]{1,0:T(8,128)(2,1)} %constant.190.clone.last_ref) | copy-start | bytes 55300
  183.7 28.4 %copy-start.9 = (f32[512]{0:T(512)S(1)}, f32[512]{0:T(512)}, u32[]{:S(2)}) copy-start(f32[512]{0:T(512)} %param.22) | copy-start | bytes 6148
  213.4 88.8 %all-gather.6.cloned.1.call-start = ((), (), s32[]{:S(2)}) async-start(), calls=%async_computation.6 | async-start | bytes 2621440 | tf_op jit(solution)/shard_map/all_gather | solution.py:406
  256.1 1.6 copy-start
  302.2 1.6 copy-start.1
Sparse Core Ops, SparseCore 0:
  8.9 163.4 all-gather.3
  213.5 42.5 all-gather.7
  257.7 44.4 all-gather.5

commit v6 on v5

--- a/solution.py
+++ b/solution.py
@@ -19,11 +19,6 @@
     size = lax.axis_size(axis)
     pairs = [(i, i + by) for i in range(size) if 0 <= i + by < size]
     return lax.ppermute(value, axis, pairs)
-
-
-def shifted(value, axis, by):
-    size = lax.axis_size(axis)
-    return lax.ppermute(value, axis, [(i, (i + by) % size) for i in range(size)])
 
 
 def gather_by_doubling(value, axis):
@@ -46,68 +41,78 @@
     return 1 if size % LANES or (size // seq_count) % CHAN_BLOCK else CHUNKS
 
 
-def project_kernel(extras, tok_ref, w_ref, taps_ref, halo_ref, *rest):
-    signal_ref, signal_t_ref, query_t_ref, acc = rest[extras:]
+def project_kernel(streams, extras, tok_ref, *refs):
+    w_refs, taps_ref, halo_ref = refs[: len(streams)], refs[len(streams)], refs[len(streams) + 1]
+    outs, acc = refs[len(streams) + 2 + extras : -1], refs[-1]
     step = pl.program_id(0)
-    rows = signal_t_ref.shape[0]
+    last = pl.num_programs(0) - 1
+    rows = acc.shape[1] - HALO
+
+    def part(w_ref):
+        return jnp.dot(tok_ref[...], w_ref[0], preferred_element_type=jnp.float32)
 
     @pl.when(step == 0)
     def _():
-        for p in range(3):
-            acc[p, HALO:, :] = jnp.dot(tok_ref[...], w_ref[p], preferred_element_type=jnp.float32)
-
-    @pl.when(step > 0)
+        for i, p in enumerate(streams):
+            acc[i, :HALO, :] = halo_ref[p].astype(jnp.float32)
+            acc[i, HALO:, :] = part(w_refs[i])
+
+    @pl.when(jnp.logical_and(step > 0, step < last))
     def _():
-        for p in range(3):
-            acc[p, HALO:, :] += jnp.dot(tok_ref[...], w_ref[p], preferred_element_type=jnp.float32)
-
-    @pl.when(step == pl.num_programs(0) - 1)
+        for i in range(len(streams)):
+            acc[i, HALO:, :] += part(w_refs[i])
+
+    @pl.when(step == last)
     def _():
-        for p in range(3):
-            acc[p, :HALO, :] = halo_ref[p].astype(jnp.float32)
-            acc[p, HALO:, :] = acc[p, HALO:, :].astype(jnp.bfloat16).astype(jnp.float32)
+        for i in range(len(streams)):
+            acc[i, HALO:, :] = (acc[i, HALO:, :] + part(w_refs[i])).astype(jnp.bfloat16).astype(jnp.float32)
         for r in range(0, rows, LANES):
-            streams = []
-            for p in range(3):
-                total = taps_ref[0, p][None, :] * acc[p, pl.ds(HALO + r, LANES), :]
+            made = {}
+            for i, p in enumerate(streams):
+                total = taps_ref[0, p][None, :] * acc[i, pl.ds(HALO + r, LANES), :]
                 for j in range(1, TAPS):
-                    total = total + taps_ref[j, p][None, :] * acc[p, pl.ds(HALO + r - j, LANES), :]
-                streams.append(total)
-            signal = streams[1] * streams[2]
-            query_t_ref[r : r + LANES, :] = streams[0].astype(query_t_ref.dtype)
-            signal_t_ref[r : r + LANES, :] = signal.astype(signal_t_ref.dtype)
-            signal_ref[:, r : r + LANES] = signal.T.astype(signal_ref.dtype)
-
-
-def project(gathered, in_weight, conv_weight, halo, lo, size, *after):
+                    total = total + taps_ref[j, p][None, :] * acc[i, pl.ds(HALO + r - j, LANES), :]
+                made[p] = total
+            if 0 in made:
+                outs[0][r : r + LANES, :] = made[0].astype(outs[0].dtype)
+            if 1 in made:
+                signal = made[1] * made[2]
+                outs[-1][r : r + LANES, :] = signal.astype(outs[-1].dtype)
+                outs[-2][:, r : r + LANES] = signal.T.astype(outs[-2].dtype)
+
+
+def project(streams, gathered, in_weight, conv_weight, halo, lo, size, *after):
     rows, depth = gathered.shape
-    step = min(DEPTH_STEP, depth)
+    step = min(DEPTH_STEP, depth // 2)
     at = lo // size
     flat = jax.ShapeDtypeStruct((rows, size), jnp.bfloat16)
-    return pl.pallas_call(
-        lambda *refs: project_kernel(len(after), *refs),
+    shapes = ([flat] if 0 in streams else []) + (
+        [jax.ShapeDtypeStruct((size, rows), jnp.bfloat16), flat] if 1 in streams else []
+    )
+
+    def weight_of(p):
+        return pl.BlockSpec((1, step, size), lambda z: (p, z, at))
+
+    return pl.pallas_call(
+        lambda *refs: project_kernel(streams, len(after), *refs),
         grid=(depth // step,),
         in_specs=[
             pl.BlockSpec((rows, step), lambda z: (0, z)),
-            pl.BlockSpec((3, step, size), lambda z: (0, z, at)),
+            *[weight_of(p) for p in streams],
             pl.BlockSpec((TAPS, 3, size), lambda z: (0, 0, at)),
             pl.BlockSpec((3, HALO, size), lambda z: (0, 0, at)),
             *[pl.BlockSpec(memory_space=pl.ANY) for _ in after],
         ],
-        out_specs=[
-            pl.BlockSpec((size, rows), lambda z: (0, 0)),
-            pl.BlockSpec((rows, size), lambda z: (0, 0)),
-            pl.BlockSpec((rows, size), lambda z: (0, 0)),
-        ],
-        out_shape=[jax.ShapeDtypeStruct((size, rows), jnp.bfloat16), flat, flat],
-        scratch_shapes=[pltpu.VMEM((3, HALO + rows, size), jnp.float32)],
+        out_specs=[pl.BlockSpec(shape.shape, lambda z: (0, 0)) for shape in shapes],
+        out_shape=shapes,
+        scratch_shapes=[pltpu.VMEM((len(streams), HALO + rows, size), jnp.float32)],
         compiler_params=pltpu.CompilerParams(vmem_limit_bytes=VMEM_BYTES),
         cost_estimate=pl.CostEstimate(
-            flops=2 * 3 * rows * depth * size,
-            bytes_accessed=2 * depth * (3 * size + rows),
+            flops=2 * len(streams) * rows * depth * size,
+            bytes_accessed=2 * depth * (len(streams) * size + rows),
             transcendentals=0,
         ),
-    )(gathered, in_weight, conv_weight, halo, *after)
+    )(gathered, *[in_weight] * len(streams), conv_weight, halo, *after)
 
 
 def transform_tables(seq_count, tok_rows):
@@ -314,64 +319,49 @@
     )(got)
 
 
-def feature_rows(out_weight, seq_count):
+def feature_slice(out_weight, seq_count):
     each = out_weight.shape[0] // seq_count
     own = lax.dynamic_slice_in_dim(out_weight, lax.axis_index("seq") * each, each, axis=0)
-    count = lax.axis_size("chan")
-    me = lax.axis_index("chan")
-    wide = out_weight.shape[1] // count
-    pieces = []
-    for by in range(count):
-        piece = lax.dynamic_slice_in_dim(own, lax.rem(me + by, count) * wide, wide, axis=1)
-        pieces.append(shifted(piece, "chan", by) if by else piece)
-    return jnp.stack(pieces)
-
-
-def combine_kernel(slots, me_ref, *refs):
-    total_ref = refs[slots + 1] if len(refs) == slots + 3 else None
-    w_ref, out_ref = refs[slots], refs[-1]
-    total = None if total_ref is None else total_ref[...]
-    for z in range(slots):
-        weight = w_ref[:, z].reshape(refs[z].shape[1], out_ref.shape[1])
-        term = jnp.dot(refs[z][...], weight, preferred_element_type=jnp.float32)
-        total = term if total is None else total + term
+    own = lax.all_to_all(own, "chan", split_axis=1, concat_axis=0, tiled=True)
+    return gather_by_doubling(own.reshape(lax.axis_size("chan"), each, own.shape[1]), "seq")
+
+
+def combine_kernel(gated_ref, w_ref, *refs):
+    out_ref = refs[-1]
+    per, count, each, tile = w_ref.shape
+    weight = jnp.concatenate([w_ref[:, z].reshape(per * each, tile) for z in range(count)], axis=0)
+    total = jnp.dot(gated_ref[...], weight, preferred_element_type=jnp.float32)
+    if len(refs) == 2:
+        total = total + refs[0][...]
     out_ref[...] = total.astype(out_ref.dtype)
 
 
 def combine(gathered, weight, lo, total, dtype):
-    tok_rows = gathered.shape[0]
+    tok_rows, depth = gathered.shape
     _, count, each, features = weight.shape
-    size = gathered.shape[1] // count
+    size = depth // count
     per = size // each
     first = lo // size
     tile = min(2 * LANES, features)
-    block = pl.BlockSpec((tok_rows, tile), lambda i, me: (0, i))
+    block = pl.BlockSpec((tok_rows, tile), lambda i: (0, i))
     given = [] if total is None else [total]
-    me = lax.axis_index("chan").astype(jnp.int32).reshape(1)
-
-    def slot(k):
-        return pl.BlockSpec((tok_rows, size), lambda i, me: (0, lax.rem(me[0] - k + count, count)))
-
-    return pl.pallas_call(
-        lambda *refs: combine_kernel(count, *refs),
-        grid_spec=pltpu.PrefetchScalarGridSpec(
-            num_scalar_prefetch=1,
-            grid=(features // tile,),
-            in_specs=[
-                *[slot(k) for k in range(count)],
-                pl.BlockSpec((per, count, each, tile), lambda i, me: (first, 0, 0, i)),
-                *[block for _ in given],
-            ],
-            out_specs=block,
-        ),
+    return pl.pallas_call(
+        combine_kernel,
+        grid=(features // tile,),
+        in_specs=[
+            pl.BlockSpec((tok_rows, depth), lambda i: (0, 0)),
+            pl.BlockSpec((per, count, each, tile), lambda i: (first, 0, 0, i)),
+            *[block for _ in given],
+        ],
+        out_specs=block,
         out_shape=jax.ShapeDtypeStruct((tok_rows, features), dtype),
         compiler_params=pltpu.CompilerParams(vmem_limit_bytes=VMEM_BYTES),
         cost_estimate=pl.CostEstimate(
-            flops=2 * tok_rows * size * count * features,
-            bytes_accessed=2 * count * size * (tok_rows + features) + 6 * tok_rows * features,
+            flops=2 * tok_rows * depth * features,
+            bytes_accessed=2 * depth * (tok_rows + features) + 6 * tok_rows * features,
             transcendentals=0,
         ),
-    )(me, *[gathered] * count, weight, *given)
+    )(gathered, weight, *given)
 
 
 def shards(tokens, in_weight, conv_weight, spectrum, skip, out_weight):
@@ -386,7 +376,7 @@
     sent = reordered_spectrum(spectrum, seq_count, chunks)
     halo, sent, out_weight = lax.optimization_barrier((halo, sent, out_weight))
     response = folded_response(sent, spectrum.shape[2])
-    weight = gather_by_doubling(feature_rows(out_weight, seq_count), "seq")
+    weight = feature_slice(out_weight, seq_count)
     halo = jnp.einsum(
         "ztd,pzdc->ptc",
         halo,
@@ -395,9 +385,12 @@
     ).astype(jnp.bfloat16)
     total = None
     for lo in range(0, chans, size):
-        signal, signal_t, query_t = project(
-            gathered, in_weight, conv_weight, halo, lo, size, response, weight
-        )
+        given = (gathered, in_weight, conv_weight, halo, lo, size, response, weight)
+        if lo == 0:
+            signal, signal_t = project((1, 2), *given)
+            (query_t,) = project((0,), *given)
+        else:
+            query_t, signal, signal_t = project((0, 1, 2), *given)
         values = signal.reshape(seq_count, size // seq_count, tok_rows)
         values = lax.all_to_all(values, "seq", split_axis=0, concat_axis=0, tiled=True)
         longconv = lax.all_to_all(

time: 317 us -> 319 us (level)
  waiting for transfers between devices: 134 us -> 109 us
  blocking collectives: 49.7 us -> 72.7 us
  Pallas kernels: 55.1 us -> 58.7 us
    all_to_all x0 -> x1, blocking collectives: none -> 35.1 us  [feature_slice(): own = lax.all_to_all(own, 'chan', split_axis=1, concat_axis=0, tiled=True)]
    ppermute x3 -> x0, waiting for transfers between devices: 16.4 us -> none  [shifted(): lax.ppermute(value, axis, [(i, (i + by) % size) for i in range(size)])]
    all_gather x1, waiting for transfers between devices: 14.3 us -> 1.34 us  [shards(): gathered = lax.all_gather(tokens, 'chan', axis=1, tiled=True)]
    all_to_all x2 -> x1, blocking collectives: 24.3 us -> 12.2 us  [shards(): lax.all_to_all(long_conv(values, response, lo // seq_count), 'seq', split...]
    ppermute x3 -> x0, starting transfers between devices: 3.87 us -> none  [shifted(): lax.ppermute(value, axis, [(i, (i + by) % size) for i in range(size)])]
    all_to_all x0 -> x1, starting transfers between devices: none -> 3.68 us  [shards(): lax.all_to_all(long_conv(values, response, lo // seq_count), 'seq', split...]
    all_to_all x0 -> x1, waiting for transfers between devices: none -> 3.51 us  [shards(): lax.all_to_all(long_conv(values, response, lo // seq_count), 'seq', split...]
    pallas_call x4 -> x5, Pallas kernels: 34.2 us -> 37.2 us  [the longest x3 25.5 us: project(): pl.pallas_call(lambda *refs: project_kernel(streams, len(after), *refs),...]
  transfers between devices with their start and end apart: 13 -> 11, of which waited for: 9 -> 8; matrix products, arithmetic and copies ran while one was open for 9% -> 9% of each run, Pallas kernels for 11% -> 12%
where the time goes in v6:
time: 319 us; the launch traced here: 317 us
  waiting for transfers between devices  109 us (34%)
  blocking collectives  72.7 us (23%)
  Pallas kernels  58.7 us (18%)
  starting transfers between devices  31.4 us (10%)
  local copies, waits for them, and re-layouts  20.6 us (6%)
  between operations  13.4 us (4%)
  matrix products  6.3 us (2%)
  other arithmetic  5.47 us (2%)
    ppermute x5, waiting for transfers between devices, gather_by_doubling(): other = lax.ppermute(held, axis, [(i, i ^ bit) for i in range(size)])  60.1 us
    all_gather x2, waiting for transfers between devices, shards(): lax.all_gather(gate(longconv, skip, lo, signal_t, query_t), 'chan', axis=...  42.2 us
    all_to_all x1, blocking collectives, feature_slice(): own = lax.all_to_all(own, 'chan', split_axis=1, concat_axis=0, tiled=True)  35.1 us
    pallas_call x3, Pallas kernels, project(): pl.pallas_call(lambda *refs: project_kernel(streams, len(after), *refs),...  25.5 us
    all_to_all x2, blocking collectives, shards(): lax.all_to_all(values, 'seq', split_axis=0, concat_axis=0, tiled=True)  25.4 us
    ppermute x5, starting transfers between devices, gather_by_doubling(): other = lax.ppermute(held, axis, [(i, i ^ bit) for i in range(size)])  20.7 us
    all_to_all x1, blocking collectives, shards(): lax.all_to_all(long_conv(values, response, lo // seq_count), 'seq', split...  12.2 us
    pallas_call x2, Pallas kernels, combine(): pl.pallas_call(combine_kernel, grid=(features // tile,), in_specs=[pl.Blo...  11.7 us
  transfers between devices with their start and end apart: 11, of which 8 were waited for; matrix products, arithmetic and copies ran while one was open for 9% of the time, Pallas kernels for 12%

profile of v6, /device:TPU:0, one launch (start us, length us, event | category | flops | bytes accessed | tf_op | source)
XLA Modules:
  0.0 317.3 jit_solution(5805338912057503737)
XLA Ops:
  6.5 0.7 all-gather.4.cloned.1.call-update
  7.3 0.8 slice.3
  8.0 2.3 collective-permute-start
  10.4 0.8 collective-permute-done
  11.2 3.4 %collective-permute-start.1 = (bf16[1,16,1024]{2,1,0:T(8,128)(2,1)S(1)}, bf16[1,16,1024]{2,1,0:T(8,128)(2,1)S(1)}, u32[]{:S(2)}, u32[]{:S(2)}) collective-permute-start(bf16[1,16,1024]{2,1,0:T(8,128)(2,1)S(1)} %bitcast.88), channel_id=1, source_target_pairs={{0,2},{1,3},{2,0},{3,1},{4,6},{5,7},{6,4},{7,5},{8,10},{9,11},{10,... | collective-permute-start | bytes 98312 | tf_op jit(solution)/shard_map/ppermute | solution.py:30
  14.6 0.7 fusion.1.order_ref
  15.4 11.3 %reshape.39.spec_ref = f32[2,1024,1024]{2,1,0:T(8,128)} reshape(f32[2,512,2,1024]{3,2,1,0:T(2,128)} %param.21) | data formatting | bytes 16777216 | tf_op jit(solution)/shard_map/reshape | solution.py:297
  26.7 0.0 collective-permute-done.1
  26.7 1.7 collective-permute-start.2
  28.4 8.5 %shard_map.172 = bf16[8,2,2,64,1024]{4,3,2,1,0:T(8,128)(2,1)} custom-call(f32[2,1024,1024]{2,1,0:T(8,128)} %reshape.39.spec_ref, bf16[1024,1024]{1,0:T(8,128)(2,1)S(1)} %fusion.1.order_ref), custom_call_target="tpu_custom_call" | custom-call | flops 4294967296 | bytes 12582912 | tf_op jit(solution)/shard_map/pallas_call | solution.py:284
  36.9 3.0 collective-permute-done.2
  39.9 1.1 constant_dynamic-slice_fusion
  41.0 35.1 %all_to_all.41 = bf16[64,4,1024]{2,0,1:T(8,128)(2,1)S(1)} all-to-all(bf16[64,4,1024]{2,0,1:T(8,128)(2,1)S(1)} %bitcast.86), channel_id=1, replica_groups=mesh['seq'=8,'chan'=4] {'chan'}, dimensions={1} | all-to-all | bytes 1048576 | tf_op jit(solution)/shard_map/all_to_all | solution.py:325
  76.2 2.3 collective-permute-start.3
  78.5 4.6 %all-to-all-start = ((bf16[8,2,2,64,1024]{4,3,2,1,0:T(8,128)(2,1)}), bf16[8,2,2,64,1024]{4,3,2,1,0:T(8,128)(2,1)}, u32[]{:S(2)}, u32[]{:S(2)}) async-start(bf16[8,2,2,64,1024]{4,3,2,1,0:T(8,128)(2,1)} %shard_map.172), calls=%async_computation | async-start | bytes 8388608 | tf_op jit(solution)/shard_map/all_to_all | solution.py:304
  83.1 8.2 %collective-permute-done.3 = bf16[1,4,64,1024]{3,2,1,0:T(8,128)(2,1)S(1)} collective-permute-done((bf16[1,4,64,1024]{3,2,1,0:T(8,128)(2,1)S(1)}, bf16[1,4,64,1024]{3,2,1,0:T(8,128)(2,1)S(1)}, u32[]{:S(2)}, u32[]{:S(2)}) %collective-permute-start.3) | collective-permute-done | bytes 524320 | tf_op jit(solution)/shard_map/ppermute | solution.py:30
  91.3 0.1 select_bitcast_fusion.5
  91.4 0.1 maximum_bitcast_fusion
  91.5 13.3 %collective-permute-start.4 = (bf16[2,4,64,1024]{3,2,1,0:T(8,128)(2,1)S(1)}, bf16[2,4,64,1024]{3,2,1,0:T(8,128)(2,1)S(1)}, u32[]{:S(2)}, u32[]{:S(2)}) collective-permute-start(bf16[2,4,64,1024]{3,2,1,0:T(8,128)(2,1)S(1)} %maximum_bitcast_fusion), channel_id=1, source_target_pairs={{0,8},{4,12},{8,0},{12,4},{16,24},{20,28},{24,16},{28,20},{1,9},{5... | collective-permute-start | bytes 3145736 | tf_op jit(solution)/shard_map/ppermute | solution.py:30
  104.8 48.9 %collective-permute-done.4 = bf16[2,4,64,1024]{3,2,1,0:T(8,128)(2,1)S(1)} collective-permute-done((bf16[2,4,64,1024]{3,2,1,0:T(8,128)(2,1)S(1)}, bf16[2,4,64,1024]{3,2,1,0:T(8,128)(2,1)S(1)}, u32[]{:S(2)}, u32[]{:S(2)}) %collective-permute-start.4) | collective-permute-done | bytes 1048608 | tf_op jit(solution)/shard_map/ppermute | solution.py:30
  153.7 0.1 select_bitcast_fusion.3
  153.8 1.5 pad_maximum_fusion.1
  155.3 0.0 collective-permute-start.5
  155.3 6.3 %fusion.3.refs_5_.refs_4_.refs_3_ = bf16[3,16,512]{2,1,0:T(8,128)(2,1)S(1)} fusion(bf16[3,4,1024,512]{3,2,1,0:T(8,128)(2,1)} %bitcast.78, bf16[4,16,1024]{2,1,0:T(8,128)(2,1)S(1)} %bitcast.87), kind=kOutput, calls=%fused_computation.9 | convolution fusion | flops 201351168 | bytes 12763136 | tf_op jit(solution)/shard_map/ztd,pzdc->ptc/dot_general | solution.py:380
  161.6 0.0 all-to-all-done.got_ref
  161.6 4.1 %shard_map.173.refs_6_.resp_ref.refs_5_.refs_4_ = bf16[2,64,72,128]{3,2,1,0:T(8,128)(2,1)S(1)} custom-call(bf16[8,2,2,64,1024]{4,3,2,1,0:T(8,128)(2,1)} %all-to-all-done.got_ref), custom_call_target="tpu_custom_call" | custom-call | flops 2097152 | bytes 6291456 | tf_op jit(solution)/shard_map/pallas_call | solution.py:307
  165.7 0.0 collective-permute-done.5
  165.7 2.5 select_bitcast_fusion.1
  168.2 0.4 pad_maximum_fusion
  168.6 0.0 copy-start.8
  168.6 2.5 copy.29
  171.1 1.3 all-gather.4.cloned.1.call-done.refs_0_
  172.5 0.0 copy-start.10
  172.5 0.0 copy-start.11
  172.5 0.0 copy-start.13
  172.5 8.6 %shard_map.177 = (bf16[256,1024]{1,0:T(8,128)(2,1)S(1)}, bf16[1024,256]{1,0:T(8,128)(2,1)S(1)}) custom-call(bf16[1024,4096]{1,0:T(8,128)(2,1)} %all-gather.4.cloned.1.call-done.refs_0_, bf16[3,4096,512]{2,1,0:T(8,128)(2,1)} %refs_1_.5, bf16[3,4096,512]{2,1,0:T(8,128)(2,1)} %refs_1_.5, f32[3,3,512]{2,1,0:T(4,128)S(1)} %copy-done.8, ...), custom_call_target="tpu_custom_call" | custom-call | flops 4294967296 | bytes 12582912 | tf_op jit(solution)/shard_map/pallas_call | solution.py:96
  181.1 13.2 %all_to_all.42.signal_ref = bf16[8,32,1024]{2,1,0:T(8,128)(2,1)S(1)} all-to-all(bf16[8,32,1024]{2,1,0:T(8,128)(2,1)S(1)} %bitcast.75), channel_id=1, replica_groups=mesh['seq'=8,'chan'=4] {'seq'}, dimensions={0} | all-to-all | bytes 1048576 | tf_op jit(solution)/shard_map/all_to_all | solution.py:395
  194.4 3.6 %shard_map.178 = bf16[8,32,1024]{2,1,0:T(8,128)(2,1)} custom-call(bf16[8,32,1024]{2,1,0:T(8,128)(2,1)S(1)} %all_to_all.42.signal_ref, bf16[2,64,72,128]{3,2,1,0:T(8,128)(2,1)S(1)} %shard_map.173.refs_6_.resp_ref.refs_5_.refs_4_, bf16[144,64]{1,0:T(8,128)(2,1)S(1)} %copy-done.9, bf16[64,144]{1,0:T(8,128)(2,1)S(1)} %copy-done.13, f32[72,128]{1,0:T(8,128)S(1)} %copy-done.10, ...), custom_call_target="tpu_custom_call" | custom-call | flops 754974720 | bytes 2228224 | tf_op jit(solution)/shard_map/pallas_call | solution.py:195
  198.0 3.7 %all-to-all-start.5 = ((bf16[8,32,1024]{2,1,0:T(8,128)(2,1)}), bf16[8,32,1024]{2,1,0:T(8,128)(2,1)S(1)}, u32[]{:S(2)}, u32[]{:S(2)}) async-start(bf16[8,32,1024]{2,1,0:T(8,128)(2,1)} %shard_map.178), calls=%async_computation.5 | async-start | bytes 1048576 | tf_op jit(solution)/shard_map/all_to_all | solution.py:396
  201.7 0.0 all-gather.8.cloned.1.call-start
  201.7 6.1 %shard_map.179.query_ref = bf16[1024,256]{1,0:T(8,128)(2,1)S(1)} custom-call(bf16[1024,4096]{1,0:T(8,128)(2,1)} %all-gather.4.cloned.1.call-done.refs_0_, bf16[3,4096,512]{2,1,0:T(8,128)(2,1)} %refs_1_.5, f32[3,3,512]{2,1,0:T(4,128)S(1)} %copy-done.8, bf16[3,16,512]{2,1,0:T(8,128)(2,1)S(1)} %fusion.3.refs_5_.refs_4_.refs_3_, ...), custom_call_target="tpu_custom_call" | custom-call | flops 2147483648 | bytes 10485760 | tf_op jit(solution)/shard_map/pallas_call | solution.py:96
  207.9 3.5 %all-to-all-done.5 = bf16[8,32,1024]{2,1,0:T(8,128)(2,1)S(1)} async-done(((bf16[8,32,1024]{2,1,0:T(8,128)(2,1)}), bf16[8,32,1024]{2,1,0:T(8,128)(2,1)S(1)}, u32[]{:S(2)}, u32[]{:S(2)}) %all-to-all-start.5) | async-done | bytes 524320 | tf_op jit(solution)/shard_map/all_to_all | solution.py:396
  211.4 1.0 copy-done.3
  212.4 0.7 copy-done.15
  213.1 1.2 shard_map.180
  214.3 0.0 all-gather.8.cloned.1.call-update
  214.3 0.0 copy-start.5
  214.4 0.0 copy-start.7
  214.4 0.0 copy-start.12
  214.4 0.0 copy-start.14
  214.4 0.0 all-gather.6.cloned.1.call-start
  214.4 10.7 %shard_map.174 = (bf16[1024,256]{1,0:T(8,128)(2,1)S(1)}, bf16[256,1024]{1,0:T(8,128)(2,1)S(1)}, bf16[1024,256]{1,0:T(8,128)(2,1)S(1)}) custom-call(bf16[1024,4096]{1,0:T(8,128)(2,1)} %all-gather.4.cloned.1.call-done.refs_0_, bf16[3,4096,512]{2,1,0:T(8,128)(2,1)} %refs_1_.5, bf16[3,4096,512]{2,1,0:T(8,128)(2,1)} %refs_1_.5, bf16[3,4096,512]{2,1,0:T(8,128)(2,1)} %refs_1_.5, ...), custom_call_target="tpu_custom_call" | custom-call | flops 6442450944 | bytes 14680064 | tf_op jit(solution)/shard_map/pallas_call | solution.py:96
  225.2 0.0 copy-start.16
  225.2 12.2 %all_to_all.43.signal_ref = bf16[8,32,1024]{2,1,0:T(8,128)(2,1)S(1)} all-to-all(bf16[8,32,1024]{2,1,0:T(8,128)(2,1)S(1)} %bitcast.74), channel_id=1, replica_groups=mesh['seq'=8,'chan'=4] {'seq'}, dimensions={0} | all-to-all | bytes 1048576 | tf_op jit(solution)/shard_map/all_to_all | solution.py:395
  237.4 2.9 shard_map.175
  240.3 12.2 %all_to_all.44 = bf16[8,32,1024]{2,1,0:T(8,128)(2,1)S(1)} all-to-all(bf16[8,32,1024]{2,1,0:T(8,128)(2,1)S(1)} %shard_map.175), channel_id=1, replica_groups=mesh['seq'=8,'chan'=4] {'seq'}, dimensions={0} | all-to-all | bytes 1048576 | tf_op jit(solution)/shard_map/all_to_all | solution.py:396
  252.5 1.2 shard_map.176
  253.7 0.0 all-gather.6.cloned.1.call-update
  253.7 3.3 %all-gather.8.cloned.1.call-done.gated_ref = bf16[1024,1024]{1,0:T(8,128)(2,1)} async-done(((bf16[1024,256]{1,0:T(8,128)(2,1)}), bf16[1024,1024]{1,0:T(8,128)(2,1)}) %all-gather.8.cloned.1.call-update) | async-done | bytes 2097168 | tf_op jit(solution)/shard_map/all_gather | solution.py:399
  257.1 1.6 copy-done
  258.6 5.6 %shard_map.181.refs_0_ = f32[1024,1024]{1,0:T(8,128)} custom-call(bf16[1024,1024]{1,0:T(8,128)(2,1)S(1)} %copy-done, bf16[8,4,64,1024]{3,2,1,0:T(8,128)(2,1)} %bitcast.82), custom_call_target="tpu_custom_call" | custom-call | flops 2147483648 | bytes 10485760 | tf_op jit(solution)/shard_map/pallas_call | solution.py:348
  264.3 38.8 %all-gather.6.cloned.1.call-done.gated_ref = bf16[1024,1024]{1,0:T(8,128)(2,1)} async-done(((bf16[1024,256]{1,0:T(8,128)(2,1)}), bf16[1024,1024]{1,0:T(8,128)(2,1)}) %all-gather.6.cloned.1.call-update) | async-done | bytes 2097168 | tf_op jit(solution)/shard_map/all_gather | solution.py:399
  303.1 1.6 copy-done.1
  304.7 6.1 %shard_map.182 = bf16[1024,1024]{1,0:T(8,128)(2,1)} custom-call(bf16[1024,1024]{1,0:T(8,128)(2,1)S(1)} %copy-done.1, bf16[8,4,64,1024]{3,2,1,0:T(8,128)(2,1)} %bitcast.83, f32[1024,1024]{1,0:T(8,128)} %shard_map.181.refs_0_), custom_call_target="tpu_custom_call" | custom-call | flops 2147483648 | bytes 10485760 | tf_op jit(solution)/shard_map/pallas_call | solution.py:348
  (30 shorter events, 0.1 us)
Async XLA Ops:
  6.5 165.9 %all-gather.4.cloned.1.call-start = ((), (), s32[]{:S(2)}) async-start(), calls=%async_computation.6 | async-start | bytes 10485760 | tf_op jit(solution)/shard_map/all_gather | solution.py:374
  8.0 3.2 %collective-permute-start = (bf16[16,1024]{1,0:T(8,128)(2,1)S(1)}, bf16[16,1024]{1,0:T(8,128)(2,1)S(1)}, u32[]{:S(2)}, u32[]{:S(2)}) collective-permute-start(bf16[16,1024]{1,0:T(8,128)(2,1)S(1)} %slice.3), channel_id=1, source_target_pairs={{0,4},{4,8},{8,12},{12,16},{16,20},{20,24},{24,28},{1,5},{5,9},{9,... | collective-permute-start | bytes 98312 | tf_op jit(solution)/shard_map/ppermute | solution.py:21
  11.2 15.5 %collective-permute-start.1 = (bf16[1,16,1024]{2,1,0:T(8,128)(2,1)S(1)}, bf16[1,16,1024]{2,1,0:T(8,128)(2,1)S(1)}, u32[]{:S(2)}, u32[]{:S(2)}) collective-permute-start(bf16[1,16,1024]{2,1,0:T(8,128)(2,1)S(1)} %bitcast.88), channel_id=1, source_target_pairs={{0,2},{1,3},{2,0},{3,1},{4,6},{5,7},{6,4},{7,5},{8,10},{9,11},{10,... | collective-permute-start | bytes 98312 | tf_op jit(solution)/shard_map/ppermute | solution.py:30
  26.7 13.1 %collective-permute-start.2 = (bf16[2,16,1024]{2,1,0:T(8,128)(2,1)S(1)}, bf16[2,16,1024]{2,1,0:T(8,128)(2,1)S(1)}, u32[]{:S(2)}, u32[]{:S(2)}) collective-permute-start(bf16[2,16,1024]{2,1,0:T(8,128)(2,1)S(1)} %maximum_bitcast_fusion.1), channel_id=1, source_target_pairs={{0,1},{1,0},{2,3},{3,2},{4,5},{5,4},{6,7},{7,6},{8,9},{9,8},{10,11... | collective-permute-start | bytes 196616 | tf_op jit(solution)/shard_map/ppermute | solution.py:30
  76.2 15.2 %collective-permute-start.3 = (bf16[1,4,64,1024]{3,2,1,0:T(8,128)(2,1)S(1)}, bf16[1,4,64,1024]{3,2,1,0:T(8,128)(2,1)S(1)}, u32[]{:S(2)}, u32[]{:S(2)}) collective-permute-start(bf16[1,4,64,1024]{3,2,1,0:T(8,128)(2,1)S(1)} %bitcast.84), channel_id=1, source_target_pairs={{0,16},{4,20},{8,24},{12,28},{16,0},{20,4},{24,8},{28,12},{1,17},{... | collective-permute-start | bytes 1572872 | tf_op jit(solution)/shard_map/ppermute | solution.py:30
  78.5 83.1 %all-to-all-start = ((bf16[8,2,2,64,1024]{4,3,2,1,0:T(8,128)(2,1)}), bf16[8,2,2,64,1024]{4,3,2,1,0:T(8,128)(2,1)}, u32[]{:S(2)}, u32[]{:S(2)}) async-start(bf16[8,2,2,64,1024]{4,3,2,1,0:T(8,128)(2,1)} %shard_map.172), calls=%async_computation | async-start | bytes 8388608 | tf_op jit(solution)/shard_map/all_to_all | solution.py:304
  91.5 62.2 %collective-permute-start.4 = (bf16[2,4,64,1024]{3,2,1,0:T(8,128)(2,1)S(1)}, bf16[2,4,64,1024]{3,2,1,0:T(8,128)(2,1)S(1)}, u32[]{:S(2)}, u32[]{:S(2)}) collective-permute-start(bf16[2,4,64,1024]{3,2,1,0:T(8,128)(2,1)S(1)} %maximum_bitcast_fusion), channel_id=1, source_target_pairs={{0,8},{4,12},{8,0},{12,4},{16,24},{20,28},{24,16},{28,20},{1,9},{5... | collective-permute-start | bytes 3145736 | tf_op jit(solution)/shard_map/ppermute | solution.py:30
  155.3 10.4 %collective-permute-start.5 = (bf16[4,4,64,1024]{3,2,1,0:T(8,128)(2,1)}, bf16[4,4,64,1024]{3,2,1,0:T(8,128)(2,1)}, u32[]{:S(2)}, u32[]{:S(2)}) collective-permute-start(bf16[4,4,64,1024]{3,2,1,0:T(8,128)(2,1)} %bitcast.22), channel_id=1, source_target_pairs={{0,4},{4,0},{8,12},{12,8},{16,20},{20,16},{24,28},{28,24},{1,5},{5... | collective-permute-start | bytes 6291464 | tf_op jit(solution)/shard_map/ppermute | solution.py:30
  168.6 3.8 %copy-start.8 = (f32[3,3,512]{2,1,0:T(4,128)S(1)}, f32[3,3,512]{2,1,0:T(4,128)}, u32[]{:S(2)}) copy-start(f32[3,3,512]{2,1,0:T(4,128)} %refs_2_.5) | copy-start | bytes 55300
  172.4 21.9 %copy-start.4 = (bf16[256,256]{1,0:T(8,128)(2,1)S(1)}, bf16[256,256]{1,0:T(8,128)(2,1)}, u32[]{:S(2)}) copy-start(bf16[256,256]{1,0:T(8,128)(2,1)} %constant.138.clone.fwd_ref) | copy-start | bytes 393220
  172.4 21.9 %copy-start.6 = (bf16[256,256]{1,0:T(8,128)(2,1)S(1)}, bf16[256,256]{1,0:T(8,128)(2,1)}, u32[]{:S(2)}) copy-start(bf16[256,256]{1,0:T(8,128)(2,1)} %constant.139.clone.bwd_ref) | copy-start | bytes 393220
  172.5 21.9 %copy-start.9 = (bf16[144,64]{1,0:T(8,128)(2,1)S(1)}, bf16[144,64]{1,0:T(8,128)(2,1)}, u32[]{:S(2)}) copy-start(bf16[144,64]{1,0:T(8,128)(2,1)} %constant.134.clone.first_ref) | copy-start | bytes 55300
  172.5 21.9 %copy-start.10 = (f32[72,128]{1,0:T(8,128)S(1)}, f32[72,128]{1,0:T(8,128)}, u32[]{:S(2)}) copy-start(f32[72,128]{1,0:T(8,128)} %constant.136.clone.cos_ref) | copy-start | bytes 110596
  172.5 21.9 %copy-start.11 = (f32[72,128]{1,0:T(8,128)S(1)}, f32[72,128]{1,0:T(8,128)}, u32[]{:S(2)}) copy-start(f32[72,128]{1,0:T(8,128)} %constant.137.clone.sin_ref) | copy-start | bytes 110596
  172.5 21.9 %copy-start.13 = (bf16[64,144]{1,0:T(8,128)(2,1)S(1)}, bf16[64,144]{1,0:T(8,128)(2,1)}, u32[]{:S(2)}) copy-start(bf16[64,144]{1,0:T(8,128)(2,1)} %constant.135.clone.last_ref) | copy-start | bytes 55300
  181.1 16.9 %copy-start.2 = (bf16[1024,256]{1,0:T(8,128)(2,1)}, bf16[1024,256]{1,0:T(8,128)(2,1)S(1)}, u32[]{:S(2)}) copy-start(bf16[1024,256]{1,0:T(8,128)(2,1)S(1)} %get-tuple-element.20.signal_ref) | copy-start | bytes 1572868
  198.0 13.4 %all-to-all-start.5 = ((bf16[8,32,1024]{2,1,0:T(8,128)(2,1)}), bf16[8,32,1024]{2,1,0:T(8,128)(2,1)S(1)}, u32[]{:S(2)}, u32[]{:S(2)}) async-start(bf16[8,32,1024]{2,1,0:T(8,128)(2,1)} %shard_map.178), calls=%async_computation.5 | async-start | bytes 1048576 | tf_op jit(solution)/shard_map/all_to_all | solution.py:396
  201.7 55.4 %all-gather.8.cloned.1.call-start = ((), (), s32[]{:S(2)}) async-start(), calls=%async_computation.8 | async-start | bytes 2621440 | tf_op jit(solution)/shard_map/all_gather | solution.py:399
  211.4 1.0 copy-start.3
  212.4 0.7 copy-start.15
  214.3 23.0 %copy-start.5 = (bf16[256,256]{1,0:T(8,128)(2,1)S(1)}, bf16[256,256]{1,0:T(8,128)(2,1)}, u32[]{:S(2)}) copy-start(bf16[256,256]{1,0:T(8,128)(2,1)} %constant.138.clone.fwd_ref) | copy-start | bytes 393220
  214.4 23.0 %copy-start.7 = (bf16[256,256]{1,0:T(8,128)(2,1)S(1)}, bf16[256,256]{1,0:T(8,128)(2,1)}, u32[]{:S(2)}) copy-start(bf16[256,256]{1,0:T(8,128)(2,1)} %constant.139.clone.bwd_ref) | copy-start | bytes 393220
  214.4 23.0 %copy-start.12 = (f32[72,128]{1,0:T(8,128)S(1)}, f32[72,128]{1,0:T(8,128)}, u32[]{:S(2)}) copy-start(f32[72,128]{1,0:T(8,128)} %constant.137.clone.sin_ref) | copy-start | bytes 110596
  214.4 23.0 %copy-start.14 = (bf16[64,144]{1,0:T(8,128)(2,1)S(1)}, bf16[64,144]{1,0:T(8,128)(2,1)}, u32[]{:S(2)}) copy-start(bf16[64,144]{1,0:T(8,128)(2,1)} %constant.135.clone.last_ref) | copy-start | bytes 55300
  214.4 88.7 %all-gather.6.cloned.1.call-start = ((), (), s32[]{:S(2)}) async-start(), calls=%async_computation.7 | async-start | bytes 2621440 | tf_op jit(solution)/shard_map/all_gather | solution.py:399
  225.2 27.3 %copy-start.16 = (f32[512]{0:T(512)S(1)}, f32[512]{0:T(512)}, u32[]{:S(2)}) copy-start(f32[512]{0:T(512)} %param.22) | copy-start | bytes 6148
  257.0 1.6 copy-start
  303.1 1.6 copy-start.1
Sparse Core Ops, SparseCore 0:
  8.9 163.4 all-gather.3
  214.5 42.5 all-gather.7
  258.6 44.4 all-gather.5

commit v7 on v6

--- a/solution.py
+++ b/solution.py
@@ -12,7 +12,7 @@
 DEPTH_STEP = 1024
 CHAN_BLOCK = 16
 CHUNKS = 2
-VMEM_BYTES = 48 * 1024 * 1024
+VMEM_BYTES = 60 * 1024 * 1024
 
 
 def from_behind(value, axis, by):
@@ -319,11 +319,11 @@
     )(got)
 
 
-def feature_slice(out_weight, seq_count):
+def feature_rows(out_weight, seq_count):
     each = out_weight.shape[0] // seq_count
     own = lax.dynamic_slice_in_dim(out_weight, lax.axis_index("seq") * each, each, axis=0)
     own = lax.all_to_all(own, "chan", split_axis=1, concat_axis=0, tiled=True)
-    return gather_by_doubling(own.reshape(lax.axis_size("chan"), each, own.shape[1]), "seq")
+    return own.reshape(lax.axis_size("chan"), each, own.shape[1])
 
 
 def combine_kernel(gated_ref, w_ref, *refs):
@@ -372,11 +372,14 @@
     chunks = chunk_count(chans, seq_count)
     size = chans // chunks
     gathered = lax.all_gather(tokens, "chan", axis=1, tiled=True)
-    halo = gather_by_doubling(from_behind(tokens[tok_rows - HALO :], "seq", 1), "chan")
+    weight = feature_rows(out_weight, seq_count)
+    last_rows = tokens[tok_rows - HALO :]
+    weight, last_rows, spectrum = lax.optimization_barrier((weight, last_rows, spectrum))
+    halo = gather_by_doubling(from_behind(last_rows, "seq", 1), "chan")
     sent = reordered_spectrum(spectrum, seq_count, chunks)
-    halo, sent, out_weight = lax.optimization_barrier((halo, sent, out_weight))
+    halo, sent, weight = lax.optimization_barrier((halo, sent, weight))
     response = folded_response(sent, spectrum.shape[2])
-    weight = feature_slice(out_weight, seq_count)
+    weight = gather_by_doubling(weight, "seq")
     halo = jnp.einsum(
         "ztd,pzdc->ptc",
         halo,
@@ -386,11 +389,7 @@
     total = None
     for lo in range(0, chans, size):
         given = (gathered, in_weight, conv_weight, halo, lo, size, response, weight)
-        if lo == 0:
-            signal, signal_t = project((1, 2), *given)
-            (query_t,) = project((0,), *given)
-        else:
-            query_t, signal, signal_t = project((0, 1, 2), *given)
+        query_t, signal, signal_t = project((0, 1, 2), *given)
         values = signal.reshape(seq_count, size // seq_count, tok_rows)
         values = lax.all_to_all(values, "seq", split_axis=0, concat_axis=0, tiled=True)
         longconv = lax.all_to_all(

time: 319 us -> 319 us (level)
  blocking collectives: 72.7 us -> 55.5 us
  waiting for transfers between devices: 109 us -> 125 us
  Pallas kernels: 58.7 us -> 65.4 us
  local copies, waits for them, and re-layouts: 20.6 us -> 16 us
    all_to_all x1 -> x0, blocking collectives: 35.1 us -> none  [feature_slice(): own = lax.all_to_all(own, 'chan', split_axis=1, concat_axis=0, tiled=True)]
    ppermute x5, waiting for transfers between devices: 60.1 us -> 29.5 us  [gather_by_doubling(): other = lax.ppermute(held, axis, [(i, i ^ bit) for i in range(size)])]
    all_to_all x1, waiting for transfers between devices: 0.01 us -> 29.2 us  [folded_response(): got = lax.all_to_all(sent, 'seq', split_axis=0, concat_axis=0, tiled=True)]
    all_to_all x1, waiting for transfers between devices: 3.51 us -> 22.6 us  [feature_rows(): own = lax.all_to_all(own, 'chan', split_axis=1, concat_axis=0, tiled=True)]
    all_to_all x1 -> x2, blocking collectives: 12.2 us -> 27.8 us  [shards(): lax.all_to_all(long_conv(values, response, lo // seq_count), 'seq', split...]
    unnamed x34 -> x0, local copies, waits for them, and re-layouts: 4.98 us -> none
    all_gather x2, waiting for transfers between devices: 42.2 us -> 37.2 us  [shards(): lax.all_gather(gate(longconv, skip, lo, signal_t, query_t), 'chan', axis=...]
    ppermute x5, starting transfers between devices: 20.7 us -> 16.8 us  [gather_by_doubling(): other = lax.ppermute(held, axis, [(i, i ^ bit) for i in range(size)])]
  transfers between devices with their start and end apart: 11 -> 11, of which waited for: 8 -> 7; matrix products, arithmetic and copies ran while one was open for 9% -> 9% of each run, Pallas kernels for 12% -> 13%
where the time goes in v7:
time: 319 us; the launch traced here: 318 us
  waiting for transfers between devices  125 us (39%)
  Pallas kernels  65.4 us (21%)
  blocking collectives  55.5 us (17%)
  starting transfers between devices  29.1 us (9%)
  local copies, waits for them, and re-layouts  16 us (5%)
  between operations  13.3 us (4%)
  matrix products  7.11 us (2%)
  other arithmetic  5.84 us (2%)
    all_gather x2, waiting for transfers between devices, shards(): lax.all_gather(gate(longconv, skip, lo, signal_t, query_t), 'chan', axis=...  37.2 us
    ppermute x5, waiting for transfers between devices, gather_by_doubling(): other = lax.ppermute(held, axis, [(i, i ^ bit) for i in range(size)])  29.5 us
    all_to_all x1, waiting for transfers between devices, folded_response(): got = lax.all_to_all(sent, 'seq', split_axis=0, concat_axis=0, tiled=True)  29.2 us
    all_to_all x2, blocking collectives, shards(): lax.all_to_all(values, 'seq', split_axis=0, concat_axis=0, tiled=True)  27.8 us
    all_to_all x2, blocking collectives, shards(): lax.all_to_all(long_conv(values, response, lo // seq_count), 'seq', split...  27.8 us
    pallas_call x2, Pallas kernels, project(): pl.pallas_call(lambda *refs: project_kernel(streams, len(after), *refs),...  23.9 us
    all_to_all x1, waiting for transfers between devices, feature_rows(): own = lax.all_to_all(own, 'chan', split_axis=1, concat_axis=0, tiled=True)  22.6 us
    ppermute x5, starting transfers between devices, gather_by_doubling(): other = lax.ppermute(held, axis, [(i, i ^ bit) for i in range(size)])  16.8 us
  transfers between devices with their start and end apart: 11, of which 7 were waited for; matrix products, arithmetic and copies ran while one was open for 9% of the time, Pallas kernels for 13%

profile of v7, /device:TPU:0, one launch (start us, length us, event | category | flops | bytes accessed | tf_op | source)
XLA Modules:
  0.0 317.6 jit_solution(5506946135550561795)
XLA Ops:
  6.5 0.0 all-gather.4.cloned.1.call-start
  6.5 0.7 all-gather.4.cloned.1.call-update
  7.3 1.1 constant_dynamic-slice_fusion
  8.3 0.8 copy.33
  9.2 6.3 %all-to-all-start = ((bf16[64,4,1024]{2,0,1:T(8,128)(2,1)}), bf16[64,4,1024]{2,0,1:T(8,128)(2,1)S(1)}, u32[]{:S(2)}, u32[]{:S(2)}) async-start(bf16[64,4,1024]{2,0,1:T(8,128)(2,1)} %bitcast.70), calls=%async_computation | async-start | bytes 1048576 | tf_op jit(solution)/shard_map/all_to_all | solution.py:325
  15.5 0.8 slice.3
  16.3 22.6 %all-to-all-done = bf16[64,4,1024]{2,0,1:T(8,128)(2,1)S(1)} async-done(((bf16[64,4,1024]{2,0,1:T(8,128)(2,1)}), bf16[64,4,1024]{2,0,1:T(8,128)(2,1)S(1)}, u32[]{:S(2)}, u32[]{:S(2)}) %all-to-all-start) | async-done | bytes 524320 | tf_op jit(solution)/shard_map/all_to_all | solution.py:325
  38.9 1.3 collective-permute-start
  40.2 0.8 collective-permute-done
  41.0 0.0 collective-permute-start.1
  41.0 2.1 fusion.1.order_ref
  43.0 10.9 %reshape.40.spec_ref = f32[2,1024,1024]{2,1,0:T(8,128)} reshape(f32[2,512,2,1024]{3,2,1,0:T(2,128)} %param.21) | data formatting | bytes 16777216 | tf_op jit(solution)/shard_map/reshape | solution.py:297
  54.0 0.0 collective-permute-done.1
  54.0 9.1 %collective-permute-start.2 = (bf16[2,16,1024]{2,1,0:T(8,128)(2,1)S(1)}, bf16[2,16,1024]{2,1,0:T(8,128)(2,1)S(1)}, u32[]{:S(2)}, u32[]{:S(2)}) collective-permute-start(bf16[2,16,1024]{2,1,0:T(8,128)(2,1)S(1)} %maximum_bitcast_fusion.1), channel_id=1, source_target_pairs={{0,1},{1,0},{2,3},{3,2},{4,5},{5,4},{6,7},{7,6},{8,9},{9,8},{10,11... | collective-permute-start | bytes 196616 | tf_op jit(solution)/shard_map/ppermute | solution.py:30
  63.1 9.2 %shard_map.172 = bf16[8,2,2,64,1024]{4,3,2,1,0:T(8,128)(2,1)} custom-call(f32[2,1024,1024]{2,1,0:T(8,128)} %reshape.40.spec_ref, bf16[1024,1024]{1,0:T(8,128)(2,1)} %fusion.1.order_ref), custom_call_target="tpu_custom_call" | custom-call | flops 4294967296 | bytes 12582912 | tf_op jit(solution)/shard_map/pallas_call | solution.py:284
  72.3 0.0 collective-permute-done.2
  72.3 6.1 %collective-permute-start.3 = (bf16[1,4,64,1024]{3,2,1,0:T(8,128)(2,1)S(1)}, bf16[1,4,64,1024]{3,2,1,0:T(8,128)(2,1)S(1)}, u32[]{:S(2)}, u32[]{:S(2)}) collective-permute-start(bf16[1,4,64,1024]{3,2,1,0:T(8,128)(2,1)S(1)} %bitcast.77), channel_id=1, source_target_pairs={{0,16},{4,20},{8,24},{12,28},{16,0},{20,4},{24,8},{28,12},{1,17},{... | collective-permute-start | bytes 1572872 | tf_op jit(solution)/shard_map/ppermute | solution.py:30
  78.4 9.3 %collective-permute-done.3 = bf16[1,4,64,1024]{3,2,1,0:T(8,128)(2,1)S(1)} collective-permute-done((bf16[1,4,64,1024]{3,2,1,0:T(8,128)(2,1)S(1)}, bf16[1,4,64,1024]{3,2,1,0:T(8,128)(2,1)S(1)}, u32[]{:S(2)}, u32[]{:S(2)}) %collective-permute-start.3) | collective-permute-done | bytes 524320 | tf_op jit(solution)/shard_map/ppermute | solution.py:30
  87.8 0.1 select_bitcast_fusion.5
  87.8 1.1 maximum_bitcast_fusion
  88.9 1.5 collective-permute-start.4
  90.4 4.6 %all-to-all-start.1 = ((bf16[8,2,2,64,1024]{4,3,2,1,0:T(8,128)(2,1)}), bf16[8,2,2,64,1024]{4,3,2,1,0:T(8,128)(2,1)}, u32[]{:S(2)}, u32[]{:S(2)}) async-start(bf16[8,2,2,64,1024]{4,3,2,1,0:T(8,128)(2,1)} %shard_map.172), calls=%async_computation.1 | async-start | bytes 8388608 | tf_op jit(solution)/shard_map/all_to_all | solution.py:304
  95.0 0.0 all-gather.8.cloned.1.call-start
  95.1 20.1 %collective-permute-done.4 = bf16[2,4,64,1024]{3,2,1,0:T(8,128)(2,1)S(1)} collective-permute-done((bf16[2,4,64,1024]{3,2,1,0:T(8,128)(2,1)}, bf16[2,4,64,1024]{3,2,1,0:T(8,128)(2,1)S(1)}, u32[]{:S(2)}, u32[]{:S(2)}) %collective-permute-start.4) | collective-permute-done | bytes 1048608 | tf_op jit(solution)/shard_map/ppermute | solution.py:30
  115.2 0.1 select_bitcast_fusion.3
  115.4 0.2 pad_maximum_fusion.1
  115.6 0.1 collective-permute-start.5
  115.7 7.1 %fusion.3.refs_5_ = bf16[3,16,512]{2,1,0:T(8,128)(2,1)} fusion(bf16[3,4,1024,512]{3,2,1,0:T(8,128)(2,1)} %bitcast.71, bf16[4,16,1024]{2,1,0:T(8,128)(2,1)S(1)} %bitcast.82), kind=kOutput, calls=%fused_computation.9 | convolution fusion | flops 201351168 | bytes 12763136 | tf_op jit(solution)/shard_map/ztd,pzdc->ptc/dot_general | solution.py:383
  122.8 0.0 collective-permute-done.5
  122.8 1.9 select_bitcast_fusion.1
  124.6 0.4 pad_maximum_fusion
  125.0 2.4 copy.29
  127.5 29.2 %all-to-all-done.1.got_ref = bf16[8,2,2,64,1024]{4,3,2,1,0:T(8,128)(2,1)} async-done(((bf16[8,2,2,64,1024]{4,3,2,1,0:T(8,128)(2,1)}), bf16[8,2,2,64,1024]{4,3,2,1,0:T(8,128)(2,1)}, u32[]{:S(2)}, u32[]{:S(2)}) %all-to-all-start.1) | async-done | bytes 4194336 | tf_op jit(solution)/shard_map/all_to_all | solution.py:304
  156.7 5.1 %shard_map.173.refs_6_.resp_ref = bf16[2,64,72,128]{3,2,1,0:T(8,128)(2,1)} custom-call(bf16[8,2,2,64,1024]{4,3,2,1,0:T(8,128)(2,1)} %all-to-all-done.1.got_ref), custom_call_target="tpu_custom_call" | custom-call | flops 2097152 | bytes 6291456 | tf_op jit(solution)/shard_map/pallas_call | solution.py:307
  161.7 5.2 %all-gather.4.cloned.1.call-done.refs_0_ = bf16[1024,4096]{1,0:T(8,128)(2,1)} async-done(((bf16[1024,1024]{1,0:T(8,128)(2,1)}), bf16[1024,4096]{1,0:T(8,128)(2,1)}) %all-gather.4.cloned.1.call-update) | async-done | bytes 8388624 | tf_op jit(solution)/shard_map/all_gather | solution.py:374
  167.0 11.9 %shard_map.177 = (bf16[1024,256]{1,0:T(8,128)(2,1)}, bf16[256,1024]{1,0:T(8,128)(2,1)}, bf16[1024,256]{1,0:T(8,128)(2,1)}) custom-call(bf16[1024,4096]{1,0:T(8,128)(2,1)} %all-gather.4.cloned.1.call-done.refs_0_, bf16[3,4096,512]{2,1,0:T(8,128)(2,1)} %refs_3_.3, bf16[3,4096,512]{2,1,0:T(8,128)(2,1)} %refs_3_.3, bf16[3,4096,512]{2,1,0:T(8,128)(2,1)} %refs_3_.3, ...), custom_call_target="tpu_custom_call" | custom-call | flops 6442450944 | bytes 14680064 | tf_op jit(solution)/shard_map/pallas_call | solution.py:96
  178.9 13.9 %all_to_all.41.signal_ref = bf16[8,32,1024]{2,1,0:T(8,128)(2,1)} all-to-all(bf16[8,32,1024]{2,1,0:T(8,128)(2,1)} %bitcast.84), channel_id=1, replica_groups=mesh['seq'=8,'chan'=4] {'seq'}, dimensions={0} | all-to-all | bytes 1048576 | tf_op jit(solution)/shard_map/all_to_all | solution.py:394
  192.8 4.7 %shard_map.178 = bf16[8,32,1024]{2,1,0:T(8,128)(2,1)} custom-call(bf16[8,32,1024]{2,1,0:T(8,128)(2,1)} %all_to_all.41.signal_ref, bf16[2,64,72,128]{3,2,1,0:T(8,128)(2,1)} %shard_map.173.refs_6_.resp_ref, bf16[144,64]{1,0:T(8,128)(2,1)} %constant.134.clone.first_ref, bf16[64,144]{1,0:T(8,128)(2,1)} %constant.135.clone.last_ref, ...), custom_call_target="tpu_custom_call" | custom-call | flops 754974720 | bytes 2228224 | tf_op jit(solution)/shard_map/pallas_call | solution.py:195
  197.5 13.9 %all_to_all.42 = bf16[8,32,1024]{2,1,0:T(8,128)(2,1)} all-to-all(bf16[8,32,1024]{2,1,0:T(8,128)(2,1)} %shard_map.178), channel_id=1, replica_groups=mesh['seq'=8,'chan'=4] {'seq'}, dimensions={0} | all-to-all | bytes 1048576 | tf_op jit(solution)/shard_map/all_to_all | solution.py:395
  211.4 2.3 shard_map.179
  213.7 0.0 all-gather.8.cloned.1.call-update
  213.7 0.0 all-gather.6.cloned.1.call-start
  213.7 12.0 %shard_map.174 = (bf16[1024,256]{1,0:T(8,128)(2,1)}, bf16[256,1024]{1,0:T(8,128)(2,1)}, bf16[1024,256]{1,0:T(8,128)(2,1)}) custom-call(bf16[1024,4096]{1,0:T(8,128)(2,1)} %all-gather.4.cloned.1.call-done.refs_0_, bf16[3,4096,512]{2,1,0:T(8,128)(2,1)} %refs_3_.3, bf16[3,4096,512]{2,1,0:T(8,128)(2,1)} %refs_3_.3, bf16[3,4096,512]{2,1,0:T(8,128)(2,1)} %refs_3_.3, ...), custom_call_target="tpu_custom_call" | custom-call | flops 6442450944 | bytes 14680064 | tf_op jit(solution)/shard_map/pallas_call | solution.py:96
  225.8 13.9 %all_to_all.43.signal_ref = bf16[8,32,1024]{2,1,0:T(8,128)(2,1)} all-to-all(bf16[8,32,1024]{2,1,0:T(8,128)(2,1)} %bitcast.83), channel_id=1, replica_groups=mesh['seq'=8,'chan'=4] {'seq'}, dimensions={0} | all-to-all | bytes 1048576 | tf_op jit(solution)/shard_map/all_to_all | solution.py:394
  239.6 4.8 %shard_map.175 = bf16[8,32,1024]{2,1,0:T(8,128)(2,1)} custom-call(bf16[8,32,1024]{2,1,0:T(8,128)(2,1)} %all_to_all.43.signal_ref, bf16[2,64,72,128]{3,2,1,0:T(8,128)(2,1)} %shard_map.173.refs_6_.resp_ref, bf16[144,64]{1,0:T(8,128)(2,1)} %constant.134.clone.first_ref, bf16[64,144]{1,0:T(8,128)(2,1)} %constant.135.clone.last_ref, ...), custom_call_target="tpu_custom_call" | custom-call | flops 754974720 | bytes 2228224 | tf_op jit(solution)/shard_map/pallas_call | solution.py:195
  244.4 13.9 %all_to_all.44 = bf16[8,32,1024]{2,1,0:T(8,128)(2,1)} all-to-all(bf16[8,32,1024]{2,1,0:T(8,128)(2,1)} %shard_map.175), channel_id=1, replica_groups=mesh['seq'=8,'chan'=4] {'seq'}, dimensions={0} | all-to-all | bytes 1048576 | tf_op jit(solution)/shard_map/all_to_all | solution.py:395
  258.3 2.2 shard_map.176
  260.5 0.0 all-gather.6.cloned.1.call-update
  260.6 0.0 all-gather.8.cloned.1.call-done.gated_ref
  260.6 6.5 %shard_map.180.refs_0_ = f32[1024,1024]{1,0:T(8,128)} custom-call(bf16[1024,1024]{1,0:T(8,128)(2,1)} %all-gather.8.cloned.1.call-done.gated_ref, bf16[8,4,64,1024]{3,2,1,0:T(8,128)(2,1)} %bitcast.74), custom_call_target="tpu_custom_call" | custom-call | flops 2147483648 | bytes 10485760 | tf_op jit(solution)/shard_map/pallas_call | solution.py:348
  267.1 37.2 %all-gather.6.cloned.1.call-done.gated_ref = bf16[1024,1024]{1,0:T(8,128)(2,1)} async-done(((bf16[1024,256]{1,0:T(8,128)(2,1)}), bf16[1024,1024]{1,0:T(8,128)(2,1)}) %all-gather.6.cloned.1.call-update) | async-done | bytes 2097168 | tf_op jit(solution)/shard_map/all_gather | solution.py:398
  304.3 6.8 %shard_map.181 = bf16[1024,1024]{1,0:T(8,128)(2,1)} custom-call(bf16[1024,1024]{1,0:T(8,128)(2,1)} %all-gather.6.cloned.1.call-done.gated_ref, bf16[8,4,64,1024]{3,2,1,0:T(8,128)(2,1)} %bitcast.75, f32[1024,1024]{1,0:T(8,128)} %shard_map.180.refs_0_), custom_call_target="tpu_custom_call" | custom-call | flops 2147483648 | bytes 10485760 | tf_op jit(solution)/shard_map/pallas_call | solution.py:348
  (7 shorter events, 0.1 us)
Async XLA Ops:
  6.5 160.5 %all-gather.4.cloned.1.call-start = ((), (), s32[]{:S(2)}) async-start(), calls=%async_computation.6 | async-start | bytes 10485760 | tf_op jit(solution)/shard_map/all_gather | solution.py:374
  9.2 29.7 %all-to-all-start = ((bf16[64,4,1024]{2,0,1:T(8,128)(2,1)}), bf16[64,4,1024]{2,0,1:T(8,128)(2,1)S(1)}, u32[]{:S(2)}, u32[]{:S(2)}) async-start(bf16[64,4,1024]{2,0,1:T(8,128)(2,1)} %bitcast.70), calls=%async_computation | async-start | bytes 1048576 | tf_op jit(solution)/shard_map/all_to_all | solution.py:325
  38.9 2.1 collective-permute-start
  41.0 13.0 %collective-permute-start.1 = (bf16[1,16,1024]{2,1,0:T(8,128)(2,1)S(1)}, bf16[1,16,1024]{2,1,0:T(8,128)(2,1)S(1)}, u32[]{:S(2)}, u32[]{:S(2)}) collective-permute-start(bf16[1,16,1024]{2,1,0:T(8,128)(2,1)S(1)} %bitcast.85), channel_id=1, source_target_pairs={{0,2},{1,3},{2,0},{3,1},{4,6},{5,7},{6,4},{7,5},{8,10},{9,11},{10,... | collective-permute-start | bytes 98312 | tf_op jit(solution)/shard_map/ppermute | solution.py:30
  54.0 18.3 %collective-permute-start.2 = (bf16[2,16,1024]{2,1,0:T(8,128)(2,1)S(1)}, bf16[2,16,1024]{2,1,0:T(8,128)(2,1)S(1)}, u32[]{:S(2)}, u32[]{:S(2)}) collective-permute-start(bf16[2,16,1024]{2,1,0:T(8,128)(2,1)S(1)} %maximum_bitcast_fusion.1), channel_id=1, source_target_pairs={{0,1},{1,0},{2,3},{3,2},{4,5},{5,4},{6,7},{7,6},{8,9},{9,8},{10,11... | collective-permute-start | bytes 196616 | tf_op jit(solution)/shard_map/ppermute | solution.py:30
  72.3 15.4 %collective-permute-start.3 = (bf16[1,4,64,1024]{3,2,1,0:T(8,128)(2,1)S(1)}, bf16[1,4,64,1024]{3,2,1,0:T(8,128)(2,1)S(1)}, u32[]{:S(2)}, u32[]{:S(2)}) collective-permute-start(bf16[1,4,64,1024]{3,2,1,0:T(8,128)(2,1)S(1)} %bitcast.77), channel_id=1, source_target_pairs={{0,16},{4,20},{8,24},{12,28},{16,0},{20,4},{24,8},{28,12},{1,17},{... | collective-permute-start | bytes 1572872 | tf_op jit(solution)/shard_map/ppermute | solution.py:30
  88.9 26.3 %collective-permute-start.4 = (bf16[2,4,64,1024]{3,2,1,0:T(8,128)(2,1)}, bf16[2,4,64,1024]{3,2,1,0:T(8,128)(2,1)S(1)}, u32[]{:S(2)}, u32[]{:S(2)}) collective-permute-start(bf16[2,4,64,1024]{3,2,1,0:T(8,128)(2,1)} %maximum_bitcast_fusion), channel_id=1, source_target_pairs={{0,8},{4,12},{8,0},{12,4},{16,24},{20,28},{24,16},{28,20},{1,9},{5... | collective-permute-start | bytes 3145736 | tf_op jit(solution)/shard_map/ppermute | solution.py:30
  90.4 66.3 %all-to-all-start.1 = ((bf16[8,2,2,64,1024]{4,3,2,1,0:T(8,128)(2,1)}), bf16[8,2,2,64,1024]{4,3,2,1,0:T(8,128)(2,1)}, u32[]{:S(2)}, u32[]{:S(2)}) async-start(bf16[8,2,2,64,1024]{4,3,2,1,0:T(8,128)(2,1)} %shard_map.172), calls=%async_computation.1 | async-start | bytes 8388608 | tf_op jit(solution)/shard_map/all_to_all | solution.py:304
  95.0 165.6 %all-gather.8.cloned.1.call-start = ((), (), s32[]{:S(2)}) async-start(), calls=%async_computation.8 | async-start | bytes 2621440 | tf_op jit(solution)/shard_map/all_gather | solution.py:398
  115.6 7.2 %collective-permute-start.5 = (bf16[4,4,64,1024]{3,2,1,0:T(8,128)(2,1)S(1)}, bf16[4,4,64,1024]{3,2,1,0:T(8,128)(2,1)}, u32[]{:S(2)}, u32[]{:S(2)}) collective-permute-start(bf16[4,4,64,1024]{3,2,1,0:T(8,128)(2,1)S(1)} %bitcast.76), channel_id=1, source_target_pairs={{0,4},{4,0},{8,12},{12,8},{16,20},{20,16},{24,28},{28,24},{1,5},{5... | collective-permute-start | bytes 6291464 | tf_op jit(solution)/shard_map/ppermute | solution.py:30
  213.7 90.6 %all-gather.6.cloned.1.call-start = ((), (), s32[]{:S(2)}) async-start(), calls=%async_computation.7 | async-start | bytes 2621440 | tf_op jit(solution)/shard_map/all_gather | solution.py:398
Sparse Core Ops, SparseCore 0:
  8.9 158.0 all-gather.3
  213.8 43.4 all-gather.7
  260.7 43.5 all-gather.5

commit v8 on v7

--- a/solution.py
+++ b/solution.py
@@ -12,7 +12,7 @@
 DEPTH_STEP = 1024
 CHAN_BLOCK = 16
 CHUNKS = 2
-VMEM_BYTES = 60 * 1024 * 1024
+MIB = 1024 * 1024
 
 
 def from_behind(value, axis, by):
@@ -106,7 +106,7 @@
         out_specs=[pl.BlockSpec(shape.shape, lambda z: (0, 0)) for shape in shapes],
         out_shape=shapes,
         scratch_shapes=[pltpu.VMEM((len(streams), HALO + rows, size), jnp.float32)],
-        compiler_params=pltpu.CompilerParams(vmem_limit_bytes=VMEM_BYTES),
+        compiler_params=pltpu.CompilerParams(vmem_limit_bytes=24 * MIB),
         cost_estimate=pl.CostEstimate(
             flops=2 * len(streams) * rows * depth * size,
             bytes_accessed=2 * depth * (len(streams) * size + rows),
@@ -207,7 +207,7 @@
             pltpu.VMEM((block * rows, 2 * LANES), jnp.bfloat16),
             pltpu.VMEM((block * rows, 2 * LANES), jnp.float32),
         ],
-        compiler_params=pltpu.CompilerParams(vmem_limit_bytes=VMEM_BYTES),
+        compiler_params=pltpu.CompilerParams(vmem_limit_bytes=12 * MIB),
         cost_estimate=pl.CostEstimate(flops=flops, bytes_accessed=moved, transcendentals=0),
     )(values, response, *tables)
 
@@ -233,7 +233,7 @@
         ],
         out_specs=flat,
         out_shape=jax.ShapeDtypeStruct((tok_rows, chans), jnp.bfloat16),
-        compiler_params=pltpu.CompilerParams(vmem_limit_bytes=VMEM_BYTES),
+        compiler_params=pltpu.CompilerParams(vmem_limit_bytes=8 * MIB),
         cost_estimate=pl.CostEstimate(flops=4 * chans * tok_rows, bytes_accessed=8 * chans * tok_rows, transcendentals=0),
     )(longconv, skip[None, :], signal, query)
 
@@ -290,7 +290,7 @@
         ],
         out_specs=pl.BlockSpec((seq_count, 1, 1, own * each, tok_rows), lambda p, j: (0, p, j, 0, 0)),
         out_shape=jax.ShapeDtypeStruct(shape, jnp.bfloat16),
-        compiler_params=pltpu.CompilerParams(vmem_limit_bytes=VMEM_BYTES),
+        compiler_params=pltpu.CompilerParams(vmem_limit_bytes=24 * MIB),
         cost_estimate=pl.CostEstimate(
             flops=2 * spectrum.size * tok_rows, bytes_accessed=6 * spectrum.size, transcendentals=0
         ),
@@ -314,7 +314,7 @@
             pltpu.VMEM((seq_count * runs * own * block, LANES), jnp.float32),
             pltpu.VMEM((block * rows, LANES), jnp.float32),
         ],
-        compiler_params=pltpu.CompilerParams(vmem_limit_bytes=VMEM_BYTES),
+        compiler_params=pltpu.CompilerParams(vmem_limit_bytes=12 * MIB),
         cost_estimate=pl.CostEstimate(flops=sent.size, bytes_accessed=3 * sent.size, transcendentals=0),
     )(got)
 
@@ -355,7 +355,7 @@
         ],
         out_specs=block,
         out_shape=jax.ShapeDtypeStruct((tok_rows, features), dtype),
-        compiler_params=pltpu.CompilerParams(vmem_limit_bytes=VMEM_BYTES),
+        compiler_params=pltpu.CompilerParams(vmem_limit_bytes=20 * MIB),
         cost_estimate=pl.CostEstimate(
             flops=2 * tok_rows * depth * features,
             bytes_accessed=2 * depth * (tok_rows + features) + 6 * tok_rows * features,
@@ -374,7 +374,7 @@
     gathered = lax.all_gather(tokens, "chan", axis=1, tiled=True)
     weight = feature_rows(out_weight, seq_count)
     last_rows = tokens[tok_rows - HALO :]
-    weight, last_rows, spectrum = lax.optimization_barrier((weight, last_rows, spectrum))
+    weight, last_rows = lax.optimization_barrier((weight, last_rows))
     halo = gather_by_doubling(from_behind(last_rows, "seq", 1), "chan")
     sent = reordered_spectrum(spectrum, seq_count, chunks)
     halo, sent, weight = lax.optimization_barrier((halo, sent, weight))

time: 319 us -> 327 us (1.025)
  local copies, waits for them, and re-layouts: 16 us -> 53.8 us
  Pallas kernels: 65.4 us -> 44.1 us
  blocking collectives: 55.5 us -> 49.7 us
    unnamed x0 -> x44, local copies, waits for them, and re-layouts: none -> 37.7 us
    pallas_call x2, Pallas kernels: 13.3 us -> 7.7 us  [combine(): pl.pallas_call(combine_kernel, grid=(features // tile,), in_specs=[pl.Blo...]
    pallas_call x2, Pallas kernels: 23.9 us -> 18.8 us  [project(): pl.pallas_call(lambda *refs: project_kernel(streams, len(after), *refs),...]
    pallas_call x1, Pallas kernels: 9.17 us -> 5.26 us  [reordered_spectrum(): pl.pallas_call(reorder_kernel, grid=(parts, chunks), in_specs=[pl.BlockSp...]
    pallas_call x2, Pallas kernels: 9.53 us -> 5.92 us  [long_conv(): pl.pallas_call(conv_kernel, grid=(chans // block,), in_specs=[pl.BlockSpe...]
    all_to_all x2, blocking collectives: 27.8 us -> 24.3 us  [shards(): lax.all_to_all(long_conv(values, response, lo // seq_count), 'seq', split...]
  transfers between devices with their start and end apart: 11 -> 11, of which waited for: 7 -> 7; matrix products, arithmetic and copies ran while one was open for 9% -> 8% of each run, Pallas kernels for 13% -> 8%
where the time goes in v8:
time: 327 us; the launch traced here: 325 us
  waiting for transfers between devices  126 us (39%)
  local copies, waits for them, and re-layouts  53.8 us (16%)
  blocking collectives  49.7 us (15%)
  Pallas kernels  44.1 us (13%)
  starting transfers between devices  28.7 us (9%)
  between operations  13.5 us (4%)
  matrix products  6.42 us (2%)
  other arithmetic  3.55 us (1%)
    unnamed x44, local copies, waits for them, and re-layouts  37.7 us
    all_gather x2, waiting for transfers between devices, shards(): lax.all_gather(gate(longconv, skip, lo, signal_t, query_t), 'chan', axis=...  34.5 us
    all_to_all x1, waiting for transfers between devices, folded_response(): got = lax.all_to_all(sent, 'seq', split_axis=0, concat_axis=0, tiled=True)  30.6 us
    ppermute x5, waiting for transfers between devices, gather_by_doubling(): other = lax.ppermute(held, axis, [(i, i ^ bit) for i in range(size)])  29.9 us
    all_to_all x2, blocking collectives, shards(): lax.all_to_all(values, 'seq', split_axis=0, concat_axis=0, tiled=True)  25.4 us
    all_to_all x2, blocking collectives, shards(): lax.all_to_all(long_conv(values, response, lo // seq_count), 'seq', split...  24.3 us
    all_to_all x1, waiting for transfers between devices, feature_rows(): own = lax.all_to_all(own, 'chan', split_axis=1, concat_axis=0, tiled=True)  22.6 us
    pallas_call x2, Pallas kernels, project(): pl.pallas_call(lambda *refs: project_kernel(streams, len(after), *refs),...  18.8 us
  transfers between devices with their start and end apart: 11, of which 7 were waited for; matrix products, arithmetic and copies ran while one was open for 8% of the time, Pallas kernels for 8%

profile of v8, /device:TPU:0, one launch (start us, length us, event | category | flops | bytes accessed | tf_op | source)
XLA Modules:
  0.0 325.4 jit_solution(5273015372339042716)
XLA Ops:
  6.5 0.7 all-gather.4.cloned.1.call-update
  7.3 1.1 constant_dynamic-slice_fusion
  8.3 0.8 copy.33
  9.2 6.3 %all-to-all-start = ((bf16[64,4,1024]{2,0,1:T(8,128)(2,1)}), bf16[64,4,1024]{2,0,1:T(8,128)(2,1)S(1)}, u32[]{:S(2)}, u32[]{:S(2)}) async-start(bf16[64,4,1024]{2,0,1:T(8,128)(2,1)} %bitcast.70), calls=%async_computation | async-start | bytes 1048576 | tf_op jit(solution)/shard_map/all_to_all | solution.py:325
  15.5 0.8 slice.3
  16.3 22.6 %all-to-all-done = bf16[64,4,1024]{2,0,1:T(8,128)(2,1)S(1)} async-done(((bf16[64,4,1024]{2,0,1:T(8,128)(2,1)}), bf16[64,4,1024]{2,0,1:T(8,128)(2,1)S(1)}, u32[]{:S(2)}, u32[]{:S(2)}) %all-to-all-start) | async-done | bytes 524320 | tf_op jit(solution)/shard_map/all_to_all | solution.py:325
  38.9 1.3 collective-permute-start
  40.2 0.8 collective-permute-done
  41.0 0.7 fusion.1.order_ref
  41.7 10.9 %reshape.40.spec_ref = f32[2,1024,1024]{2,1,0:T(8,128)} reshape(f32[2,512,2,1024]{3,2,1,0:T(2,128)} %param.21) | data formatting | bytes 16777216 | tf_op jit(solution)/shard_map/reshape | solution.py:297
  52.7 9.1 %collective-permute-start.2 = (bf16[2,16,1024]{2,1,0:T(8,128)(2,1)S(1)}, bf16[2,16,1024]{2,1,0:T(8,128)(2,1)S(1)}, u32[]{:S(2)}, u32[]{:S(2)}) collective-permute-start(bf16[2,16,1024]{2,1,0:T(8,128)(2,1)S(1)} %maximum_bitcast_fusion.1), channel_id=1, source_target_pairs={{0,1},{1,0},{2,3},{3,2},{4,5},{5,4},{6,7},{7,6},{8,9},{9,8},{10,11... | collective-permute-start | bytes 196616 | tf_op jit(solution)/shard_map/ppermute | solution.py:30
  61.8 3.4 %copy-done.10 = f32[2,1024,1024]{2,1,0:T(8,128)S(1)} copy-done((f32[2,1024,1024]{2,1,0:T(8,128)S(1)}, f32[2,1024,1024]{2,1,0:T(8,128)}, u32[]{:S(2)}) %copy-start.10) | copy-done | bytes 8388632
  65.3 5.3 %shard_map.172 = bf16[8,2,2,64,1024]{4,3,2,1,0:T(8,128)(2,1)S(1)} custom-call(f32[2,1024,1024]{2,1,0:T(8,128)S(1)} %copy-done.10, bf16[1024,1024]{1,0:T(8,128)(2,1)S(1)} %fusion.1.order_ref), custom_call_target="tpu_custom_call" | custom-call | flops 4294967296 | bytes 12582912 | tf_op jit(solution)/shard_map/pallas_call | solution.py:284
  70.6 1.9 copy-done.11
  72.5 5.2 %collective-permute-start.3 = (bf16[1,4,64,1024]{3,2,1,0:T(8,128)(2,1)S(1)}, bf16[1,4,64,1024]{3,2,1,0:T(8,128)(2,1)S(1)}, u32[]{:S(2)}, u32[]{:S(2)}) collective-permute-start(bf16[1,4,64,1024]{3,2,1,0:T(8,128)(2,1)S(1)} %bitcast.83), channel_id=1, source_target_pairs={{0,16},{4,20},{8,24},{12,28},{16,0},{20,4},{24,8},{28,12},{1,17},{... | collective-permute-start | bytes 1572872 | tf_op jit(solution)/shard_map/ppermute | solution.py:30
  77.8 10.1 %collective-permute-done.3 = bf16[1,4,64,1024]{3,2,1,0:T(8,128)(2,1)S(1)} collective-permute-done((bf16[1,4,64,1024]{3,2,1,0:T(8,128)(2,1)S(1)}, bf16[1,4,64,1024]{3,2,1,0:T(8,128)(2,1)S(1)}, u32[]{:S(2)}, u32[]{:S(2)}) %collective-permute-start.3) | collective-permute-done | bytes 524320 | tf_op jit(solution)/shard_map/ppermute | solution.py:30
  87.9 0.1 select_bitcast_fusion.5
  88.0 0.1 maximum_bitcast_fusion
  88.1 1.6 collective-permute-start.4
  89.7 4.6 %all-to-all-start.1 = ((bf16[8,2,2,64,1024]{4,3,2,1,0:T(8,128)(2,1)}), bf16[8,2,2,64,1024]{4,3,2,1,0:T(8,128)(2,1)}, u32[]{:S(2)}, u32[]{:S(2)}) async-start(bf16[8,2,2,64,1024]{4,3,2,1,0:T(8,128)(2,1)} %copy-done.11), calls=%async_computation.1 | async-start | bytes 8388608 | tf_op jit(solution)/shard_map/all_to_all | solution.py:304
  94.2 0.2 all-gather.8.cloned.1.call-start
  94.5 19.8 %collective-permute-done.4 = bf16[2,4,64,1024]{3,2,1,0:T(8,128)(2,1)S(1)} collective-permute-done((bf16[2,4,64,1024]{3,2,1,0:T(8,128)(2,1)S(1)}, bf16[2,4,64,1024]{3,2,1,0:T(8,128)(2,1)S(1)}, u32[]{:S(2)}, u32[]{:S(2)}) %collective-permute-start.4) | collective-permute-done | bytes 1048608 | tf_op jit(solution)/shard_map/ppermute | solution.py:30
  114.3 0.1 select_bitcast_fusion.3
  114.4 0.2 pad_maximum_fusion.1
  114.6 0.1 collective-permute-start.5
  114.7 6.4 %fusion.3.refs_5_ = bf16[3,16,512]{2,1,0:T(8,128)(2,1)S(1)} fusion(bf16[3,4,1024,512]{3,2,1,0:T(8,128)(2,1)} %bitcast.71, bf16[4,16,1024]{2,1,0:T(8,128)(2,1)S(1)} %bitcast.86), kind=kOutput, calls=%fused_computation.9 | convolution fusion | flops 201351168 | bytes 12763136 | tf_op jit(solution)/shard_map/ztd,pzdc->ptc/dot_general | solution.py:383
  121.1 1.9 select_bitcast_fusion.1
  123.0 0.4 pad_maximum_fusion
  123.4 2.5 copy.29
  125.9 30.6 %all-to-all-done.1.got_ref = bf16[8,2,2,64,1024]{4,3,2,1,0:T(8,128)(2,1)} async-done(((bf16[8,2,2,64,1024]{4,3,2,1,0:T(8,128)(2,1)}), bf16[8,2,2,64,1024]{4,3,2,1,0:T(8,128)(2,1)}, u32[]{:S(2)}, u32[]{:S(2)}) %all-to-all-start.1) | async-done | bytes 4194336 | tf_op jit(solution)/shard_map/all_to_all | solution.py:304
  156.5 4.0 %shard_map.173.refs_6_.resp_ref = bf16[2,64,72,128]{3,2,1,0:T(8,128)(2,1)S(1)} custom-call(bf16[8,2,2,64,1024]{4,3,2,1,0:T(8,128)(2,1)} %all-to-all-done.1.got_ref), custom_call_target="tpu_custom_call" | custom-call | flops 2097152 | bytes 6291456 | tf_op jit(solution)/shard_map/pallas_call | solution.py:307
  160.6 6.4 %all-gather.4.cloned.1.call-done.refs_0_ = bf16[1024,4096]{1,0:T(8,128)(2,1)} async-done(((bf16[1024,1024]{1,0:T(8,128)(2,1)}), bf16[1024,4096]{1,0:T(8,128)(2,1)}) %all-gather.4.cloned.1.call-update) | async-done | bytes 8388624 | tf_op jit(solution)/shard_map/all_gather | solution.py:374
  167.0 4.6 %copy-done = bf16[3,4096,512]{2,1,0:T(8,128)(2,1)S(1)} copy-done((bf16[3,4096,512]{2,1,0:T(8,128)(2,1)S(1)}, bf16[3,4096,512]{2,1,0:T(8,128)(2,1)}, u32[]{:S(2)}) %copy-start) | copy-done | bytes 12582936
  171.6 2.2 copy-done.2
  173.8 3.4 %copy-done.6 = bf16[1024,4096]{1,0:T(8,128)(2,1)S(1)} copy-done((bf16[1024,4096]{1,0:T(8,128)(2,1)S(1)}, bf16[1024,4096]{1,0:T(8,128)(2,1)}, u32[]{:S(2)}) %copy-start.6) | copy-done | bytes 8388632
  177.2 0.0 copy-start.18
  177.2 0.0 copy-start.19
  177.2 9.4 %shard_map.177 = (bf16[1024,256]{1,0:T(8,128)(2,1)S(1)}, bf16[256,1024]{1,0:T(8,128)(2,1)S(1)}, bf16[1024,256]{1,0:T(8,128)(2,1)S(1)}) custom-call(bf16[1024,4096]{1,0:T(8,128)(2,1)S(1)} %copy-done.6, bf16[3,4096,512]{2,1,0:T(8,128)(2,1)S(1)} %copy-done, bf16[3,4096,512]{2,1,0:T(8,128)(2,1)S(1)} %copy-done, bf16[3,4096,512]{2,1,0:T(8,128)(2,1)S(1)} %copy-done, ...), custom_call_target="tpu_custom_call" | custom-call | flops 6442450944 | bytes 14680064 | tf_op jit(solution)/shard_map/pallas_call | solution.py:96
  186.6 0.0 copy-start.21
  186.6 13.3 %all_to_all.41.signal_ref = bf16[8,32,1024]{2,1,0:T(8,128)(2,1)S(1)} all-to-all(bf16[8,32,1024]{2,1,0:T(8,128)(2,1)S(1)} %bitcast.79), channel_id=1, replica_groups=mesh['seq'=8,'chan'=4] {'seq'}, dimensions={0} | all-to-all | bytes 1048576 | tf_op jit(solution)/shard_map/all_to_all | solution.py:394
  199.9 3.0 shard_map.178
  202.9 12.2 %all_to_all.42 = bf16[8,32,1024]{2,1,0:T(8,128)(2,1)S(1)} all-to-all(bf16[8,32,1024]{2,1,0:T(8,128)(2,1)S(1)} %shard_map.178), channel_id=1, replica_groups=mesh['seq'=8,'chan'=4] {'seq'}, dimensions={0} | all-to-all | bytes 1048576 | tf_op jit(solution)/shard_map/all_to_all | solution.py:395
  215.0 1.2 shard_map.179
  216.3 0.0 all-gather.8.cloned.1.call-update
  216.3 0.3 all-gather.6.cloned.1.call-start
  216.6 4.8 %copy-done.1 = bf16[3,4096,512]{2,1,0:T(8,128)(2,1)S(1)} copy-done((bf16[3,4096,512]{2,1,0:T(8,128)(2,1)S(1)}, bf16[3,4096,512]{2,1,0:T(8,128)(2,1)}, u32[]{:S(2)}) %copy-start.1) | copy-done | bytes 12582936
  221.4 2.3 copy-done.3
  223.6 3.4 %copy-done.7 = bf16[1024,4096]{1,0:T(8,128)(2,1)S(1)} copy-done((bf16[1024,4096]{1,0:T(8,128)(2,1)S(1)}, bf16[1024,4096]{1,0:T(8,128)(2,1)}, u32[]{:S(2)}) %copy-start.7) | copy-done | bytes 8388632
  227.1 9.4 %shard_map.174 = (bf16[1024,256]{1,0:T(8,128)(2,1)S(1)}, bf16[256,1024]{1,0:T(8,128)(2,1)S(1)}, bf16[1024,256]{1,0:T(8,128)(2,1)S(1)}) custom-call(bf16[1024,4096]{1,0:T(8,128)(2,1)S(1)} %copy-done.7, bf16[3,4096,512]{2,1,0:T(8,128)(2,1)S(1)} %copy-done.1, bf16[3,4096,512]{2,1,0:T(8,128)(2,1)S(1)} %copy-done.1, bf16[3,4096,512]{2,1,0:T(8,128)(2,1)S(1)} %copy-done.1, ...), custom_call_target="tpu_custom_call" | custom-call | flops 6442450944 | bytes 14680064 | tf_op jit(solution)/shard_map/pallas_call | solution.py:96
  236.4 12.2 %all_to_all.43.signal_ref = bf16[8,32,1024]{2,1,0:T(8,128)(2,1)S(1)} all-to-all(bf16[8,32,1024]{2,1,0:T(8,128)(2,1)S(1)} %bitcast.78), channel_id=1, replica_groups=mesh['seq'=8,'chan'=4] {'seq'}, dimensions={0} | all-to-all | bytes 1048576 | tf_op jit(solution)/shard_map/all_to_all | solution.py:394
  248.6 3.0 shard_map.175
  251.5 12.2 %all_to_all.44 = bf16[8,32,1024]{2,1,0:T(8,128)(2,1)S(1)} all-to-all(bf16[8,32,1024]{2,1,0:T(8,128)(2,1)S(1)} %shard_map.175), channel_id=1, replica_groups=mesh['seq'=8,'chan'=4] {'seq'}, dimensions={0} | all-to-all | bytes 1048576 | tf_op jit(solution)/shard_map/all_to_all | solution.py:395
  263.7 1.2 shard_map.176
  264.9 0.0 all-gather.6.cloned.1.call-update
  264.9 0.0 all-gather.8.cloned.1.call-done.gated_ref
  265.0 2.2 copy-done.4
  267.2 1.6 copy-done.12
  268.8 3.4 %shard_map.180.refs_0_ = f32[1024,1024]{1,0:T(8,128)S(1)} custom-call(bf16[1024,1024]{1,0:T(8,128)(2,1)S(1)} %copy-done.12, bf16[8,4,64,1024]{3,2,1,0:T(8,128)(2,1)S(1)} %bitcast.74), custom_call_target="tpu_custom_call" | custom-call | flops 2147483648 | bytes 10485760 | tf_op jit(solution)/shard_map/pallas_call | solution.py:348
  272.2 1.9 copy-done.8
  274.1 34.5 %all-gather.6.cloned.1.call-done.gated_ref = bf16[1024,1024]{1,0:T(8,128)(2,1)} async-done(((bf16[1024,256]{1,0:T(8,128)(2,1)}), bf16[1024,1024]{1,0:T(8,128)(2,1)}) %all-gather.6.cloned.1.call-update) | async-done | bytes 2097168 | tf_op jit(solution)/shard_map/all_gather | solution.py:398
  308.6 2.2 copy-done.5
  310.8 2.2 copy-done.9
  313.0 1.6 copy-done.13
  314.6 4.3 %shard_map.181 = bf16[1024,1024]{1,0:T(8,128)(2,1)} custom-call(bf16[1024,1024]{1,0:T(8,128)(2,1)S(1)} %copy-done.13, bf16[8,4,64,1024]{3,2,1,0:T(8,128)(2,1)S(1)} %bitcast.75, f32[1024,1024]{1,0:T(8,128)S(1)} %copy-done.9), custom_call_target="tpu_custom_call" | custom-call | flops 2147483648 | bytes 10485760 | tf_op jit(solution)/shard_map/pallas_call | solution.py:348
  (39 shorter events, 0.1 us)
Async XLA Ops:
  6.5 160.5 %all-gather.4.cloned.1.call-start = ((), (), s32[]{:S(2)}) async-start(), calls=%async_computation.6 | async-start | bytes 10485760 | tf_op jit(solution)/shard_map/all_gather | solution.py:374
  9.2 29.7 %all-to-all-start = ((bf16[64,4,1024]{2,0,1:T(8,128)(2,1)}), bf16[64,4,1024]{2,0,1:T(8,128)(2,1)S(1)}, u32[]{:S(2)}, u32[]{:S(2)}) async-start(bf16[64,4,1024]{2,0,1:T(8,128)(2,1)} %bitcast.70), calls=%async_computation | async-start | bytes 1048576 | tf_op jit(solution)/shard_map/all_to_all | solution.py:325
  38.9 2.1 collective-permute-start
  41.0 11.7 %collective-permute-start.1 = (bf16[1,16,1024]{2,1,0:T(8,128)(2,1)S(1)}, bf16[1,16,1024]{2,1,0:T(8,128)(2,1)S(1)}, u32[]{:S(2)}, u32[]{:S(2)}) collective-permute-start(bf16[1,16,1024]{2,1,0:T(8,128)(2,1)S(1)} %bitcast.87), channel_id=1, source_target_pairs={{0,2},{1,3},{2,0},{3,1},{4,6},{5,7},{6,4},{7,5},{8,10},{9,11},{10,... | collective-permute-start | bytes 98312 | tf_op jit(solution)/shard_map/ppermute | solution.py:30
  52.7 19.8 %collective-permute-start.2 = (bf16[2,16,1024]{2,1,0:T(8,128)(2,1)S(1)}, bf16[2,16,1024]{2,1,0:T(8,128)(2,1)S(1)}, u32[]{:S(2)}, u32[]{:S(2)}) collective-permute-start(bf16[2,16,1024]{2,1,0:T(8,128)(2,1)S(1)} %maximum_bitcast_fusion.1), channel_id=1, source_target_pairs={{0,1},{1,0},{2,3},{3,2},{4,5},{5,4},{6,7},{7,6},{8,9},{9,8},{10,11... | collective-permute-start | bytes 196616 | tf_op jit(solution)/shard_map/ppermute | solution.py:30
  61.8 3.4 %copy-start.10 = (f32[2,1024,1024]{2,1,0:T(8,128)S(1)}, f32[2,1024,1024]{2,1,0:T(8,128)}, u32[]{:S(2)}) copy-start(f32[2,1024,1024]{2,1,0:T(8,128)} %reshape.40.spec_ref) | copy-start | bytes 25165828
  70.5 2.0 copy-start.11
  72.5 15.4 %collective-permute-start.3 = (bf16[1,4,64,1024]{3,2,1,0:T(8,128)(2,1)S(1)}, bf16[1,4,64,1024]{3,2,1,0:T(8,128)(2,1)S(1)}, u32[]{:S(2)}, u32[]{:S(2)}) collective-permute-start(bf16[1,4,64,1024]{3,2,1,0:T(8,128)(2,1)S(1)} %bitcast.83), channel_id=1, source_target_pairs={{0,16},{4,20},{8,24},{12,28},{16,0},{20,4},{24,8},{28,12},{1,17},{... | collective-permute-start | bytes 1572872 | tf_op jit(solution)/shard_map/ppermute | solution.py:30
  88.1 26.2 %collective-permute-start.4 = (bf16[2,4,64,1024]{3,2,1,0:T(8,128)(2,1)S(1)}, bf16[2,4,64,1024]{3,2,1,0:T(8,128)(2,1)S(1)}, u32[]{:S(2)}, u32[]{:S(2)}) collective-permute-start(bf16[2,4,64,1024]{3,2,1,0:T(8,128)(2,1)S(1)} %maximum_bitcast_fusion), channel_id=1, source_target_pairs={{0,8},{4,12},{8,0},{12,4},{16,24},{20,28},{24,16},{28,20},{1,9},{5... | collective-permute-start | bytes 3145736 | tf_op jit(solution)/shard_map/ppermute | solution.py:30
  89.7 66.9 %all-to-all-start.1 = ((bf16[8,2,2,64,1024]{4,3,2,1,0:T(8,128)(2,1)}), bf16[8,2,2,64,1024]{4,3,2,1,0:T(8,128)(2,1)}, u32[]{:S(2)}, u32[]{:S(2)}) async-start(bf16[8,2,2,64,1024]{4,3,2,1,0:T(8,128)(2,1)} %copy-done.11), calls=%async_computation.1 | async-start | bytes 8388608 | tf_op jit(solution)/shard_map/all_to_all | solution.py:304
  94.2 170.7 %all-gather.8.cloned.1.call-start = ((), (), s32[]{:S(2)}) async-start(), calls=%async_computation.8 | async-start | bytes 2621440 | tf_op jit(solution)/shard_map/all_gather | solution.py:398
  114.6 6.5 %collective-permute-start.5 = (bf16[4,4,64,1024]{3,2,1,0:T(8,128)(2,1)S(1)}, bf16[4,4,64,1024]{3,2,1,0:T(8,128)(2,1)}, u32[]{:S(2)}, u32[]{:S(2)}) collective-permute-start(bf16[4,4,64,1024]{3,2,1,0:T(8,128)(2,1)S(1)} %bitcast.82), channel_id=1, source_target_pairs={{0,4},{4,0},{8,12},{12,8},{16,20},{20,16},{24,28},{28,24},{1,5},{5... | collective-permute-start | bytes 6291464 | tf_op jit(solution)/shard_map/ppermute | solution.py:30
  125.9 41.1 %copy-start.20 = (f32[3,3,512]{2,1,0:T(4,128)S(1)}, f32[3,3,512]{2,1,0:T(4,128)}, u32[]{:S(2)}) copy-start(f32[3,3,512]{2,1,0:T(4,128)} %refs_4_.3) | copy-start | bytes 55300
  167.0 4.6 %copy-start = (bf16[3,4096,512]{2,1,0:T(8,128)(2,1)S(1)}, bf16[3,4096,512]{2,1,0:T(8,128)(2,1)}, u32[]{:S(2)}) copy-start(bf16[3,4096,512]{2,1,0:T(8,128)(2,1)} %refs_3_.3) | copy-start | bytes 37748740
  171.6 2.2 copy-start.2
  173.8 3.4 %copy-start.6 = (bf16[1024,4096]{1,0:T(8,128)(2,1)S(1)}, bf16[1024,4096]{1,0:T(8,128)(2,1)}, u32[]{:S(2)}) copy-start(bf16[1024,4096]{1,0:T(8,128)(2,1)} %all-gather.4.cloned.1.call-done.refs_0_) | copy-start | bytes 25165828
  177.1 22.7 %copy-start.14 = (bf16[256,256]{1,0:T(8,128)(2,1)S(1)}, bf16[256,256]{1,0:T(8,128)(2,1)}, u32[]{:S(2)}) copy-start(bf16[256,256]{1,0:T(8,128)(2,1)} %constant.138.clone.fwd_ref) | copy-start | bytes 393220
  177.1 22.7 %copy-start.15 = (bf16[256,256]{1,0:T(8,128)(2,1)S(1)}, bf16[256,256]{1,0:T(8,128)(2,1)}, u32[]{:S(2)}) copy-start(bf16[256,256]{1,0:T(8,128)(2,1)} %constant.139.clone.bwd_ref) | copy-start | bytes 393220
  177.1 22.7 %copy-start.16 = (bf16[144,64]{1,0:T(8,128)(2,1)S(1)}, bf16[144,64]{1,0:T(8,128)(2,1)}, u32[]{:S(2)}) copy-start(bf16[144,64]{1,0:T(8,128)(2,1)} %constant.134.clone.first_ref) | copy-start | bytes 55300
  177.1 22.7 %copy-start.17 = (f32[72,128]{1,0:T(8,128)S(1)}, f32[72,128]{1,0:T(8,128)}, u32[]{:S(2)}) copy-start(f32[72,128]{1,0:T(8,128)} %constant.136.clone.cos_ref) | copy-start | bytes 110596
  177.2 22.7 %copy-start.18 = (f32[72,128]{1,0:T(8,128)S(1)}, f32[72,128]{1,0:T(8,128)}, u32[]{:S(2)}) copy-start(f32[72,128]{1,0:T(8,128)} %constant.137.clone.sin_ref) | copy-start | bytes 110596
  177.2 22.7 %copy-start.19 = (bf16[64,144]{1,0:T(8,128)(2,1)S(1)}, bf16[64,144]{1,0:T(8,128)(2,1)}, u32[]{:S(2)}) copy-start(bf16[64,144]{1,0:T(8,128)(2,1)} %constant.135.clone.last_ref) | copy-start | bytes 55300
  186.6 28.5 %copy-start.21 = (f32[512]{0:T(512)S(1)}, f32[512]{0:T(512)}, u32[]{:S(2)}) copy-start(f32[512]{0:T(512)} %param.22) | copy-start | bytes 6148
  216.3 92.3 %all-gather.6.cloned.1.call-start = ((), (), s32[]{:S(2)}) async-start(), calls=%async_computation.7 | async-start | bytes 2621440 | tf_op jit(solution)/shard_map/all_gather | solution.py:398
  216.6 4.8 %copy-start.1 = (bf16[3,4096,512]{2,1,0:T(8,128)(2,1)S(1)}, bf16[3,4096,512]{2,1,0:T(8,128)(2,1)}, u32[]{:S(2)}) copy-start(bf16[3,4096,512]{2,1,0:T(8,128)(2,1)} %refs_3_.3) | copy-start | bytes 37748740
  221.4 2.3 copy-start.3
  223.6 3.4 %copy-start.7 = (bf16[1024,4096]{1,0:T(8,128)(2,1)S(1)}, bf16[1024,4096]{1,0:T(8,128)(2,1)}, u32[]{:S(2)}) copy-start(bf16[1024,4096]{1,0:T(8,128)(2,1)} %all-gather.4.cloned.1.call-done.refs_0_) | copy-start | bytes 25165828
  265.0 2.2 copy-start.4
  267.2 1.6 copy-start.12
  272.2 2.0 copy-start.8
  308.6 2.2 copy-start.5
  310.8 2.2 copy-start.9
  313.0 1.6 copy-start.13
Sparse Core Ops, SparseCore 0:
  8.9 158.0 all-gather.3
  216.4 43.4 all-gather.7
  265.1 43.4 all-gather.5

commit v9 on v8

--- a/solution.py
+++ b/solution.py
@@ -9,7 +9,7 @@
 TAPS = 3
 LANES = 128
 HALO = 16
-DEPTH_STEP = 1024
+DEPTH_STEP = 512
 CHAN_BLOCK = 16
 CHUNKS = 2
 MIB = 1024 * 1024
@@ -106,7 +106,7 @@
         out_specs=[pl.BlockSpec(shape.shape, lambda z: (0, 0)) for shape in shapes],
         out_shape=shapes,
         scratch_shapes=[pltpu.VMEM((len(streams), HALO + rows, size), jnp.float32)],
-        compiler_params=pltpu.CompilerParams(vmem_limit_bytes=24 * MIB),
+        compiler_params=pltpu.CompilerParams(vmem_limit_bytes=48 * MIB),
         cost_estimate=pl.CostEstimate(
             flops=2 * len(streams) * rows * depth * size,
             bytes_accessed=2 * depth * (len(streams) * size + rows),
@@ -290,7 +290,7 @@
         ],
         out_specs=pl.BlockSpec((seq_count, 1, 1, own * each, tok_rows), lambda p, j: (0, p, j, 0, 0)),
         out_shape=jax.ShapeDtypeStruct(shape, jnp.bfloat16),
-        compiler_params=pltpu.CompilerParams(vmem_limit_bytes=24 * MIB),
+        compiler_params=pltpu.CompilerParams(vmem_limit_bytes=48 * MIB),
         cost_estimate=pl.CostEstimate(
             flops=2 * spectrum.size * tok_rows, bytes_accessed=6 * spectrum.size, transcendentals=0
         ),
@@ -328,20 +328,15 @@
 
 def combine_kernel(gated_ref, w_ref, *refs):
     out_ref = refs[-1]
-    per, count, each, tile = w_ref.shape
-    weight = jnp.concatenate([w_ref[:, z].reshape(per * each, tile) for z in range(count)], axis=0)
-    total = jnp.dot(gated_ref[...], weight, preferred_element_type=jnp.float32)
+    total = jnp.dot(gated_ref[...], w_ref[0], preferred_element_type=jnp.float32)
     if len(refs) == 2:
         total = total + refs[0][...]
     out_ref[...] = total.astype(out_ref.dtype)
 
 
-def combine(gathered, weight, lo, total, dtype):
+def combine(gathered, weight, chunk, total, dtype):
     tok_rows, depth = gathered.shape
-    _, count, each, features = weight.shape
-    size = depth // count
-    per = size // each
-    first = lo // size
+    features = weight.shape[2]
     tile = min(2 * LANES, features)
     block = pl.BlockSpec((tok_rows, tile), lambda i: (0, i))
     given = [] if total is None else [total]
@@ -350,12 +345,12 @@
         grid=(features // tile,),
         in_specs=[
             pl.BlockSpec((tok_rows, depth), lambda i: (0, 0)),
-            pl.BlockSpec((per, count, each, tile), lambda i: (first, 0, 0, i)),
+            pl.BlockSpec((1, depth, tile), lambda i: (chunk, 0, i)),
             *[block for _ in given],
         ],
         out_specs=block,
         out_shape=jax.ShapeDtypeStruct((tok_rows, features), dtype),
-        compiler_params=pltpu.CompilerParams(vmem_limit_bytes=20 * MIB),
+        compiler_params=pltpu.CompilerParams(vmem_limit_bytes=60 * MIB),
         cost_estimate=pl.CostEstimate(
             flops=2 * tok_rows * depth * features,
             bytes_accessed=2 * depth * (tok_rows + features) + 6 * tok_rows * features,
@@ -380,6 +375,8 @@
     halo, sent, weight = lax.optimization_barrier((halo, sent, weight))
     response = folded_response(sent, spectrum.shape[2])
     weight = gather_by_doubling(weight, "seq")
+    weight = weight.reshape((chunks, seq_count // chunks) + weight.shape[1:]).transpose(0, 2, 1, 3, 4)
+    weight = weight.reshape(chunks, chan_count * size, weight.shape[4])
     halo = jnp.einsum(
         "ztd,pzdc->ptc",
         halo,
@@ -387,7 +384,7 @@
         preferred_element_type=jnp.float32,
     ).astype(jnp.bfloat16)
     total = None
-    for lo in range(0, chans, size):
+    for j, lo in enumerate(range(0, chans, size)):
         given = (gathered, in_weight, conv_weight, halo, lo, size, response, weight)
         query_t, signal, signal_t = project((0, 1, 2), *given)
         values = signal.reshape(seq_count, size // seq_count, tok_rows)
@@ -397,7 +394,7 @@
         ).reshape(size, tok_rows)
         gated = lax.all_gather(gate(longconv, skip, lo, signal_t, query_t), "chan", axis=1, tiled=True)
         dtype = jnp.bfloat16 if lo + size == chans else jnp.float32
-        total = combine(gated, weight, lo, total, dtype)
+        total = combine(gated, weight, j, total, dtype)
     return total
 
 

time: 327 us -> 313 us (0.957)
  local copies, waits for them, and re-layouts: 53.8 us -> 16.8 us
  Pallas kernels: 44.1 us -> 58.5 us
  waiting for transfers between devices: 126 us -> 134 us
    unnamed x44 -> x16, local copies, waits for them, and re-layouts: 37.7 us -> 0.04 us
    all_gather x2, waiting for transfers between devices: 34.5 us -> 42.5 us  [shards(): lax.all_gather(gate(longconv, skip, lo, signal_t, query_t), 'chan', axis=...]
    pallas_call x2, Pallas kernels: 18.8 us -> 24.4 us  [project(): pl.pallas_call(lambda *refs: project_kernel(streams, len(after), *refs),...]
    pallas_call x2, Pallas kernels: 7.7 us -> 13.2 us  [combine(): pl.pallas_call(combine_kernel, grid=(features // tile,), in_specs=[pl.Blo...]
    all_gather x1, waiting for transfers between devices: 6.41 us -> 9.77 us  [shards(): gathered = lax.all_gather(tokens, 'chan', axis=1, tiled=True)]
    pallas_call x1, Pallas kernels: 5.26 us -> 8.57 us  [reordered_spectrum(): pl.pallas_call(reorder_kernel, grid=(parts, chunks), in_specs=[pl.BlockSp...]
  transfers between devices with their start and end apart: 11 -> 11, of which waited for: 7 -> 8; matrix products, arithmetic and copies ran while one was open for 8% -> 9% of each run, Pallas kernels for 8% -> 11%
where the time goes in v9:
time: 313 us; the launch traced here: 312 us
  waiting for transfers between devices  134 us (43%)
  Pallas kernels  58.5 us (19%)
  blocking collectives  49.7 us (16%)
  starting transfers between devices  29.7 us (9%)
  local copies, waits for them, and re-layouts  16.8 us (5%)
  between operations  13.4 us (4%)
  matrix products  6.3 us (2%)
  other arithmetic  3.57 us (1%)
    all_gather x2, waiting for transfers between devices, shards(): lax.all_gather(gate(longconv, skip, lo, signal_t, query_t), 'chan', axis=...  42.5 us
    all_to_all x1, waiting for transfers between devices, folded_response(): got = lax.all_to_all(sent, 'seq', split_axis=0, concat_axis=0, tiled=True)  28.8 us
    ppermute x5, waiting for transfers between devices, gather_by_doubling(): other = lax.ppermute(held, axis, [(i, i ^ bit) for i in range(size)])  28.7 us
    all_to_all x2, blocking collectives, shards(): lax.all_to_all(values, 'seq', split_axis=0, concat_axis=0, tiled=True)  25.4 us
    pallas_call x2, Pallas kernels, project(): pl.pallas_call(lambda *refs: project_kernel(streams, len(after), *refs),...  24.4 us
    all_to_all x2, blocking collectives, shards(): lax.all_to_all(long_conv(values, response, lo // seq_count), 'seq', split...  24.3 us
    all_to_all x1, waiting for transfers between devices, feature_rows(): own = lax.all_to_all(own, 'chan', split_axis=1, concat_axis=0, tiled=True)  22.6 us
    ppermute x5, starting transfers between devices, gather_by_doubling(): other = lax.ppermute(held, axis, [(i, i ^ bit) for i in range(size)])  17.4 us
  transfers between devices with their start and end apart: 11, of which 8 were waited for; matrix products, arithmetic and copies ran while one was open for 9% of the time, Pallas kernels for 11%

profile of v9, /device:TPU:0, one launch (start us, length us, event | category | flops | bytes accessed | tf_op | source)
XLA Modules:
  0.0 311.9 jit_solution(8710101561032870272)
XLA Ops:
  6.5 0.0 all-gather.4.cloned.1.call-start
  6.5 0.7 all-gather.4.cloned.1.call-update
  7.3 1.1 constant_dynamic-slice_fusion
  8.3 0.8 copy.35
  9.2 6.3 %all-to-all-start = ((bf16[64,4,1024]{2,0,1:T(8,128)(2,1)}), bf16[64,4,1024]{2,0,1:T(8,128)(2,1)S(1)}, u32[]{:S(2)}, u32[]{:S(2)}) async-start(bf16[64,4,1024]{2,0,1:T(8,128)(2,1)} %bitcast.73), calls=%async_computation | async-start | bytes 1048576 | tf_op jit(solution)/shard_map/all_to_all | solution.py:325
  15.5 0.8 slice.3
  16.3 22.6 %all-to-all-done = bf16[64,4,1024]{2,0,1:T(8,128)(2,1)S(1)} async-done(((bf16[64,4,1024]{2,0,1:T(8,128)(2,1)}), bf16[64,4,1024]{2,0,1:T(8,128)(2,1)S(1)}, u32[]{:S(2)}, u32[]{:S(2)}) %all-to-all-start) | async-done | bytes 524320 | tf_op jit(solution)/shard_map/all_to_all | solution.py:325
  38.9 1.3 collective-permute-start
  40.2 0.8 collective-permute-done
  41.0 0.0 collective-permute-start.1
  41.0 0.7 fusion.1.order_ref
  41.7 10.9 %reshape.40.spec_ref = f32[2,1024,1024]{2,1,0:T(8,128)} reshape(f32[2,512,2,1024]{3,2,1,0:T(2,128)} %param.21) | data formatting | bytes 16777216 | tf_op jit(solution)/shard_map/reshape | solution.py:297
  52.6 0.0 collective-permute-done.1
  52.7 9.1 %collective-permute-start.2 = (bf16[2,16,1024]{2,1,0:T(8,128)(2,1)S(1)}, bf16[2,16,1024]{2,1,0:T(8,128)(2,1)S(1)}, u32[]{:S(2)}, u32[]{:S(2)}) collective-permute-start(bf16[2,16,1024]{2,1,0:T(8,128)(2,1)S(1)} %maximum_bitcast_fusion.1), channel_id=1, source_target_pairs={{0,1},{1,0},{2,3},{3,2},{4,5},{5,4},{6,7},{7,6},{8,9},{9,8},{10,11... | collective-permute-start | bytes 196616 | tf_op jit(solution)/shard_map/ppermute | solution.py:30
  61.8 8.6 %shard_map.172 = bf16[8,2,2,64,1024]{4,3,2,1,0:T(8,128)(2,1)} custom-call(f32[2,1024,1024]{2,1,0:T(8,128)} %reshape.40.spec_ref, bf16[1024,1024]{1,0:T(8,128)(2,1)S(1)} %fusion.1.order_ref), custom_call_target="tpu_custom_call" | custom-call | flops 4294967296 | bytes 12582912 | tf_op jit(solution)/shard_map/pallas_call | solution.py:284
  70.4 0.0 collective-permute-done.2
  70.4 6.6 %collective-permute-start.3 = (bf16[1,4,64,1024]{3,2,1,0:T(8,128)(2,1)S(1)}, bf16[1,4,64,1024]{3,2,1,0:T(8,128)(2,1)S(1)}, u32[]{:S(2)}, u32[]{:S(2)}) collective-permute-start(bf16[1,4,64,1024]{3,2,1,0:T(8,128)(2,1)S(1)} %bitcast.87), channel_id=1, source_target_pairs={{0,16},{4,20},{8,24},{12,28},{16,0},{20,4},{24,8},{28,12},{1,17},{... | collective-permute-start | bytes 1572872 | tf_op jit(solution)/shard_map/ppermute | solution.py:30
  77.1 8.7 %collective-permute-done.3 = bf16[1,4,64,1024]{3,2,1,0:T(8,128)(2,1)S(1)} collective-permute-done((bf16[1,4,64,1024]{3,2,1,0:T(8,128)(2,1)S(1)}, bf16[1,4,64,1024]{3,2,1,0:T(8,128)(2,1)S(1)}, u32[]{:S(2)}, u32[]{:S(2)}) %collective-permute-start.3) | collective-permute-done | bytes 524320 | tf_op jit(solution)/shard_map/ppermute | solution.py:30
  85.8 0.1 select_bitcast_fusion.5
  85.9 0.1 maximum_bitcast_fusion
  86.0 1.6 collective-permute-start.4
  87.6 4.6 %all-to-all-start.1 = ((bf16[8,2,2,64,1024]{4,3,2,1,0:T(8,128)(2,1)}), bf16[8,2,2,64,1024]{4,3,2,1,0:T(8,128)(2,1)}, u32[]{:S(2)}, u32[]{:S(2)}) async-start(bf16[8,2,2,64,1024]{4,3,2,1,0:T(8,128)(2,1)} %shard_map.172), calls=%async_computation.1 | async-start | bytes 8388608 | tf_op jit(solution)/shard_map/all_to_all | solution.py:304
  92.2 0.0 all-gather.8.cloned.1.call-start
  92.2 19.9 %collective-permute-done.4 = bf16[2,4,64,1024]{3,2,1,0:T(8,128)(2,1)S(1)} collective-permute-done((bf16[2,4,64,1024]{3,2,1,0:T(8,128)(2,1)S(1)}, bf16[2,4,64,1024]{3,2,1,0:T(8,128)(2,1)S(1)}, u32[]{:S(2)}, u32[]{:S(2)}) %collective-permute-start.4) | collective-permute-done | bytes 1048608 | tf_op jit(solution)/shard_map/ppermute | solution.py:30
  112.2 0.1 select_bitcast_fusion.3
  112.3 0.2 pad_maximum_fusion.1
  112.5 0.1 collective-permute-start.5
  112.6 6.3 %fusion.3.refs_5_ = bf16[3,16,512]{2,1,0:T(8,128)(2,1)S(1)} fusion(bf16[3,4,1024,512]{3,2,1,0:T(8,128)(2,1)} %bitcast.80, bf16[4,16,1024]{2,1,0:T(8,128)(2,1)S(1)} %bitcast.90), kind=kOutput, calls=%fused_computation.9 | convolution fusion | flops 201351168 | bytes 12763136 | tf_op jit(solution)/shard_map/ztd,pzdc->ptc/dot_general | solution.py:380
  118.9 0.0 collective-permute-done.5
  118.9 1.9 select_bitcast_fusion.1
  120.8 0.4 pad_maximum_fusion
  121.2 0.7 copy.30
  121.9 2.4 copy.31
  124.4 28.8 %all-to-all-done.1.got_ref = bf16[8,2,2,64,1024]{4,3,2,1,0:T(8,128)(2,1)} async-done(((bf16[8,2,2,64,1024]{4,3,2,1,0:T(8,128)(2,1)}), bf16[8,2,2,64,1024]{4,3,2,1,0:T(8,128)(2,1)}, u32[]{:S(2)}, u32[]{:S(2)}) %all-to-all-start.1) | async-done | bytes 4194336 | tf_op jit(solution)/shard_map/all_to_all | solution.py:304
  153.2 4.0 %shard_map.173.refs_6_.resp_ref = bf16[2,64,72,128]{3,2,1,0:T(8,128)(2,1)S(1)} custom-call(bf16[8,2,2,64,1024]{4,3,2,1,0:T(8,128)(2,1)} %all-to-all-done.1.got_ref), custom_call_target="tpu_custom_call" | custom-call | flops 2097152 | bytes 6291456 | tf_op jit(solution)/shard_map/pallas_call | solution.py:307
  157.2 9.8 %all-gather.4.cloned.1.call-done.refs_0_ = bf16[1024,4096]{1,0:T(8,128)(2,1)} async-done(((bf16[1024,1024]{1,0:T(8,128)(2,1)}), bf16[1024,4096]{1,0:T(8,128)(2,1)}) %all-gather.4.cloned.1.call-update) | async-done | bytes 8388624 | tf_op jit(solution)/shard_map/all_gather | solution.py:369
  167.0 0.0 copy-done.6
  167.0 0.0 copy-start.3
  167.0 0.0 copy-start.4
  167.0 0.0 copy-start.5
  167.0 12.2 %shard_map.177 = (bf16[1024,256]{1,0:T(8,128)(2,1)S(1)}, bf16[256,1024]{1,0:T(8,128)(2,1)S(1)}, bf16[1024,256]{1,0:T(8,128)(2,1)S(1)}) custom-call(bf16[1024,4096]{1,0:T(8,128)(2,1)} %all-gather.4.cloned.1.call-done.refs_0_, bf16[3,4096,512]{2,1,0:T(8,128)(2,1)} %refs_3_.3, bf16[3,4096,512]{2,1,0:T(8,128)(2,1)} %refs_3_.3, bf16[3,4096,512]{2,1,0:T(8,128)(2,1)} %refs_3_.3, ...), custom_call_target="tpu_custom_call" | custom-call | flops 6442450944 | bytes 14680064 | tf_op jit(solution)/shard_map/pallas_call | solution.py:96
  179.2 0.0 copy-start.7
  179.2 13.3 %all_to_all.41.signal_ref = bf16[8,32,1024]{2,1,0:T(8,128)(2,1)S(1)} all-to-all(bf16[8,32,1024]{2,1,0:T(8,128)(2,1)S(1)} %bitcast.77), channel_id=1, replica_groups=mesh['seq'=8,'chan'=4] {'seq'}, dimensions={0} | all-to-all | bytes 1048576 | tf_op jit(solution)/shard_map/all_to_all | solution.py:391
  192.5 0.0 copy-done
  192.5 0.0 copy-done.1
  192.5 0.0 copy-done.2
  192.5 0.0 copy-done.3
  192.5 0.0 copy-done.4
  192.5 3.0 shard_map.178
  195.5 12.2 %all_to_all.42 = bf16[8,32,1024]{2,1,0:T(8,128)(2,1)S(1)} all-to-all(bf16[8,32,1024]{2,1,0:T(8,128)(2,1)S(1)} %shard_map.178), channel_id=1, replica_groups=mesh['seq'=8,'chan'=4] {'seq'}, dimensions={0} | all-to-all | bytes 1048576 | tf_op jit(solution)/shard_map/all_to_all | solution.py:392
  207.7 0.0 copy-done.7
  207.7 1.2 shard_map.179
  208.9 0.0 all-gather.8.cloned.1.call-update
  208.9 0.0 all-gather.6.cloned.1.call-start
  209.0 12.2 %shard_map.174 = (bf16[1024,256]{1,0:T(8,128)(2,1)S(1)}, bf16[256,1024]{1,0:T(8,128)(2,1)S(1)}, bf16[1024,256]{1,0:T(8,128)(2,1)S(1)}) custom-call(bf16[1024,4096]{1,0:T(8,128)(2,1)} %all-gather.4.cloned.1.call-done.refs_0_, bf16[3,4096,512]{2,1,0:T(8,128)(2,1)} %refs_3_.3, bf16[3,4096,512]{2,1,0:T(8,128)(2,1)} %refs_3_.3, bf16[3,4096,512]{2,1,0:T(8,128)(2,1)} %refs_3_.3, ...), custom_call_target="tpu_custom_call" | custom-call | flops 6442450944 | bytes 14680064 | tf_op jit(solution)/shard_map/pallas_call | solution.py:96
  221.2 12.2 %all_to_all.43.signal_ref = bf16[8,32,1024]{2,1,0:T(8,128)(2,1)S(1)} all-to-all(bf16[8,32,1024]{2,1,0:T(8,128)(2,1)S(1)} %bitcast.76), channel_id=1, replica_groups=mesh['seq'=8,'chan'=4] {'seq'}, dimensions={0} | all-to-all | bytes 1048576 | tf_op jit(solution)/shard_map/all_to_all | solution.py:391
  233.3 3.0 shard_map.175
  236.3 12.2 %all_to_all.44 = bf16[8,32,1024]{2,1,0:T(8,128)(2,1)S(1)} all-to-all(bf16[8,32,1024]{2,1,0:T(8,128)(2,1)S(1)} %shard_map.175), channel_id=1, replica_groups=mesh['seq'=8,'chan'=4] {'seq'}, dimensions={0} | all-to-all | bytes 1048576 | tf_op jit(solution)/shard_map/all_to_all | solution.py:392
  248.5 1.2 shard_map.176
  249.7 0.0 all-gather.6.cloned.1.call-update
  249.7 2.8 all-gather.8.cloned.1.call-done.gated_ref
  252.5 6.4 %shard_map.180.refs_0_ = f32[1024,1024]{1,0:T(8,128)} custom-call(bf16[1024,1024]{1,0:T(8,128)(2,1)} %all-gather.8.cloned.1.call-done.gated_ref, bf16[2,1024,1024]{2,1,0:T(8,128)(2,1)} %bitcast.83), custom_call_target="tpu_custom_call" | custom-call | flops 2147483648 | bytes 10485760 | tf_op jit(solution)/shard_map/pallas_call | solution.py:343
  258.9 39.7 %all-gather.6.cloned.1.call-done.gated_ref = bf16[1024,1024]{1,0:T(8,128)(2,1)} async-done(((bf16[1024,256]{1,0:T(8,128)(2,1)}), bf16[1024,1024]{1,0:T(8,128)(2,1)}) %all-gather.6.cloned.1.call-update) | async-done | bytes 2097168 | tf_op jit(solution)/shard_map/all_gather | solution.py:395
  298.6 6.8 %shard_map.181 = bf16[1024,1024]{1,0:T(8,128)(2,1)} custom-call(bf16[1024,1024]{1,0:T(8,128)(2,1)} %all-gather.6.cloned.1.call-done.gated_ref, bf16[2,1024,1024]{2,1,0:T(8,128)(2,1)} %bitcast.84, f32[1024,1024]{1,0:T(8,128)} %shard_map.180.refs_0_), custom_call_target="tpu_custom_call" | custom-call | flops 2147483648 | bytes 10485760 | tf_op jit(solution)/shard_map/pallas_call | solution.py:343
  (12 shorter events, 0.1 us)
Async XLA Ops:
  6.5 160.5 %all-gather.4.cloned.1.call-start = ((), (), s32[]{:S(2)}) async-start(), calls=%async_computation.6 | async-start | bytes 10485760 | tf_op jit(solution)/shard_map/all_gather | solution.py:369
  9.2 29.7 %all-to-all-start = ((bf16[64,4,1024]{2,0,1:T(8,128)(2,1)}), bf16[64,4,1024]{2,0,1:T(8,128)(2,1)S(1)}, u32[]{:S(2)}, u32[]{:S(2)}) async-start(bf16[64,4,1024]{2,0,1:T(8,128)(2,1)} %bitcast.73), calls=%async_computation | async-start | bytes 1048576 | tf_op jit(solution)/shard_map/all_to_all | solution.py:325
  38.9 2.1 collective-permute-start
  41.0 11.7 %collective-permute-start.1 = (bf16[1,16,1024]{2,1,0:T(8,128)(2,1)S(1)}, bf16[1,16,1024]{2,1,0:T(8,128)(2,1)S(1)}, u32[]{:S(2)}, u32[]{:S(2)}) collective-permute-start(bf16[1,16,1024]{2,1,0:T(8,128)(2,1)S(1)} %bitcast.91), channel_id=1, source_target_pairs={{0,2},{1,3},{2,0},{3,1},{4,6},{5,7},{6,4},{7,5},{8,10},{9,11},{10,... | collective-permute-start | bytes 98312 | tf_op jit(solution)/shard_map/ppermute | solution.py:30
  52.7 17.7 %collective-permute-start.2 = (bf16[2,16,1024]{2,1,0:T(8,128)(2,1)S(1)}, bf16[2,16,1024]{2,1,0:T(8,128)(2,1)S(1)}, u32[]{:S(2)}, u32[]{:S(2)}) collective-permute-start(bf16[2,16,1024]{2,1,0:T(8,128)(2,1)S(1)} %maximum_bitcast_fusion.1), channel_id=1, source_target_pairs={{0,1},{1,0},{2,3},{3,2},{4,5},{5,4},{6,7},{7,6},{8,9},{9,8},{10,11... | collective-permute-start | bytes 196616 | tf_op jit(solution)/shard_map/ppermute | solution.py:30
  70.4 15.4 %collective-permute-start.3 = (bf16[1,4,64,1024]{3,2,1,0:T(8,128)(2,1)S(1)}, bf16[1,4,64,1024]{3,2,1,0:T(8,128)(2,1)S(1)}, u32[]{:S(2)}, u32[]{:S(2)}) collective-permute-start(bf16[1,4,64,1024]{3,2,1,0:T(8,128)(2,1)S(1)} %bitcast.87), channel_id=1, source_target_pairs={{0,16},{4,20},{8,24},{12,28},{16,0},{20,4},{24,8},{28,12},{1,17},{... | collective-permute-start | bytes 1572872 | tf_op jit(solution)/shard_map/ppermute | solution.py:30
  86.0 26.2 %collective-permute-start.4 = (bf16[2,4,64,1024]{3,2,1,0:T(8,128)(2,1)S(1)}, bf16[2,4,64,1024]{3,2,1,0:T(8,128)(2,1)S(1)}, u32[]{:S(2)}, u32[]{:S(2)}) collective-permute-start(bf16[2,4,64,1024]{3,2,1,0:T(8,128)(2,1)S(1)} %maximum_bitcast_fusion), channel_id=1, source_target_pairs={{0,8},{4,12},{8,0},{12,4},{16,24},{20,28},{24,16},{28,20},{1,9},{5... | collective-permute-start | bytes 3145736 | tf_op jit(solution)/shard_map/ppermute | solution.py:30
  87.6 65.6 %all-to-all-start.1 = ((bf16[8,2,2,64,1024]{4,3,2,1,0:T(8,128)(2,1)}), bf16[8,2,2,64,1024]{4,3,2,1,0:T(8,128)(2,1)}, u32[]{:S(2)}, u32[]{:S(2)}) async-start(bf16[8,2,2,64,1024]{4,3,2,1,0:T(8,128)(2,1)} %shard_map.172), calls=%async_computation.1 | async-start | bytes 8388608 | tf_op jit(solution)/shard_map/all_to_all | solution.py:304
  92.2 160.4 %all-gather.8.cloned.1.call-start = ((), (), s32[]{:S(2)}) async-start(), calls=%async_computation.8 | async-start | bytes 2621440 | tf_op jit(solution)/shard_map/all_gather | solution.py:395
  112.5 6.4 %collective-permute-start.5 = (bf16[4,4,64,1024]{3,2,1,0:T(8,128)(2,1)S(1)}, bf16[4,4,64,1024]{3,2,1,0:T(8,128)(2,1)}, u32[]{:S(2)}, u32[]{:S(2)}) collective-permute-start(bf16[4,4,64,1024]{3,2,1,0:T(8,128)(2,1)S(1)} %bitcast.86), channel_id=1, source_target_pairs={{0,4},{4,0},{8,12},{12,8},{16,20},{20,16},{24,28},{28,24},{1,5},{5... | collective-permute-start | bytes 6291464 | tf_op jit(solution)/shard_map/ppermute | solution.py:30
  124.4 42.6 %copy-start.6 = (f32[3,3,512]{2,1,0:T(4,128)S(1)}, f32[3,3,512]{2,1,0:T(4,128)}, u32[]{:S(2)}) copy-start(f32[3,3,512]{2,1,0:T(4,128)} %refs_4_.3) | copy-start | bytes 55300
  167.0 25.5 %copy-start = (bf16[256,256]{1,0:T(8,128)(2,1)S(1)}, bf16[256,256]{1,0:T(8,128)(2,1)}, u32[]{:S(2)}) copy-start(bf16[256,256]{1,0:T(8,128)(2,1)} %constant.138.clone.fwd_ref) | copy-start | bytes 393220
  167.0 25.5 %copy-start.1 = (bf16[256,256]{1,0:T(8,128)(2,1)S(1)}, bf16[256,256]{1,0:T(8,128)(2,1)}, u32[]{:S(2)}) copy-start(bf16[256,256]{1,0:T(8,128)(2,1)} %constant.139.clone.bwd_ref) | copy-start | bytes 393220
  167.0 25.5 %copy-start.2 = (bf16[144,64]{1,0:T(8,128)(2,1)S(1)}, bf16[144,64]{1,0:T(8,128)(2,1)}, u32[]{:S(2)}) copy-start(bf16[144,64]{1,0:T(8,128)(2,1)} %constant.134.clone.first_ref) | copy-start | bytes 55300
  167.0 25.5 %copy-start.3 = (f32[72,128]{1,0:T(8,128)S(1)}, f32[72,128]{1,0:T(8,128)}, u32[]{:S(2)}) copy-start(f32[72,128]{1,0:T(8,128)} %constant.136.clone.cos_ref) | copy-start | bytes 110596
  167.0 25.5 %copy-start.4 = (f32[72,128]{1,0:T(8,128)S(1)}, f32[72,128]{1,0:T(8,128)}, u32[]{:S(2)}) copy-start(f32[72,128]{1,0:T(8,128)} %constant.137.clone.sin_ref) | copy-start | bytes 110596
  167.0 25.5 %copy-start.5 = (bf16[64,144]{1,0:T(8,128)(2,1)S(1)}, bf16[64,144]{1,0:T(8,128)(2,1)}, u32[]{:S(2)}) copy-start(bf16[64,144]{1,0:T(8,128)(2,1)} %constant.135.clone.last_ref) | copy-start | bytes 55300
  179.2 28.5 %copy-start.7 = (f32[512]{0:T(512)S(1)}, f32[512]{0:T(512)}, u32[]{:S(2)}) copy-start(f32[512]{0:T(512)} %param.22) | copy-start | bytes 6148
  208.9 89.7 %all-gather.6.cloned.1.call-start = ((), (), s32[]{:S(2)}) async-start(), calls=%async_computation.7 | async-start | bytes 2621440 | tf_op jit(solution)/shard_map/all_gather | solution.py:395
Sparse Core Ops, SparseCore 0:
  8.9 158.0 all-gather.3
  209.0 43.4 all-gather.7
  254.1 44.4 all-gather.5

commit v10 on v9

--- a/solution.py
+++ b/solution.py
@@ -9,7 +9,7 @@
 TAPS = 3
 LANES = 128
 HALO = 16
-DEPTH_STEP = 512
+DEPTH_STEP = 1024
 CHAN_BLOCK = 16
 CHUNKS = 2
 MIB = 1024 * 1024
@@ -77,18 +77,16 @@
                 outs[0][r : r + LANES, :] = made[0].astype(outs[0].dtype)
             if 1 in made:
                 signal = made[1] * made[2]
-                outs[-1][r : r + LANES, :] = signal.astype(outs[-1].dtype)
-                outs[-2][:, r : r + LANES] = signal.T.astype(outs[-2].dtype)
+                outs[-1][:, r : r + LANES] = signal.T.astype(outs[-1].dtype)
 
 
 def project(streams, gathered, in_weight, conv_weight, halo, lo, size, *after):
     rows, depth = gathered.shape
     step = min(DEPTH_STEP, depth // 2)
     at = lo // size
-    flat = jax.ShapeDtypeStruct((rows, size), jnp.bfloat16)
-    shapes = ([flat] if 0 in streams else []) + (
-        [jax.ShapeDtypeStruct((size, rows), jnp.bfloat16), flat] if 1 in streams else []
-    )
+    shapes = [jax.ShapeDtypeStruct((rows, size), jnp.bfloat16)] if 0 in streams else []
+    if 1 in streams:
+        shapes.append(jax.ShapeDtypeStruct((size, rows), jnp.bfloat16))
 
     def weight_of(p):
         return pl.BlockSpec((1, step, size), lambda z: (p, z, at))
@@ -213,29 +211,24 @@
 
 
 def gate_kernel(conv_ref, skip_ref, signal_ref, query_ref, out_ref):
-    conv = conv_ref[...].astype(jnp.float32).T
-    inner = conv + skip_ref[...] * signal_ref[...].astype(jnp.float32)
-    out_ref[...] = (query_ref[...].astype(jnp.float32) * inner).astype(out_ref.dtype)
+    inner = conv_ref[...].astype(jnp.float32) + skip_ref[...] * signal_ref[...].astype(jnp.float32)
+    out_ref[...] = (query_ref[...].astype(jnp.float32) * inner.T).astype(out_ref.dtype)
 
 
 def gate(longconv, skip, lo, signal, query):
     chans, tok_rows = longconv.shape
     first = lo // LANES
+    rows = pl.BlockSpec((LANES, tok_rows), lambda i: (i, 0))
     flat = pl.BlockSpec((tok_rows, LANES), lambda i: (0, i))
     return pl.pallas_call(
         gate_kernel,
         grid=(chans // LANES,),
-        in_specs=[
-            pl.BlockSpec((LANES, tok_rows), lambda i: (i, 0)),
-            pl.BlockSpec((1, LANES), lambda i: (0, first + i)),
-            flat,
-            flat,
-        ],
+        in_specs=[rows, pl.BlockSpec((LANES, 1), lambda i: (first + i, 0)), rows, flat],
         out_specs=flat,
         out_shape=jax.ShapeDtypeStruct((tok_rows, chans), jnp.bfloat16),
         compiler_params=pltpu.CompilerParams(vmem_limit_bytes=8 * MIB),
         cost_estimate=pl.CostEstimate(flops=4 * chans * tok_rows, bytes_accessed=8 * chans * tok_rows, transcendentals=0),
-    )(longconv, skip[None, :], signal, query)
+    )(longconv, skip[:, None], signal, query)
 
 
 def reorder_kernel(spec_ref, order_ref, out_ref):
@@ -337,7 +330,7 @@
 def combine(gathered, weight, chunk, total, dtype):
     tok_rows, depth = gathered.shape
     features = weight.shape[2]
-    tile = min(2 * LANES, features)
+    tile = min(4 * LANES, features)
     block = pl.BlockSpec((tok_rows, tile), lambda i: (0, i))
     given = [] if total is None else [total]
     return pl.pallas_call(
@@ -386,13 +379,13 @@
     total = None
     for j, lo in enumerate(range(0, chans, size)):
         given = (gathered, in_weight, conv_weight, halo, lo, size, response, weight)
-        query_t, signal, signal_t = project((0, 1, 2), *given)
+        query, signal = project((0, 1, 2), *given)
         values = signal.reshape(seq_count, size // seq_count, tok_rows)
         values = lax.all_to_all(values, "seq", split_axis=0, concat_axis=0, tiled=True)
         longconv = lax.all_to_all(
             long_conv(values, response, lo // seq_count), "seq", split_axis=0, concat_axis=0, tiled=True
         ).reshape(size, tok_rows)
-        gated = lax.all_gather(gate(longconv, skip, lo, signal_t, query_t), "chan", axis=1, tiled=True)
+        gated = lax.all_gather(gate(longconv, skip, lo, signal, query), "chan", axis=1, tiled=True)
         dtype = jnp.bfloat16 if lo + size == chans else jnp.float32
         total = combine(gated, weight, j, total, dtype)
     return total

time: 313 us -> 316 us (level)
  blocking collectives: 49.7 us -> 37.6 us
  waiting for transfers between devices: 134 us -> 144 us
  starting transfers between devices: 29.7 us -> 34.3 us
  local copies, waits for them, and re-layouts: 16.8 us -> 20.3 us
  Pallas kernels: 58.5 us -> 55.3 us
    all_to_all x2 -> x1, blocking collectives: 24.3 us -> 12.2 us  [shards(): lax.all_to_all(long_conv(values, response, lo // seq_count), 'seq', split...]
    all_to_all x0 -> x1, waiting for transfers between devices: none -> 8.87 us  [shards(): lax.all_to_all(long_conv(values, response, lo // seq_count), 'seq', split...]
    all_to_all x0 -> x1, starting transfers between devices: none -> 4.15 us  [shards(): lax.all_to_all(long_conv(values, response, lo // seq_count), 'seq', split...]
  transfers between devices with their start and end apart: 11 -> 12, of which waited for: 8 -> 9; matrix products, arithmetic and copies ran while one was open for 9% -> 9% of each run, Pallas kernels for 11% -> 11%
where the time goes in v10:
time: 316 us; the launch traced here: 315 us
  waiting for transfers between devices  144 us (46%)
  Pallas kernels  55.3 us (18%)
  blocking collectives  37.6 us (12%)
  starting transfers between devices  34.3 us (11%)
  local copies, waits for them, and re-layouts  20.3 us (6%)
  between operations  13.5 us (4%)
  matrix products  6.3 us (2%)
  other arithmetic  3.57 us (1%)
    all_gather x2, waiting for transfers between devices, shards(): lax.all_gather(gate(longconv, skip, lo, signal, query), 'chan', axis=1, t...  44.2 us
    all_to_all x1, waiting for transfers between devices, folded_response(): got = lax.all_to_all(sent, 'seq', split_axis=0, concat_axis=0, tiled=True)  28.8 us
    ppermute x5, waiting for transfers between devices, gather_by_doubling(): other = lax.ppermute(held, axis, [(i, i ^ bit) for i in range(size)])  28.5 us
    all_to_all x2, blocking collectives, shards(): lax.all_to_all(values, 'seq', split_axis=0, concat_axis=0, tiled=True)  25.4 us
    all_to_all x1, waiting for transfers between devices, feature_rows(): own = lax.all_to_all(own, 'chan', split_axis=1, concat_axis=0, tiled=True)  22.6 us
    pallas_call x2, Pallas kernels, project(): pl.pallas_call(lambda *refs: project_kernel(streams, len(after), *refs),...  21.5 us
    ppermute x5, starting transfers between devices, gather_by_doubling(): other = lax.ppermute(held, axis, [(i, i ^ bit) for i in range(size)])  17.5 us
    all_to_all x1, blocking collectives, shards(): lax.all_to_all(long_conv(values, response, lo // seq_count), 'seq', split...  12.2 us
  transfers between devices with their start and end apart: 12, of which 9 were waited for; matrix products, arithmetic and copies ran while one was open for 9% of the time, Pallas kernels for 11%

profile of v10, /device:TPU:0, one launch (start us, length us, event | category | flops | bytes accessed | tf_op | source)
XLA Modules:
  0.0 315.1 jit_solution(2073270091540402387)
XLA Ops:
  6.5 0.7 all-gather.4.cloned.1.call-update
  7.3 1.1 constant_dynamic-slice_fusion
  8.3 0.8 copy.41
  9.2 6.3 %all-to-all-start = ((bf16[64,4,1024]{2,0,1:T(8,128)(2,1)}), bf16[64,4,1024]{2,0,1:T(8,128)(2,1)S(1)}, u32[]{:S(2)}, u32[]{:S(2)}) async-start(bf16[64,4,1024]{2,0,1:T(8,128)(2,1)} %bitcast.73), calls=%async_computation | async-start | bytes 1048576 | tf_op jit(solution)/shard_map/all_to_all | solution.py:318
  15.5 0.8 slice.3
  16.3 22.6 %all-to-all-done = bf16[64,4,1024]{2,0,1:T(8,128)(2,1)S(1)} async-done(((bf16[64,4,1024]{2,0,1:T(8,128)(2,1)}), bf16[64,4,1024]{2,0,1:T(8,128)(2,1)S(1)}, u32[]{:S(2)}, u32[]{:S(2)}) %all-to-all-start) | async-done | bytes 524320 | tf_op jit(solution)/shard_map/all_to_all | solution.py:318
  38.9 1.3 collective-permute-start
  40.2 0.8 collective-permute-done
  41.0 0.0 collective-permute-start.1
  41.0 0.7 fusion.1.order_ref
  41.7 10.9 %reshape.40.spec_ref = f32[2,1024,1024]{2,1,0:T(8,128)} reshape(f32[2,512,2,1024]{3,2,1,0:T(2,128)} %param.21) | data formatting | bytes 16777216 | tf_op jit(solution)/shard_map/reshape | solution.py:290
  52.7 0.0 collective-permute-done.1
  52.7 9.1 %collective-permute-start.2 = (bf16[2,16,1024]{2,1,0:T(8,128)(2,1)S(1)}, bf16[2,16,1024]{2,1,0:T(8,128)(2,1)S(1)}, u32[]{:S(2)}, u32[]{:S(2)}) collective-permute-start(bf16[2,16,1024]{2,1,0:T(8,128)(2,1)S(1)} %maximum_bitcast_fusion.1), channel_id=1, source_target_pairs={{0,1},{1,0},{2,3},{3,2},{4,5},{5,4},{6,7},{7,6},{8,9},{9,8},{10,11... | collective-permute-start | bytes 196616 | tf_op jit(solution)/shard_map/ppermute | solution.py:30
  61.8 8.5 %shard_map.172 = bf16[8,2,2,64,1024]{4,3,2,1,0:T(8,128)(2,1)} custom-call(f32[2,1024,1024]{2,1,0:T(8,128)} %reshape.40.spec_ref, bf16[1024,1024]{1,0:T(8,128)(2,1)S(1)} %fusion.1.order_ref), custom_call_target="tpu_custom_call" | custom-call | flops 4294967296 | bytes 12582912 | tf_op jit(solution)/shard_map/pallas_call | solution.py:277
  70.4 0.0 collective-permute-done.2
  70.4 6.7 %collective-permute-start.3 = (bf16[1,4,64,1024]{3,2,1,0:T(8,128)(2,1)S(1)}, bf16[1,4,64,1024]{3,2,1,0:T(8,128)(2,1)S(1)}, u32[]{:S(2)}, u32[]{:S(2)}) collective-permute-start(bf16[1,4,64,1024]{3,2,1,0:T(8,128)(2,1)S(1)} %bitcast.84), channel_id=1, source_target_pairs={{0,16},{4,20},{8,24},{12,28},{16,0},{20,4},{24,8},{28,12},{1,17},{... | collective-permute-start | bytes 1572872 | tf_op jit(solution)/shard_map/ppermute | solution.py:30
  77.1 8.7 %collective-permute-done.3 = bf16[1,4,64,1024]{3,2,1,0:T(8,128)(2,1)S(1)} collective-permute-done((bf16[1,4,64,1024]{3,2,1,0:T(8,128)(2,1)S(1)}, bf16[1,4,64,1024]{3,2,1,0:T(8,128)(2,1)S(1)}, u32[]{:S(2)}, u32[]{:S(2)}) %collective-permute-start.3) | collective-permute-done | bytes 524320 | tf_op jit(solution)/shard_map/ppermute | solution.py:30
  85.8 0.1 select_bitcast_fusion.5
  85.9 0.1 maximum_bitcast_fusion
  86.0 1.6 collective-permute-start.4
  87.5 4.8 %all-to-all-start.1 = ((bf16[8,2,2,64,1024]{4,3,2,1,0:T(8,128)(2,1)}), bf16[8,2,2,64,1024]{4,3,2,1,0:T(8,128)(2,1)}, u32[]{:S(2)}, u32[]{:S(2)}) async-start(bf16[8,2,2,64,1024]{4,3,2,1,0:T(8,128)(2,1)} %shard_map.172), calls=%async_computation.1 | async-start | bytes 8388608 | tf_op jit(solution)/shard_map/all_to_all | solution.py:297
  92.3 19.8 %collective-permute-done.4 = bf16[2,4,64,1024]{3,2,1,0:T(8,128)(2,1)S(1)} collective-permute-done((bf16[2,4,64,1024]{3,2,1,0:T(8,128)(2,1)S(1)}, bf16[2,4,64,1024]{3,2,1,0:T(8,128)(2,1)S(1)}, u32[]{:S(2)}, u32[]{:S(2)}) %collective-permute-start.4) | collective-permute-done | bytes 1048608 | tf_op jit(solution)/shard_map/ppermute | solution.py:30
  112.1 0.1 select_bitcast_fusion.3
  112.3 0.2 pad_maximum_fusion.1
  112.5 0.1 collective-permute-start.5
  112.6 6.3 %fusion.3.refs_5_ = bf16[3,16,512]{2,1,0:T(8,128)(2,1)S(1)} fusion(bf16[3,4,1024,512]{3,2,1,0:T(8,128)(2,1)} %bitcast.77, bf16[4,16,1024]{2,1,0:T(8,128)(2,1)S(1)} %bitcast.87), kind=kOutput, calls=%fused_computation.9 | convolution fusion | flops 201351168 | bytes 12763136 | tf_op jit(solution)/shard_map/ztd,pzdc->ptc/dot_general | solution.py:373
  118.9 0.0 collective-permute-done.5
  118.9 1.9 select_bitcast_fusion.1
  120.8 0.4 pad_maximum_fusion
  121.2 0.7 copy.34
  121.9 2.5 copy.35
  124.4 28.8 %all-to-all-done.1.got_ref = bf16[8,2,2,64,1024]{4,3,2,1,0:T(8,128)(2,1)} async-done(((bf16[8,2,2,64,1024]{4,3,2,1,0:T(8,128)(2,1)}), bf16[8,2,2,64,1024]{4,3,2,1,0:T(8,128)(2,1)}, u32[]{:S(2)}, u32[]{:S(2)}) %all-to-all-start.1) | async-done | bytes 4194336 | tf_op jit(solution)/shard_map/all_to_all | solution.py:297
  153.1 4.0 %shard_map.173.refs_6_.resp_ref = bf16[2,64,72,128]{3,2,1,0:T(8,128)(2,1)S(1)} custom-call(bf16[8,2,2,64,1024]{4,3,2,1,0:T(8,128)(2,1)} %all-to-all-done.1.got_ref), custom_call_target="tpu_custom_call" | custom-call | flops 2097152 | bytes 6291456 | tf_op jit(solution)/shard_map/pallas_call | solution.py:300
  157.2 9.8 %all-gather.4.cloned.1.call-done.refs_0_ = bf16[1024,4096]{1,0:T(8,128)(2,1)} async-done(((bf16[1024,1024]{1,0:T(8,128)(2,1)}), bf16[1024,4096]{1,0:T(8,128)(2,1)}) %all-gather.4.cloned.1.call-update) | async-done | bytes 8388624 | tf_op jit(solution)/shard_map/all_gather | solution.py:362
  167.0 0.0 copy-start.6
  167.0 0.0 copy-start.7
  167.0 0.0 copy-start.9
  167.0 10.7 %shard_map.177 = (bf16[1024,256]{1,0:T(8,128)(2,1)S(1)}, bf16[256,1024]{1,0:T(8,128)(2,1)S(1)}) custom-call(bf16[1024,4096]{1,0:T(8,128)(2,1)} %all-gather.4.cloned.1.call-done.refs_0_, bf16[3,4096,512]{2,1,0:T(8,128)(2,1)} %refs_3_.3, bf16[3,4096,512]{2,1,0:T(8,128)(2,1)} %refs_3_.3, bf16[3,4096,512]{2,1,0:T(8,128)(2,1)} %refs_3_.3, ...), custom_call_target="tpu_custom_call" | custom-call | flops 6442450944 | bytes 14680064 | tf_op jit(solution)/shard_map/pallas_call | solution.py:94
  177.8 0.0 copy-start.3
  177.8 0.8 copy-done.3
  178.6 13.3 %all_to_all.41.signal_ref = bf16[8,32,1024]{2,1,0:T(8,128)(2,1)S(1)} all-to-all(bf16[8,32,1024]{2,1,0:T(8,128)(2,1)S(1)} %bitcast.74), channel_id=1, replica_groups=mesh['seq'=8,'chan'=4] {'seq'}, dimensions={0} | all-to-all | bytes 1048576 | tf_op jit(solution)/shard_map/all_to_all | solution.py:384
  191.9 2.9 shard_map.178
  194.8 0.0 copy-start
  194.8 0.8 copy-done
  195.6 4.2 %all-to-all-start.5 = ((bf16[8,32,1024]{2,1,0:T(8,128)(2,1)}), bf16[8,32,1024]{2,1,0:T(8,128)(2,1)}, u32[]{:S(2)}, u32[]{:S(2)}) async-start(bf16[8,32,1024]{2,1,0:T(8,128)(2,1)} %copy-done), calls=%async_computation.5 | async-start | bytes 1048576 | tf_op jit(solution)/shard_map/all_to_all | solution.py:385
  199.8 0.0 all-gather.8.cloned.1.call-start
  199.8 0.8 copy.36.skip_ref
  200.7 8.9 %all-to-all-done.5 = bf16[8,32,1024]{2,1,0:T(8,128)(2,1)} async-done(((bf16[8,32,1024]{2,1,0:T(8,128)(2,1)}), bf16[8,32,1024]{2,1,0:T(8,128)(2,1)}, u32[]{:S(2)}, u32[]{:S(2)}) %all-to-all-start.5) | async-done | bytes 524320 | tf_op jit(solution)/shard_map/all_to_all | solution.py:385
  209.5 1.0 copy-done.4
  210.6 2.2 shard_map.179
  212.8 0.0 all-gather.8.cloned.1.call-update
  212.8 0.3 all-gather.6.cloned.1.call-start
  213.1 0.0 copy-start.8
  213.1 0.0 copy-start.10
  213.1 10.7 %shard_map.174 = (bf16[1024,256]{1,0:T(8,128)(2,1)S(1)}, bf16[256,1024]{1,0:T(8,128)(2,1)S(1)}) custom-call(bf16[1024,4096]{1,0:T(8,128)(2,1)} %all-gather.4.cloned.1.call-done.refs_0_, bf16[3,4096,512]{2,1,0:T(8,128)(2,1)} %refs_3_.3, bf16[3,4096,512]{2,1,0:T(8,128)(2,1)} %refs_3_.3, bf16[3,4096,512]{2,1,0:T(8,128)(2,1)} %refs_3_.3, ...), custom_call_target="tpu_custom_call" | custom-call | flops 6442450944 | bytes 14680064 | tf_op jit(solution)/shard_map/pallas_call | solution.py:94
  223.9 12.2 %all_to_all.42.signal_ref = bf16[8,32,1024]{2,1,0:T(8,128)(2,1)S(1)} all-to-all(bf16[8,32,1024]{2,1,0:T(8,128)(2,1)S(1)} %bitcast.75), channel_id=1, replica_groups=mesh['seq'=8,'chan'=4] {'seq'}, dimensions={0} | all-to-all | bytes 1048576 | tf_op jit(solution)/shard_map/all_to_all | solution.py:384
  236.0 2.9 shard_map.175
  239.0 12.2 %all_to_all.43 = bf16[8,32,1024]{2,1,0:T(8,128)(2,1)S(1)} all-to-all(bf16[8,32,1024]{2,1,0:T(8,128)(2,1)S(1)} %shard_map.175), channel_id=1, replica_groups=mesh['seq'=8,'chan'=4] {'seq'}, dimensions={0} | all-to-all | bytes 1048576 | tf_op jit(solution)/shard_map/all_to_all | solution.py:385
  251.1 1.4 shard_map.176
  252.5 0.0 all-gather.6.cloned.1.call-update
  252.5 3.9 %all-gather.8.cloned.1.call-done.gated_ref = bf16[1024,1024]{1,0:T(8,128)(2,1)} async-done(((bf16[1024,256]{1,0:T(8,128)(2,1)}), bf16[1024,1024]{1,0:T(8,128)(2,1)}) %all-gather.8.cloned.1.call-update) | async-done | bytes 2097168 | tf_op jit(solution)/shard_map/all_gather | solution.py:388
  256.5 5.8 %shard_map.180.refs_0_ = f32[1024,1024]{1,0:T(8,128)} custom-call(bf16[1024,1024]{1,0:T(8,128)(2,1)} %all-gather.8.cloned.1.call-done.gated_ref, bf16[2,1024,1024]{2,1,0:T(8,128)(2,1)} %bitcast.80), custom_call_target="tpu_custom_call" | custom-call | flops 2147483648 | bytes 10485760 | tf_op jit(solution)/shard_map/pallas_call | solution.py:336
  262.3 40.3 %all-gather.6.cloned.1.call-done.gated_ref = bf16[1024,1024]{1,0:T(8,128)(2,1)} async-done(((bf16[1024,256]{1,0:T(8,128)(2,1)}), bf16[1024,1024]{1,0:T(8,128)(2,1)}) %all-gather.6.cloned.1.call-update) | async-done | bytes 2097168 | tf_op jit(solution)/shard_map/all_gather | solution.py:388
  302.5 6.0 %shard_map.181 = bf16[1024,1024]{1,0:T(8,128)(2,1)} custom-call(bf16[1024,1024]{1,0:T(8,128)(2,1)} %all-gather.6.cloned.1.call-done.gated_ref, bf16[2,1024,1024]{2,1,0:T(8,128)(2,1)} %bitcast.81, f32[1024,1024]{1,0:T(8,128)} %shard_map.180.refs_0_), custom_call_target="tpu_custom_call" | custom-call | flops 2147483648 | bytes 10485760 | tf_op jit(solution)/shard_map/pallas_call | solution.py:336
  (22 shorter events, 0.1 us)
Async XLA Ops:
  6.5 160.5 %all-gather.4.cloned.1.call-start = ((), (), s32[]{:S(2)}) async-start(), calls=%async_computation.6 | async-start | bytes 10485760 | tf_op jit(solution)/shard_map/all_gather | solution.py:362
  9.2 29.7 %all-to-all-start = ((bf16[64,4,1024]{2,0,1:T(8,128)(2,1)}), bf16[64,4,1024]{2,0,1:T(8,128)(2,1)S(1)}, u32[]{:S(2)}, u32[]{:S(2)}) async-start(bf16[64,4,1024]{2,0,1:T(8,128)(2,1)} %bitcast.73), calls=%async_computation | async-start | bytes 1048576 | tf_op jit(solution)/shard_map/all_to_all | solution.py:318
  38.9 2.1 collective-permute-start
  41.0 11.7 %collective-permute-start.1 = (bf16[1,16,1024]{2,1,0:T(8,128)(2,1)S(1)}, bf16[1,16,1024]{2,1,0:T(8,128)(2,1)S(1)}, u32[]{:S(2)}, u32[]{:S(2)}) collective-permute-start(bf16[1,16,1024]{2,1,0:T(8,128)(2,1)S(1)} %bitcast.88), channel_id=1, source_target_pairs={{0,2},{1,3},{2,0},{3,1},{4,6},{5,7},{6,4},{7,5},{8,10},{9,11},{10,... | collective-permute-start | bytes 98312 | tf_op jit(solution)/shard_map/ppermute | solution.py:30
  52.7 17.7 %collective-permute-start.2 = (bf16[2,16,1024]{2,1,0:T(8,128)(2,1)S(1)}, bf16[2,16,1024]{2,1,0:T(8,128)(2,1)S(1)}, u32[]{:S(2)}, u32[]{:S(2)}) collective-permute-start(bf16[2,16,1024]{2,1,0:T(8,128)(2,1)S(1)} %maximum_bitcast_fusion.1), channel_id=1, source_target_pairs={{0,1},{1,0},{2,3},{3,2},{4,5},{5,4},{6,7},{7,6},{8,9},{9,8},{10,11... | collective-permute-start | bytes 196616 | tf_op jit(solution)/shard_map/ppermute | solution.py:30
  70.4 15.4 %collective-permute-start.3 = (bf16[1,4,64,1024]{3,2,1,0:T(8,128)(2,1)S(1)}, bf16[1,4,64,1024]{3,2,1,0:T(8,128)(2,1)S(1)}, u32[]{:S(2)}, u32[]{:S(2)}) collective-permute-start(bf16[1,4,64,1024]{3,2,1,0:T(8,128)(2,1)S(1)} %bitcast.84), channel_id=1, source_target_pairs={{0,16},{4,20},{8,24},{12,28},{16,0},{20,4},{24,8},{28,12},{1,17},{... | collective-permute-start | bytes 1572872 | tf_op jit(solution)/shard_map/ppermute | solution.py:30
  86.0 26.2 %collective-permute-start.4 = (bf16[2,4,64,1024]{3,2,1,0:T(8,128)(2,1)S(1)}, bf16[2,4,64,1024]{3,2,1,0:T(8,128)(2,1)S(1)}, u32[]{:S(2)}, u32[]{:S(2)}) collective-permute-start(bf16[2,4,64,1024]{3,2,1,0:T(8,128)(2,1)S(1)} %maximum_bitcast_fusion), channel_id=1, source_target_pairs={{0,8},{4,12},{8,0},{12,4},{16,24},{20,28},{24,16},{28,20},{1,9},{5... | collective-permute-start | bytes 3145736 | tf_op jit(solution)/shard_map/ppermute | solution.py:30
  87.5 65.6 %all-to-all-start.1 = ((bf16[8,2,2,64,1024]{4,3,2,1,0:T(8,128)(2,1)}), bf16[8,2,2,64,1024]{4,3,2,1,0:T(8,128)(2,1)}, u32[]{:S(2)}, u32[]{:S(2)}) async-start(bf16[8,2,2,64,1024]{4,3,2,1,0:T(8,128)(2,1)} %shard_map.172), calls=%async_computation.1 | async-start | bytes 8388608 | tf_op jit(solution)/shard_map/all_to_all | solution.py:297
  112.5 6.4 %collective-permute-start.5 = (bf16[4,4,64,1024]{3,2,1,0:T(8,128)(2,1)S(1)}, bf16[4,4,64,1024]{3,2,1,0:T(8,128)(2,1)}, u32[]{:S(2)}, u32[]{:S(2)}) collective-permute-start(bf16[4,4,64,1024]{3,2,1,0:T(8,128)(2,1)S(1)} %bitcast.83), channel_id=1, source_target_pairs={{0,4},{4,0},{8,12},{12,8},{16,20},{20,16},{24,28},{28,24},{1,5},{5... | collective-permute-start | bytes 6291464 | tf_op jit(solution)/shard_map/ppermute | solution.py:30
  124.4 42.6 %copy-start.11 = (f32[3,3,512]{2,1,0:T(4,128)S(1)}, f32[3,3,512]{2,1,0:T(4,128)}, u32[]{:S(2)}) copy-start(f32[3,3,512]{2,1,0:T(4,128)} %refs_4_.3) | copy-start | bytes 55300
  167.0 24.8 %copy-start.1 = (bf16[256,256]{1,0:T(8,128)(2,1)S(1)}, bf16[256,256]{1,0:T(8,128)(2,1)}, u32[]{:S(2)}) copy-start(bf16[256,256]{1,0:T(8,128)(2,1)} %constant.138.clone.fwd_ref) | copy-start | bytes 393220
  167.0 24.8 %copy-start.2 = (bf16[256,256]{1,0:T(8,128)(2,1)S(1)}, bf16[256,256]{1,0:T(8,128)(2,1)}, u32[]{:S(2)}) copy-start(bf16[256,256]{1,0:T(8,128)(2,1)} %constant.139.clone.bwd_ref) | copy-start | bytes 393220
  167.0 24.9 %copy-start.5 = (bf16[144,64]{1,0:T(8,128)(2,1)S(1)}, bf16[144,64]{1,0:T(8,128)(2,1)}, u32[]{:S(2)}) copy-start(bf16[144,64]{1,0:T(8,128)(2,1)} %constant.134.clone.first_ref) | copy-start | bytes 55300
  167.0 24.9 %copy-start.6 = (f32[72,128]{1,0:T(8,128)S(1)}, f32[72,128]{1,0:T(8,128)}, u32[]{:S(2)}) copy-start(f32[72,128]{1,0:T(8,128)} %constant.136.clone.cos_ref) | copy-start | bytes 110596
  167.0 24.8 %copy-start.7 = (f32[72,128]{1,0:T(8,128)S(1)}, f32[72,128]{1,0:T(8,128)}, u32[]{:S(2)}) copy-start(f32[72,128]{1,0:T(8,128)} %constant.137.clone.sin_ref) | copy-start | bytes 110596
  167.0 24.8 %copy-start.9 = (bf16[64,144]{1,0:T(8,128)(2,1)S(1)}, bf16[64,144]{1,0:T(8,128)(2,1)}, u32[]{:S(2)}) copy-start(bf16[64,144]{1,0:T(8,128)(2,1)} %constant.135.clone.last_ref) | copy-start | bytes 55300
  177.8 0.8 copy-start.3
  194.8 0.8 copy-start
  195.6 13.9 %all-to-all-start.5 = ((bf16[8,32,1024]{2,1,0:T(8,128)(2,1)}), bf16[8,32,1024]{2,1,0:T(8,128)(2,1)}, u32[]{:S(2)}, u32[]{:S(2)}) async-start(bf16[8,32,1024]{2,1,0:T(8,128)(2,1)} %copy-done), calls=%async_computation.5 | async-start | bytes 1048576 | tf_op jit(solution)/shard_map/all_to_all | solution.py:385
  199.8 56.7 %all-gather.8.cloned.1.call-start = ((), (), s32[]{:S(2)}) async-start(), calls=%async_computation.8 | async-start | bytes 2621440 | tf_op jit(solution)/shard_map/all_gather | solution.py:388
  209.5 1.0 copy-start.4
  212.8 89.7 %all-gather.6.cloned.1.call-start = ((), (), s32[]{:S(2)}) async-start(), calls=%async_computation.7 | async-start | bytes 2621440 | tf_op jit(solution)/shard_map/all_gather | solution.py:388
  213.1 22.9 %copy-start.8 = (f32[72,128]{1,0:T(8,128)S(1)}, f32[72,128]{1,0:T(8,128)}, u32[]{:S(2)}) copy-start(f32[72,128]{1,0:T(8,128)} %constant.137.clone.sin_ref) | copy-start | bytes 110596
  213.1 22.9 %copy-start.10 = (bf16[64,144]{1,0:T(8,128)(2,1)S(1)}, bf16[64,144]{1,0:T(8,128)(2,1)}, u32[]{:S(2)}) copy-start(bf16[64,144]{1,0:T(8,128)(2,1)} %constant.135.clone.last_ref) | copy-start | bytes 55300
Sparse Core Ops, SparseCore 0:
  8.9 158.0 all-gather.3
  213.0 43.4 all-gather.7
  258.0 44.4 all-gather.5

commit v11 on v9

--- a/solution.py
+++ b/solution.py
@@ -9,7 +9,6 @@
 TAPS = 3
 LANES = 128
 HALO = 16
-DEPTH_STEP = 512
 CHAN_BLOCK = 16
 CHUNKS = 2
 MIB = 1024 * 1024
@@ -49,7 +48,7 @@
     rows = acc.shape[1] - HALO
 
     def part(w_ref):
-        return jnp.dot(tok_ref[...], w_ref[0], preferred_element_type=jnp.float32)
+        return jnp.dot(tok_ref[0], w_ref[0], preferred_element_type=jnp.float32)
 
     @pl.when(step == 0)
     def _():
@@ -82,8 +81,8 @@
 
 
 def project(streams, gathered, in_weight, conv_weight, halo, lo, size, *after):
-    rows, depth = gathered.shape
-    step = min(DEPTH_STEP, depth // 2)
+    count, rows, step = gathered.shape
+    depth = count * step
     at = lo // size
     flat = jax.ShapeDtypeStruct((rows, size), jnp.bfloat16)
     shapes = ([flat] if 0 in streams else []) + (
@@ -95,9 +94,9 @@
 
     return pl.pallas_call(
         lambda *refs: project_kernel(streams, len(after), *refs),
-        grid=(depth // step,),
+        grid=(count,),
         in_specs=[
-            pl.BlockSpec((rows, step), lambda z: (0, z)),
+            pl.BlockSpec((1, rows, step), lambda z: (z, 0, 0)),
             *[weight_of(p) for p in streams],
             pl.BlockSpec((TAPS, 3, size), lambda z: (0, 0, at)),
             pl.BlockSpec((3, HALO, size), lambda z: (0, 0, at)),
@@ -328,23 +327,25 @@
 
 def combine_kernel(gated_ref, w_ref, *refs):
     out_ref = refs[-1]
-    total = jnp.dot(gated_ref[...], w_ref[0], preferred_element_type=jnp.float32)
+    gated = jnp.concatenate([gated_ref[z] for z in range(gated_ref.shape[0])], axis=1)
+    total = jnp.dot(gated, w_ref[0], preferred_element_type=jnp.float32)
     if len(refs) == 2:
         total = total + refs[0][...]
     out_ref[...] = total.astype(out_ref.dtype)
 
 
 def combine(gathered, weight, chunk, total, dtype):
-    tok_rows, depth = gathered.shape
+    count, tok_rows, size = gathered.shape
+    depth = count * size
     features = weight.shape[2]
-    tile = min(2 * LANES, features)
+    tile = min(4 * LANES, features)
     block = pl.BlockSpec((tok_rows, tile), lambda i: (0, i))
     given = [] if total is None else [total]
     return pl.pallas_call(
         combine_kernel,
         grid=(features // tile,),
         in_specs=[
-            pl.BlockSpec((tok_rows, depth), lambda i: (0, 0)),
+            pl.BlockSpec((count, tok_rows, size), lambda i: (0, 0, 0)),
             pl.BlockSpec((1, depth, tile), lambda i: (chunk, 0, i)),
             *[block for _ in given],
         ],
@@ -366,7 +367,7 @@
     chans = in_weight.shape[2]
     chunks = chunk_count(chans, seq_count)
     size = chans // chunks
-    gathered = lax.all_gather(tokens, "chan", axis=1, tiled=True)
+    gathered = lax.all_gather(tokens, "chan")
     weight = feature_rows(out_weight, seq_count)
     last_rows = tokens[tok_rows - HALO :]
     weight, last_rows = lax.optimization_barrier((weight, last_rows))
@@ -392,7 +393,7 @@
         longconv = lax.all_to_all(
             long_conv(values, response, lo // seq_count), "seq", split_axis=0, concat_axis=0, tiled=True
         ).reshape(size, tok_rows)
-        gated = lax.all_gather(gate(longconv, skip, lo, signal_t, query_t), "chan", axis=1, tiled=True)
+        gated = lax.all_gather(gate(longconv, skip, lo, signal_t, query_t), "chan")
         dtype = jnp.bfloat16 if lo + size == chans else jnp.float32
         total = combine(gated, weight, j, total, dtype)
     return total

time: 313 us -> 311 us (level)
  Pallas kernels: 58.5 us -> 54.3 us
where the time goes in v11:
time: 311 us; the launch traced here: 310 us
  waiting for transfers between devices  135 us (43%)
  Pallas kernels  54.3 us (17%)
  blocking collectives  49.7 us (16%)
  starting transfers between devices  30.1 us (10%)
  local copies, waits for them, and re-layouts  16.8 us (5%)
  between operations  13.4 us (4%)
  matrix products  6.3 us (2%)
  other arithmetic  3.57 us (1%)
    all_gather x2, waiting for transfers between devices, shards(): gated = lax.all_gather(gate(longconv, skip, lo, signal_t, query_t), 'chan')  44.3 us
    all_to_all x1, waiting for transfers between devices, folded_response(): got = lax.all_to_all(sent, 'seq', split_axis=0, concat_axis=0, tiled=True)  28.8 us
    ppermute x5, waiting for transfers between devices, gather_by_doubling(): other = lax.ppermute(held, axis, [(i, i ^ bit) for i in range(size)])  28.5 us
    all_to_all x2, blocking collectives, shards(): lax.all_to_all(values, 'seq', split_axis=0, concat_axis=0, tiled=True)  25.4 us
    all_to_all x2, blocking collectives, shards(): lax.all_to_all(long_conv(values, response, lo // seq_count), 'seq', split...  24.3 us
    all_to_all x1, waiting for transfers between devices, feature_rows(): own = lax.all_to_all(own, 'chan', split_axis=1, concat_axis=0, tiled=True)  22.6 us
    pallas_call x2, Pallas kernels, project(): pl.pallas_call(lambda *refs: project_kernel(streams, len(after), *refs),...  21.5 us
    ppermute x5, starting transfers between devices, gather_by_doubling(): other = lax.ppermute(held, axis, [(i, i ^ bit) for i in range(size)])  17.4 us
  transfers between devices with their start and end apart: 11, of which 8 were waited for; matrix products, arithmetic and copies ran while one was open for 9% of the time, Pallas kernels for 11%

profile of v11, /device:TPU:0, one launch (start us, length us, event | category | flops | bytes accessed | tf_op | source)
XLA Modules:
  0.0 309.7 jit_solution(13289687335572030168)
XLA Ops:
  6.5 0.0 all-gather.7.cloned.1.call-start
  6.5 0.7 all-gather.7.cloned.1.call-update
  7.3 1.1 constant_dynamic-slice_fusion
  8.3 0.8 copy.35
  9.2 6.3 %all-to-all-start = ((bf16[64,4,1024]{2,0,1:T(8,128)(2,1)}), bf16[64,4,1024]{2,0,1:T(8,128)(2,1)S(1)}, u32[]{:S(2)}, u32[]{:S(2)}) async-start(bf16[64,4,1024]{2,0,1:T(8,128)(2,1)} %bitcast.76), calls=%async_computation | async-start | bytes 1048576 | tf_op jit(solution)/shard_map/all_to_all | solution.py:324
  15.5 0.8 slice.3
  16.3 22.6 %all-to-all-done = bf16[64,4,1024]{2,0,1:T(8,128)(2,1)S(1)} async-done(((bf16[64,4,1024]{2,0,1:T(8,128)(2,1)}), bf16[64,4,1024]{2,0,1:T(8,128)(2,1)S(1)}, u32[]{:S(2)}, u32[]{:S(2)}) %all-to-all-start) | async-done | bytes 524320 | tf_op jit(solution)/shard_map/all_to_all | solution.py:324
  38.9 1.3 collective-permute-start
  40.2 0.8 collective-permute-done
  41.0 0.0 collective-permute-start.1
  41.0 0.7 fusion.1.order_ref
  41.7 10.9 %reshape.40.spec_ref = f32[2,1024,1024]{2,1,0:T(8,128)} reshape(f32[2,512,2,1024]{3,2,1,0:T(2,128)} %param.21) | data formatting | bytes 16777216 | tf_op jit(solution)/shard_map/reshape | solution.py:296
  52.6 0.0 collective-permute-done.1
  52.7 9.1 %collective-permute-start.2 = (bf16[2,16,1024]{2,1,0:T(8,128)(2,1)S(1)}, bf16[2,16,1024]{2,1,0:T(8,128)(2,1)S(1)}, u32[]{:S(2)}, u32[]{:S(2)}) collective-permute-start(bf16[2,16,1024]{2,1,0:T(8,128)(2,1)S(1)} %maximum_bitcast_fusion.1), channel_id=1, source_target_pairs={{0,1},{1,0},{2,3},{3,2},{4,5},{5,4},{6,7},{7,6},{8,9},{9,8},{10,11... | collective-permute-start | bytes 196616 | tf_op jit(solution)/shard_map/ppermute | solution.py:29
  61.8 8.6 %shard_map.172 = bf16[8,2,2,64,1024]{4,3,2,1,0:T(8,128)(2,1)} custom-call(f32[2,1024,1024]{2,1,0:T(8,128)} %reshape.40.spec_ref, bf16[1024,1024]{1,0:T(8,128)(2,1)S(1)} %fusion.1.order_ref), custom_call_target="tpu_custom_call" | custom-call | flops 4294967296 | bytes 12582912 | tf_op jit(solution)/shard_map/pallas_call | solution.py:283
  70.4 0.0 collective-permute-done.2
  70.4 6.6 %collective-permute-start.3 = (bf16[1,4,64,1024]{3,2,1,0:T(8,128)(2,1)S(1)}, bf16[1,4,64,1024]{3,2,1,0:T(8,128)(2,1)S(1)}, u32[]{:S(2)}, u32[]{:S(2)}) collective-permute-start(bf16[1,4,64,1024]{3,2,1,0:T(8,128)(2,1)S(1)} %bitcast.93), channel_id=1, source_target_pairs={{0,16},{4,20},{8,24},{12,28},{16,0},{20,4},{24,8},{28,12},{1,17},{... | collective-permute-start | bytes 1572872 | tf_op jit(solution)/shard_map/ppermute | solution.py:29
  77.1 8.7 %collective-permute-done.3 = bf16[1,4,64,1024]{3,2,1,0:T(8,128)(2,1)S(1)} collective-permute-done((bf16[1,4,64,1024]{3,2,1,0:T(8,128)(2,1)S(1)}, bf16[1,4,64,1024]{3,2,1,0:T(8,128)(2,1)S(1)}, u32[]{:S(2)}, u32[]{:S(2)}) %collective-permute-start.3) | collective-permute-done | bytes 524320 | tf_op jit(solution)/shard_map/ppermute | solution.py:29
  85.8 0.1 select_bitcast_fusion.5
  85.9 0.1 maximum_bitcast_fusion
  86.0 1.6 collective-permute-start.4
  87.6 4.6 %all-to-all-start.1 = ((bf16[8,2,2,64,1024]{4,3,2,1,0:T(8,128)(2,1)}), bf16[8,2,2,64,1024]{4,3,2,1,0:T(8,128)(2,1)}, u32[]{:S(2)}, u32[]{:S(2)}) async-start(bf16[8,2,2,64,1024]{4,3,2,1,0:T(8,128)(2,1)} %shard_map.172), calls=%async_computation.1 | async-start | bytes 8388608 | tf_op jit(solution)/shard_map/all_to_all | solution.py:303
  92.2 0.2 all-gather.11.cloned.1.call-start
  92.4 19.7 %collective-permute-done.4 = bf16[2,4,64,1024]{3,2,1,0:T(8,128)(2,1)S(1)} collective-permute-done((bf16[2,4,64,1024]{3,2,1,0:T(8,128)(2,1)S(1)}, bf16[2,4,64,1024]{3,2,1,0:T(8,128)(2,1)S(1)}, u32[]{:S(2)}, u32[]{:S(2)}) %collective-permute-start.4) | collective-permute-done | bytes 1048608 | tf_op jit(solution)/shard_map/ppermute | solution.py:29
  112.2 0.1 select_bitcast_fusion.3
  112.3 0.2 pad_maximum_fusion.1
  112.5 0.1 collective-permute-start.5
  112.6 6.3 %fusion.3.refs_5_ = bf16[3,16,512]{2,1,0:T(8,128)(2,1)S(1)} fusion(bf16[3,4,1024,512]{3,2,1,0:T(8,128)(2,1)} %bitcast.83, bf16[4,16,1024]{2,1,0:T(8,128)(2,1)S(1)} %bitcast.97), kind=kOutput, calls=%fused_computation.9 | convolution fusion | flops 201351168 | bytes 12763136 | tf_op jit(solution)/shard_map/ztd,pzdc->ptc/dot_general | solution.py:381
  118.9 0.0 collective-permute-done.5
  118.9 1.9 select_bitcast_fusion.1
  120.8 0.4 pad_maximum_fusion
  121.2 0.7 copy.30
  121.9 2.4 copy.31
  124.4 28.8 %all-to-all-done.1.got_ref = bf16[8,2,2,64,1024]{4,3,2,1,0:T(8,128)(2,1)} async-done(((bf16[8,2,2,64,1024]{4,3,2,1,0:T(8,128)(2,1)}), bf16[8,2,2,64,1024]{4,3,2,1,0:T(8,128)(2,1)}, u32[]{:S(2)}, u32[]{:S(2)}) %all-to-all-start.1) | async-done | bytes 4194336 | tf_op jit(solution)/shard_map/all_to_all | solution.py:303
  153.2 4.0 %shard_map.173.refs_6_.resp_ref = bf16[2,64,72,128]{3,2,1,0:T(8,128)(2,1)S(1)} custom-call(bf16[8,2,2,64,1024]{4,3,2,1,0:T(8,128)(2,1)} %all-to-all-done.1.got_ref), custom_call_target="tpu_custom_call" | custom-call | flops 2097152 | bytes 6291456 | tf_op jit(solution)/shard_map/pallas_call | solution.py:306
  157.2 9.8 %all-gather.7.cloned.1.call-done = bf16[4096,1024]{1,0:T(8,128)(2,1)} async-done(((bf16[1024,1024]{1,0:T(8,128)(2,1)}), bf16[4096,1024]{1,0:T(8,128)(2,1)}) %all-gather.7.cloned.1.call-update) | async-done | bytes 8388624 | tf_op jit(solution)/shard_map/all_gather | solution.py:370
  167.0 0.0 copy-done.6
  167.0 0.0 copy-start.3
  167.0 0.0 copy-start.4
  167.0 0.0 copy-start.5
  167.0 10.7 %shard_map.177 = (bf16[1024,256]{1,0:T(8,128)(2,1)S(1)}, bf16[256,1024]{1,0:T(8,128)(2,1)S(1)}, bf16[1024,256]{1,0:T(8,128)(2,1)S(1)}) custom-call(bf16[4,1024,1024]{2,1,0:T(8,128)(2,1)} %bitcast.88, bf16[3,4096,512]{2,1,0:T(8,128)(2,1)} %refs_3_.3, bf16[3,4096,512]{2,1,0:T(8,128)(2,1)} %refs_3_.3, bf16[3,4096,512]{2,1,0:T(8,128)(2,1)} %refs_3_.3, ...), custom_call_target="tpu_custom_call" | custom-call | flops 6442450944 | bytes 14680064 | tf_op jit(solution)/shard_map/pallas_call | solution.py:95
  177.8 0.0 copy-start.7
  177.8 13.3 %all_to_all.41.signal_ref = bf16[8,32,1024]{2,1,0:T(8,128)(2,1)S(1)} all-to-all(bf16[8,32,1024]{2,1,0:T(8,128)(2,1)S(1)} %bitcast.80), channel_id=1, replica_groups=mesh['seq'=8,'chan'=4] {'seq'}, dimensions={0} | all-to-all | bytes 1048576 | tf_op jit(solution)/shard_map/all_to_all | solution.py:392
  191.0 0.0 copy-done
  191.1 0.0 copy-done.2
  191.1 0.0 copy-done.3
  191.1 0.0 copy-done.4
  191.1 0.0 copy-done.5
  191.1 3.0 shard_map.178
  194.1 12.2 %all_to_all.42 = bf16[8,32,1024]{2,1,0:T(8,128)(2,1)S(1)} all-to-all(bf16[8,32,1024]{2,1,0:T(8,128)(2,1)S(1)} %shard_map.178), channel_id=1, replica_groups=mesh['seq'=8,'chan'=4] {'seq'}, dimensions={0} | all-to-all | bytes 1048576 | tf_op jit(solution)/shard_map/all_to_all | solution.py:393
  206.2 0.0 copy-done.7
  206.2 1.2 shard_map.179
  207.4 0.0 all-gather.11.cloned.1.call-update
  207.5 0.3 all-gather.9.cloned.1.call-start
  207.7 10.8 %shard_map.174 = (bf16[1024,256]{1,0:T(8,128)(2,1)S(1)}, bf16[256,1024]{1,0:T(8,128)(2,1)S(1)}, bf16[1024,256]{1,0:T(8,128)(2,1)S(1)}) custom-call(bf16[4,1024,1024]{2,1,0:T(8,128)(2,1)} %bitcast.89, bf16[3,4096,512]{2,1,0:T(8,128)(2,1)} %refs_3_.3, bf16[3,4096,512]{2,1,0:T(8,128)(2,1)} %refs_3_.3, bf16[3,4096,512]{2,1,0:T(8,128)(2,1)} %refs_3_.3, ...), custom_call_target="tpu_custom_call" | custom-call | flops 6442450944 | bytes 14680064 | tf_op jit(solution)/shard_map/pallas_call | solution.py:95
  218.5 12.2 %all_to_all.43.signal_ref = bf16[8,32,1024]{2,1,0:T(8,128)(2,1)S(1)} all-to-all(bf16[8,32,1024]{2,1,0:T(8,128)(2,1)S(1)} %bitcast.79), channel_id=1, replica_groups=mesh['seq'=8,'chan'=4] {'seq'}, dimensions={0} | all-to-all | bytes 1048576 | tf_op jit(solution)/shard_map/all_to_all | solution.py:392
  230.7 3.0 shard_map.175
  233.6 12.2 %all_to_all.44 = bf16[8,32,1024]{2,1,0:T(8,128)(2,1)S(1)} all-to-all(bf16[8,32,1024]{2,1,0:T(8,128)(2,1)S(1)} %shard_map.175), channel_id=1, replica_groups=mesh['seq'=8,'chan'=4] {'seq'}, dimensions={0} | all-to-all | bytes 1048576 | tf_op jit(solution)/shard_map/all_to_all | solution.py:393
  245.8 1.2 shard_map.176
  247.0 0.0 all-gather.9.cloned.1.call-update
  247.0 3.8 %all-gather.11.cloned.1.call-done = bf16[4096,256]{1,0:T(8,128)(2,1)} async-done(((bf16[1024,256]{1,0:T(8,128)(2,1)}), bf16[4096,256]{1,0:T(8,128)(2,1)}) %all-gather.11.cloned.1.call-update) | async-done | bytes 2097168 | tf_op jit(solution)/shard_map/all_gather | solution.py:396
  250.8 5.8 %shard_map.180.refs_0_ = f32[1024,1024]{1,0:T(8,128)} custom-call(bf16[4,1024,256]{2,1,0:T(8,128)(2,1)} %bitcast.92, bf16[2,1024,1024]{2,1,0:T(8,128)(2,1)} %bitcast.86), custom_call_target="tpu_custom_call" | custom-call | flops 2147483648 | bytes 10485760 | tf_op jit(solution)/shard_map/pallas_call | solution.py:344
  256.6 40.5 %all-gather.9.cloned.1.call-done = bf16[4096,256]{1,0:T(8,128)(2,1)} async-done(((bf16[1024,256]{1,0:T(8,128)(2,1)}), bf16[4096,256]{1,0:T(8,128)(2,1)}) %all-gather.9.cloned.1.call-update) | async-done | bytes 2097168 | tf_op jit(solution)/shard_map/all_gather | solution.py:396
  297.1 6.0 %shard_map.181 = bf16[1024,1024]{1,0:T(8,128)(2,1)} custom-call(bf16[4,1024,256]{2,1,0:T(8,128)(2,1)} %bitcast.96, bf16[2,1024,1024]{2,1,0:T(8,128)(2,1)} %bitcast.87, f32[1024,1024]{1,0:T(8,128)} %shard_map.180.refs_0_), custom_call_target="tpu_custom_call" | custom-call | flops 2147483648 | bytes 10485760 | tf_op jit(solution)/shard_map/pallas_call | solution.py:344
  (12 shorter events, 0.1 us)
Async XLA Ops:
  6.5 160.5 %all-gather.7.cloned.1.call-start = ((), (), s32[]{:S(2)}) async-start(), calls=%async_computation.6 | async-start | bytes 10485760 | tf_op jit(solution)/shard_map/all_gather | solution.py:370
  9.2 29.7 %all-to-all-start = ((bf16[64,4,1024]{2,0,1:T(8,128)(2,1)}), bf16[64,4,1024]{2,0,1:T(8,128)(2,1)S(1)}, u32[]{:S(2)}, u32[]{:S(2)}) async-start(bf16[64,4,1024]{2,0,1:T(8,128)(2,1)} %bitcast.76), calls=%async_computation | async-start | bytes 1048576 | tf_op jit(solution)/shard_map/all_to_all | solution.py:324
  38.9 2.1 collective-permute-start
  41.0 11.7 %collective-permute-start.1 = (bf16[1,16,1024]{2,1,0:T(8,128)(2,1)S(1)}, bf16[1,16,1024]{2,1,0:T(8,128)(2,1)S(1)}, u32[]{:S(2)}, u32[]{:S(2)}) collective-permute-start(bf16[1,16,1024]{2,1,0:T(8,128)(2,1)S(1)} %bitcast.98), channel_id=1, source_target_pairs={{0,2},{1,3},{2,0},{3,1},{4,6},{5,7},{6,4},{7,5},{8,10},{9,11},{10,... | collective-permute-start | bytes 98312 | tf_op jit(solution)/shard_map/ppermute | solution.py:29
  52.7 17.7 %collective-permute-start.2 = (bf16[2,16,1024]{2,1,0:T(8,128)(2,1)S(1)}, bf16[2,16,1024]{2,1,0:T(8,128)(2,1)S(1)}, u32[]{:S(2)}, u32[]{:S(2)}) collective-permute-start(bf16[2,16,1024]{2,1,0:T(8,128)(2,1)S(1)} %maximum_bitcast_fusion.1), channel_id=1, source_target_pairs={{0,1},{1,0},{2,3},{3,2},{4,5},{5,4},{6,7},{7,6},{8,9},{9,8},{10,11... | collective-permute-start | bytes 196616 | tf_op jit(solution)/shard_map/ppermute | solution.py:29
  70.4 15.4 %collective-permute-start.3 = (bf16[1,4,64,1024]{3,2,1,0:T(8,128)(2,1)S(1)}, bf16[1,4,64,1024]{3,2,1,0:T(8,128)(2,1)S(1)}, u32[]{:S(2)}, u32[]{:S(2)}) collective-permute-start(bf16[1,4,64,1024]{3,2,1,0:T(8,128)(2,1)S(1)} %bitcast.93), channel_id=1, source_target_pairs={{0,16},{4,20},{8,24},{12,28},{16,0},{20,4},{24,8},{28,12},{1,17},{... | collective-permute-start | bytes 1572872 | tf_op jit(solution)/shard_map/ppermute | solution.py:29
  86.0 26.2 %collective-permute-start.4 = (bf16[2,4,64,1024]{3,2,1,0:T(8,128)(2,1)S(1)}, bf16[2,4,64,1024]{3,2,1,0:T(8,128)(2,1)S(1)}, u32[]{:S(2)}, u32[]{:S(2)}) collective-permute-start(bf16[2,4,64,1024]{3,2,1,0:T(8,128)(2,1)S(1)} %maximum_bitcast_fusion), channel_id=1, source_target_pairs={{0,8},{4,12},{8,0},{12,4},{16,24},{20,28},{24,16},{28,20},{1,9},{5... | collective-permute-start | bytes 3145736 | tf_op jit(solution)/shard_map/ppermute | solution.py:29
  87.6 65.6 %all-to-all-start.1 = ((bf16[8,2,2,64,1024]{4,3,2,1,0:T(8,128)(2,1)}), bf16[8,2,2,64,1024]{4,3,2,1,0:T(8,128)(2,1)}, u32[]{:S(2)}, u32[]{:S(2)}) async-start(bf16[8,2,2,64,1024]{4,3,2,1,0:T(8,128)(2,1)} %shard_map.172), calls=%async_computation.1 | async-start | bytes 8388608 | tf_op jit(solution)/shard_map/all_to_all | solution.py:303
  92.2 158.6 %all-gather.11.cloned.1.call-start = ((), (), s32[]{:S(2)}) async-start(), calls=%async_computation.8 | async-start | bytes 2621440 | tf_op jit(solution)/shard_map/all_gather | solution.py:396
  112.5 6.4 %collective-permute-start.5 = (bf16[4,4,64,1024]{3,2,1,0:T(8,128)(2,1)S(1)}, bf16[4,4,64,1024]{3,2,1,0:T(8,128)(2,1)}, u32[]{:S(2)}, u32[]{:S(2)}) collective-permute-start(bf16[4,4,64,1024]{3,2,1,0:T(8,128)(2,1)S(1)} %bitcast.91), channel_id=1, source_target_pairs={{0,4},{4,0},{8,12},{12,8},{16,20},{20,16},{24,28},{28,24},{1,5},{5... | collective-permute-start | bytes 6291464 | tf_op jit(solution)/shard_map/ppermute | solution.py:29
  124.4 42.6 %copy-start.6 = (f32[3,3,512]{2,1,0:T(4,128)S(1)}, f32[3,3,512]{2,1,0:T(4,128)}, u32[]{:S(2)}) copy-start(f32[3,3,512]{2,1,0:T(4,128)} %refs_4_.3) | copy-start | bytes 55300
  167.0 24.1 %copy-start = (bf16[256,256]{1,0:T(8,128)(2,1)S(1)}, bf16[256,256]{1,0:T(8,128)(2,1)}, u32[]{:S(2)}) copy-start(bf16[256,256]{1,0:T(8,128)(2,1)} %constant.138.clone.fwd_ref) | copy-start | bytes 393220
  167.0 24.1 %copy-start.1 = (bf16[256,256]{1,0:T(8,128)(2,1)S(1)}, bf16[256,256]{1,0:T(8,128)(2,1)}, u32[]{:S(2)}) copy-start(bf16[256,256]{1,0:T(8,128)(2,1)} %constant.139.clone.bwd_ref) | copy-start | bytes 393220
  167.0 24.1 %copy-start.2 = (bf16[144,64]{1,0:T(8,128)(2,1)S(1)}, bf16[144,64]{1,0:T(8,128)(2,1)}, u32[]{:S(2)}) copy-start(bf16[144,64]{1,0:T(8,128)(2,1)} %constant.134.clone.first_ref) | copy-start | bytes 55300
  167.0 24.1 %copy-start.3 = (f32[72,128]{1,0:T(8,128)S(1)}, f32[72,128]{1,0:T(8,128)}, u32[]{:S(2)}) copy-start(f32[72,128]{1,0:T(8,128)} %constant.136.clone.cos_ref) | copy-start | bytes 110596
  167.0 24.1 %copy-start.4 = (f32[72,128]{1,0:T(8,128)S(1)}, f32[72,128]{1,0:T(8,128)}, u32[]{:S(2)}) copy-start(f32[72,128]{1,0:T(8,128)} %constant.137.clone.sin_ref) | copy-start | bytes 110596
  167.0 24.1 %copy-start.5 = (bf16[64,144]{1,0:T(8,128)(2,1)S(1)}, bf16[64,144]{1,0:T(8,128)(2,1)}, u32[]{:S(2)}) copy-start(bf16[64,144]{1,0:T(8,128)(2,1)} %constant.135.clone.last_ref) | copy-start | bytes 55300
  177.8 28.4 %copy-start.7 = (f32[512]{0:T(512)S(1)}, f32[512]{0:T(512)}, u32[]{:S(2)}) copy-start(f32[512]{0:T(512)} %param.22) | copy-start | bytes 6148
  207.5 89.6 %all-gather.9.cloned.1.call-start = ((), (), s32[]{:S(2)}) async-start(), calls=%async_computation.7 | async-start | bytes 2621440 | tf_op jit(solution)/shard_map/all_gather | solution.py:396
Sparse Core Ops, SparseCore 0:
  8.9 158.0 all-gather.6
  207.6 43.1 all-gather.10
  252.4 44.6 all-gather.8

commit v12 on v11

--- a/solution.py
+++ b/solution.py
@@ -40,78 +40,72 @@
     return 1 if size % LANES or (size // seq_count) % CHAN_BLOCK else CHUNKS
 
 
-def project_kernel(streams, extras, tok_ref, *refs):
-    w_refs, taps_ref, halo_ref = refs[: len(streams)], refs[len(streams)], refs[len(streams) + 1]
-    outs, acc = refs[len(streams) + 2 + extras : -1], refs[-1]
+def project_kernel(extras, tok_ref, wq_ref, wk_ref, wv_ref, taps_ref, halo_ref, *rest):
+    query_t_ref, signal_ref, signal_t_ref, acc = rest[extras:]
     step = pl.program_id(0)
     last = pl.num_programs(0) - 1
-    rows = acc.shape[1] - HALO
-
-    def part(w_ref):
-        return jnp.dot(tok_ref[0], w_ref[0], preferred_element_type=jnp.float32)
+    rows, size = query_t_ref.shape
+
+    def part():
+        weight = jnp.concatenate([wq_ref[0], wk_ref[0], wv_ref[0]], axis=1)
+        return jnp.dot(tok_ref[0], weight, preferred_element_type=jnp.float32)
+
+    def filtered(p, r):
+        lanes = slice(p * size, (p + 1) * size)
+        total = taps_ref[0, p][None, :] * acc[pl.ds(HALO + r, LANES), lanes]
+        for j in range(1, TAPS):
+            total = total + taps_ref[j, p][None, :] * acc[pl.ds(HALO + r - j, LANES), lanes]
+        return total
 
     @pl.when(step == 0)
     def _():
-        for i, p in enumerate(streams):
-            acc[i, :HALO, :] = halo_ref[p].astype(jnp.float32)
-            acc[i, HALO:, :] = part(w_refs[i])
+        for p in range(3):
+            acc[:HALO, p * size : (p + 1) * size] = halo_ref[p].astype(jnp.float32)
+        acc[HALO:, :] = part()
 
     @pl.when(jnp.logical_and(step > 0, step < last))
     def _():
-        for i in range(len(streams)):
-            acc[i, HALO:, :] += part(w_refs[i])
+        acc[HALO:, :] += part()
 
     @pl.when(step == last)
     def _():
-        for i in range(len(streams)):
-            acc[i, HALO:, :] = (acc[i, HALO:, :] + part(w_refs[i])).astype(jnp.bfloat16).astype(jnp.float32)
+        acc[HALO:, :] = (acc[HALO:, :] + part()).astype(jnp.bfloat16).astype(jnp.float32)
         for r in range(0, rows, LANES):
-            made = {}
-            for i, p in enumerate(streams):
-                total = taps_ref[0, p][None, :] * acc[i, pl.ds(HALO + r, LANES), :]
-                for j in range(1, TAPS):
-                    total = total + taps_ref[j, p][None, :] * acc[i, pl.ds(HALO + r - j, LANES), :]
-                made[p] = total
-            if 0 in made:
-                outs[0][r : r + LANES, :] = made[0].astype(outs[0].dtype)
-            if 1 in made:
-                signal = made[1] * made[2]
-                outs[-1][r : r + LANES, :] = signal.astype(outs[-1].dtype)
-                outs[-2][:, r : r + LANES] = signal.T.astype(outs[-2].dtype)
-
-
-def project(streams, gathered, in_weight, conv_weight, halo, lo, size, *after):
+            query_t_ref[r : r + LANES, :] = filtered(0, r).astype(query_t_ref.dtype)
+            signal = filtered(1, r) * filtered(2, r)
+            signal_t_ref[r : r + LANES, :] = signal.astype(signal_t_ref.dtype)
+            signal_ref[:, r : r + LANES] = signal.T.astype(signal_ref.dtype)
+
+
+def project(gathered, in_weight, conv_weight, halo, lo, size, *after):
     count, rows, step = gathered.shape
-    depth = count * step
     at = lo // size
     flat = jax.ShapeDtypeStruct((rows, size), jnp.bfloat16)
-    shapes = ([flat] if 0 in streams else []) + (
-        [jax.ShapeDtypeStruct((size, rows), jnp.bfloat16), flat] if 1 in streams else []
-    )
+    shapes = [flat, jax.ShapeDtypeStruct((size, rows), jnp.bfloat16), flat]
 
     def weight_of(p):
         return pl.BlockSpec((1, step, size), lambda z: (p, z, at))
 
     return pl.pallas_call(
-        lambda *refs: project_kernel(streams, len(after), *refs),
+        lambda *refs: project_kernel(len(after), *refs),
         grid=(count,),
         in_specs=[
             pl.BlockSpec((1, rows, step), lambda z: (z, 0, 0)),
-            *[weight_of(p) for p in streams],
+            *[weight_of(p) for p in range(3)],
             pl.BlockSpec((TAPS, 3, size), lambda z: (0, 0, at)),
             pl.BlockSpec((3, HALO, size), lambda z: (0, 0, at)),
             *[pl.BlockSpec(memory_space=pl.ANY) for _ in after],
         ],
         out_specs=[pl.BlockSpec(shape.shape, lambda z: (0, 0)) for shape in shapes],
         out_shape=shapes,
-        scratch_shapes=[pltpu.VMEM((len(streams), HALO + rows, size), jnp.float32)],
+        scratch_shapes=[pltpu.VMEM((HALO + rows, 3 * size), jnp.float32)],
         compiler_params=pltpu.CompilerParams(vmem_limit_bytes=48 * MIB),
         cost_estimate=pl.CostEstimate(
-            flops=2 * len(streams) * rows * depth * size,
-            bytes_accessed=2 * depth * (len(streams) * size + rows),
+            flops=2 * 3 * rows * count * step * size,
+            bytes_accessed=2 * count * step * (3 * size + rows),
             transcendentals=0,
         ),
-    )(gathered, *[in_weight] * len(streams), conv_weight, halo, *after)
+    )(gathered, in_weight, in_weight, in_weight, conv_weight, halo, *after)
 
 
 def transform_tables(seq_count, tok_rows):
@@ -387,7 +381,7 @@
     total = None
     for j, lo in enumerate(range(0, chans, size)):
         given = (gathered, in_weight, conv_weight, halo, lo, size, response, weight)
-        query_t, signal, signal_t = project((0, 1, 2), *given)
+        query_t, signal, signal_t = project(*given)
         values = signal.reshape(seq_count, size // seq_count, tok_rows)
         values = lax.all_to_all(values, "seq", split_axis=0, concat_axis=0, tiled=True)
         longconv = lax.all_to_all(

time: 311 us -> 310 us (level)
  no operation moved by 1% of the time
where the time goes in v12:
time: 310 us
  waiting for transfers between devices  136 us (44%)
  Pallas kernels  54 us (17%)
  blocking collectives  49.7 us (16%)
  starting transfers between devices  30.1 us (10%)
  local copies, waits for them, and re-layouts  16.8 us (5%)
  between operations  13.4 us (4%)
  matrix products  6.3 us (2%)
  other arithmetic  3.57 us (1%)
    all_gather x2, waiting for transfers between devices, shards(): gated = lax.all_gather(gate(longconv, skip, lo, signal_t, query_t), 'chan')  44.4 us
    all_to_all x1, waiting for transfers between devices, folded_response(): got = lax.all_to_all(sent, 'seq', split_axis=0, concat_axis=0, tiled=True)  28.8 us
    ppermute x5, waiting for transfers between devices, gather_by_doubling(): other = lax.ppermute(held, axis, [(i, i ^ bit) for i in range(size)])  28.5 us
    all_to_all x2, blocking collectives, shards(): lax.all_to_all(values, 'seq', split_axis=0, concat_axis=0, tiled=True)  25.4 us
    all_to_all x2, blocking collectives, shards(): lax.all_to_all(long_conv(values, response, lo // seq_count), 'seq', split...  24.3 us
    all_to_all x1, waiting for transfers between devices, feature_rows(): own = lax.all_to_all(own, 'chan', split_axis=1, concat_axis=0, tiled=True)  22.6 us
    pallas_call x2, Pallas kernels, project(): pl.pallas_call(lambda *refs: project_kernel(len(after), *refs), grid=(cou...  21.2 us
    ppermute x5, starting transfers between devices, gather_by_doubling(): other = lax.ppermute(held, axis, [(i, i ^ bit) for i in range(size)])  17.4 us
  transfers between devices with their start and end apart: 11, of which 8 were waited for; matrix products, arithmetic and copies ran while one was open for 9% of the time, Pallas kernels for 11%

profile of v12, /device:TPU:0, one launch (start us, length us, event | category | flops | bytes accessed | tf_op | source)
XLA Modules:
  0.0 309.5 jit_solution(11199227020559866327)
XLA Ops:
  6.5 0.0 all-gather.7.cloned.1.call-start
  6.5 0.7 all-gather.7.cloned.1.call-update
  7.3 1.1 constant_dynamic-slice_fusion
  8.3 0.8 copy.35
  9.2 6.3 %all-to-all-start = ((bf16[64,4,1024]{2,0,1:T(8,128)(2,1)}), bf16[64,4,1024]{2,0,1:T(8,128)(2,1)S(1)}, u32[]{:S(2)}, u32[]{:S(2)}) async-start(bf16[64,4,1024]{2,0,1:T(8,128)(2,1)} %bitcast.76), calls=%async_computation | async-start | bytes 1048576 | tf_op jit(solution)/shard_map/all_to_all | solution.py:318
  15.5 0.8 slice.3
  16.3 22.6 %all-to-all-done = bf16[64,4,1024]{2,0,1:T(8,128)(2,1)S(1)} async-done(((bf16[64,4,1024]{2,0,1:T(8,128)(2,1)}), bf16[64,4,1024]{2,0,1:T(8,128)(2,1)S(1)}, u32[]{:S(2)}, u32[]{:S(2)}) %all-to-all-start) | async-done | bytes 524320 | tf_op jit(solution)/shard_map/all_to_all | solution.py:318
  38.9 1.3 collective-permute-start
  40.2 0.8 collective-permute-done
  41.0 0.0 collective-permute-start.1
  41.0 0.7 fusion.1.order_ref
  41.7 10.9 %reshape.40.spec_ref = f32[2,1024,1024]{2,1,0:T(8,128)} reshape(f32[2,512,2,1024]{3,2,1,0:T(2,128)} %param.21) | data formatting | bytes 16777216 | tf_op jit(solution)/shard_map/reshape | solution.py:290
  52.6 0.0 collective-permute-done.1
  52.7 9.1 %collective-permute-start.2 = (bf16[2,16,1024]{2,1,0:T(8,128)(2,1)S(1)}, bf16[2,16,1024]{2,1,0:T(8,128)(2,1)S(1)}, u32[]{:S(2)}, u32[]{:S(2)}) collective-permute-start(bf16[2,16,1024]{2,1,0:T(8,128)(2,1)S(1)} %maximum_bitcast_fusion.1), channel_id=1, source_target_pairs={{0,1},{1,0},{2,3},{3,2},{4,5},{5,4},{6,7},{7,6},{8,9},{9,8},{10,11... | collective-permute-start | bytes 196616 | tf_op jit(solution)/shard_map/ppermute | solution.py:29
  61.8 8.6 %shard_map.172 = bf16[8,2,2,64,1024]{4,3,2,1,0:T(8,128)(2,1)} custom-call(f32[2,1024,1024]{2,1,0:T(8,128)} %reshape.40.spec_ref, bf16[1024,1024]{1,0:T(8,128)(2,1)S(1)} %fusion.1.order_ref), custom_call_target="tpu_custom_call" | custom-call | flops 4294967296 | bytes 12582912 | tf_op jit(solution)/shard_map/pallas_call | solution.py:277
  70.4 0.0 collective-permute-done.2
  70.4 6.6 %collective-permute-start.3 = (bf16[1,4,64,1024]{3,2,1,0:T(8,128)(2,1)S(1)}, bf16[1,4,64,1024]{3,2,1,0:T(8,128)(2,1)S(1)}, u32[]{:S(2)}, u32[]{:S(2)}) collective-permute-start(bf16[1,4,64,1024]{3,2,1,0:T(8,128)(2,1)S(1)} %bitcast.93), channel_id=1, source_target_pairs={{0,16},{4,20},{8,24},{12,28},{16,0},{20,4},{24,8},{28,12},{1,17},{... | collective-permute-start | bytes 1572872 | tf_op jit(solution)/shard_map/ppermute | solution.py:29
  77.1 8.7 %collective-permute-done.3 = bf16[1,4,64,1024]{3,2,1,0:T(8,128)(2,1)S(1)} collective-permute-done((bf16[1,4,64,1024]{3,2,1,0:T(8,128)(2,1)S(1)}, bf16[1,4,64,1024]{3,2,1,0:T(8,128)(2,1)S(1)}, u32[]{:S(2)}, u32[]{:S(2)}) %collective-permute-start.3) | collective-permute-done | bytes 524320 | tf_op jit(solution)/shard_map/ppermute | solution.py:29
  85.8 0.1 select_bitcast_fusion.5
  85.9 0.1 maximum_bitcast_fusion
  86.0 1.6 collective-permute-start.4
  87.6 4.6 %all-to-all-start.1 = ((bf16[8,2,2,64,1024]{4,3,2,1,0:T(8,128)(2,1)}), bf16[8,2,2,64,1024]{4,3,2,1,0:T(8,128)(2,1)}, u32[]{:S(2)}, u32[]{:S(2)}) async-start(bf16[8,2,2,64,1024]{4,3,2,1,0:T(8,128)(2,1)} %shard_map.172), calls=%async_computation.1 | async-start | bytes 8388608 | tf_op jit(solution)/shard_map/all_to_all | solution.py:297
  92.2 0.2 all-gather.11.cloned.1.call-start
  92.4 19.7 %collective-permute-done.4 = bf16[2,4,64,1024]{3,2,1,0:T(8,128)(2,1)S(1)} collective-permute-done((bf16[2,4,64,1024]{3,2,1,0:T(8,128)(2,1)S(1)}, bf16[2,4,64,1024]{3,2,1,0:T(8,128)(2,1)S(1)}, u32[]{:S(2)}, u32[]{:S(2)}) %collective-permute-start.4) | collective-permute-done | bytes 1048608 | tf_op jit(solution)/shard_map/ppermute | solution.py:29
  112.2 0.1 select_bitcast_fusion.3
  112.3 0.2 pad_maximum_fusion.1
  112.5 0.1 collective-permute-start.5
  112.6 6.3 %fusion.3.refs_5_ = bf16[3,16,512]{2,1,0:T(8,128)(2,1)S(1)} fusion(bf16[3,4,1024,512]{3,2,1,0:T(8,128)(2,1)} %bitcast.83, bf16[4,16,1024]{2,1,0:T(8,128)(2,1)S(1)} %bitcast.97), kind=kOutput, calls=%fused_computation.9 | convolution fusion | flops 201351168 | bytes 12763136 | tf_op jit(solution)/shard_map/ztd,pzdc->ptc/dot_general | solution.py:375
  118.9 0.0 collective-permute-done.5
  118.9 1.9 select_bitcast_fusion.1
  120.8 0.4 pad_maximum_fusion
  121.2 0.7 copy.30
  121.9 2.4 copy.31
  124.4 28.8 %all-to-all-done.1.got_ref = bf16[8,2,2,64,1024]{4,3,2,1,0:T(8,128)(2,1)} async-done(((bf16[8,2,2,64,1024]{4,3,2,1,0:T(8,128)(2,1)}), bf16[8,2,2,64,1024]{4,3,2,1,0:T(8,128)(2,1)}, u32[]{:S(2)}, u32[]{:S(2)}) %all-to-all-start.1) | async-done | bytes 4194336 | tf_op jit(solution)/shard_map/all_to_all | solution.py:297
  153.2 4.0 %shard_map.173.refs_6_.resp_ref = bf16[2,64,72,128]{3,2,1,0:T(8,128)(2,1)S(1)} custom-call(bf16[8,2,2,64,1024]{4,3,2,1,0:T(8,128)(2,1)} %all-to-all-done.1.got_ref), custom_call_target="tpu_custom_call" | custom-call | flops 2097152 | bytes 6291456 | tf_op jit(solution)/shard_map/pallas_call | solution.py:300
  157.2 9.8 %all-gather.7.cloned.1.call-done = bf16[4096,1024]{1,0:T(8,128)(2,1)} async-done(((bf16[1024,1024]{1,0:T(8,128)(2,1)}), bf16[4096,1024]{1,0:T(8,128)(2,1)}) %all-gather.7.cloned.1.call-update) | async-done | bytes 8388624 | tf_op jit(solution)/shard_map/all_gather | solution.py:364
  167.0 0.0 copy-done.6
  167.0 0.0 copy-start.3
  167.0 0.0 copy-start.4
  167.0 0.0 copy-start.5
  167.0 10.6 %shard_map.177 = (bf16[1024,256]{1,0:T(8,128)(2,1)S(1)}, bf16[256,1024]{1,0:T(8,128)(2,1)S(1)}, bf16[1024,256]{1,0:T(8,128)(2,1)S(1)}) custom-call(bf16[4,1024,1024]{2,1,0:T(8,128)(2,1)} %bitcast.88, bf16[3,4096,512]{2,1,0:T(8,128)(2,1)} %refs_3_.3, bf16[3,4096,512]{2,1,0:T(8,128)(2,1)} %refs_3_.3, bf16[3,4096,512]{2,1,0:T(8,128)(2,1)} %refs_3_.3, ...), custom_call_target="tpu_custom_call" | custom-call | flops 6442450944 | bytes 14680064 | tf_op jit(solution)/shard_map/pallas_call | solution.py:89
  177.6 0.0 copy-start.7
  177.6 13.3 %all_to_all.41.signal_ref = bf16[8,32,1024]{2,1,0:T(8,128)(2,1)S(1)} all-to-all(bf16[8,32,1024]{2,1,0:T(8,128)(2,1)S(1)} %bitcast.80), channel_id=1, replica_groups=mesh['seq'=8,'chan'=4] {'seq'}, dimensions={0} | all-to-all | bytes 1048576 | tf_op jit(solution)/shard_map/all_to_all | solution.py:386
  190.9 0.0 copy-done
  190.9 0.0 copy-done.1
  190.9 0.0 copy-done.2
  190.9 0.0 copy-done.3
  190.9 0.0 copy-done.4
  191.0 3.0 shard_map.178
  193.9 12.2 %all_to_all.42 = bf16[8,32,1024]{2,1,0:T(8,128)(2,1)S(1)} all-to-all(bf16[8,32,1024]{2,1,0:T(8,128)(2,1)S(1)} %shard_map.178), channel_id=1, replica_groups=mesh['seq'=8,'chan'=4] {'seq'}, dimensions={0} | all-to-all | bytes 1048576 | tf_op jit(solution)/shard_map/all_to_all | solution.py:387
  206.1 0.0 copy-done.7
  206.1 1.2 shard_map.179
  207.3 0.0 all-gather.11.cloned.1.call-update
  207.3 0.3 all-gather.9.cloned.1.call-start
  207.6 10.6 %shard_map.174 = (bf16[1024,256]{1,0:T(8,128)(2,1)S(1)}, bf16[256,1024]{1,0:T(8,128)(2,1)S(1)}, bf16[1024,256]{1,0:T(8,128)(2,1)S(1)}) custom-call(bf16[4,1024,1024]{2,1,0:T(8,128)(2,1)} %bitcast.89, bf16[3,4096,512]{2,1,0:T(8,128)(2,1)} %refs_3_.3, bf16[3,4096,512]{2,1,0:T(8,128)(2,1)} %refs_3_.3, bf16[3,4096,512]{2,1,0:T(8,128)(2,1)} %refs_3_.3, ...), custom_call_target="tpu_custom_call" | custom-call | flops 6442450944 | bytes 14680064 | tf_op jit(solution)/shard_map/pallas_call | solution.py:89
  218.3 12.2 %all_to_all.43.signal_ref = bf16[8,32,1024]{2,1,0:T(8,128)(2,1)S(1)} all-to-all(bf16[8,32,1024]{2,1,0:T(8,128)(2,1)S(1)} %bitcast.79), channel_id=1, replica_groups=mesh['seq'=8,'chan'=4] {'seq'}, dimensions={0} | all-to-all | bytes 1048576 | tf_op jit(solution)/shard_map/all_to_all | solution.py:386
  230.4 3.0 shard_map.175
  233.4 12.2 %all_to_all.44 = bf16[8,32,1024]{2,1,0:T(8,128)(2,1)S(1)} all-to-all(bf16[8,32,1024]{2,1,0:T(8,128)(2,1)S(1)} %shard_map.175), channel_id=1, replica_groups=mesh['seq'=8,'chan'=4] {'seq'}, dimensions={0} | all-to-all | bytes 1048576 | tf_op jit(solution)/shard_map/all_to_all | solution.py:387
  245.5 1.2 shard_map.176
  246.7 0.0 all-gather.9.cloned.1.call-update
  246.8 3.9 %all-gather.11.cloned.1.call-done = bf16[4096,256]{1,0:T(8,128)(2,1)} async-done(((bf16[1024,256]{1,0:T(8,128)(2,1)}), bf16[4096,256]{1,0:T(8,128)(2,1)}) %all-gather.11.cloned.1.call-update) | async-done | bytes 2097168 | tf_op jit(solution)/shard_map/all_gather | solution.py:390
  250.7 5.8 %shard_map.180.refs_0_ = f32[1024,1024]{1,0:T(8,128)} custom-call(bf16[4,1024,256]{2,1,0:T(8,128)(2,1)} %bitcast.92, bf16[2,1024,1024]{2,1,0:T(8,128)(2,1)} %bitcast.86), custom_call_target="tpu_custom_call" | custom-call | flops 2147483648 | bytes 10485760 | tf_op jit(solution)/shard_map/pallas_call | solution.py:338
  256.5 40.5 %all-gather.9.cloned.1.call-done = bf16[4096,256]{1,0:T(8,128)(2,1)} async-done(((bf16[1024,256]{1,0:T(8,128)(2,1)}), bf16[4096,256]{1,0:T(8,128)(2,1)}) %all-gather.9.cloned.1.call-update) | async-done | bytes 2097168 | tf_op jit(solution)/shard_map/all_gather | solution.py:390
  297.0 6.0 %shard_map.181 = bf16[1024,1024]{1,0:T(8,128)(2,1)} custom-call(bf16[4,1024,256]{2,1,0:T(8,128)(2,1)} %bitcast.96, bf16[2,1024,1024]{2,1,0:T(8,128)(2,1)} %bitcast.87, f32[1024,1024]{1,0:T(8,128)} %shard_map.180.refs_0_), custom_call_target="tpu_custom_call" | custom-call | flops 2147483648 | bytes 10485760 | tf_op jit(solution)/shard_map/pallas_call | solution.py:338
  (12 shorter events, 0.1 us)
Async XLA Ops:
  6.5 160.5 %all-gather.7.cloned.1.call-start = ((), (), s32[]{:S(2)}) async-start(), calls=%async_computation.6 | async-start | bytes 10485760 | tf_op jit(solution)/shard_map/all_gather | solution.py:364
  9.2 29.7 %all-to-all-start = ((bf16[64,4,1024]{2,0,1:T(8,128)(2,1)}), bf16[64,4,1024]{2,0,1:T(8,128)(2,1)S(1)}, u32[]{:S(2)}, u32[]{:S(2)}) async-start(bf16[64,4,1024]{2,0,1:T(8,128)(2,1)} %bitcast.76), calls=%async_computation | async-start | bytes 1048576 | tf_op jit(solution)/shard_map/all_to_all | solution.py:318
  38.9 2.1 collective-permute-start
  41.0 11.7 %collective-permute-start.1 = (bf16[1,16,1024]{2,1,0:T(8,128)(2,1)S(1)}, bf16[1,16,1024]{2,1,0:T(8,128)(2,1)S(1)}, u32[]{:S(2)}, u32[]{:S(2)}) collective-permute-start(bf16[1,16,1024]{2,1,0:T(8,128)(2,1)S(1)} %bitcast.98), channel_id=1, source_target_pairs={{0,2},{1,3},{2,0},{3,1},{4,6},{5,7},{6,4},{7,5},{8,10},{9,11},{10,... | collective-permute-start | bytes 98312 | tf_op jit(solution)/shard_map/ppermute | solution.py:29
  52.7 17.7 %collective-permute-start.2 = (bf16[2,16,1024]{2,1,0:T(8,128)(2,1)S(1)}, bf16[2,16,1024]{2,1,0:T(8,128)(2,1)S(1)}, u32[]{:S(2)}, u32[]{:S(2)}) collective-permute-start(bf16[2,16,1024]{2,1,0:T(8,128)(2,1)S(1)} %maximum_bitcast_fusion.1), channel_id=1, source_target_pairs={{0,1},{1,0},{2,3},{3,2},{4,5},{5,4},{6,7},{7,6},{8,9},{9,8},{10,11... | collective-permute-start | bytes 196616 | tf_op jit(solution)/shard_map/ppermute | solution.py:29
  70.4 15.4 %collective-permute-start.3 = (bf16[1,4,64,1024]{3,2,1,0:T(8,128)(2,1)S(1)}, bf16[1,4,64,1024]{3,2,1,0:T(8,128)(2,1)S(1)}, u32[]{:S(2)}, u32[]{:S(2)}) collective-permute-start(bf16[1,4,64,1024]{3,2,1,0:T(8,128)(2,1)S(1)} %bitcast.93), channel_id=1, source_target_pairs={{0,16},{4,20},{8,24},{12,28},{16,0},{20,4},{24,8},{28,12},{1,17},{... | collective-permute-start | bytes 1572872 | tf_op jit(solution)/shard_map/ppermute | solution.py:29
  86.0 26.2 %collective-permute-start.4 = (bf16[2,4,64,1024]{3,2,1,0:T(8,128)(2,1)S(1)}, bf16[2,4,64,1024]{3,2,1,0:T(8,128)(2,1)S(1)}, u32[]{:S(2)}, u32[]{:S(2)}) collective-permute-start(bf16[2,4,64,1024]{3,2,1,0:T(8,128)(2,1)S(1)} %maximum_bitcast_fusion), channel_id=1, source_target_pairs={{0,8},{4,12},{8,0},{12,4},{16,24},{20,28},{24,16},{28,20},{1,9},{5... | collective-permute-start | bytes 3145736 | tf_op jit(solution)/shard_map/ppermute | solution.py:29
  87.6 65.6 %all-to-all-start.1 = ((bf16[8,2,2,64,1024]{4,3,2,1,0:T(8,128)(2,1)}), bf16[8,2,2,64,1024]{4,3,2,1,0:T(8,128)(2,1)}, u32[]{:S(2)}, u32[]{:S(2)}) async-start(bf16[8,2,2,64,1024]{4,3,2,1,0:T(8,128)(2,1)} %shard_map.172), calls=%async_computation.1 | async-start | bytes 8388608 | tf_op jit(solution)/shard_map/all_to_all | solution.py:297
  92.2 158.5 %all-gather.11.cloned.1.call-start = ((), (), s32[]{:S(2)}) async-start(), calls=%async_computation.8 | async-start | bytes 2621440 | tf_op jit(solution)/shard_map/all_gather | solution.py:390
  112.5 6.4 %collective-permute-start.5 = (bf16[4,4,64,1024]{3,2,1,0:T(8,128)(2,1)S(1)}, bf16[4,4,64,1024]{3,2,1,0:T(8,128)(2,1)}, u32[]{:S(2)}, u32[]{:S(2)}) collective-permute-start(bf16[4,4,64,1024]{3,2,1,0:T(8,128)(2,1)S(1)} %bitcast.91), channel_id=1, source_target_pairs={{0,4},{4,0},{8,12},{12,8},{16,20},{20,16},{24,28},{28,24},{1,5},{5... | collective-permute-start | bytes 6291464 | tf_op jit(solution)/shard_map/ppermute | solution.py:29
  124.4 42.6 %copy-start.6 = (f32[3,3,512]{2,1,0:T(4,128)S(1)}, f32[3,3,512]{2,1,0:T(4,128)}, u32[]{:S(2)}) copy-start(f32[3,3,512]{2,1,0:T(4,128)} %refs_4_.3) | copy-start | bytes 55300
  167.0 23.9 %copy-start = (bf16[256,256]{1,0:T(8,128)(2,1)S(1)}, bf16[256,256]{1,0:T(8,128)(2,1)}, u32[]{:S(2)}) copy-start(bf16[256,256]{1,0:T(8,128)(2,1)} %constant.138.clone.fwd_ref) | copy-start | bytes 393220
  167.0 23.9 %copy-start.1 = (bf16[256,256]{1,0:T(8,128)(2,1)S(1)}, bf16[256,256]{1,0:T(8,128)(2,1)}, u32[]{:S(2)}) copy-start(bf16[256,256]{1,0:T(8,128)(2,1)} %constant.139.clone.bwd_ref) | copy-start | bytes 393220
  167.0 23.9 %copy-start.2 = (bf16[144,64]{1,0:T(8,128)(2,1)S(1)}, bf16[144,64]{1,0:T(8,128)(2,1)}, u32[]{:S(2)}) copy-start(bf16[144,64]{1,0:T(8,128)(2,1)} %constant.134.clone.first_ref) | copy-start | bytes 55300
  167.0 23.9 %copy-start.3 = (f32[72,128]{1,0:T(8,128)S(1)}, f32[72,128]{1,0:T(8,128)}, u32[]{:S(2)}) copy-start(f32[72,128]{1,0:T(8,128)} %constant.136.clone.cos_ref) | copy-start | bytes 110596
  167.0 23.9 %copy-start.4 = (f32[72,128]{1,0:T(8,128)S(1)}, f32[72,128]{1,0:T(8,128)}, u32[]{:S(2)}) copy-start(f32[72,128]{1,0:T(8,128)} %constant.137.clone.sin_ref) | copy-start | bytes 110596
  167.0 23.9 %copy-start.5 = (bf16[64,144]{1,0:T(8,128)(2,1)S(1)}, bf16[64,144]{1,0:T(8,128)(2,1)}, u32[]{:S(2)}) copy-start(bf16[64,144]{1,0:T(8,128)(2,1)} %constant.135.clone.last_ref) | copy-start | bytes 55300
  177.6 28.5 %copy-start.7 = (f32[512]{0:T(512)S(1)}, f32[512]{0:T(512)}, u32[]{:S(2)}) copy-start(f32[512]{0:T(512)} %param.22) | copy-start | bytes 6148
  207.3 89.6 %all-gather.9.cloned.1.call-start = ((), (), s32[]{:S(2)}) async-start(), calls=%async_computation.7 | async-start | bytes 2621440 | tf_op jit(solution)/shard_map/all_gather | solution.py:390
Sparse Core Ops, SparseCore 0:
  8.9 158.0 all-gather.6
  207.5 43.1 all-gather.10
  252.3 44.6 all-gather.8

commit v13 on v12

--- a/solution.py
+++ b/solution.py
@@ -18,6 +18,15 @@
     size = lax.axis_size(axis)
     pairs = [(i, i + by) for i in range(size) if 0 <= i + by < size]
     return lax.ppermute(value, axis, pairs)
+
+
+def along_line(value, axis):
+    size = lax.axis_size(axis)
+    before, after = [value], [value]
+    for k in range(1, size):
+        before.append(lax.ppermute(before[-1], axis, [(i, i + 1) for i in range(k - 1, size - 1)]))
+        after.append(lax.ppermute(after[-1], axis, [(i, i - 1) for i in range(1, size - k + 1)]))
+    return before, after[1:]
 
 
 def gather_by_doubling(value, axis):
@@ -40,15 +49,22 @@
     return 1 if size % LANES or (size // seq_count) % CHAN_BLOCK else CHUNKS
 
 
-def project_kernel(extras, tok_ref, wq_ref, wk_ref, wv_ref, taps_ref, halo_ref, *rest):
-    query_t_ref, signal_ref, signal_t_ref, acc = rest[extras:]
+def project_kernel(count, extras, me_ref, *refs):
+    before_refs, after_refs = refs[:count], refs[count : 2 * count - 1]
+    wq_ref, wk_ref, wv_ref, taps_ref, halo_ref = refs[2 * count - 1 : 2 * count + 4]
+    query_t_ref, signal_ref, signal_t_ref, before, after, acc, sems = refs[2 * count + 4 + extras :]
     step = pl.program_id(0)
-    last = pl.num_programs(0) - 1
     rows, size = query_t_ref.shape
-
-    def part():
+    copies = []
+    for k in range(count):
+        given = [pltpu.make_async_copy(before_refs[k], before.at[k], sems.at[2 * k])]
+        if k > 0:
+            given.append(pltpu.make_async_copy(after_refs[count - k - 1], after.at[k - 1], sems.at[2 * k + 1]))
+        copies.append(given)
+
+    def part(tokens):
         weight = jnp.concatenate([wq_ref[0], wk_ref[0], wv_ref[0]], axis=1)
-        return jnp.dot(tok_ref[0], weight, preferred_element_type=jnp.float32)
+        return jnp.dot(tokens, weight, preferred_element_type=jnp.float32)
 
     def filtered(p, r):
         lanes = slice(p * size, (p + 1) * size)
@@ -59,17 +75,30 @@
 
     @pl.when(step == 0)
     def _():
+        for given in copies:
+            for copy in given:
+                copy.start()
         for p in range(3):
             acc[:HALO, p * size : (p + 1) * size] = halo_ref[p].astype(jnp.float32)
-        acc[HALO:, :] = part()
-
-    @pl.when(jnp.logical_and(step > 0, step < last))
+
+    for k in range(count):
+
+        @pl.when(step == k)
+        def _():
+            for copy in copies[k]:
+                copy.wait()
+
+    @pl.when(step == 0)
     def _():
-        acc[HALO:, :] += part()
-
-    @pl.when(step == last)
+        acc[HALO:, :] = part(before[0])
+
+    @pl.when(step > 0)
     def _():
-        acc[HALO:, :] = (acc[HALO:, :] + part()).astype(jnp.bfloat16).astype(jnp.float32)
+        acc[HALO:, :] += part(before[step] + after[step - 1])
+
+    @pl.when(step == count - 1)
+    def _():
+        acc[HALO:, :] = acc[HALO:, :].astype(jnp.bfloat16).astype(jnp.float32)
         for r in range(0, rows, LANES):
             query_t_ref[r : r + LANES, :] = filtered(0, r).astype(query_t_ref.dtype)
             signal = filtered(1, r) * filtered(2, r)
@@ -77,35 +106,51 @@
             signal_ref[:, r : r + LANES] = signal.T.astype(signal_ref.dtype)
 
 
-def project(gathered, in_weight, conv_weight, halo, lo, size, *after):
-    count, rows, step = gathered.shape
+def slot_owner(me, k, count):
+    return lax.rem(me[0] - k + count, count)
+
+
+def project(line, in_weight, conv_weight, halo, lo, size, *following):
+    before, after = line
+    count = len(before)
+    rows, step = before[0].shape
     at = lo // size
     flat = jax.ShapeDtypeStruct((rows, size), jnp.bfloat16)
     shapes = [flat, jax.ShapeDtypeStruct((size, rows), jnp.bfloat16), flat]
+    me = lax.axis_index("chan").astype(jnp.int32).reshape(1)
 
     def weight_of(p):
-        return pl.BlockSpec((1, step, size), lambda z: (p, z, at))
-
-    return pl.pallas_call(
-        lambda *refs: project_kernel(len(after), *refs),
-        grid=(count,),
-        in_specs=[
-            pl.BlockSpec((1, rows, step), lambda z: (z, 0, 0)),
-            *[weight_of(p) for p in range(3)],
-            pl.BlockSpec((TAPS, 3, size), lambda z: (0, 0, at)),
-            pl.BlockSpec((3, HALO, size), lambda z: (0, 0, at)),
-            *[pl.BlockSpec(memory_space=pl.ANY) for _ in after],
-        ],
-        out_specs=[pl.BlockSpec(shape.shape, lambda z: (0, 0)) for shape in shapes],
+        return pl.BlockSpec((1, step, size), lambda z, me: (p, slot_owner(me, z, count), at))
+
+    anywhere = pl.BlockSpec(memory_space=pl.ANY)
+    return pl.pallas_call(
+        lambda *refs: project_kernel(count, len(following), *refs),
+        grid_spec=pltpu.PrefetchScalarGridSpec(
+            num_scalar_prefetch=1,
+            grid=(count,),
+            in_specs=[
+                *[anywhere] * (2 * count - 1),
+                *[weight_of(p) for p in range(3)],
+                pl.BlockSpec((TAPS, 3, size), lambda z, me: (0, 0, at)),
+                pl.BlockSpec((3, HALO, size), lambda z, me: (0, 0, at)),
+                *[anywhere] * len(following),
+            ],
+            out_specs=[pl.BlockSpec(shape.shape, lambda z, me: (0, 0)) for shape in shapes],
+            scratch_shapes=[
+                pltpu.VMEM((count, rows, step), jnp.bfloat16),
+                pltpu.VMEM((count - 1, rows, step), jnp.bfloat16),
+                pltpu.VMEM((HALO + rows, 3 * size), jnp.float32),
+                pltpu.SemaphoreType.DMA((2 * count,)),
+            ],
+        ),
         out_shape=shapes,
-        scratch_shapes=[pltpu.VMEM((HALO + rows, 3 * size), jnp.float32)],
-        compiler_params=pltpu.CompilerParams(vmem_limit_bytes=48 * MIB),
+        compiler_params=pltpu.CompilerParams(vmem_limit_bytes=56 * MIB),
         cost_estimate=pl.CostEstimate(
             flops=2 * 3 * rows * count * step * size,
             bytes_accessed=2 * count * step * (3 * size + rows),
             transcendentals=0,
         ),
-    )(gathered, in_weight, in_weight, in_weight, conv_weight, halo, *after)
+    )(me, *before, *after, in_weight, in_weight, in_weight, conv_weight, halo, *following)
 
 
 def transform_tables(seq_count, tok_rows):
@@ -319,39 +364,51 @@
     return own.reshape(lax.axis_size("chan"), each, own.shape[1])
 
 
-def combine_kernel(gated_ref, w_ref, *refs):
+def combine_kernel(count, me_ref, *refs):
+    before, after, weights = refs[:count], refs[count : 2 * count - 1], refs[2 * count - 1 : 3 * count - 1]
     out_ref = refs[-1]
-    gated = jnp.concatenate([gated_ref[z] for z in range(gated_ref.shape[0])], axis=1)
-    total = jnp.dot(gated, w_ref[0], preferred_element_type=jnp.float32)
-    if len(refs) == 2:
-        total = total + refs[0][...]
+    gated = [before[0][...]] + [before[k][...] + after[count - k - 1][...] for k in range(1, count)]
+    weight = jnp.concatenate([ref[0, 0] for ref in weights], axis=0)
+    total = jnp.dot(jnp.concatenate(gated, axis=1), weight, preferred_element_type=jnp.float32)
+    if len(refs) == 3 * count + 1:
+        total = total + refs[-2][...]
     out_ref[...] = total.astype(out_ref.dtype)
 
 
-def combine(gathered, weight, chunk, total, dtype):
-    count, tok_rows, size = gathered.shape
-    depth = count * size
-    features = weight.shape[2]
+def combine(line, weight, chunk, total, dtype):
+    before, after = line
+    count = len(before)
+    tok_rows, size = before[0].shape
+    features = weight.shape[3]
     tile = min(4 * LANES, features)
-    block = pl.BlockSpec((tok_rows, tile), lambda i: (0, i))
+    whole = pl.BlockSpec((tok_rows, size), lambda i, me: (0, 0))
+    block = pl.BlockSpec((tok_rows, tile), lambda i, me: (0, i))
     given = [] if total is None else [total]
-    return pl.pallas_call(
-        combine_kernel,
-        grid=(features // tile,),
-        in_specs=[
-            pl.BlockSpec((count, tok_rows, size), lambda i: (0, 0, 0)),
-            pl.BlockSpec((1, depth, tile), lambda i: (chunk, 0, i)),
-            *[block for _ in given],
-        ],
-        out_specs=block,
+    me = lax.axis_index("chan").astype(jnp.int32).reshape(1)
+
+    def weight_of(k):
+        return pl.BlockSpec((1, 1, size, tile), lambda i, me: (chunk, slot_owner(me, k, count), 0, i))
+
+    return pl.pallas_call(
+        lambda *refs: combine_kernel(count, *refs),
+        grid_spec=pltpu.PrefetchScalarGridSpec(
+            num_scalar_prefetch=1,
+            grid=(features // tile,),
+            in_specs=[
+                *[whole] * (2 * count - 1),
+                *[weight_of(k) for k in range(count)],
+                *[block for _ in given],
+            ],
+            out_specs=block,
+        ),
         out_shape=jax.ShapeDtypeStruct((tok_rows, features), dtype),
-        compiler_params=pltpu.CompilerParams(vmem_limit_bytes=60 * MIB),
+        compiler_params=pltpu.CompilerParams(vmem_limit_bytes=56 * MIB),
         cost_estimate=pl.CostEstimate(
-            flops=2 * tok_rows * depth * features,
-            bytes_accessed=2 * depth * (tok_rows + features) + 6 * tok_rows * features,
+            flops=2 * tok_rows * size * count * features,
+            bytes_accessed=2 * size * count * (tok_rows + features) + 6 * tok_rows * features,
             transcendentals=0,
         ),
-    )(gathered, weight, *given)
+    )(me, *before, *after, *[weight] * count, *given)
 
 
 def shards(tokens, in_weight, conv_weight, spectrum, skip, out_weight):
@@ -361,17 +418,20 @@
     chans = in_weight.shape[2]
     chunks = chunk_count(chans, seq_count)
     size = chans // chunks
-    gathered = lax.all_gather(tokens, "chan")
+    before, after = along_line(tokens, "chan")
+    near = (before[1], after[0])
+    *near, out_weight, last_rows, spectrum = lax.optimization_barrier(
+        (*near, out_weight, tokens[tok_rows - HALO :], spectrum)
+    )
+    before[1], after[0] = near
     weight = feature_rows(out_weight, seq_count)
-    last_rows = tokens[tok_rows - HALO :]
-    weight, last_rows = lax.optimization_barrier((weight, last_rows))
     halo = gather_by_doubling(from_behind(last_rows, "seq", 1), "chan")
     sent = reordered_spectrum(spectrum, seq_count, chunks)
     halo, sent, weight = lax.optimization_barrier((halo, sent, weight))
     response = folded_response(sent, spectrum.shape[2])
     weight = gather_by_doubling(weight, "seq")
     weight = weight.reshape((chunks, seq_count // chunks) + weight.shape[1:]).transpose(0, 2, 1, 3, 4)
-    weight = weight.reshape(chunks, chan_count * size, weight.shape[4])
+    weight = weight.reshape(chunks, chan_count, size, weight.shape[4])
     halo = jnp.einsum(
         "ztd,pzdc->ptc",
         halo,
@@ -380,14 +440,14 @@
     ).astype(jnp.bfloat16)
     total = None
     for j, lo in enumerate(range(0, chans, size)):
-        given = (gathered, in_weight, conv_weight, halo, lo, size, response, weight)
+        given = ((before, after), in_weight, conv_weight, halo, lo, size, response, weight)
         query_t, signal, signal_t = project(*given)
         values = signal.reshape(seq_count, size // seq_count, tok_rows)
         values = lax.all_to_all(values, "seq", split_axis=0, concat_axis=0, tiled=True)
         longconv = lax.all_to_all(
             long_conv(values, response, lo // seq_count), "seq", split_axis=0, concat_axis=0, tiled=True
         ).reshape(size, tok_rows)
-        gated = lax.all_gather(gate(longconv, skip, lo, signal_t, query_t), "chan")
+        gated = along_line(gate(longconv, skip, lo, signal_t, query_t), "chan")
         dtype = jnp.bfloat16 if lo + size == chans else jnp.float32
         total = combine(gated, weight, j, total, dtype)
     return total

time: 310 us -> 350 us (1.13)
  blocking collectives: 49.7 us -> 0 us
  waiting for transfers between devices: 136 us -> 177 us
  starting transfers between devices: 30.1 us -> 60.8 us
  local copies, waits for them, and re-layouts: 16.8 us -> 32.8 us
  between operations: 13.4 us -> 0.69 us
  Pallas kernels: 54 us -> 60.7 us
  other arithmetic: 3.57 us -> 8.88 us
    ppermute x0 -> x18, waiting for transfers between devices: none -> 141 us  [the longest x9 91.6 us: along_line(): lax.ppermute(after[-1], axis, [(i, i - 1) for i in range(1, size - k + 1)])]
    all_gather x3 -> x0, waiting for transfers between devices: 54.2 us -> none  [the longest x2 44.4 us: shards(): gated = lax.all_gather(gate(longconv, skip, lo, signal_t, query_t), 'chan')]
    all_to_all x4 -> x0, blocking collectives: 49.7 us -> none  [the longest x2 25.4 us: shards(): lax.all_to_all(values, 'seq', split_axis=0, concat_axis=0, tiled=True)]
    all_to_all x1, waiting for transfers between devices: 28.8 us -> 0.85 us  [folded_response(): got = lax.all_to_all(sent, 'seq', split_axis=0, concat_axis=0, tiled=True)]
    ppermute x0 -> x18, starting transfers between devices: none -> 25.2 us  [the longest x9 13.5 us: along_line(): lax.ppermute(before[-1], axis, [(i, i + 1) for i in range(k - 1, size - 1)])]
    all_to_all x1, waiting for transfers between devices: 22.6 us -> 0.01 us  [feature_rows(): own = lax.all_to_all(own, 'chan', split_axis=1, concat_axis=0, tiled=True)]
    unnamed x16 -> x74, local copies, waits for them, and re-layouts: 0.04 us -> 16 us
    all_to_all x0 -> x4, starting transfers between devices: none -> 14.6 us  [the longest x2 7.65 us: shards(): lax.all_to_all(values, 'seq', split_axis=0, concat_axis=0, tiled=True)]
  transfers between devices with their start and end apart: 11 -> 30, of which waited for: 8 -> 19; matrix products, arithmetic and copies ran while one was open for 9% -> 9% of each run, Pallas kernels for 11% -> 12%
where the time goes in v13:
time: 350 us; the launch traced here: 348 us
  waiting for transfers between devices  177 us (51%)
  starting transfers between devices  60.8 us (17%)
  Pallas kernels  60.7 us (17%)
  local copies, waits for them, and re-layouts  32.8 us (9%)
  other arithmetic  8.88 us (3%)
  matrix products  6.95 us (2%)
    ppermute x9, waiting for transfers between devices, along_line(): lax.ppermute(after[-1], axis, [(i, i - 1) for i in range(1, size - k + 1)])  91.6 us
    ppermute x9, waiting for transfers between devices, along_line(): lax.ppermute(before[-1], axis, [(i, i + 1) for i in range(k - 1, size - 1)])  49.3 us
    pallas_call x2, Pallas kernels, project(): pl.pallas_call(lambda *refs: project_kernel(count, len(following), *refs)...  27.4 us
    ppermute x5, waiting for transfers between devices, gather_by_doubling(): other = lax.ppermute(held, axis, [(i, i ^ bit) for i in range(size)])  27 us
    unnamed x74, local copies, waits for them, and re-layouts  16 us
    ppermute x9, starting transfers between devices, along_line(): lax.ppermute(before[-1], axis, [(i, i + 1) for i in range(k - 1, size - 1)])  13.5 us
    pallas_call x2, Pallas kernels, combine(): pl.pallas_call(lambda *refs: combine_kernel(count, *refs), grid_spec=pltp...  13 us
    ppermute x9, starting transfers between devices, along_line(): lax.ppermute(after[-1], axis, [(i, i - 1) for i in range(1, size - k + 1)])  11.7 us
  transfers between devices with their start and end apart: 30, of which 19 were waited for; matrix products, arithmetic and copies ran while one was open for 9% of the time, Pallas kernels for 12%

profile of v13, /device:TPU:0, one launch (start us, length us, event | category | flops | bytes accessed | tf_op | source)
XLA Modules:
  0.0 348.0 jit_solution(6758195139178322061)
XLA Ops:
  0.0 5.1 %collective-permute-start = (bf16[1024,1024]{1,0:T(8,128)(2,1)}, bf16[1024,1024]{1,0:T(8,128)(2,1)S(1)}, u32[]{:S(2)}, u32[]{:S(2)}) collective-permute-start(bf16[1024,1024]{1,0:T(8,128)(2,1)} %refs_1_.3), channel_id=1, source_target_pairs={{0,1},{1,2},{2,3},{4,5},{5,6},{6,7},{8,9},{9,10},{10,11},{12,13},{... | collective-permute-start | bytes 6291464 | tf_op jit(solution)/shard_map/ppermute | solution.py:27
  5.1 1.3 collective-permute-start.1
  7.2 43.0 %collective-permute-done.refs_2_ = bf16[1024,1024]{1,0:T(8,128)(2,1)S(1)} collective-permute-done((bf16[1024,1024]{1,0:T(8,128)(2,1)}, bf16[1024,1024]{1,0:T(8,128)(2,1)S(1)}, u32[]{:S(2)}, u32[]{:S(2)}) %collective-permute-start) | collective-permute-done | bytes 2097184 | tf_op jit(solution)/shard_map/ppermute | solution.py:27
  50.1 4.2 %collective-permute-done.1.refs_5_ = bf16[1024,1024]{1,0:T(8,128)(2,1)} collective-permute-done((bf16[1024,1024]{1,0:T(8,128)(2,1)}, bf16[1024,1024]{1,0:T(8,128)(2,1)}, u32[]{:S(2)}, u32[]{:S(2)}) %collective-permute-start.1) | collective-permute-done | bytes 2097184 | tf_op jit(solution)/shard_map/ppermute | solution.py:28
  54.4 1.3 collective-permute-start.6
  56.5 2.5 collective-permute-start.7
  59.0 1.1 constant_dynamic-slice_fusion
  60.9 3.5 all-to-all-start
  64.4 10.9 %reshape.47.spec_ref = f32[2,1024,1024]{2,1,0:T(8,128)} reshape(f32[2,512,2,1024]{3,2,1,0:T(2,128)} %param.21) | data formatting | bytes 16777216 | tf_op jit(solution)/shard_map/reshape | solution.py:335
  75.4 2.0 collective-permute-start.8
  77.4 8.5 %shard_map.172 = bf16[8,2,2,64,1024]{4,3,2,1,0:T(8,128)(2,1)} custom-call(f32[2,1024,1024]{2,1,0:T(8,128)} %reshape.47.spec_ref, bf16[1024,1024]{1,0:T(8,128)(2,1)S(1)} %fusion.1.order_ref), custom_call_target="tpu_custom_call" | custom-call | flops 4294967296 | bytes 12582912 | tf_op jit(solution)/shard_map/pallas_call | solution.py:322
  86.0 5.6 %collective-permute-start.9 = (bf16[1,4,64,1024]{3,2,1,0:T(8,128)(2,1)S(1)}, bf16[1,4,64,1024]{3,2,1,0:T(8,128)(2,1)}, u32[]{:S(2)}, u32[]{:S(2)}) collective-permute-start(bf16[1,4,64,1024]{3,2,1,0:T(8,128)(2,1)S(1)} %bitcast.91), channel_id=1, source_target_pairs={{0,16},{4,20},{8,24},{12,28},{16,0},{20,4},{24,8},{28,12},{1,17},{... | collective-permute-start | bytes 1572872 | tf_op jit(solution)/shard_map/ppermute | solution.py:38
  91.5 10.0 %collective-permute-done.9 = bf16[1,4,64,1024]{3,2,1,0:T(8,128)(2,1)} collective-permute-done((bf16[1,4,64,1024]{3,2,1,0:T(8,128)(2,1)S(1)}, bf16[1,4,64,1024]{3,2,1,0:T(8,128)(2,1)}, u32[]{:S(2)}, u32[]{:S(2)}) %collective-permute-start.9) | collective-permute-done | bytes 524320 | tf_op jit(solution)/shard_map/ppermute | solution.py:38
  101.5 1.3 select_bitcast_fusion.5
  102.8 1.1 maximum_bitcast_fusion
  103.9 1.5 collective-permute-start.10
  105.4 2.0 collective-permute-start.2
  107.3 1.3 collective-permute-start.4
  108.6 4.6 %all-to-all-start.1 = ((bf16[8,2,2,64,1024]{4,3,2,1,0:T(8,128)(2,1)}), bf16[8,2,2,64,1024]{4,3,2,1,0:T(8,128)(2,1)}, u32[]{:S(2)}, u32[]{:S(2)}) async-start(bf16[8,2,2,64,1024]{4,3,2,1,0:T(8,128)(2,1)} %shard_map.172), calls=%async_computation.1 | async-start | bytes 8388608 | tf_op jit(solution)/shard_map/all_to_all | solution.py:342
  113.3 17.0 %collective-permute-done.10 = bf16[2,4,64,1024]{3,2,1,0:T(8,128)(2,1)} collective-permute-done((bf16[2,4,64,1024]{3,2,1,0:T(8,128)(2,1)}, bf16[2,4,64,1024]{3,2,1,0:T(8,128)(2,1)}, u32[]{:S(2)}, u32[]{:S(2)}) %collective-permute-start.10) | collective-permute-done | bytes 1048608 | tf_op jit(solution)/shard_map/ppermute | solution.py:38
  130.3 1.4 select_bitcast_fusion.3
  131.7 1.5 pad_maximum_fusion.1
  133.9 22.6 %collective-permute-done.4.refs_6_ = bf16[1024,1024]{1,0:T(8,128)(2,1)} collective-permute-done((bf16[1024,1024]{1,0:T(8,128)(2,1)}, bf16[1024,1024]{1,0:T(8,128)(2,1)}, u32[]{:S(2)}, u32[]{:S(2)}) %collective-permute-start.4) | collective-permute-done | bytes 2097184 | tf_op jit(solution)/shard_map/ppermute | solution.py:28
  156.5 1.5 collective-permute-start.5
  158.0 6.9 %fusion.3.refs_12_ = bf16[3,16,512]{2,1,0:T(8,128)(2,1)} fusion(bf16[3,4,1024,512]{3,2,1,0:T(8,128)(2,1)} %bitcast.79, bf16[4,16,1024]{2,1,0:T(8,128)(2,1)S(1)} %bitcast.94), kind=kOutput, calls=%fused_computation.9 | convolution fusion | flops 201351168 | bytes 12763136 | tf_op jit(solution)/shard_map/ztd,pzdc->ptc/dot_general | solution.py:435
  164.9 2.5 select_bitcast_fusion.1
  168.5 2.4 copy.31
  171.8 4.0 %shard_map.173.refs_13_.resp_ref = bf16[2,64,72,128]{3,2,1,0:T(8,128)(2,1)S(1)} custom-call(bf16[8,2,2,64,1024]{4,3,2,1,0:T(8,128)(2,1)} %all-to-all-done.1.got_ref), custom_call_target="tpu_custom_call" | custom-call | flops 2097152 | bytes 6291456 | tf_op jit(solution)/shard_map/pallas_call | solution.py:345
  175.9 1.4 copy-done
  177.3 25.3 %collective-permute-done.5.refs_7_ = bf16[1024,1024]{1,0:T(8,128)(2,1)} collective-permute-done((bf16[1024,1024]{1,0:T(8,128)(2,1)}, bf16[1024,1024]{1,0:T(8,128)(2,1)}, u32[]{:S(2)}, u32[]{:S(2)}) %collective-permute-start.5) | collective-permute-done | bytes 2097184 | tf_op jit(solution)/shard_map/ppermute | solution.py:28
  202.6 13.6 %shard_map.177 = (bf16[1024,256]{1,0:T(8,128)(2,1)}, bf16[256,1024]{1,0:T(8,128)(2,1)}, bf16[1024,256]{1,0:T(8,128)(2,1)}) custom-call(s32[1]{0:T(128)} %bitcast.refs_0_, bf16[1024,1024]{1,0:T(8,128)(2,1)} %refs_1_.3, bf16[1024,1024]{1,0:T(8,128)(2,1)} %copy-done.21, bf16[1024,1024]{1,0:T(8,128)(2,1)} %collective-permute-done.2.refs_3_, ...), custom_call_target="tpu_custom_call" | custom-call | flops 6442450944 | bytes 14680064 | tf_op jit(solution)/shard_map/pallas_call | solution.py:126
  216.2 3.5 %all-to-all-start.4 = ((bf16[8,32,1024]{2,1,0:T(8,128)(2,1)}), bf16[8,32,1024]{2,1,0:T(8,128)(2,1)S(1)}, u32[]{:S(2)}, u32[]{:S(2)}) async-start(bf16[8,32,1024]{2,1,0:T(8,128)(2,1)} %bitcast.96), calls=%async_computation.4 | async-start | bytes 1048576 | tf_op jit(solution)/shard_map/all_to_all | solution.py:446
  219.7 13.8 %shard_map.174 = (bf16[1024,256]{1,0:T(8,128)(2,1)}, bf16[256,1024]{1,0:T(8,128)(2,1)}, bf16[1024,256]{1,0:T(8,128)(2,1)}) custom-call(s32[1]{0:T(128)} %bitcast.refs_0_, bf16[1024,1024]{1,0:T(8,128)(2,1)} %refs_1_.3, bf16[1024,1024]{1,0:T(8,128)(2,1)} %copy-done.21, bf16[1024,1024]{1,0:T(8,128)(2,1)} %collective-permute-done.2.refs_3_, ...), custom_call_target="tpu_custom_call" | custom-call | flops 6442450944 | bytes 14680064 | tf_op jit(solution)/shard_map/pallas_call | solution.py:126
  233.5 4.1 %all-to-all-start.2 = ((bf16[8,32,1024]{2,1,0:T(8,128)(2,1)}), bf16[8,32,1024]{2,1,0:T(8,128)(2,1)S(1)}, u32[]{:S(2)}, u32[]{:S(2)}) async-start(bf16[8,32,1024]{2,1,0:T(8,128)(2,1)} %bitcast.95), calls=%async_computation.2 | async-start | bytes 1048576 | tf_op jit(solution)/shard_map/all_to_all | solution.py:446
  237.7 0.9 copy-done.10
  241.7 2.9 shard_map.178
  245.4 2.0 all-to-all-done.2.signal_ref
  247.4 3.5 %all-to-all-start.5 = ((bf16[8,32,1024]{2,1,0:T(8,128)(2,1)}), bf16[8,32,1024]{2,1,0:T(8,128)(2,1)S(1)}, u32[]{:S(2)}, u32[]{:S(2)}) async-start(bf16[8,32,1024]{2,1,0:T(8,128)(2,1)} %copy-done.4), calls=%async_computation.5 | async-start | bytes 1048576 | tf_op jit(solution)/shard_map/all_to_all | solution.py:447
  254.9 3.6 %shard_map.175 = bf16[8,32,1024]{2,1,0:T(8,128)(2,1)} custom-call(bf16[8,32,1024]{2,1,0:T(8,128)(2,1)S(1)} %all-to-all-done.2.signal_ref, bf16[2,64,72,128]{3,2,1,0:T(8,128)(2,1)S(1)} %copy-done.1, bf16[144,64]{1,0:T(8,128)(2,1)S(1)} %copy-done.13, bf16[64,144]{1,0:T(8,128)(2,1)S(1)} %copy-done.19, f32[72,128]{1,0:T(8,128)S(1)} %copy-done.15, ...), custom_call_target="tpu_custom_call" | custom-call | flops 754974720 | bytes 2228224 | tf_op jit(solution)/shard_map/pallas_call | solution.py:233
  258.5 2.1 all-to-all-done.5
  260.6 3.5 %all-to-all-start.3 = ((bf16[8,32,1024]{2,1,0:T(8,128)(2,1)}), bf16[8,32,1024]{2,1,0:T(8,128)(2,1)S(1)}, u32[]{:S(2)}, u32[]{:S(2)}) async-start(bf16[8,32,1024]{2,1,0:T(8,128)(2,1)} %shard_map.175), calls=%async_computation.3 | async-start | bytes 1048576 | tf_op jit(solution)/shard_map/all_to_all | solution.py:447
  264.1 1.0 copy-done.7
  265.2 1.0 copy-done.8
  266.8 1.5 collective-permute-start.18
  268.3 1.3 collective-permute-start.21
  269.6 4.2 %all-to-all-done.3 = bf16[8,32,1024]{2,1,0:T(8,128)(2,1)S(1)} async-done(((bf16[8,32,1024]{2,1,0:T(8,128)(2,1)}), bf16[8,32,1024]{2,1,0:T(8,128)(2,1)S(1)}, u32[]{:S(2)}, u32[]{:S(2)}) %all-to-all-start.3) | async-done | bytes 524320 | tf_op jit(solution)/shard_map/all_to_all | solution.py:447
  273.8 1.0 copy-done.5
  274.8 1.0 copy-done.6
  276.5 1.5 collective-permute-start.12
  278.0 1.3 collective-permute-start.15
  279.3 1.2 collective-permute-done.18.refs_2_
  281.2 3.8 %collective-permute-done.21.refs_5_ = bf16[1024,256]{1,0:T(8,128)(2,1)S(1)} collective-permute-done((bf16[1024,256]{1,0:T(8,128)(2,1)S(1)}, bf16[1024,256]{1,0:T(8,128)(2,1)S(1)}, u32[]{:S(2)}, u32[]{:S(2)}) %collective-permute-start.21) | collective-permute-done | bytes 524320 | tf_op jit(solution)/shard_map/ppermute | solution.py:28
  284.9 1.3 collective-permute-start.22
  286.2 5.1 %collective-permute-done.12.refs_2_ = bf16[1024,256]{1,0:T(8,128)(2,1)S(1)} collective-permute-done((bf16[1024,256]{1,0:T(8,128)(2,1)S(1)}, bf16[1024,256]{1,0:T(8,128)(2,1)S(1)}, u32[]{:S(2)}, u32[]{:S(2)}) %collective-permute-start.12) | collective-permute-done | bytes 524320 | tf_op jit(solution)/shard_map/ppermute | solution.py:27
  292.1 4.1 %collective-permute-done.15.refs_5_ = bf16[1024,256]{1,0:T(8,128)(2,1)S(1)} collective-permute-done((bf16[1024,256]{1,0:T(8,128)(2,1)S(1)}, bf16[1024,256]{1,0:T(8,128)(2,1)S(1)}, u32[]{:S(2)}, u32[]{:S(2)}) %collective-permute-start.15) | collective-permute-done | bytes 524320 | tf_op jit(solution)/shard_map/ppermute | solution.py:28
  296.2 1.3 collective-permute-start.16
  298.2 9.2 %collective-permute-done.22.refs_6_ = bf16[1024,256]{1,0:T(8,128)(2,1)S(1)} collective-permute-done((bf16[1024,256]{1,0:T(8,128)(2,1)S(1)}, bf16[1024,256]{1,0:T(8,128)(2,1)S(1)}, u32[]{:S(2)}, u32[]{:S(2)}) %collective-permute-start.22) | collective-permute-done | bytes 524320 | tf_op jit(solution)/shard_map/ppermute | solution.py:28
  307.4 1.3 collective-permute-start.23
  309.4 9.2 %collective-permute-done.16.refs_6_ = bf16[1024,256]{1,0:T(8,128)(2,1)S(1)} collective-permute-done((bf16[1024,256]{1,0:T(8,128)(2,1)S(1)}, bf16[1024,256]{1,0:T(8,128)(2,1)S(1)}, u32[]{:S(2)}, u32[]{:S(2)}) %collective-permute-start.16) | collective-permute-done | bytes 524320 | tf_op jit(solution)/shard_map/ppermute | solution.py:28
  318.6 1.3 collective-permute-start.17
  320.0 9.9 %collective-permute-done.23.refs_7_ = bf16[1024,256]{1,0:T(8,128)(2,1)S(1)} collective-permute-done((bf16[1024,256]{1,0:T(8,128)(2,1)S(1)}, bf16[1024,256]{1,0:T(8,128)(2,1)S(1)}, u32[]{:S(2)}, u32[]{:S(2)}) %collective-permute-start.23) | collective-permute-done | bytes 524320 | tf_op jit(solution)/shard_map/ppermute | solution.py:28
  330.7 6.4 %shard_map.180.refs_12_ = f32[1024,1024]{1,0:T(8,128)} custom-call(s32[1]{0:T(128)} %bitcast.refs_0_, bf16[1024,256]{1,0:T(8,128)(2,1)} %copy-done.2, bf16[1024,256]{1,0:T(8,128)(2,1)} %copy-done.25, bf16[1024,256]{1,0:T(8,128)(2,1)} %copy-done.30, bf16[1024,256]{1,0:T(8,128)(2,1)} %copy-done.34, bf16[1024,256]{1,0:T(8,128)(2,1)} %copy-done.27, ...), custom_call_target="tpu_custom_call" | custom-call | flops 2147483648 | bytes 10485760 | tf_op jit(solution)/shard_map/pallas_call | solution.py:392
  337.2 3.3 collective-permute-done.17.refs_7_
  341.3 6.7 %shard_map.181 = bf16[1024,1024]{1,0:T(8,128)(2,1)} custom-call(s32[1]{0:T(128)} %bitcast.refs_0_, bf16[1024,256]{1,0:T(8,128)(2,1)} %copy-done.3, bf16[1024,256]{1,0:T(8,128)(2,1)} %copy-done.26, bf16[1024,256]{1,0:T(8,128)(2,1)} %copy-done.29, bf16[1024,256]{1,0:T(8,128)(2,1)} %copy-done.33, bf16[1024,256]{1,0:T(8,128)(2,1)} %copy-done.28, ...), custom_call_target="tpu_custom_call" | custom-call | flops 2147483648 | bytes 10485760 | tf_op jit(solution)/shard_map/pallas_call | solution.py:392
  (101 shorter events, 18.7 us)
Async XLA Ops:
  0.0 50.1 %collective-permute-start = (bf16[1024,1024]{1,0:T(8,128)(2,1)}, bf16[1024,1024]{1,0:T(8,128)(2,1)S(1)}, u32[]{:S(2)}, u32[]{:S(2)}) collective-permute-start(bf16[1024,1024]{1,0:T(8,128)(2,1)} %refs_1_.3), channel_id=1, source_target_pairs={{0,1},{1,2},{2,3},{4,5},{5,6},{6,7},{8,9},{9,10},{10,11},{12,13},{... | collective-permute-start | bytes 6291464 | tf_op jit(solution)/shard_map/ppermute | solution.py:27
  5.1 49.3 %collective-permute-start.1 = (bf16[1024,1024]{1,0:T(8,128)(2,1)}, bf16[1024,1024]{1,0:T(8,128)(2,1)}, u32[]{:S(2)}, u32[]{:S(2)}) collective-permute-start(bf16[1024,1024]{1,0:T(8,128)(2,1)} %refs_1_.3), channel_id=1, source_target_pairs={{1,0},{2,1},{3,2},{5,4},{6,5},{7,6},{9,8},{10,9},{11,10},{13,12},{... | collective-permute-start | bytes 6291464 | tf_op jit(solution)/shard_map/ppermute | solution.py:28
  50.1 5.5 %copy-start.21 = (bf16[1024,1024]{1,0:T(8,128)(2,1)}, bf16[1024,1024]{1,0:T(8,128)(2,1)S(1)}, u32[]{:S(2)}) copy-start(bf16[1024,1024]{1,0:T(8,128)(2,1)S(1)} %collective-permute-done.refs_2_) | copy-start | bytes 6291460
  54.4 2.1 collective-permute-start.6
  56.5 18.8 %collective-permute-start.7 = (bf16[1,16,1024]{2,1,0:T(8,128)(2,1)S(1)}, bf16[1,16,1024]{2,1,0:T(8,128)(2,1)S(1)}, u32[]{:S(2)}, u32[]{:S(2)}) collective-permute-start(bf16[1,16,1024]{2,1,0:T(8,128)(2,1)S(1)} %bitcast.97), channel_id=1, source_target_pairs={{0,2},{1,3},{2,0},{3,1},{4,6},{5,7},{6,4},{7,5},{8,10},{9,11},{10,... | collective-permute-start | bytes 98312 | tf_op jit(solution)/shard_map/ppermute | solution.py:38
  60.9 25.0 %all-to-all-start = ((bf16[64,4,1024]{2,0,1:T(8,128)(2,1)}), bf16[64,4,1024]{2,0,1:T(8,128)(2,1)S(1)}, u32[]{:S(2)}, u32[]{:S(2)}) async-start(bf16[64,4,1024]{2,0,1:T(8,128)(2,1)} %bitcast.74), calls=%async_computation | async-start | bytes 1048576 | tf_op jit(solution)/shard_map/all_to_all | solution.py:363
  75.4 10.6 %collective-permute-start.8 = (bf16[2,16,1024]{2,1,0:T(8,128)(2,1)S(1)}, bf16[2,16,1024]{2,1,0:T(8,128)(2,1)S(1)}, u32[]{:S(2)}, u32[]{:S(2)}) collective-permute-start(bf16[2,16,1024]{2,1,0:T(8,128)(2,1)S(1)} %maximum_bitcast_fusion.1), channel_id=1, source_target_pairs={{0,1},{1,0},{2,3},{3,2},{4,5},{5,4},{6,7},{7,6},{8,9},{9,8},{10,11... | collective-permute-start | bytes 196616 | tf_op jit(solution)/shard_map/ppermute | solution.py:38
  85.9 19.5 %copy-start.22 = (bf16[1024,1024]{1,0:T(8,128)(2,1)S(1)}, bf16[1024,1024]{1,0:T(8,128)(2,1)}, u32[]{:S(2)}) copy-start(bf16[1024,1024]{1,0:T(8,128)(2,1)} %copy-done.21) | copy-start | bytes 6291460
  86.0 5.6 %copy-start.24 = (bf16[64,4,1024]{2,0,1:T(8,128)(2,1)}, bf16[64,4,1024]{2,0,1:T(8,128)(2,1)S(1)}, u32[]{:S(2)}) copy-start(bf16[64,4,1024]{2,0,1:T(8,128)(2,1)S(1)} %all-to-all-done) | copy-start | bytes 1572868
  86.0 15.5 %collective-permute-start.9 = (bf16[1,4,64,1024]{3,2,1,0:T(8,128)(2,1)S(1)}, bf16[1,4,64,1024]{3,2,1,0:T(8,128)(2,1)}, u32[]{:S(2)}, u32[]{:S(2)}) collective-permute-start(bf16[1,4,64,1024]{3,2,1,0:T(8,128)(2,1)S(1)} %bitcast.91), channel_id=1, source_target_pairs={{0,16},{4,20},{8,24},{12,28},{16,0},{20,4},{24,8},{28,12},{1,17},{... | collective-permute-start | bytes 1572872 | tf_op jit(solution)/shard_map/ppermute | solution.py:38
  103.9 26.4 %collective-permute-start.10 = (bf16[2,4,64,1024]{3,2,1,0:T(8,128)(2,1)}, bf16[2,4,64,1024]{3,2,1,0:T(8,128)(2,1)}, u32[]{:S(2)}, u32[]{:S(2)}) collective-permute-start(bf16[2,4,64,1024]{3,2,1,0:T(8,128)(2,1)} %maximum_bitcast_fusion), channel_id=1, source_target_pairs={{0,8},{4,12},{8,0},{12,4},{16,24},{20,28},{24,16},{28,20},{1,9},{5... | collective-permute-start | bytes 3145736 | tf_op jit(solution)/shard_map/ppermute | solution.py:38
  105.4 27.8 %collective-permute-start.2 = (bf16[1024,1024]{1,0:T(8,128)(2,1)S(1)}, bf16[1024,1024]{1,0:T(8,128)(2,1)}, u32[]{:S(2)}, u32[]{:S(2)}) collective-permute-start(bf16[1024,1024]{1,0:T(8,128)(2,1)S(1)} %copy-done.22), channel_id=1, source_target_pairs={{1,2},{2,3},{5,6},{6,7},{9,10},{10,11},{13,14},{14,15},{17,18},{18... | collective-permute-start | bytes 6291464 | tf_op jit(solution)/shard_map/ppermute | solution.py:27
  107.3 49.1 %collective-permute-start.4 = (bf16[1024,1024]{1,0:T(8,128)(2,1)}, bf16[1024,1024]{1,0:T(8,128)(2,1)}, u32[]{:S(2)}, u32[]{:S(2)}) collective-permute-start(bf16[1024,1024]{1,0:T(8,128)(2,1)} %collective-permute-done.1.refs_5_), channel_id=1, source_target_pairs={{1,0},{2,1},{5,4},{6,5},{9,8},{10,9},{13,12},{14,13},{17,16},{18,1... | collective-permute-start | bytes 6291464 | tf_op jit(solution)/shard_map/ppermute | solution.py:28
  108.6 63.2 %all-to-all-start.1 = ((bf16[8,2,2,64,1024]{4,3,2,1,0:T(8,128)(2,1)}), bf16[8,2,2,64,1024]{4,3,2,1,0:T(8,128)(2,1)}, u32[]{:S(2)}, u32[]{:S(2)}) async-start(bf16[8,2,2,64,1024]{4,3,2,1,0:T(8,128)(2,1)} %shard_map.172), calls=%async_computation.1 | async-start | bytes 8388608 | tf_op jit(solution)/shard_map/all_to_all | solution.py:342
  133.1 31.8 %collective-permute-start.11 = (bf16[4,4,64,1024]{3,2,1,0:T(8,128)(2,1)}, bf16[4,4,64,1024]{3,2,1,0:T(8,128)(2,1)}, u32[]{:S(2)}, u32[]{:S(2)}) collective-permute-start(bf16[4,4,64,1024]{3,2,1,0:T(8,128)(2,1)} %bitcast.22), channel_id=1, source_target_pairs={{0,4},{4,0},{8,12},{12,8},{16,20},{20,16},{24,28},{28,24},{1,5},{5... | collective-permute-start | bytes 6291464 | tf_op jit(solution)/shard_map/ppermute | solution.py:38
  133.1 44.1 %collective-permute-start.3 = (bf16[1024,1024]{1,0:T(8,128)(2,1)}, bf16[1024,1024]{1,0:T(8,128)(2,1)S(1)}, u32[]{:S(2)}, u32[]{:S(2)}) collective-permute-start(bf16[1024,1024]{1,0:T(8,128)(2,1)} %collective-permute-done.2.refs_3_), channel_id=1, source_target_pairs={{2,3},{6,7},{10,11},{14,15},{18,19},{22,23},{26,27},{30,31}} | collective-permute-start | bytes 6291464 | tf_op jit(solution)/shard_map/ppermute | solution.py:27
  156.5 46.1 %collective-permute-start.5 = (bf16[1024,1024]{1,0:T(8,128)(2,1)}, bf16[1024,1024]{1,0:T(8,128)(2,1)}, u32[]{:S(2)}, u32[]{:S(2)}) collective-permute-start(bf16[1024,1024]{1,0:T(8,128)(2,1)} %collective-permute-done.4.refs_6_), channel_id=1, source_target_pairs={{1,0},{5,4},{9,8},{13,12},{17,16},{21,20},{25,24},{29,28}} | collective-permute-start | bytes 6291464 | tf_op jit(solution)/shard_map/ppermute | solution.py:28
  175.9 1.4 copy-start
  177.3 25.3 %copy-start.23 = (bf16[1024,1024]{1,0:T(8,128)(2,1)}, bf16[1024,1024]{1,0:T(8,128)(2,1)S(1)}, u32[]{:S(2)}) copy-start(bf16[1024,1024]{1,0:T(8,128)(2,1)S(1)} %collective-permute-done.3.refs_4_) | copy-start | bytes 6291460
  216.2 17.4 %all-to-all-start.4 = ((bf16[8,32,1024]{2,1,0:T(8,128)(2,1)}), bf16[8,32,1024]{2,1,0:T(8,128)(2,1)S(1)}, u32[]{:S(2)}, u32[]{:S(2)}) async-start(bf16[8,32,1024]{2,1,0:T(8,128)(2,1)} %bitcast.96), calls=%async_computation.4 | async-start | bytes 1048576 | tf_op jit(solution)/shard_map/all_to_all | solution.py:446
  219.7 18.0 %copy-start.1 = (bf16[2,64,72,128]{3,2,1,0:T(8,128)(2,1)S(1)}, bf16[2,64,72,128]{3,2,1,0:T(8,128)(2,1)}, u32[]{:S(2)}) copy-start(bf16[2,64,72,128]{3,2,1,0:T(8,128)(2,1)} %copy-done) | copy-start | bytes 7077892
  219.7 18.0 %copy-start.9 = (bf16[256,256]{1,0:T(8,128)(2,1)S(1)}, bf16[256,256]{1,0:T(8,128)(2,1)}, u32[]{:S(2)}) copy-start(bf16[256,256]{1,0:T(8,128)(2,1)} %constant.138.clone.fwd_ref) | copy-start | bytes 393220
  233.5 13.9 %all-to-all-start.2 = ((bf16[8,32,1024]{2,1,0:T(8,128)(2,1)}), bf16[8,32,1024]{2,1,0:T(8,128)(2,1)S(1)}, u32[]{:S(2)}, u32[]{:S(2)}) async-start(bf16[8,32,1024]{2,1,0:T(8,128)(2,1)} %bitcast.95), calls=%async_computation.2 | async-start | bytes 1048576 | tf_op jit(solution)/shard_map/all_to_all | solution.py:446
  237.7 0.9 copy-start.10
  238.6 0.8 copy-start.12
  239.4 0.8 copy-start.14
  240.1 0.8 copy-start.16
  241.7 22.4 %copy-start.20 = (f32[512]{0:T(512)S(1)}, f32[512]{0:T(512)}, u32[]{:S(2)}) copy-start(f32[512]{0:T(512)} %param.22) | copy-start | bytes 6148
  244.6 0.8 copy-start.4
  247.4 13.2 %all-to-all-start.5 = ((bf16[8,32,1024]{2,1,0:T(8,128)(2,1)}), bf16[8,32,1024]{2,1,0:T(8,128)(2,1)S(1)}, u32[]{:S(2)}, u32[]{:S(2)}) async-start(bf16[8,32,1024]{2,1,0:T(8,128)(2,1)} %copy-done.4), calls=%async_computation.5 | async-start | bytes 1048576 | tf_op jit(solution)/shard_map/all_to_all | solution.py:447
  250.9 0.9 copy-start.11
  251.8 0.8 copy-start.13
  252.6 0.8 copy-start.15
  260.6 13.2 %all-to-all-start.3 = ((bf16[8,32,1024]{2,1,0:T(8,128)(2,1)}), bf16[8,32,1024]{2,1,0:T(8,128)(2,1)S(1)}, u32[]{:S(2)}, u32[]{:S(2)}) async-start(bf16[8,32,1024]{2,1,0:T(8,128)(2,1)} %shard_map.175), calls=%async_computation.3 | async-start | bytes 1048576 | tf_op jit(solution)/shard_map/all_to_all | solution.py:447
  264.1 1.0 copy-start.7
  265.2 1.0 copy-start.8
  266.8 63.1 %copy-start.2 = (bf16[1024,256]{1,0:T(8,128)(2,1)}, bf16[1024,256]{1,0:T(8,128)(2,1)S(1)}, u32[]{:S(2)}) copy-start(bf16[1024,256]{1,0:T(8,128)(2,1)S(1)} %shard_map.179.refs_1_) | copy-start | bytes 1572868
  266.8 13.7 %collective-permute-start.18 = (bf16[1024,256]{1,0:T(8,128)(2,1)S(1)}, bf16[1024,256]{1,0:T(8,128)(2,1)S(1)}, u32[]{:S(2)}, u32[]{:S(2)}) collective-permute-start(bf16[1024,256]{1,0:T(8,128)(2,1)S(1)} %shard_map.179.refs_1_), channel_id=1, source_target_pairs={{0,1},{1,2},{2,3},{4,5},{5,6},{6,7},{8,9},{9,10},{10,11},{12,13},{... | collective-permute-start | bytes 1572872 | tf_op jit(solution)/shard_map/ppermute | solution.py:27
  268.3 16.6 %collective-permute-start.21 = (bf16[1024,256]{1,0:T(8,128)(2,1)S(1)}, bf16[1024,256]{1,0:T(8,128)(2,1)S(1)}, u32[]{:S(2)}, u32[]{:S(2)}) collective-permute-start(bf16[1024,256]{1,0:T(8,128)(2,1)S(1)} %shard_map.179.refs_1_), channel_id=1, source_target_pairs={{1,0},{2,1},{3,2},{5,4},{6,5},{7,6},{9,8},{10,9},{11,10},{13,12},{... | collective-permute-start | bytes 1572872 | tf_op jit(solution)/shard_map/ppermute | solution.py:28
  273.8 1.0 copy-start.5
  274.8 1.0 copy-start.6
  276.5 60.6 %copy-start.3 = (bf16[1024,256]{1,0:T(8,128)(2,1)}, bf16[1024,256]{1,0:T(8,128)(2,1)S(1)}, u32[]{:S(2)}) copy-start(bf16[1024,256]{1,0:T(8,128)(2,1)S(1)} %shard_map.176.refs_1_) | copy-start | bytes 1572868
  276.5 14.9 %collective-permute-start.12 = (bf16[1024,256]{1,0:T(8,128)(2,1)S(1)}, bf16[1024,256]{1,0:T(8,128)(2,1)S(1)}, u32[]{:S(2)}, u32[]{:S(2)}) collective-permute-start(bf16[1024,256]{1,0:T(8,128)(2,1)S(1)} %shard_map.176.refs_1_), channel_id=1, source_target_pairs={{0,1},{1,2},{2,3},{4,5},{5,6},{6,7},{8,9},{9,10},{10,11},{12,13},{... | collective-permute-start | bytes 1572872 | tf_op jit(solution)/shard_map/ppermute | solution.py:27
  278.0 18.2 %collective-permute-start.15 = (bf16[1024,256]{1,0:T(8,128)(2,1)S(1)}, bf16[1024,256]{1,0:T(8,128)(2,1)S(1)}, u32[]{:S(2)}, u32[]{:S(2)}) collective-permute-start(bf16[1024,256]{1,0:T(8,128)(2,1)S(1)} %shard_map.176.refs_1_), channel_id=1, source_target_pairs={{1,0},{2,1},{3,2},{5,4},{6,5},{7,6},{9,8},{10,9},{11,10},{13,12},{... | collective-permute-start | bytes 1572872 | tf_op jit(solution)/shard_map/ppermute | solution.py:28
  280.5 49.4 %copy-start.25 = (bf16[1024,256]{1,0:T(8,128)(2,1)}, bf16[1024,256]{1,0:T(8,128)(2,1)S(1)}, u32[]{:S(2)}) copy-start(bf16[1024,256]{1,0:T(8,128)(2,1)S(1)} %collective-permute-done.18.refs_2_) | copy-start | bytes 1572868
  280.5 17.0 %collective-permute-start.19 = (bf16[1024,256]{1,0:T(8,128)(2,1)S(1)}, bf16[1024,256]{1,0:T(8,128)(2,1)S(1)}, u32[]{:S(2)}, u32[]{:S(2)}) collective-permute-start(bf16[1024,256]{1,0:T(8,128)(2,1)S(1)} %collective-permute-done.18.refs_2_), channel_id=1, source_target_pairs={{1,2},{2,3},{5,6},{6,7},{9,10},{10,11},{13,14},{14,15},{17,18},{18... | collective-permute-start | bytes 1572872 | tf_op jit(solution)/shard_map/ppermute | solution.py:27
  284.9 44.9 %copy-start.27 = (bf16[1024,256]{1,0:T(8,128)(2,1)}, bf16[1024,256]{1,0:T(8,128)(2,1)S(1)}, u32[]{:S(2)}) copy-start(bf16[1024,256]{1,0:T(8,128)(2,1)S(1)} %collective-permute-done.21.refs_5_) | copy-start | bytes 1572868
  284.9 22.5 %collective-permute-start.22 = (bf16[1024,256]{1,0:T(8,128)(2,1)S(1)}, bf16[1024,256]{1,0:T(8,128)(2,1)S(1)}, u32[]{:S(2)}, u32[]{:S(2)}) collective-permute-start(bf16[1024,256]{1,0:T(8,128)(2,1)S(1)} %collective-permute-done.21.refs_5_), channel_id=1, source_target_pairs={{1,0},{2,1},{5,4},{6,5},{9,8},{10,9},{13,12},{14,13},{17,16},{18,1... | collective-permute-start | bytes 1572872 | tf_op jit(solution)/shard_map/ppermute | solution.py:28
  291.4 45.7 %copy-start.26 = (bf16[1024,256]{1,0:T(8,128)(2,1)}, bf16[1024,256]{1,0:T(8,128)(2,1)S(1)}, u32[]{:S(2)}) copy-start(bf16[1024,256]{1,0:T(8,128)(2,1)S(1)} %collective-permute-done.12.refs_2_) | copy-start | bytes 1572868
  291.4 17.3 %collective-permute-start.13 = (bf16[1024,256]{1,0:T(8,128)(2,1)S(1)}, bf16[1024,256]{1,0:T(8,128)(2,1)S(1)}, u32[]{:S(2)}, u32[]{:S(2)}) collective-permute-start(bf16[1024,256]{1,0:T(8,128)(2,1)S(1)} %collective-permute-done.12.refs_2_), channel_id=1, source_target_pairs={{1,2},{2,3},{5,6},{6,7},{9,10},{10,11},{13,14},{14,15},{17,18},{18... | collective-permute-start | bytes 1572872 | tf_op jit(solution)/shard_map/ppermute | solution.py:27
  296.2 40.9 %copy-start.28 = (bf16[1024,256]{1,0:T(8,128)(2,1)}, bf16[1024,256]{1,0:T(8,128)(2,1)S(1)}, u32[]{:S(2)}) copy-start(bf16[1024,256]{1,0:T(8,128)(2,1)S(1)} %collective-permute-done.15.refs_5_) | copy-start | bytes 1572868
  296.2 22.5 %collective-permute-start.16 = (bf16[1024,256]{1,0:T(8,128)(2,1)S(1)}, bf16[1024,256]{1,0:T(8,128)(2,1)S(1)}, u32[]{:S(2)}, u32[]{:S(2)}) collective-permute-start(bf16[1024,256]{1,0:T(8,128)(2,1)S(1)} %collective-permute-done.15.refs_5_), channel_id=1, source_target_pairs={{1,0},{2,1},{5,4},{6,5},{9,8},{10,9},{13,12},{14,13},{17,16},{18,1... | collective-permute-start | bytes 1572872 | tf_op jit(solution)/shard_map/ppermute | solution.py:28
  297.5 32.4 %copy-start.30 = (bf16[1024,256]{1,0:T(8,128)(2,1)}, bf16[1024,256]{1,0:T(8,128)(2,1)S(1)}, u32[]{:S(2)}) copy-start(bf16[1024,256]{1,0:T(8,128)(2,1)S(1)} %collective-permute-done.19.refs_3_) | copy-start | bytes 1572868
  297.5 22.5 %collective-permute-start.20 = (bf16[1024,256]{1,0:T(8,128)(2,1)S(1)}, bf16[1024,256]{1,0:T(8,128)(2,1)S(1)}, u32[]{:S(2)}, u32[]{:S(2)}) collective-permute-start(bf16[1024,256]{1,0:T(8,128)(2,1)S(1)} %collective-permute-done.19.refs_3_), channel_id=1, source_target_pairs={{2,3},{6,7},{10,11},{14,15},{18,19},{22,23},{26,27},{30,31}} | collective-permute-start | bytes 1572872 | tf_op jit(solution)/shard_map/ppermute | solution.py:27
  307.4 22.5 %copy-start.32 = (bf16[1024,256]{1,0:T(8,128)(2,1)}, bf16[1024,256]{1,0:T(8,128)(2,1)S(1)}, u32[]{:S(2)}) copy-start(bf16[1024,256]{1,0:T(8,128)(2,1)S(1)} %collective-permute-done.22.refs_6_) | copy-start | bytes 1572868
  307.4 22.5 %collective-permute-start.23 = (bf16[1024,256]{1,0:T(8,128)(2,1)S(1)}, bf16[1024,256]{1,0:T(8,128)(2,1)S(1)}, u32[]{:S(2)}, u32[]{:S(2)}) collective-permute-start(bf16[1024,256]{1,0:T(8,128)(2,1)S(1)} %collective-permute-done.22.refs_6_), channel_id=1, source_target_pairs={{1,0},{5,4},{9,8},{13,12},{17,16},{21,20},{25,24},{29,28}} | collective-permute-start | bytes 1572872 | tf_op jit(solution)/shard_map/ppermute | solution.py:28
  308.7 28.4 %copy-start.29 = (bf16[1024,256]{1,0:T(8,128)(2,1)}, bf16[1024,256]{1,0:T(8,128)(2,1)S(1)}, u32[]{:S(2)}) copy-start(bf16[1024,256]{1,0:T(8,128)(2,1)S(1)} %collective-permute-done.13.refs_3_) | copy-start | bytes 1572868
  308.7 28.4 %collective-permute-start.14 = (bf16[1024,256]{1,0:T(8,128)(2,1)S(1)}, bf16[1024,256]{1,0:T(8,128)(2,1)S(1)}, u32[]{:S(2)}, u32[]{:S(2)}) collective-permute-start(bf16[1024,256]{1,0:T(8,128)(2,1)S(1)} %collective-permute-done.13.refs_3_), channel_id=1, source_target_pairs={{2,3},{6,7},{10,11},{14,15},{18,19},{22,23},{26,27},{30,31}} | collective-permute-start | bytes 1572872 | tf_op jit(solution)/shard_map/ppermute | solution.py:27
  318.6 18.5 %copy-start.31 = (bf16[1024,256]{1,0:T(8,128)(2,1)}, bf16[1024,256]{1,0:T(8,128)(2,1)S(1)}, u32[]{:S(2)}) copy-start(bf16[1024,256]{1,0:T(8,128)(2,1)S(1)} %collective-permute-done.16.refs_6_) | copy-start | bytes 1572868
  318.6 21.8 %collective-permute-start.17 = (bf16[1024,256]{1,0:T(8,128)(2,1)S(1)}, bf16[1024,256]{1,0:T(8,128)(2,1)S(1)}, u32[]{:S(2)}, u32[]{:S(2)}) collective-permute-start(bf16[1024,256]{1,0:T(8,128)(2,1)S(1)} %collective-permute-done.16.refs_6_), channel_id=1, source_target_pairs={{1,0},{5,4},{9,8},{13,12},{17,16},{21,20},{25,24},{29,28}} | collective-permute-start | bytes 1572872 | tf_op jit(solution)/shard_map/ppermute | solution.py:28
  319.9 10.0 %copy-start.34 = (bf16[1024,256]{1,0:T(8,128)(2,1)}, bf16[1024,256]{1,0:T(8,128)(2,1)S(1)}, u32[]{:S(2)}) copy-start(bf16[1024,256]{1,0:T(8,128)(2,1)S(1)} %collective-permute-done.20.refs_4_) | copy-start | bytes 1572868
  329.9 0.8 copy-start.36
  337.2 3.3 copy-start.33
  340.4 0.8 copy-start.35
  (3 other events, 2.3 us)

commit v14 on v13

--- a/solution.py
+++ b/solution.py
@@ -420,14 +420,11 @@
     size = chans // chunks
     before, after = along_line(tokens, "chan")
     near = (before[1], after[0])
-    *near, out_weight, last_rows, spectrum = lax.optimization_barrier(
-        (*near, out_weight, tokens[tok_rows - HALO :], spectrum)
-    )
+    weight = feature_rows(out_weight, seq_count)
+    halo = gather_by_doubling(from_behind(tokens[tok_rows - HALO :], "seq", 1), "chan")
+    *near, spectrum = lax.optimization_barrier((*near, spectrum))
     before[1], after[0] = near
-    weight = feature_rows(out_weight, seq_count)
-    halo = gather_by_doubling(from_behind(last_rows, "seq", 1), "chan")
     sent = reordered_spectrum(spectrum, seq_count, chunks)
-    halo, sent, weight = lax.optimization_barrier((halo, sent, weight))
     response = folded_response(sent, spectrum.shape[2])
     weight = gather_by_doubling(weight, "seq")
     weight = weight.reshape((chunks, seq_count // chunks) + weight.shape[1:]).transpose(0, 2, 1, 3, 4)

time: 350 us -> 380 us (1.086)
  waiting for transfers between devices: 177 us -> 99.3 us
  blocking collectives: 0 us -> 57.7 us
  starting transfers between devices: 60.8 us -> 112 us
    all_to_all x0 -> x1, blocking collectives: none -> 57.7 us  [feature_rows(): own = lax.all_to_all(own, 'chan', split_axis=1, concat_axis=0, tiled=True)]
    all_to_all x2, starting transfers between devices: 7.65 us -> 59.8 us  [shards(): lax.all_to_all(values, 'seq', split_axis=0, concat_axis=0, tiled=True)]
    ppermute x9, waiting for transfers between devices: 91.6 us -> 39.6 us  [along_line(): lax.ppermute(after[-1], axis, [(i, i - 1) for i in range(1, size - k + 1)])]
    ppermute x9, waiting for transfers between devices: 49.3 us -> 6.27 us  [along_line(): lax.ppermute(before[-1], axis, [(i, i + 1) for i in range(k - 1, size - 1)])]
    ppermute x5, waiting for transfers between devices: 27 us -> 44.3 us  [gather_by_doubling(): other = lax.ppermute(held, axis, [(i, i ^ bit) for i in range(size)])]
    unnamed x74 -> x68, local copies, waits for them, and re-layouts: 16 us -> 17.3 us
  transfers between devices with their start and end apart: 30 -> 29, of which waited for: 19 -> 15; matrix products, arithmetic and copies ran while one was open for 9% -> 8% of each run, Pallas kernels for 12% -> 11%
where the time goes in v14:
time: 380 us; the launch traced here: 378 us
  starting transfers between devices  112 us (29%)
  waiting for transfers between devices  99.3 us (26%)
  Pallas kernels  60.8 us (16%)
  blocking collectives  57.7 us (15%)
  local copies, waits for them, and re-layouts  33.3 us (9%)
  other arithmetic  7.66 us (2%)
  matrix products  6.94 us (2%)
    all_to_all x2, starting transfers between devices, shards(): lax.all_to_all(values, 'seq', split_axis=0, concat_axis=0, tiled=True)  59.8 us
    all_to_all x1, blocking collectives, feature_rows(): own = lax.all_to_all(own, 'chan', split_axis=1, concat_axis=0, tiled=True)  57.7 us
    ppermute x5, waiting for transfers between devices, gather_by_doubling(): other = lax.ppermute(held, axis, [(i, i ^ bit) for i in range(size)])  44.3 us
    ppermute x9, waiting for transfers between devices, along_line(): lax.ppermute(after[-1], axis, [(i, i - 1) for i in range(1, size - k + 1)])  39.6 us
    pallas_call x2, Pallas kernels, project(): pl.pallas_call(lambda *refs: project_kernel(count, len(following), *refs)...  27.4 us
    unnamed x68, local copies, waits for them, and re-layouts  17.3 us
    ppermute x9, starting transfers between devices, along_line(): lax.ppermute(before[-1], axis, [(i, i + 1) for i in range(k - 1, size - 1)])  14.8 us
    pallas_call x2, Pallas kernels, combine(): pl.pallas_call(lambda *refs: combine_kernel(count, *refs), grid_spec=pltp...  13 us
  transfers between devices with their start and end apart: 29, of which 15 were waited for; matrix products, arithmetic and copies ran while one was open for 8% of the time, Pallas kernels for 11%

profile of v14, /device:TPU:0, one launch (start us, length us, event | category | flops | bytes accessed | tf_op | source)
XLA Modules:
  0.0 377.9 jit_solution(3607458032492669758)
XLA Ops:
  0.0 6.2 %collective-permute-start = (bf16[1024,1024]{1,0:T(8,128)(2,1)}, bf16[1024,1024]{1,0:T(8,128)(2,1)}, u32[]{:S(2)}, u32[]{:S(2)}) collective-permute-start(bf16[1024,1024]{1,0:T(8,128)(2,1)} %refs_1_.3), channel_id=1, source_target_pairs={{0,1},{1,2},{2,3},{4,5},{5,6},{6,7},{8,9},{9,10},{10,11},{12,13},{... | collective-permute-start | bytes 6291464 | tf_op jit(solution)/shard_map/ppermute | solution.py:27
  6.2 1.3 collective-permute-start.1
  7.5 1.1 constant_dynamic-slice_fusion
  8.6 57.7 %all_to_all.41 = bf16[64,4,1024]{2,0,1:T(8,128)(2,1)S(1)} all-to-all(bf16[64,4,1024]{2,0,1:T(8,128)(2,1)S(1)} %bitcast.92), channel_id=1, replica_groups=mesh['seq'=8,'chan'=4] {'chan'}, dimensions={1} | all-to-all | bytes 1048576 | tf_op jit(solution)/shard_map/all_to_all | solution.py:363
  66.4 1.5 collective-permute-start.9
  67.9 10.9 %collective-permute-done.9 = bf16[1,4,64,1024]{3,2,1,0:T(8,128)(2,1)S(1)} collective-permute-done((bf16[1,4,64,1024]{3,2,1,0:T(8,128)(2,1)S(1)}, bf16[1,4,64,1024]{3,2,1,0:T(8,128)(2,1)S(1)}, u32[]{:S(2)}, u32[]{:S(2)}) %collective-permute-start.9) | collective-permute-done | bytes 524320 | tf_op jit(solution)/shard_map/ppermute | solution.py:38
  78.9 1.1 maximum_bitcast_fusion
  80.0 1.5 collective-permute-start.10
  81.5 2.0 collective-permute-start.2
  83.5 1.3 collective-permute-start.4
  85.5 11.0 %reshape.47.spec_ref = f32[2,1024,1024]{2,1,0:T(8,128)} reshape(f32[2,512,2,1024]{3,2,1,0:T(2,128)} %param.21) | data formatting | bytes 16777216 | tf_op jit(solution)/shard_map/reshape | solution.py:335
  96.4 8.6 %shard_map.172 = bf16[8,2,2,64,1024]{4,3,2,1,0:T(8,128)(2,1)} custom-call(f32[2,1024,1024]{2,1,0:T(8,128)} %reshape.47.spec_ref, bf16[1024,1024]{1,0:T(8,128)(2,1)S(1)} %fusion.1.order_ref), custom_call_target="tpu_custom_call" | custom-call | flops 4294967296 | bytes 12582912 | tf_op jit(solution)/shard_map/pallas_call | solution.py:322
  105.0 4.6 %all-to-all-start = ((bf16[8,2,2,64,1024]{4,3,2,1,0:T(8,128)(2,1)}), bf16[8,2,2,64,1024]{4,3,2,1,0:T(8,128)(2,1)}, u32[]{:S(2)}, u32[]{:S(2)}) async-start(bf16[8,2,2,64,1024]{4,3,2,1,0:T(8,128)(2,1)} %shard_map.172), calls=%async_computation | async-start | bytes 8388608 | tf_op jit(solution)/shard_map/all_to_all | solution.py:342
  109.6 1.4 select_bitcast_fusion.3
  111.0 1.5 pad_maximum_fusion.1
  113.6 2.1 collective-permute-start.6
  115.7 1.0 collective-permute-done.6
  116.7 4.3 %collective-permute-start.7 = (bf16[1,16,1024]{2,1,0:T(8,128)(2,1)S(1)}, bf16[1,16,1024]{2,1,0:T(8,128)(2,1)S(1)}, u32[]{:S(2)}, u32[]{:S(2)}) collective-permute-start(bf16[1,16,1024]{2,1,0:T(8,128)(2,1)S(1)} %bitcast.96), channel_id=1, source_target_pairs={{0,2},{1,3},{2,0},{3,1},{4,6},{5,7},{6,4},{7,5},{8,10},{9,11},{10,... | collective-permute-start | bytes 98312 | tf_op jit(solution)/shard_map/ppermute | solution.py:38
  121.0 9.9 %collective-permute-done.7 = bf16[1,16,1024]{2,1,0:T(8,128)(2,1)S(1)} collective-permute-done((bf16[1,16,1024]{2,1,0:T(8,128)(2,1)S(1)}, bf16[1,16,1024]{2,1,0:T(8,128)(2,1)S(1)}, u32[]{:S(2)}, u32[]{:S(2)}) %collective-permute-start.7) | collective-permute-done | bytes 32800 | tf_op jit(solution)/shard_map/ppermute | solution.py:38
  131.7 1.5 collective-permute-start.5
  133.2 3.9 %collective-permute-start.8 = (bf16[2,16,1024]{2,1,0:T(8,128)(2,1)S(1)}, bf16[2,16,1024]{2,1,0:T(8,128)(2,1)S(1)}, u32[]{:S(2)}, u32[]{:S(2)}) collective-permute-start(bf16[2,16,1024]{2,1,0:T(8,128)(2,1)S(1)} %maximum_bitcast_fusion.1), channel_id=1, source_target_pairs={{0,1},{1,0},{2,3},{3,2},{4,5},{5,4},{6,7},{7,6},{8,9},{9,8},{10,11... | collective-permute-start | bytes 196616 | tf_op jit(solution)/shard_map/ppermute | solution.py:38
  137.1 23.5 %collective-permute-done.8 = bf16[2,16,1024]{2,1,0:T(8,128)(2,1)S(1)} collective-permute-done((bf16[2,16,1024]{2,1,0:T(8,128)(2,1)S(1)}, bf16[2,16,1024]{2,1,0:T(8,128)(2,1)S(1)}, u32[]{:S(2)}, u32[]{:S(2)}) %collective-permute-start.8) | collective-permute-done | bytes 65568 | tf_op jit(solution)/shard_map/ppermute | solution.py:38
  160.6 6.9 %fusion.3.refs_12_ = bf16[3,16,512]{2,1,0:T(8,128)(2,1)} fusion(bf16[4,16,1024,1]{2,1,0,3:T(8,128)(2,1)S(1)} %bitcast.93, bf16[3,4,1024,512]{3,2,1,0:T(8,128)(2,1)} %bitcast.78), kind=kOutput, calls=%fused_computation.9 | convolution fusion | flops 201351168 | bytes 12763136 | tf_op jit(solution)/shard_map/ztd,pzdc->ptc/dot_general | solution.py:432
  167.5 2.5 select_bitcast_fusion.1
  171.1 2.4 copy.32
  173.6 4.0 %shard_map.173.refs_13_.resp_ref = bf16[2,64,72,128]{3,2,1,0:T(8,128)(2,1)S(1)} custom-call(bf16[8,2,2,64,1024]{4,3,2,1,0:T(8,128)(2,1)} %all-to-all-done.got_ref), custom_call_target="tpu_custom_call" | custom-call | flops 2097152 | bytes 6291456 | tf_op jit(solution)/shard_map/pallas_call | solution.py:345
  177.6 1.4 copy-done
  179.1 1.3 copy-done.21
  180.4 13.6 %shard_map.177 = (bf16[1024,256]{1,0:T(8,128)(2,1)}, bf16[256,1024]{1,0:T(8,128)(2,1)}, bf16[1024,256]{1,0:T(8,128)(2,1)}) custom-call(s32[1]{0:T(128)} %bitcast.refs_0_, bf16[1024,1024]{1,0:T(8,128)(2,1)} %refs_1_.3, bf16[1024,1024]{1,0:T(8,128)(2,1)} %collective-permute-done.refs_2_, bf16[1024,1024]{1,0:T(8,128)(2,1)} %collective-permute-done.2.refs_3_, ...), custom_call_target="tpu_custom_call" | custom-call | flops 6442450944 | bytes 14680064 | tf_op jit(solution)/shard_map/pallas_call | solution.py:126
  193.9 55.6 %all-to-all-start.4 = ((bf16[8,32,1024]{2,1,0:T(8,128)(2,1)}), bf16[8,32,1024]{2,1,0:T(8,128)(2,1)S(1)}, u32[]{:S(2)}, u32[]{:S(2)}) async-start(bf16[8,32,1024]{2,1,0:T(8,128)(2,1)} %bitcast.95), calls=%async_computation.4 | async-start | bytes 1048576 | tf_op jit(solution)/shard_map/all_to_all | solution.py:443
  249.5 13.9 %shard_map.174 = (bf16[1024,256]{1,0:T(8,128)(2,1)}, bf16[256,1024]{1,0:T(8,128)(2,1)}, bf16[1024,256]{1,0:T(8,128)(2,1)}) custom-call(s32[1]{0:T(128)} %bitcast.refs_0_, bf16[1024,1024]{1,0:T(8,128)(2,1)} %refs_1_.3, bf16[1024,1024]{1,0:T(8,128)(2,1)} %collective-permute-done.refs_2_, bf16[1024,1024]{1,0:T(8,128)(2,1)} %collective-permute-done.2.refs_3_, ...), custom_call_target="tpu_custom_call" | custom-call | flops 6442450944 | bytes 14680064 | tf_op jit(solution)/shard_map/pallas_call | solution.py:126
  263.4 4.2 %all-to-all-start.2 = ((bf16[8,32,1024]{2,1,0:T(8,128)(2,1)}), bf16[8,32,1024]{2,1,0:T(8,128)(2,1)S(1)}, u32[]{:S(2)}, u32[]{:S(2)}) async-start(bf16[8,32,1024]{2,1,0:T(8,128)(2,1)} %bitcast.94), calls=%async_computation.2 | async-start | bytes 1048576 | tf_op jit(solution)/shard_map/all_to_all | solution.py:443
  267.7 0.9 copy-done.10
  271.6 2.9 shard_map.178
  274.6 0.8 copy-done.4
  275.4 2.0 all-to-all-done.2.signal_ref
  277.4 3.5 all-to-all-start.5
  280.9 0.9 copy-done.11
  284.9 3.6 shard_map.175
  288.5 2.1 all-to-all-done.5
  290.6 3.5 all-to-all-start.3
  294.1 1.0 copy-done.7
  295.1 1.0 copy-done.8
  296.8 1.6 collective-permute-start.18
  298.3 1.3 collective-permute-start.21
  299.6 4.1 %all-to-all-done.3 = bf16[8,32,1024]{2,1,0:T(8,128)(2,1)S(1)} async-done(((bf16[8,32,1024]{2,1,0:T(8,128)(2,1)}), bf16[8,32,1024]{2,1,0:T(8,128)(2,1)S(1)}, u32[]{:S(2)}, u32[]{:S(2)}) %all-to-all-start.3) | async-done | bytes 524320 | tf_op jit(solution)/shard_map/all_to_all | solution.py:444
  303.7 1.0 copy-done.5
  304.8 1.0 copy-done.6
  306.4 1.6 collective-permute-start.12
  308.0 1.3 collective-permute-start.15
  309.3 1.2 collective-permute-done.18.refs_2_
  311.2 3.8 collective-permute-done.21.refs_5_
  315.0 1.3 collective-permute-start.22
  316.3 5.0 %collective-permute-done.12.refs_2_ = bf16[1024,256]{1,0:T(8,128)(2,1)S(1)} collective-permute-done((bf16[1024,256]{1,0:T(8,128)(2,1)S(1)}, bf16[1024,256]{1,0:T(8,128)(2,1)S(1)}, u32[]{:S(2)}, u32[]{:S(2)}) %collective-permute-start.12) | collective-permute-done | bytes 524320 | tf_op jit(solution)/shard_map/ppermute | solution.py:27
  322.0 4.2 %collective-permute-done.15.refs_5_ = bf16[1024,256]{1,0:T(8,128)(2,1)S(1)} collective-permute-done((bf16[1024,256]{1,0:T(8,128)(2,1)S(1)}, bf16[1024,256]{1,0:T(8,128)(2,1)S(1)}, u32[]{:S(2)}, u32[]{:S(2)}) %collective-permute-start.15) | collective-permute-done | bytes 524320 | tf_op jit(solution)/shard_map/ppermute | solution.py:28
  326.2 1.3 collective-permute-start.16
  328.2 9.2 %collective-permute-done.22.refs_6_ = bf16[1024,256]{1,0:T(8,128)(2,1)S(1)} collective-permute-done((bf16[1024,256]{1,0:T(8,128)(2,1)S(1)}, bf16[1024,256]{1,0:T(8,128)(2,1)S(1)}, u32[]{:S(2)}, u32[]{:S(2)}) %collective-permute-start.22) | collective-permute-done | bytes 524320 | tf_op jit(solution)/shard_map/ppermute | solution.py:28
  337.5 1.3 collective-permute-start.23
  339.5 9.2 %collective-permute-done.16.refs_6_ = bf16[1024,256]{1,0:T(8,128)(2,1)S(1)} collective-permute-done((bf16[1024,256]{1,0:T(8,128)(2,1)S(1)}, bf16[1024,256]{1,0:T(8,128)(2,1)S(1)}, u32[]{:S(2)}, u32[]{:S(2)}) %collective-permute-start.16) | collective-permute-done | bytes 524320 | tf_op jit(solution)/shard_map/ppermute | solution.py:28
  348.7 1.3 collective-permute-start.17
  350.0 9.9 %collective-permute-done.23.refs_7_ = bf16[1024,256]{1,0:T(8,128)(2,1)S(1)} collective-permute-done((bf16[1024,256]{1,0:T(8,128)(2,1)S(1)}, bf16[1024,256]{1,0:T(8,128)(2,1)S(1)}, u32[]{:S(2)}, u32[]{:S(2)}) %collective-permute-start.23) | collective-permute-done | bytes 524320 | tf_op jit(solution)/shard_map/ppermute | solution.py:28
  360.8 6.4 %shard_map.180.refs_12_ = f32[1024,1024]{1,0:T(8,128)} custom-call(s32[1]{0:T(128)} %bitcast.refs_0_, bf16[1024,256]{1,0:T(8,128)(2,1)} %copy-done.2, bf16[1024,256]{1,0:T(8,128)(2,1)} %copy-done.22, bf16[1024,256]{1,0:T(8,128)(2,1)} %copy-done.27, bf16[1024,256]{1,0:T(8,128)(2,1)} %copy-done.31, bf16[1024,256]{1,0:T(8,128)(2,1)} %copy-done.24, ...), custom_call_target="tpu_custom_call" | custom-call | flops 2147483648 | bytes 10485760 | tf_op jit(solution)/shard_map/pallas_call | solution.py:392
  367.2 3.2 collective-permute-done.17.refs_7_
  371.2 6.7 %shard_map.181 = bf16[1024,1024]{1,0:T(8,128)(2,1)} custom-call(s32[1]{0:T(128)} %bitcast.refs_0_, bf16[1024,256]{1,0:T(8,128)(2,1)} %copy-done.3, bf16[1024,256]{1,0:T(8,128)(2,1)} %copy-done.23, bf16[1024,256]{1,0:T(8,128)(2,1)} %copy-done.26, bf16[1024,256]{1,0:T(8,128)(2,1)} %copy-done.30, bf16[1024,256]{1,0:T(8,128)(2,1)} %copy-done.25, ...), custom_call_target="tpu_custom_call" | custom-call | flops 2147483648 | bytes 10485760 | tf_op jit(solution)/shard_map/pallas_call | solution.py:392
  (95 shorter events, 15.7 us)
Async XLA Ops:
  0.0 81.5 %collective-permute-start = (bf16[1024,1024]{1,0:T(8,128)(2,1)}, bf16[1024,1024]{1,0:T(8,128)(2,1)}, u32[]{:S(2)}, u32[]{:S(2)}) collective-permute-start(bf16[1024,1024]{1,0:T(8,128)(2,1)} %refs_1_.3), channel_id=1, source_target_pairs={{0,1},{1,2},{2,3},{4,5},{5,6},{6,7},{8,9},{9,10},{10,11},{12,13},{... | collective-permute-start | bytes 6291464 | tf_op jit(solution)/shard_map/ppermute | solution.py:27
  6.2 77.2 %collective-permute-start.1 = (bf16[1024,1024]{1,0:T(8,128)(2,1)}, bf16[1024,1024]{1,0:T(8,128)(2,1)}, u32[]{:S(2)}, u32[]{:S(2)}) collective-permute-start(bf16[1024,1024]{1,0:T(8,128)(2,1)} %refs_1_.3), channel_id=1, source_target_pairs={{1,0},{2,1},{3,2},{5,4},{6,5},{7,6},{9,8},{10,9},{11,10},{13,12},{... | collective-permute-start | bytes 6291464 | tf_op jit(solution)/shard_map/ppermute | solution.py:28
  66.4 12.5 %collective-permute-start.9 = (bf16[1,4,64,1024]{3,2,1,0:T(8,128)(2,1)S(1)}, bf16[1,4,64,1024]{3,2,1,0:T(8,128)(2,1)S(1)}, u32[]{:S(2)}, u32[]{:S(2)}) collective-permute-start(bf16[1,4,64,1024]{3,2,1,0:T(8,128)(2,1)S(1)} %bitcast.90), channel_id=1, source_target_pairs={{0,16},{4,20},{8,24},{12,28},{16,0},{20,4},{24,8},{28,12},{1,17},{... | collective-permute-start | bytes 1572872 | tf_op jit(solution)/shard_map/ppermute | solution.py:38
  80.0 29.6 %collective-permute-start.10 = (bf16[2,4,64,1024]{3,2,1,0:T(8,128)(2,1)}, bf16[2,4,64,1024]{3,2,1,0:T(8,128)(2,1)}, u32[]{:S(2)}, u32[]{:S(2)}) collective-permute-start(bf16[2,4,64,1024]{3,2,1,0:T(8,128)(2,1)} %maximum_bitcast_fusion), channel_id=1, source_target_pairs={{0,8},{4,12},{8,0},{12,4},{16,24},{20,28},{24,16},{28,20},{1,9},{5... | collective-permute-start | bytes 3145736 | tf_op jit(solution)/shard_map/ppermute | solution.py:38
  81.5 49.4 %collective-permute-start.2 = (bf16[1024,1024]{1,0:T(8,128)(2,1)}, bf16[1024,1024]{1,0:T(8,128)(2,1)}, u32[]{:S(2)}, u32[]{:S(2)}) collective-permute-start(bf16[1024,1024]{1,0:T(8,128)(2,1)} %collective-permute-done.refs_2_), channel_id=1, source_target_pairs={{1,2},{2,3},{5,6},{6,7},{9,10},{10,11},{13,14},{14,15},{17,18},{18... | collective-permute-start | bytes 6291464 | tf_op jit(solution)/shard_map/ppermute | solution.py:27
  83.5 48.2 %collective-permute-start.4 = (bf16[1024,1024]{1,0:T(8,128)(2,1)}, bf16[1024,1024]{1,0:T(8,128)(2,1)}, u32[]{:S(2)}, u32[]{:S(2)}) collective-permute-start(bf16[1024,1024]{1,0:T(8,128)(2,1)} %collective-permute-done.1.refs_5_), channel_id=1, source_target_pairs={{1,0},{2,1},{5,4},{6,5},{9,8},{10,9},{13,12},{14,13},{17,16},{18,1... | collective-permute-start | bytes 6291464 | tf_op jit(solution)/shard_map/ppermute | solution.py:28
  105.0 68.6 %all-to-all-start = ((bf16[8,2,2,64,1024]{4,3,2,1,0:T(8,128)(2,1)}), bf16[8,2,2,64,1024]{4,3,2,1,0:T(8,128)(2,1)}, u32[]{:S(2)}, u32[]{:S(2)}) async-start(bf16[8,2,2,64,1024]{4,3,2,1,0:T(8,128)(2,1)} %shard_map.172), calls=%async_computation | async-start | bytes 8388608 | tf_op jit(solution)/shard_map/all_to_all | solution.py:342
  112.5 55.0 %collective-permute-start.11 = (bf16[4,4,64,1024]{3,2,1,0:T(8,128)(2,1)}, bf16[4,4,64,1024]{3,2,1,0:T(8,128)(2,1)}, u32[]{:S(2)}, u32[]{:S(2)}) collective-permute-start(bf16[4,4,64,1024]{3,2,1,0:T(8,128)(2,1)} %bitcast.22), channel_id=1, source_target_pairs={{0,4},{4,0},{8,12},{12,8},{16,20},{20,16},{24,28},{28,24},{1,5},{5... | collective-permute-start | bytes 6291464 | tf_op jit(solution)/shard_map/ppermute | solution.py:38
  113.6 3.1 collective-permute-start.6
  116.7 14.2 %collective-permute-start.7 = (bf16[1,16,1024]{2,1,0:T(8,128)(2,1)S(1)}, bf16[1,16,1024]{2,1,0:T(8,128)(2,1)S(1)}, u32[]{:S(2)}, u32[]{:S(2)}) collective-permute-start(bf16[1,16,1024]{2,1,0:T(8,128)(2,1)S(1)} %bitcast.96), channel_id=1, source_target_pairs={{0,2},{1,3},{2,0},{3,1},{4,6},{5,7},{6,4},{7,5},{8,10},{9,11},{10,... | collective-permute-start | bytes 98312 | tf_op jit(solution)/shard_map/ppermute | solution.py:38
  130.9 48.2 %collective-permute-start.3 = (bf16[1024,1024]{1,0:T(8,128)(2,1)}, bf16[1024,1024]{1,0:T(8,128)(2,1)S(1)}, u32[]{:S(2)}, u32[]{:S(2)}) collective-permute-start(bf16[1024,1024]{1,0:T(8,128)(2,1)} %collective-permute-done.2.refs_3_), channel_id=1, source_target_pairs={{2,3},{6,7},{10,11},{14,15},{18,19},{22,23},{26,27},{30,31}} | collective-permute-start | bytes 6291464 | tf_op jit(solution)/shard_map/ppermute | solution.py:27
  131.7 47.4 %collective-permute-start.5 = (bf16[1024,1024]{1,0:T(8,128)(2,1)}, bf16[1024,1024]{1,0:T(8,128)(2,1)}, u32[]{:S(2)}, u32[]{:S(2)}) collective-permute-start(bf16[1024,1024]{1,0:T(8,128)(2,1)} %collective-permute-done.4.refs_6_), channel_id=1, source_target_pairs={{1,0},{5,4},{9,8},{13,12},{17,16},{21,20},{25,24},{29,28}} | collective-permute-start | bytes 6291464 | tf_op jit(solution)/shard_map/ppermute | solution.py:28
  133.2 27.3 %collective-permute-start.8 = (bf16[2,16,1024]{2,1,0:T(8,128)(2,1)S(1)}, bf16[2,16,1024]{2,1,0:T(8,128)(2,1)S(1)}, u32[]{:S(2)}, u32[]{:S(2)}) collective-permute-start(bf16[2,16,1024]{2,1,0:T(8,128)(2,1)S(1)} %maximum_bitcast_fusion.1), channel_id=1, source_target_pairs={{0,1},{1,0},{2,3},{3,2},{4,5},{5,4},{6,7},{7,6},{8,9},{9,8},{10,11... | collective-permute-start | bytes 196616 | tf_op jit(solution)/shard_map/ppermute | solution.py:38
  177.6 1.4 copy-start
  179.1 1.3 copy-start.21
  193.9 69.5 %all-to-all-start.4 = ((bf16[8,32,1024]{2,1,0:T(8,128)(2,1)}), bf16[8,32,1024]{2,1,0:T(8,128)(2,1)S(1)}, u32[]{:S(2)}, u32[]{:S(2)}) async-start(bf16[8,32,1024]{2,1,0:T(8,128)(2,1)} %bitcast.95), calls=%async_computation.4 | async-start | bytes 1048576 | tf_op jit(solution)/shard_map/all_to_all | solution.py:443
  249.5 18.1 %copy-start.1 = (bf16[2,64,72,128]{3,2,1,0:T(8,128)(2,1)S(1)}, bf16[2,64,72,128]{3,2,1,0:T(8,128)(2,1)}, u32[]{:S(2)}) copy-start(bf16[2,64,72,128]{3,2,1,0:T(8,128)(2,1)} %copy-done) | copy-start | bytes 7077892
  249.5 18.1 %copy-start.9 = (bf16[256,256]{1,0:T(8,128)(2,1)S(1)}, bf16[256,256]{1,0:T(8,128)(2,1)}, u32[]{:S(2)}) copy-start(bf16[256,256]{1,0:T(8,128)(2,1)} %constant.138.clone.fwd_ref) | copy-start | bytes 393220
  263.4 14.0 %all-to-all-start.2 = ((bf16[8,32,1024]{2,1,0:T(8,128)(2,1)}), bf16[8,32,1024]{2,1,0:T(8,128)(2,1)S(1)}, u32[]{:S(2)}, u32[]{:S(2)}) async-start(bf16[8,32,1024]{2,1,0:T(8,128)(2,1)} %bitcast.94), calls=%async_computation.2 | async-start | bytes 1048576 | tf_op jit(solution)/shard_map/all_to_all | solution.py:443
  267.6 0.9 copy-start.10
  268.6 0.8 copy-start.12
  269.3 0.8 copy-start.14
  270.1 0.8 copy-start.16
  270.9 0.8 copy-start.18
  271.6 22.4 %copy-start.20 = (f32[512]{0:T(512)S(1)}, f32[512]{0:T(512)}, u32[]{:S(2)}) copy-start(f32[512]{0:T(512)} %param.22) | copy-start | bytes 6148
  274.6 0.8 copy-start.4
  277.4 13.2 %all-to-all-start.5 = ((bf16[8,32,1024]{2,1,0:T(8,128)(2,1)}), bf16[8,32,1024]{2,1,0:T(8,128)(2,1)S(1)}, u32[]{:S(2)}, u32[]{:S(2)}) async-start(bf16[8,32,1024]{2,1,0:T(8,128)(2,1)} %copy-done.4), calls=%async_computation.5 | async-start | bytes 1048576 | tf_op jit(solution)/shard_map/all_to_all | solution.py:444
  280.9 0.9 copy-start.11
  281.8 0.8 copy-start.13
  282.6 0.8 copy-start.15
  283.3 0.8 copy-start.17
  284.1 0.8 copy-start.19
  290.6 13.2 %all-to-all-start.3 = ((bf16[8,32,1024]{2,1,0:T(8,128)(2,1)}), bf16[8,32,1024]{2,1,0:T(8,128)(2,1)S(1)}, u32[]{:S(2)}, u32[]{:S(2)}) async-start(bf16[8,32,1024]{2,1,0:T(8,128)(2,1)} %shard_map.175), calls=%async_computation.3 | async-start | bytes 1048576 | tf_op jit(solution)/shard_map/all_to_all | solution.py:444
  294.1 1.0 copy-start.7
  295.1 1.0 copy-start.8
  296.8 63.2 %copy-start.2 = (bf16[1024,256]{1,0:T(8,128)(2,1)}, bf16[1024,256]{1,0:T(8,128)(2,1)S(1)}, u32[]{:S(2)}) copy-start(bf16[1024,256]{1,0:T(8,128)(2,1)S(1)} %shard_map.179.refs_1_) | copy-start | bytes 1572868
  296.8 13.8 %collective-permute-start.18 = (bf16[1024,256]{1,0:T(8,128)(2,1)S(1)}, bf16[1024,256]{1,0:T(8,128)(2,1)S(1)}, u32[]{:S(2)}, u32[]{:S(2)}) collective-permute-start(bf16[1024,256]{1,0:T(8,128)(2,1)S(1)} %shard_map.179.refs_1_), channel_id=1, source_target_pairs={{0,1},{1,2},{2,3},{4,5},{5,6},{6,7},{8,9},{9,10},{10,11},{12,13},{... | collective-permute-start | bytes 1572872 | tf_op jit(solution)/shard_map/ppermute | solution.py:27
  298.3 16.7 %collective-permute-start.21 = (bf16[1024,256]{1,0:T(8,128)(2,1)S(1)}, bf16[1024,256]{1,0:T(8,128)(2,1)S(1)}, u32[]{:S(2)}, u32[]{:S(2)}) collective-permute-start(bf16[1024,256]{1,0:T(8,128)(2,1)S(1)} %shard_map.179.refs_1_), channel_id=1, source_target_pairs={{1,0},{2,1},{3,2},{5,4},{6,5},{7,6},{9,8},{10,9},{11,10},{13,12},{... | collective-permute-start | bytes 1572872 | tf_op jit(solution)/shard_map/ppermute | solution.py:28
  303.7 1.0 copy-start.5
  304.8 1.0 copy-start.6
  306.4 60.7 %copy-start.3 = (bf16[1024,256]{1,0:T(8,128)(2,1)}, bf16[1024,256]{1,0:T(8,128)(2,1)S(1)}, u32[]{:S(2)}) copy-start(bf16[1024,256]{1,0:T(8,128)(2,1)S(1)} %shard_map.176.refs_1_) | copy-start | bytes 1572868
  306.4 14.9 %collective-permute-start.12 = (bf16[1024,256]{1,0:T(8,128)(2,1)S(1)}, bf16[1024,256]{1,0:T(8,128)(2,1)S(1)}, u32[]{:S(2)}, u32[]{:S(2)}) collective-permute-start(bf16[1024,256]{1,0:T(8,128)(2,1)S(1)} %shard_map.176.refs_1_), channel_id=1, source_target_pairs={{0,1},{1,2},{2,3},{4,5},{5,6},{6,7},{8,9},{9,10},{10,11},{12,13},{... | collective-permute-start | bytes 1572872 | tf_op jit(solution)/shard_map/ppermute | solution.py:27
  308.0 18.2 %collective-permute-start.15 = (bf16[1024,256]{1,0:T(8,128)(2,1)S(1)}, bf16[1024,256]{1,0:T(8,128)(2,1)S(1)}, u32[]{:S(2)}, u32[]{:S(2)}) collective-permute-start(bf16[1024,256]{1,0:T(8,128)(2,1)S(1)} %shard_map.176.refs_1_), channel_id=1, source_target_pairs={{1,0},{2,1},{3,2},{5,4},{6,5},{7,6},{9,8},{10,9},{11,10},{13,12},{... | collective-permute-start | bytes 1572872 | tf_op jit(solution)/shard_map/ppermute | solution.py:28
  310.5 49.4 %copy-start.22 = (bf16[1024,256]{1,0:T(8,128)(2,1)}, bf16[1024,256]{1,0:T(8,128)(2,1)S(1)}, u32[]{:S(2)}) copy-start(bf16[1024,256]{1,0:T(8,128)(2,1)S(1)} %collective-permute-done.18.refs_2_) | copy-start | bytes 1572868
  310.5 17.0 %collective-permute-start.19 = (bf16[1024,256]{1,0:T(8,128)(2,1)S(1)}, bf16[1024,256]{1,0:T(8,128)(2,1)S(1)}, u32[]{:S(2)}, u32[]{:S(2)}) collective-permute-start(bf16[1024,256]{1,0:T(8,128)(2,1)S(1)} %collective-permute-done.18.refs_2_), channel_id=1, source_target_pairs={{1,2},{2,3},{5,6},{6,7},{9,10},{10,11},{13,14},{14,15},{17,18},{18... | collective-permute-start | bytes 1572872 | tf_op jit(solution)/shard_map/ppermute | solution.py:27
  315.0 44.9 %copy-start.24 = (bf16[1024,256]{1,0:T(8,128)(2,1)}, bf16[1024,256]{1,0:T(8,128)(2,1)S(1)}, u32[]{:S(2)}) copy-start(bf16[1024,256]{1,0:T(8,128)(2,1)S(1)} %collective-permute-done.21.refs_5_) | copy-start | bytes 1572868
  315.0 22.5 %collective-permute-start.22 = (bf16[1024,256]{1,0:T(8,128)(2,1)S(1)}, bf16[1024,256]{1,0:T(8,128)(2,1)S(1)}, u32[]{:S(2)}, u32[]{:S(2)}) collective-permute-start(bf16[1024,256]{1,0:T(8,128)(2,1)S(1)} %collective-permute-done.21.refs_5_), channel_id=1, source_target_pairs={{1,0},{2,1},{5,4},{6,5},{9,8},{10,9},{13,12},{14,13},{17,16},{18,1... | collective-permute-start | bytes 1572872 | tf_op jit(solution)/shard_map/ppermute | solution.py:28
  321.3 45.8 %copy-start.23 = (bf16[1024,256]{1,0:T(8,128)(2,1)}, bf16[1024,256]{1,0:T(8,128)(2,1)S(1)}, u32[]{:S(2)}) copy-start(bf16[1024,256]{1,0:T(8,128)(2,1)S(1)} %collective-permute-done.12.refs_2_) | copy-start | bytes 1572868
  321.3 17.4 %collective-permute-start.13 = (bf16[1024,256]{1,0:T(8,128)(2,1)S(1)}, bf16[1024,256]{1,0:T(8,128)(2,1)S(1)}, u32[]{:S(2)}, u32[]{:S(2)}) collective-permute-start(bf16[1024,256]{1,0:T(8,128)(2,1)S(1)} %collective-permute-done.12.refs_2_), channel_id=1, source_target_pairs={{1,2},{2,3},{5,6},{6,7},{9,10},{10,11},{13,14},{14,15},{17,18},{18... | collective-permute-start | bytes 1572872 | tf_op jit(solution)/shard_map/ppermute | solution.py:27
  326.2 40.9 %copy-start.25 = (bf16[1024,256]{1,0:T(8,128)(2,1)}, bf16[1024,256]{1,0:T(8,128)(2,1)S(1)}, u32[]{:S(2)}) copy-start(bf16[1024,256]{1,0:T(8,128)(2,1)S(1)} %collective-permute-done.15.refs_5_) | copy-start | bytes 1572868
  326.2 22.5 %collective-permute-start.16 = (bf16[1024,256]{1,0:T(8,128)(2,1)S(1)}, bf16[1024,256]{1,0:T(8,128)(2,1)S(1)}, u32[]{:S(2)}, u32[]{:S(2)}) collective-permute-start(bf16[1024,256]{1,0:T(8,128)(2,1)S(1)} %collective-permute-done.15.refs_5_), channel_id=1, source_target_pairs={{1,0},{2,1},{5,4},{6,5},{9,8},{10,9},{13,12},{14,13},{17,16},{18,1... | collective-permute-start | bytes 1572872 | tf_op jit(solution)/shard_map/ppermute | solution.py:28
  327.5 32.4 %copy-start.27 = (bf16[1024,256]{1,0:T(8,128)(2,1)}, bf16[1024,256]{1,0:T(8,128)(2,1)S(1)}, u32[]{:S(2)}) copy-start(bf16[1024,256]{1,0:T(8,128)(2,1)S(1)} %collective-permute-done.19.refs_3_) | copy-start | bytes 1572868
  327.5 22.5 %collective-permute-start.20 = (bf16[1024,256]{1,0:T(8,128)(2,1)S(1)}, bf16[1024,256]{1,0:T(8,128)(2,1)S(1)}, u32[]{:S(2)}, u32[]{:S(2)}) collective-permute-start(bf16[1024,256]{1,0:T(8,128)(2,1)S(1)} %collective-permute-done.19.refs_3_), channel_id=1, source_target_pairs={{2,3},{6,7},{10,11},{14,15},{18,19},{22,23},{26,27},{30,31}} | collective-permute-start | bytes 1572872 | tf_op jit(solution)/shard_map/ppermute | solution.py:27
  337.5 22.5 %copy-start.29 = (bf16[1024,256]{1,0:T(8,128)(2,1)}, bf16[1024,256]{1,0:T(8,128)(2,1)S(1)}, u32[]{:S(2)}) copy-start(bf16[1024,256]{1,0:T(8,128)(2,1)S(1)} %collective-permute-done.22.refs_6_) | copy-start | bytes 1572868
  337.5 22.5 %collective-permute-start.23 = (bf16[1024,256]{1,0:T(8,128)(2,1)S(1)}, bf16[1024,256]{1,0:T(8,128)(2,1)S(1)}, u32[]{:S(2)}, u32[]{:S(2)}) collective-permute-start(bf16[1024,256]{1,0:T(8,128)(2,1)S(1)} %collective-permute-done.22.refs_6_), channel_id=1, source_target_pairs={{1,0},{5,4},{9,8},{13,12},{17,16},{21,20},{25,24},{29,28}} | collective-permute-start | bytes 1572872 | tf_op jit(solution)/shard_map/ppermute | solution.py:28
  338.8 28.4 %copy-start.26 = (bf16[1024,256]{1,0:T(8,128)(2,1)}, bf16[1024,256]{1,0:T(8,128)(2,1)S(1)}, u32[]{:S(2)}) copy-start(bf16[1024,256]{1,0:T(8,128)(2,1)S(1)} %collective-permute-done.13.refs_3_) | copy-start | bytes 1572868
  338.8 28.4 %collective-permute-start.14 = (bf16[1024,256]{1,0:T(8,128)(2,1)S(1)}, bf16[1024,256]{1,0:T(8,128)(2,1)S(1)}, u32[]{:S(2)}, u32[]{:S(2)}) collective-permute-start(bf16[1024,256]{1,0:T(8,128)(2,1)S(1)} %collective-permute-done.13.refs_3_), channel_id=1, source_target_pairs={{2,3},{6,7},{10,11},{14,15},{18,19},{22,23},{26,27},{30,31}} | collective-permute-start | bytes 1572872 | tf_op jit(solution)/shard_map/ppermute | solution.py:27
  348.7 18.5 %copy-start.28 = (bf16[1024,256]{1,0:T(8,128)(2,1)}, bf16[1024,256]{1,0:T(8,128)(2,1)S(1)}, u32[]{:S(2)}) copy-start(bf16[1024,256]{1,0:T(8,128)(2,1)S(1)} %collective-permute-done.16.refs_6_) | copy-start | bytes 1572868
  348.7 21.7 %collective-permute-start.17 = (bf16[1024,256]{1,0:T(8,128)(2,1)S(1)}, bf16[1024,256]{1,0:T(8,128)(2,1)S(1)}, u32[]{:S(2)}, u32[]{:S(2)}) collective-permute-start(bf16[1024,256]{1,0:T(8,128)(2,1)S(1)} %collective-permute-done.16.refs_6_), channel_id=1, source_target_pairs={{1,0},{5,4},{9,8},{13,12},{17,16},{21,20},{25,24},{29,28}} | collective-permute-start | bytes 1572872 | tf_op jit(solution)/shard_map/ppermute | solution.py:28
  350.0 10.0 %copy-start.31 = (bf16[1024,256]{1,0:T(8,128)(2,1)}, bf16[1024,256]{1,0:T(8,128)(2,1)S(1)}, u32[]{:S(2)}) copy-start(bf16[1024,256]{1,0:T(8,128)(2,1)S(1)} %collective-permute-done.20.refs_4_) | copy-start | bytes 1572868
  360.0 0.8 copy-start.33
  367.2 3.2 copy-start.30
  370.4 0.8 copy-start.32

commit v15 on v11

--- a/solution.py
+++ b/solution.py
@@ -330,11 +330,11 @@
     gated = jnp.concatenate([gated_ref[z] for z in range(gated_ref.shape[0])], axis=1)
     total = jnp.dot(gated, w_ref[0], preferred_element_type=jnp.float32)
     if len(refs) == 2:
-        total = total + refs[0][...]
+        total = total + refs[0][...].astype(jnp.float32)
     out_ref[...] = total.astype(out_ref.dtype)
 
 
-def combine(gathered, weight, chunk, total, dtype):
+def combine(gathered, weight, chunk, total):
     count, tok_rows, size = gathered.shape
     depth = count * size
     features = weight.shape[2]
@@ -350,7 +350,7 @@
             *[block for _ in given],
         ],
         out_specs=block,
-        out_shape=jax.ShapeDtypeStruct((tok_rows, features), dtype),
+        out_shape=jax.ShapeDtypeStruct((tok_rows, features), jnp.bfloat16),
         compiler_params=pltpu.CompilerParams(vmem_limit_bytes=60 * MIB),
         cost_estimate=pl.CostEstimate(
             flops=2 * tok_rows * depth * features,
@@ -387,15 +387,18 @@
     total = None
     for j, lo in enumerate(range(0, chans, size)):
         given = (gathered, in_weight, conv_weight, halo, lo, size, response, weight)
-        query_t, signal, signal_t = project((0, 1, 2), *given)
+        if lo == 0 and chunks > 1:
+            signal, signal_t = project((1, 2), *given)
+            (query_t,) = project((0,), *given)
+        else:
+            query_t, signal, signal_t = project((0, 1, 2), *given)
         values = signal.reshape(seq_count, size // seq_count, tok_rows)
         values = lax.all_to_all(values, "seq", split_axis=0, concat_axis=0, tiled=True)
         longconv = lax.all_to_all(
             long_conv(values, response, lo // seq_count), "seq", split_axis=0, concat_axis=0, tiled=True
         ).reshape(size, tok_rows)
         gated = lax.all_gather(gate(longconv, skip, lo, signal_t, query_t), "chan")
-        dtype = jnp.bfloat16 if lo + size == chans else jnp.float32
-        total = combine(gated, weight, j, total, dtype)
+        total = combine(gated, weight, j, total)
     return total
 
 

time: 311 us -> 312 us (level)
  blocking collectives: 49.7 us -> 37.6 us
  waiting for transfers between devices: 135 us -> 140 us
  Pallas kernels: 54.3 us -> 58.2 us
    all_to_all x2 -> x1, blocking collectives: 24.3 us -> 12.2 us  [shards(): lax.all_to_all(long_conv(values, response, lo // seq_count), 'seq', split...]
    pallas_call x2 -> x3, Pallas kernels: 21.5 us -> 25.5 us  [project(): pl.pallas_call(lambda *refs: project_kernel(streams, len(after), *refs),...]
    all_to_all x0 -> x1, waiting for transfers between devices: none -> 3.54 us  [shards(): lax.all_to_all(long_conv(values, response, lo // seq_count), 'seq', split...]
    all_to_all x0 -> x1, starting transfers between devices: none -> 3.49 us  [shards(): lax.all_to_all(long_conv(values, response, lo // seq_count), 'seq', split...]
  transfers between devices with their start and end apart: 11 -> 12, of which waited for: 8 -> 9; matrix products, arithmetic and copies ran while one was open for 9% -> 9% of each run, Pallas kernels for 11% -> 13%
where the time goes in v15:
time: 312 us; the launch traced here: 311 us
  waiting for transfers between devices  140 us (45%)
  Pallas kernels  58.2 us (19%)
  blocking collectives  37.6 us (12%)
  starting transfers between devices  33.2 us (11%)
  local copies, waits for them, and re-layouts  18.5 us (6%)
  between operations  13.5 us (4%)
  matrix products  6.3 us (2%)
  other arithmetic  3.57 us (1%)
    all_gather x2, waiting for transfers between devices, shards(): gated = lax.all_gather(gate(longconv, skip, lo, signal_t, query_t), 'chan')  44.8 us
    all_to_all x1, waiting for transfers between devices, folded_response(): got = lax.all_to_all(sent, 'seq', split_axis=0, concat_axis=0, tiled=True)  28.8 us
    ppermute x5, waiting for transfers between devices, gather_by_doubling(): other = lax.ppermute(held, axis, [(i, i ^ bit) for i in range(size)])  28.7 us
    pallas_call x3, Pallas kernels, project(): pl.pallas_call(lambda *refs: project_kernel(streams, len(after), *refs),...  25.5 us
    all_to_all x2, blocking collectives, shards(): lax.all_to_all(values, 'seq', split_axis=0, concat_axis=0, tiled=True)  25.4 us
    all_to_all x1, waiting for transfers between devices, feature_rows(): own = lax.all_to_all(own, 'chan', split_axis=1, concat_axis=0, tiled=True)  22.6 us
    ppermute x5, starting transfers between devices, gather_by_doubling(): other = lax.ppermute(held, axis, [(i, i ^ bit) for i in range(size)])  17.5 us
    all_to_all x1, blocking collectives, shards(): lax.all_to_all(long_conv(values, response, lo // seq_count), 'seq', split...  12.2 us
  transfers between devices with their start and end apart: 12, of which 9 were waited for; matrix products, arithmetic and copies ran while one was open for 9% of the time, Pallas kernels for 13%

profile of v15, /device:TPU:0, one launch (start us, length us, event | category | flops | bytes accessed | tf_op | source)
XLA Modules:
  0.0 310.6 jit_solution(11879728912655353065)
XLA Ops:
  6.5 0.7 all-gather.7.cloned.1.call-update
  7.3 1.1 constant_dynamic-slice_fusion
  8.3 0.8 copy.35
  9.2 6.3 %all-to-all-start = ((bf16[64,4,1024]{2,0,1:T(8,128)(2,1)}), bf16[64,4,1024]{2,0,1:T(8,128)(2,1)S(1)}, u32[]{:S(2)}, u32[]{:S(2)}) async-start(bf16[64,4,1024]{2,0,1:T(8,128)(2,1)} %bitcast.76), calls=%async_computation | async-start | bytes 1048576 | tf_op jit(solution)/shard_map/all_to_all | solution.py:324
  15.5 0.8 slice.3
  16.3 22.6 %all-to-all-done = bf16[64,4,1024]{2,0,1:T(8,128)(2,1)S(1)} async-done(((bf16[64,4,1024]{2,0,1:T(8,128)(2,1)}), bf16[64,4,1024]{2,0,1:T(8,128)(2,1)S(1)}, u32[]{:S(2)}, u32[]{:S(2)}) %all-to-all-start) | async-done | bytes 524320 | tf_op jit(solution)/shard_map/all_to_all | solution.py:324
  38.9 1.3 collective-permute-start
  40.2 0.8 collective-permute-done
  41.0 0.0 collective-permute-start.1
  41.0 0.7 fusion.1.order_ref
  41.7 10.9 %reshape.40.spec_ref = f32[2,1024,1024]{2,1,0:T(8,128)} reshape(f32[2,512,2,1024]{3,2,1,0:T(2,128)} %param.21) | data formatting | bytes 16777216 | tf_op jit(solution)/shard_map/reshape | solution.py:296
  52.6 0.0 collective-permute-done.1
  52.7 9.1 %collective-permute-start.2 = (bf16[2,16,1024]{2,1,0:T(8,128)(2,1)S(1)}, bf16[2,16,1024]{2,1,0:T(8,128)(2,1)S(1)}, u32[]{:S(2)}, u32[]{:S(2)}) collective-permute-start(bf16[2,16,1024]{2,1,0:T(8,128)(2,1)S(1)} %maximum_bitcast_fusion.1), channel_id=1, source_target_pairs={{0,1},{1,0},{2,3},{3,2},{4,5},{5,4},{6,7},{7,6},{8,9},{9,8},{10,11... | collective-permute-start | bytes 196616 | tf_op jit(solution)/shard_map/ppermute | solution.py:29
  61.8 8.5 %shard_map.172 = bf16[8,2,2,64,1024]{4,3,2,1,0:T(8,128)(2,1)} custom-call(f32[2,1024,1024]{2,1,0:T(8,128)} %reshape.40.spec_ref, bf16[1024,1024]{1,0:T(8,128)(2,1)S(1)} %fusion.1.order_ref), custom_call_target="tpu_custom_call" | custom-call | flops 4294967296 | bytes 12582912 | tf_op jit(solution)/shard_map/pallas_call | solution.py:283
  70.3 0.0 collective-permute-done.2
  70.4 6.7 %collective-permute-start.3 = (bf16[1,4,64,1024]{3,2,1,0:T(8,128)(2,1)S(1)}, bf16[1,4,64,1024]{3,2,1,0:T(8,128)(2,1)S(1)}, u32[]{:S(2)}, u32[]{:S(2)}) collective-permute-start(bf16[1,4,64,1024]{3,2,1,0:T(8,128)(2,1)S(1)} %bitcast.95), channel_id=1, source_target_pairs={{0,16},{4,20},{8,24},{12,28},{16,0},{20,4},{24,8},{28,12},{1,17},{... | collective-permute-start | bytes 1572872 | tf_op jit(solution)/shard_map/ppermute | solution.py:29
  77.1 8.7 %collective-permute-done.3 = bf16[1,4,64,1024]{3,2,1,0:T(8,128)(2,1)S(1)} collective-permute-done((bf16[1,4,64,1024]{3,2,1,0:T(8,128)(2,1)S(1)}, bf16[1,4,64,1024]{3,2,1,0:T(8,128)(2,1)S(1)}, u32[]{:S(2)}, u32[]{:S(2)}) %collective-permute-start.3) | collective-permute-done | bytes 524320 | tf_op jit(solution)/shard_map/ppermute | solution.py:29
  85.8 0.1 select_bitcast_fusion.5
  85.9 0.1 maximum_bitcast_fusion
  86.0 1.6 collective-permute-start.4
  87.5 4.6 %all-to-all-start.1 = ((bf16[8,2,2,64,1024]{4,3,2,1,0:T(8,128)(2,1)}), bf16[8,2,2,64,1024]{4,3,2,1,0:T(8,128)(2,1)}, u32[]{:S(2)}, u32[]{:S(2)}) async-start(bf16[8,2,2,64,1024]{4,3,2,1,0:T(8,128)(2,1)} %shard_map.172), calls=%async_computation.1 | async-start | bytes 8388608 | tf_op jit(solution)/shard_map/all_to_all | solution.py:303
  92.1 20.0 %collective-permute-done.4 = bf16[2,4,64,1024]{3,2,1,0:T(8,128)(2,1)S(1)} collective-permute-done((bf16[2,4,64,1024]{3,2,1,0:T(8,128)(2,1)S(1)}, bf16[2,4,64,1024]{3,2,1,0:T(8,128)(2,1)S(1)}, u32[]{:S(2)}, u32[]{:S(2)}) %collective-permute-start.4) | collective-permute-done | bytes 1048608 | tf_op jit(solution)/shard_map/ppermute | solution.py:29
  112.1 0.1 select_bitcast_fusion.3
  112.3 0.2 pad_maximum_fusion.1
  112.5 0.1 collective-permute-start.5
  112.6 6.3 %fusion.3.refs_5_.refs_4_.refs_3_ = bf16[3,16,512]{2,1,0:T(8,128)(2,1)S(1)} fusion(bf16[3,4,1024,512]{3,2,1,0:T(8,128)(2,1)} %bitcast.83, bf16[4,16,1024]{2,1,0:T(8,128)(2,1)S(1)} %bitcast.99), kind=kOutput, calls=%fused_computation.9 | convolution fusion | flops 201351168 | bytes 12763136 | tf_op jit(solution)/shard_map/ztd,pzdc->ptc/dot_general | solution.py:381
  118.9 0.0 collective-permute-done.5
  118.9 1.9 select_bitcast_fusion.1
  120.8 0.4 pad_maximum_fusion
  121.2 0.7 copy.30
  121.9 2.5 copy.31
  124.4 28.8 %all-to-all-done.1.got_ref = bf16[8,2,2,64,1024]{4,3,2,1,0:T(8,128)(2,1)} async-done(((bf16[8,2,2,64,1024]{4,3,2,1,0:T(8,128)(2,1)}), bf16[8,2,2,64,1024]{4,3,2,1,0:T(8,128)(2,1)}, u32[]{:S(2)}, u32[]{:S(2)}) %all-to-all-start.1) | async-done | bytes 4194336 | tf_op jit(solution)/shard_map/all_to_all | solution.py:303
  153.1 4.0 %shard_map.173.refs_6_.resp_ref.refs_5_.refs_4_ = bf16[2,64,72,128]{3,2,1,0:T(8,128)(2,1)S(1)} custom-call(bf16[8,2,2,64,1024]{4,3,2,1,0:T(8,128)(2,1)} %all-to-all-done.1.got_ref), custom_call_target="tpu_custom_call" | custom-call | flops 2097152 | bytes 6291456 | tf_op jit(solution)/shard_map/pallas_call | solution.py:306
  157.2 9.8 %all-gather.7.cloned.1.call-done = bf16[4096,1024]{1,0:T(8,128)(2,1)} async-done(((bf16[1024,1024]{1,0:T(8,128)(2,1)}), bf16[4096,1024]{1,0:T(8,128)(2,1)}) %all-gather.7.cloned.1.call-update) | async-done | bytes 8388624 | tf_op jit(solution)/shard_map/all_gather | solution.py:370
  167.0 0.0 copy-start.8
  167.0 0.0 copy-start.9
  167.0 0.0 copy-start.11
  167.0 8.6 %shard_map.177 = (bf16[256,1024]{1,0:T(8,128)(2,1)S(1)}, bf16[1024,256]{1,0:T(8,128)(2,1)S(1)}) custom-call(bf16[4,1024,1024]{2,1,0:T(8,128)(2,1)} %bitcast.89, bf16[3,4096,512]{2,1,0:T(8,128)(2,1)} %refs_1_.5, bf16[3,4096,512]{2,1,0:T(8,128)(2,1)} %refs_1_.5, f32[3,3,512]{2,1,0:T(4,128)S(1)} %copy-done.6, ...), custom_call_target="tpu_custom_call" | custom-call | flops 4294967296 | bytes 12582912 | tf_op jit(solution)/shard_map/pallas_call | solution.py:95
  175.6 13.3 %all_to_all.41.signal_ref = bf16[8,32,1024]{2,1,0:T(8,128)(2,1)S(1)} all-to-all(bf16[8,32,1024]{2,1,0:T(8,128)(2,1)S(1)} %bitcast.80), channel_id=1, replica_groups=mesh['seq'=8,'chan'=4] {'seq'}, dimensions={0} | all-to-all | bytes 1048576 | tf_op jit(solution)/shard_map/all_to_all | solution.py:396
  188.9 3.6 %shard_map.178 = bf16[8,32,1024]{2,1,0:T(8,128)(2,1)} custom-call(bf16[8,32,1024]{2,1,0:T(8,128)(2,1)S(1)} %all_to_all.41.signal_ref, bf16[2,64,72,128]{3,2,1,0:T(8,128)(2,1)S(1)} %shard_map.173.refs_6_.resp_ref.refs_5_.refs_4_, bf16[144,64]{1,0:T(8,128)(2,1)S(1)} %copy-done.7, bf16[64,144]{1,0:T(8,128)(2,1)S(1)} %copy-done.11, f32[72,128]{1,0:T(8,128)S(1)} %copy-done.8, ...), custom_call_target="tpu_custom_call" | custom-call | flops 754974720 | bytes 2228224 | tf_op jit(solution)/shard_map/pallas_call | solution.py:194
  192.6 3.5 %all-to-all-start.5 = ((bf16[8,32,1024]{2,1,0:T(8,128)(2,1)}), bf16[8,32,1024]{2,1,0:T(8,128)(2,1)S(1)}, u32[]{:S(2)}, u32[]{:S(2)}) async-start(bf16[8,32,1024]{2,1,0:T(8,128)(2,1)} %shard_map.178), calls=%async_computation.5 | async-start | bytes 1048576 | tf_op jit(solution)/shard_map/all_to_all | solution.py:397
  196.1 0.0 all-gather.11.cloned.1.call-start
  196.1 6.1 %shard_map.179.query_ref = bf16[1024,256]{1,0:T(8,128)(2,1)S(1)} custom-call(bf16[4,1024,1024]{2,1,0:T(8,128)(2,1)} %bitcast.90, bf16[3,4096,512]{2,1,0:T(8,128)(2,1)} %refs_1_.5, f32[3,3,512]{2,1,0:T(4,128)S(1)} %copy-done.6, bf16[3,16,512]{2,1,0:T(8,128)(2,1)S(1)} %fusion.3.refs_5_.refs_4_.refs_3_, ...), custom_call_target="tpu_custom_call" | custom-call | flops 2147483648 | bytes 10485760 | tf_op jit(solution)/shard_map/pallas_call | solution.py:95
  202.2 3.5 %all-to-all-done.5 = bf16[8,32,1024]{2,1,0:T(8,128)(2,1)S(1)} async-done(((bf16[8,32,1024]{2,1,0:T(8,128)(2,1)}), bf16[8,32,1024]{2,1,0:T(8,128)(2,1)S(1)}, u32[]{:S(2)}, u32[]{:S(2)}) %all-to-all-start.5) | async-done | bytes 524320 | tf_op jit(solution)/shard_map/all_to_all | solution.py:397
  205.7 1.0 copy-done.1
  206.8 0.7 copy-done.13
  207.5 1.2 shard_map.180
  208.7 0.0 all-gather.11.cloned.1.call-update
  208.7 0.0 copy-start.3
  208.7 0.0 copy-start.5
  208.7 0.0 copy-start.10
  208.8 0.0 copy-start.12
  208.8 0.0 all-gather.9.cloned.1.call-start
  208.8 10.8 %shard_map.174 = (bf16[1024,256]{1,0:T(8,128)(2,1)S(1)}, bf16[256,1024]{1,0:T(8,128)(2,1)S(1)}, bf16[1024,256]{1,0:T(8,128)(2,1)S(1)}) custom-call(bf16[4,1024,1024]{2,1,0:T(8,128)(2,1)} %bitcast.91, bf16[3,4096,512]{2,1,0:T(8,128)(2,1)} %refs_1_.5, bf16[3,4096,512]{2,1,0:T(8,128)(2,1)} %refs_1_.5, bf16[3,4096,512]{2,1,0:T(8,128)(2,1)} %refs_1_.5, ...), custom_call_target="tpu_custom_call" | custom-call | flops 6442450944 | bytes 14680064 | tf_op jit(solution)/shard_map/pallas_call | solution.py:95
  219.6 0.0 copy-start.14
  219.6 12.2 %all_to_all.42.signal_ref = bf16[8,32,1024]{2,1,0:T(8,128)(2,1)S(1)} all-to-all(bf16[8,32,1024]{2,1,0:T(8,128)(2,1)S(1)} %bitcast.79), channel_id=1, replica_groups=mesh['seq'=8,'chan'=4] {'seq'}, dimensions={0} | all-to-all | bytes 1048576 | tf_op jit(solution)/shard_map/all_to_all | solution.py:396
  231.8 3.0 shard_map.175
  234.8 12.2 %all_to_all.43 = bf16[8,32,1024]{2,1,0:T(8,128)(2,1)S(1)} all-to-all(bf16[8,32,1024]{2,1,0:T(8,128)(2,1)S(1)} %shard_map.175), channel_id=1, replica_groups=mesh['seq'=8,'chan'=4] {'seq'}, dimensions={0} | all-to-all | bytes 1048576 | tf_op jit(solution)/shard_map/all_to_all | solution.py:397
  246.9 1.2 shard_map.176
  248.1 0.0 all-gather.9.cloned.1.call-update
  248.2 3.9 %all-gather.11.cloned.1.call-done = bf16[4096,256]{1,0:T(8,128)(2,1)} async-done(((bf16[1024,256]{1,0:T(8,128)(2,1)}), bf16[4096,256]{1,0:T(8,128)(2,1)}) %all-gather.11.cloned.1.call-update) | async-done | bytes 2097168 | tf_op jit(solution)/shard_map/all_gather | solution.py:400
  252.1 5.4 %shard_map.181.refs_0_ = bf16[1024,1024]{1,0:T(8,128)(2,1)} custom-call(bf16[4,1024,256]{2,1,0:T(8,128)(2,1)} %bitcast.98, bf16[2,1024,1024]{2,1,0:T(8,128)(2,1)} %bitcast.87), custom_call_target="tpu_custom_call" | custom-call | flops 2147483648 | bytes 10485760 | tf_op jit(solution)/shard_map/pallas_call | solution.py:344
  257.5 40.9 %all-gather.9.cloned.1.call-done = bf16[4096,256]{1,0:T(8,128)(2,1)} async-done(((bf16[1024,256]{1,0:T(8,128)(2,1)}), bf16[4096,256]{1,0:T(8,128)(2,1)}) %all-gather.9.cloned.1.call-update) | async-done | bytes 2097168 | tf_op jit(solution)/shard_map/all_gather | solution.py:400
  298.4 5.7 %shard_map.182 = bf16[1024,1024]{1,0:T(8,128)(2,1)} custom-call(bf16[4,1024,256]{2,1,0:T(8,128)(2,1)} %bitcast.94, bf16[2,1024,1024]{2,1,0:T(8,128)(2,1)} %bitcast.88, bf16[1024,1024]{1,0:T(8,128)(2,1)} %shard_map.181.refs_0_), custom_call_target="tpu_custom_call" | custom-call | flops 2147483648 | bytes 10485760 | tf_op jit(solution)/shard_map/pallas_call | solution.py:344
  (28 shorter events, 0.1 us)
Async XLA Ops:
  6.5 160.5 %all-gather.7.cloned.1.call-start = ((), (), s32[]{:S(2)}) async-start(), calls=%async_computation.6 | async-start | bytes 10485760 | tf_op jit(solution)/shard_map/all_gather | solution.py:370
  9.2 29.7 %all-to-all-start = ((bf16[64,4,1024]{2,0,1:T(8,128)(2,1)}), bf16[64,4,1024]{2,0,1:T(8,128)(2,1)S(1)}, u32[]{:S(2)}, u32[]{:S(2)}) async-start(bf16[64,4,1024]{2,0,1:T(8,128)(2,1)} %bitcast.76), calls=%async_computation | async-start | bytes 1048576 | tf_op jit(solution)/shard_map/all_to_all | solution.py:324
  38.9 2.1 collective-permute-start
  41.0 11.7 %collective-permute-start.1 = (bf16[1,16,1024]{2,1,0:T(8,128)(2,1)S(1)}, bf16[1,16,1024]{2,1,0:T(8,128)(2,1)S(1)}, u32[]{:S(2)}, u32[]{:S(2)}) collective-permute-start(bf16[1,16,1024]{2,1,0:T(8,128)(2,1)S(1)} %bitcast.100), channel_id=1, source_target_pairs={{0,2},{1,3},{2,0},{3,1},{4,6},{5,7},{6,4},{7,5},{8,10},{9,11},{10,... | collective-permute-start | bytes 98312 | tf_op jit(solution)/shard_map/ppermute | solution.py:29
  52.7 17.7 %collective-permute-start.2 = (bf16[2,16,1024]{2,1,0:T(8,128)(2,1)S(1)}, bf16[2,16,1024]{2,1,0:T(8,128)(2,1)S(1)}, u32[]{:S(2)}, u32[]{:S(2)}) collective-permute-start(bf16[2,16,1024]{2,1,0:T(8,128)(2,1)S(1)} %maximum_bitcast_fusion.1), channel_id=1, source_target_pairs={{0,1},{1,0},{2,3},{3,2},{4,5},{5,4},{6,7},{7,6},{8,9},{9,8},{10,11... | collective-permute-start | bytes 196616 | tf_op jit(solution)/shard_map/ppermute | solution.py:29
  70.4 15.4 %collective-permute-start.3 = (bf16[1,4,64,1024]{3,2,1,0:T(8,128)(2,1)S(1)}, bf16[1,4,64,1024]{3,2,1,0:T(8,128)(2,1)S(1)}, u32[]{:S(2)}, u32[]{:S(2)}) collective-permute-start(bf16[1,4,64,1024]{3,2,1,0:T(8,128)(2,1)S(1)} %bitcast.95), channel_id=1, source_target_pairs={{0,16},{4,20},{8,24},{12,28},{16,0},{20,4},{24,8},{28,12},{1,17},{... | collective-permute-start | bytes 1572872 | tf_op jit(solution)/shard_map/ppermute | solution.py:29
  86.0 26.2 %collective-permute-start.4 = (bf16[2,4,64,1024]{3,2,1,0:T(8,128)(2,1)S(1)}, bf16[2,4,64,1024]{3,2,1,0:T(8,128)(2,1)S(1)}, u32[]{:S(2)}, u32[]{:S(2)}) collective-permute-start(bf16[2,4,64,1024]{3,2,1,0:T(8,128)(2,1)S(1)} %maximum_bitcast_fusion), channel_id=1, source_target_pairs={{0,8},{4,12},{8,0},{12,4},{16,24},{20,28},{24,16},{28,20},{1,9},{5... | collective-permute-start | bytes 3145736 | tf_op jit(solution)/shard_map/ppermute | solution.py:29
  87.5 65.6 %all-to-all-start.1 = ((bf16[8,2,2,64,1024]{4,3,2,1,0:T(8,128)(2,1)}), bf16[8,2,2,64,1024]{4,3,2,1,0:T(8,128)(2,1)}, u32[]{:S(2)}, u32[]{:S(2)}) async-start(bf16[8,2,2,64,1024]{4,3,2,1,0:T(8,128)(2,1)} %shard_map.172), calls=%async_computation.1 | async-start | bytes 8388608 | tf_op jit(solution)/shard_map/all_to_all | solution.py:303
  112.5 6.4 %collective-permute-start.5 = (bf16[4,4,64,1024]{3,2,1,0:T(8,128)(2,1)S(1)}, bf16[4,4,64,1024]{3,2,1,0:T(8,128)(2,1)}, u32[]{:S(2)}, u32[]{:S(2)}) collective-permute-start(bf16[4,4,64,1024]{3,2,1,0:T(8,128)(2,1)S(1)} %bitcast.93), channel_id=1, source_target_pairs={{0,4},{4,0},{8,12},{12,8},{16,20},{20,16},{24,28},{28,24},{1,5},{5... | collective-permute-start | bytes 6291464 | tf_op jit(solution)/shard_map/ppermute | solution.py:29
  124.3 42.6 %copy-start.6 = (f32[3,3,512]{2,1,0:T(4,128)S(1)}, f32[3,3,512]{2,1,0:T(4,128)}, u32[]{:S(2)}) copy-start(f32[3,3,512]{2,1,0:T(4,128)} %refs_2_.5) | copy-start | bytes 55300
  167.0 21.9 %copy-start.2 = (bf16[256,256]{1,0:T(8,128)(2,1)S(1)}, bf16[256,256]{1,0:T(8,128)(2,1)}, u32[]{:S(2)}) copy-start(bf16[256,256]{1,0:T(8,128)(2,1)} %constant.138.clone.fwd_ref) | copy-start | bytes 393220
  167.0 21.9 %copy-start.4 = (bf16[256,256]{1,0:T(8,128)(2,1)S(1)}, bf16[256,256]{1,0:T(8,128)(2,1)}, u32[]{:S(2)}) copy-start(bf16[256,256]{1,0:T(8,128)(2,1)} %constant.139.clone.bwd_ref) | copy-start | bytes 393220
  167.0 21.9 %copy-start.7 = (bf16[144,64]{1,0:T(8,128)(2,1)S(1)}, bf16[144,64]{1,0:T(8,128)(2,1)}, u32[]{:S(2)}) copy-start(bf16[144,64]{1,0:T(8,128)(2,1)} %constant.134.clone.first_ref) | copy-start | bytes 55300
  167.0 21.9 %copy-start.8 = (f32[72,128]{1,0:T(8,128)S(1)}, f32[72,128]{1,0:T(8,128)}, u32[]{:S(2)}) copy-start(f32[72,128]{1,0:T(8,128)} %constant.136.clone.cos_ref) | copy-start | bytes 110596
  167.0 21.9 %copy-start.9 = (f32[72,128]{1,0:T(8,128)S(1)}, f32[72,128]{1,0:T(8,128)}, u32[]{:S(2)}) copy-start(f32[72,128]{1,0:T(8,128)} %constant.137.clone.sin_ref) | copy-start | bytes 110596
  167.0 21.9 %copy-start.11 = (bf16[64,144]{1,0:T(8,128)(2,1)S(1)}, bf16[64,144]{1,0:T(8,128)(2,1)}, u32[]{:S(2)}) copy-start(bf16[64,144]{1,0:T(8,128)(2,1)} %constant.135.clone.last_ref) | copy-start | bytes 55300
  175.6 16.9 %copy-start = (bf16[1024,256]{1,0:T(8,128)(2,1)}, bf16[1024,256]{1,0:T(8,128)(2,1)S(1)}, u32[]{:S(2)}) copy-start(bf16[1024,256]{1,0:T(8,128)(2,1)S(1)} %get-tuple-element.24.signal_ref) | copy-start | bytes 1572868
  192.6 13.2 %all-to-all-start.5 = ((bf16[8,32,1024]{2,1,0:T(8,128)(2,1)}), bf16[8,32,1024]{2,1,0:T(8,128)(2,1)S(1)}, u32[]{:S(2)}, u32[]{:S(2)}) async-start(bf16[8,32,1024]{2,1,0:T(8,128)(2,1)} %shard_map.178), calls=%async_computation.5 | async-start | bytes 1048576 | tf_op jit(solution)/shard_map/all_to_all | solution.py:397
  196.1 56.0 %all-gather.11.cloned.1.call-start = ((), (), s32[]{:S(2)}) async-start(), calls=%async_computation.8 | async-start | bytes 2621440 | tf_op jit(solution)/shard_map/all_gather | solution.py:400
  205.7 1.0 copy-start.1
  206.8 0.7 copy-start.13
  208.7 23.1 %copy-start.3 = (bf16[256,256]{1,0:T(8,128)(2,1)S(1)}, bf16[256,256]{1,0:T(8,128)(2,1)}, u32[]{:S(2)}) copy-start(bf16[256,256]{1,0:T(8,128)(2,1)} %constant.138.clone.fwd_ref) | copy-start | bytes 393220
  208.7 23.1 %copy-start.5 = (bf16[256,256]{1,0:T(8,128)(2,1)S(1)}, bf16[256,256]{1,0:T(8,128)(2,1)}, u32[]{:S(2)}) copy-start(bf16[256,256]{1,0:T(8,128)(2,1)} %constant.139.clone.bwd_ref) | copy-start | bytes 393220
  208.7 23.1 %copy-start.10 = (f32[72,128]{1,0:T(8,128)S(1)}, f32[72,128]{1,0:T(8,128)}, u32[]{:S(2)}) copy-start(f32[72,128]{1,0:T(8,128)} %constant.137.clone.sin_ref) | copy-start | bytes 110596
  208.8 23.0 %copy-start.12 = (bf16[64,144]{1,0:T(8,128)(2,1)S(1)}, bf16[64,144]{1,0:T(8,128)(2,1)}, u32[]{:S(2)}) copy-start(bf16[64,144]{1,0:T(8,128)(2,1)} %constant.135.clone.last_ref) | copy-start | bytes 55300
  208.8 89.6 %all-gather.9.cloned.1.call-start = ((), (), s32[]{:S(2)}) async-start(), calls=%async_computation.7 | async-start | bytes 2621440 | tf_op jit(solution)/shard_map/all_gather | solution.py:400
  219.6 27.3 %copy-start.14 = (f32[512]{0:T(512)S(1)}, f32[512]{0:T(512)}, u32[]{:S(2)}) copy-start(f32[512]{0:T(512)} %param.22) | copy-start | bytes 6148
Sparse Core Ops, SparseCore 0:
  8.9 158.0 all-gather.6
  208.8 43.1 all-gather.10
  253.6 44.6 all-gather.8

commit v16 on v12

--- a/solution.py
+++ b/solution.py
@@ -196,7 +196,7 @@
         out_specs=pl.BlockSpec((seq_count, block, tok_rows), lambda i: (0, i, 0)),
         out_shape=jax.ShapeDtypeStruct((seq_count, chans, tok_rows), jnp.bfloat16),
         scratch_shapes=[
-            pltpu.VMEM((block * span, LANES), jnp.float32),
+            pltpu.VMEM((block * span + span, LANES), jnp.float32),
             pltpu.VMEM((block * rows, 2 * LANES), jnp.bfloat16),
             pltpu.VMEM((block * rows, 2 * LANES), jnp.float32),
         ],
@@ -260,7 +260,7 @@
                 elif k1 > 0:
                     value = value + sign * came[pl.ds((other // 2 * runs + r) * pairs + other % 2, chans, stride=2), :]
                 held[pl.ds(k1 * runs + r, chans, stride=rows), :] = value
-        out_ref[part] = held[...].reshape(chans, rows, LANES).astype(out_ref.dtype)
+        out_ref[part] = held[: chans * rows, :].reshape(chans, rows, LANES).astype(out_ref.dtype)
 
 
 def reordered_spectrum(spectrum, seq_count, chunks):
@@ -304,8 +304,8 @@
         out_specs=pl.BlockSpec((parts, block, rows, LANES), lambda j, i: (0, j * (each // block) + i, 0, 0)),
         out_shape=jax.ShapeDtypeStruct((parts, chunks * each, rows, LANES), jnp.bfloat16),
         scratch_shapes=[
-            pltpu.VMEM((seq_count * runs * own * block, LANES), jnp.float32),
-            pltpu.VMEM((block * rows, LANES), jnp.float32),
+            pltpu.VMEM((seq_count * runs * own * block + 8, LANES), jnp.float32),
+            pltpu.VMEM((block * rows + rows, LANES), jnp.float32),
         ],
         compiler_params=pltpu.CompilerParams(vmem_limit_bytes=12 * MIB),
         cost_estimate=pl.CostEstimate(flops=sent.size, bytes_accessed=3 * sent.size, transcendentals=0),

time: 310 us -> 310 us (level)
  no operation moved by 1% of the time
where the time goes in v16:
time: 310 us
  waiting for transfers between devices  136 us (44%)
  Pallas kernels  54 us (17%)
  blocking collectives  49.7 us (16%)
  starting transfers between devices  30.1 us (10%)
  local copies, waits for them, and re-layouts  16.8 us (5%)
  between operations  13.4 us (4%)
  matrix products  6.3 us (2%)
  other arithmetic  3.57 us (1%)
    all_gather x2, waiting for transfers between devices, shards(): gated = lax.all_gather(gate(longconv, skip, lo, signal_t, query_t), 'chan')  44.4 us
    all_to_all x1, waiting for transfers between devices, folded_response(): got = lax.all_to_all(sent, 'seq', split_axis=0, concat_axis=0, tiled=True)  28.8 us
    ppermute x5, waiting for transfers between devices, gather_by_doubling(): other = lax.ppermute(held, axis, [(i, i ^ bit) for i in range(size)])  28.5 us
    all_to_all x2, blocking collectives, shards(): lax.all_to_all(values, 'seq', split_axis=0, concat_axis=0, tiled=True)  25.4 us
    all_to_all x2, blocking collectives, shards(): lax.all_to_all(long_conv(values, response, lo // seq_count), 'seq', split...  24.3 us
    all_to_all x1, waiting for transfers between devices, feature_rows(): own = lax.all_to_all(own, 'chan', split_axis=1, concat_axis=0, tiled=True)  22.6 us
    pallas_call x2, Pallas kernels, project(): pl.pallas_call(lambda *refs: project_kernel(len(after), *refs), grid=(cou...  21.2 us
    ppermute x5, starting transfers between devices, gather_by_doubling(): other = lax.ppermute(held, axis, [(i, i ^ bit) for i in range(size)])  17.4 us
  transfers between devices with their start and end apart: 11, of which 8 were waited for; matrix products, arithmetic and copies ran while one was open for 9% of the time, Pallas kernels for 11%

profile of v16, /device:TPU:0, one launch (start us, length us, event | category | flops | bytes accessed | tf_op | source)
XLA Modules:
  0.0 309.5 jit_solution(18041176696755993437)
XLA Ops:
  6.5 0.0 all-gather.7.cloned.1.call-start
  6.5 0.7 all-gather.7.cloned.1.call-update
  7.3 1.1 constant_dynamic-slice_fusion
  8.3 0.8 copy.35
  9.2 6.3 %all-to-all-start = ((bf16[64,4,1024]{2,0,1:T(8,128)(2,1)}), bf16[64,4,1024]{2,0,1:T(8,128)(2,1)S(1)}, u32[]{:S(2)}, u32[]{:S(2)}) async-start(bf16[64,4,1024]{2,0,1:T(8,128)(2,1)} %bitcast.76), calls=%async_computation | async-start | bytes 1048576 | tf_op jit(solution)/shard_map/all_to_all | solution.py:318
  15.5 0.8 slice.3
  16.3 22.6 %all-to-all-done = bf16[64,4,1024]{2,0,1:T(8,128)(2,1)S(1)} async-done(((bf16[64,4,1024]{2,0,1:T(8,128)(2,1)}), bf16[64,4,1024]{2,0,1:T(8,128)(2,1)S(1)}, u32[]{:S(2)}, u32[]{:S(2)}) %all-to-all-start) | async-done | bytes 524320 | tf_op jit(solution)/shard_map/all_to_all | solution.py:318
  38.9 1.3 collective-permute-start
  40.2 0.8 collective-permute-done
  41.0 0.0 collective-permute-start.1
  41.0 0.7 fusion.1.order_ref
  41.7 10.9 %reshape.40.spec_ref = f32[2,1024,1024]{2,1,0:T(8,128)} reshape(f32[2,512,2,1024]{3,2,1,0:T(2,128)} %param.21) | data formatting | bytes 16777216 | tf_op jit(solution)/shard_map/reshape | solution.py:290
  52.6 0.0 collective-permute-done.1
  52.7 9.1 %collective-permute-start.2 = (bf16[2,16,1024]{2,1,0:T(8,128)(2,1)S(1)}, bf16[2,16,1024]{2,1,0:T(8,128)(2,1)S(1)}, u32[]{:S(2)}, u32[]{:S(2)}) collective-permute-start(bf16[2,16,1024]{2,1,0:T(8,128)(2,1)S(1)} %maximum_bitcast_fusion.1), channel_id=1, source_target_pairs={{0,1},{1,0},{2,3},{3,2},{4,5},{5,4},{6,7},{7,6},{8,9},{9,8},{10,11... | collective-permute-start | bytes 196616 | tf_op jit(solution)/shard_map/ppermute | solution.py:29
  61.8 8.6 %shard_map.172 = bf16[8,2,2,64,1024]{4,3,2,1,0:T(8,128)(2,1)} custom-call(f32[2,1024,1024]{2,1,0:T(8,128)} %reshape.40.spec_ref, bf16[1024,1024]{1,0:T(8,128)(2,1)S(1)} %fusion.1.order_ref), custom_call_target="tpu_custom_call" | custom-call | flops 4294967296 | bytes 12582912 | tf_op jit(solution)/shard_map/pallas_call | solution.py:277
  70.4 0.0 collective-permute-done.2
  70.4 6.6 %collective-permute-start.3 = (bf16[1,4,64,1024]{3,2,1,0:T(8,128)(2,1)S(1)}, bf16[1,4,64,1024]{3,2,1,0:T(8,128)(2,1)S(1)}, u32[]{:S(2)}, u32[]{:S(2)}) collective-permute-start(bf16[1,4,64,1024]{3,2,1,0:T(8,128)(2,1)S(1)} %bitcast.93), channel_id=1, source_target_pairs={{0,16},{4,20},{8,24},{12,28},{16,0},{20,4},{24,8},{28,12},{1,17},{... | collective-permute-start | bytes 1572872 | tf_op jit(solution)/shard_map/ppermute | solution.py:29
  77.1 8.7 %collective-permute-done.3 = bf16[1,4,64,1024]{3,2,1,0:T(8,128)(2,1)S(1)} collective-permute-done((bf16[1,4,64,1024]{3,2,1,0:T(8,128)(2,1)S(1)}, bf16[1,4,64,1024]{3,2,1,0:T(8,128)(2,1)S(1)}, u32[]{:S(2)}, u32[]{:S(2)}) %collective-permute-start.3) | collective-permute-done | bytes 524320 | tf_op jit(solution)/shard_map/ppermute | solution.py:29
  85.8 0.1 select_bitcast_fusion.5
  85.9 0.1 maximum_bitcast_fusion
  86.0 1.6 collective-permute-start.4
  87.6 4.6 %all-to-all-start.1 = ((bf16[8,2,2,64,1024]{4,3,2,1,0:T(8,128)(2,1)}), bf16[8,2,2,64,1024]{4,3,2,1,0:T(8,128)(2,1)}, u32[]{:S(2)}, u32[]{:S(2)}) async-start(bf16[8,2,2,64,1024]{4,3,2,1,0:T(8,128)(2,1)} %shard_map.172), calls=%async_computation.1 | async-start | bytes 8388608 | tf_op jit(solution)/shard_map/all_to_all | solution.py:297
  92.2 0.2 all-gather.11.cloned.1.call-start
  92.4 19.7 %collective-permute-done.4 = bf16[2,4,64,1024]{3,2,1,0:T(8,128)(2,1)S(1)} collective-permute-done((bf16[2,4,64,1024]{3,2,1,0:T(8,128)(2,1)S(1)}, bf16[2,4,64,1024]{3,2,1,0:T(8,128)(2,1)S(1)}, u32[]{:S(2)}, u32[]{:S(2)}) %collective-permute-start.4) | collective-permute-done | bytes 1048608 | tf_op jit(solution)/shard_map/ppermute | solution.py:29
  112.2 0.1 select_bitcast_fusion.3
  112.3 0.2 pad_maximum_fusion.1
  112.5 0.1 collective-permute-start.5
  112.6 6.3 %fusion.3.refs_5_ = bf16[3,16,512]{2,1,0:T(8,128)(2,1)S(1)} fusion(bf16[3,4,1024,512]{3,2,1,0:T(8,128)(2,1)} %bitcast.83, bf16[4,16,1024]{2,1,0:T(8,128)(2,1)S(1)} %bitcast.97), kind=kOutput, calls=%fused_computation.9 | convolution fusion | flops 201351168 | bytes 12763136 | tf_op jit(solution)/shard_map/ztd,pzdc->ptc/dot_general | solution.py:375
  118.9 0.0 collective-permute-done.5
  118.9 1.9 select_bitcast_fusion.1
  120.8 0.4 pad_maximum_fusion
  121.2 0.7 copy.30
  121.9 2.4 copy.31
  124.4 28.8 %all-to-all-done.1.got_ref = bf16[8,2,2,64,1024]{4,3,2,1,0:T(8,128)(2,1)} async-done(((bf16[8,2,2,64,1024]{4,3,2,1,0:T(8,128)(2,1)}), bf16[8,2,2,64,1024]{4,3,2,1,0:T(8,128)(2,1)}, u32[]{:S(2)}, u32[]{:S(2)}) %all-to-all-start.1) | async-done | bytes 4194336 | tf_op jit(solution)/shard_map/all_to_all | solution.py:297
  153.2 4.0 %shard_map.173.refs_6_.resp_ref = bf16[2,64,72,128]{3,2,1,0:T(8,128)(2,1)S(1)} custom-call(bf16[8,2,2,64,1024]{4,3,2,1,0:T(8,128)(2,1)} %all-to-all-done.1.got_ref), custom_call_target="tpu_custom_call" | custom-call | flops 2097152 | bytes 6291456 | tf_op jit(solution)/shard_map/pallas_call | solution.py:300
  157.2 9.8 %all-gather.7.cloned.1.call-done = bf16[4096,1024]{1,0:T(8,128)(2,1)} async-done(((bf16[1024,1024]{1,0:T(8,128)(2,1)}), bf16[4096,1024]{1,0:T(8,128)(2,1)}) %all-gather.7.cloned.1.call-update) | async-done | bytes 8388624 | tf_op jit(solution)/shard_map/all_gather | solution.py:364
  167.0 0.0 copy-done.6
  167.0 0.0 copy-start.3
  167.0 0.0 copy-start.4
  167.0 0.0 copy-start.5
  167.0 10.6 %shard_map.177 = (bf16[1024,256]{1,0:T(8,128)(2,1)S(1)}, bf16[256,1024]{1,0:T(8,128)(2,1)S(1)}, bf16[1024,256]{1,0:T(8,128)(2,1)S(1)}) custom-call(bf16[4,1024,1024]{2,1,0:T(8,128)(2,1)} %bitcast.88, bf16[3,4096,512]{2,1,0:T(8,128)(2,1)} %refs_3_.3, bf16[3,4096,512]{2,1,0:T(8,128)(2,1)} %refs_3_.3, bf16[3,4096,512]{2,1,0:T(8,128)(2,1)} %refs_3_.3, ...), custom_call_target="tpu_custom_call" | custom-call | flops 6442450944 | bytes 14680064 | tf_op jit(solution)/shard_map/pallas_call | solution.py:89
  177.6 0.0 copy-start.7
  177.6 13.3 %all_to_all.41.signal_ref = bf16[8,32,1024]{2,1,0:T(8,128)(2,1)S(1)} all-to-all(bf16[8,32,1024]{2,1,0:T(8,128)(2,1)S(1)} %bitcast.80), channel_id=1, replica_groups=mesh['seq'=8,'chan'=4] {'seq'}, dimensions={0} | all-to-all | bytes 1048576 | tf_op jit(solution)/shard_map/all_to_all | solution.py:386
  190.9 0.0 copy-done
  190.9 0.0 copy-done.1
  190.9 0.0 copy-done.2
  190.9 0.0 copy-done.3
  190.9 0.0 copy-done.4
  191.0 3.0 shard_map.178
  193.9 12.2 %all_to_all.42 = bf16[8,32,1024]{2,1,0:T(8,128)(2,1)S(1)} all-to-all(bf16[8,32,1024]{2,1,0:T(8,128)(2,1)S(1)} %shard_map.178), channel_id=1, replica_groups=mesh['seq'=8,'chan'=4] {'seq'}, dimensions={0} | all-to-all | bytes 1048576 | tf_op jit(solution)/shard_map/all_to_all | solution.py:387
  206.1 0.0 copy-done.7
  206.1 1.2 shard_map.179
  207.3 0.0 all-gather.11.cloned.1.call-update
  207.3 0.3 all-gather.9.cloned.1.call-start
  207.6 10.6 %shard_map.174 = (bf16[1024,256]{1,0:T(8,128)(2,1)S(1)}, bf16[256,1024]{1,0:T(8,128)(2,1)S(1)}, bf16[1024,256]{1,0:T(8,128)(2,1)S(1)}) custom-call(bf16[4,1024,1024]{2,1,0:T(8,128)(2,1)} %bitcast.89, bf16[3,4096,512]{2,1,0:T(8,128)(2,1)} %refs_3_.3, bf16[3,4096,512]{2,1,0:T(8,128)(2,1)} %refs_3_.3, bf16[3,4096,512]{2,1,0:T(8,128)(2,1)} %refs_3_.3, ...), custom_call_target="tpu_custom_call" | custom-call | flops 6442450944 | bytes 14680064 | tf_op jit(solution)/shard_map/pallas_call | solution.py:89
  218.3 12.2 %all_to_all.43.signal_ref = bf16[8,32,1024]{2,1,0:T(8,128)(2,1)S(1)} all-to-all(bf16[8,32,1024]{2,1,0:T(8,128)(2,1)S(1)} %bitcast.79), channel_id=1, replica_groups=mesh['seq'=8,'chan'=4] {'seq'}, dimensions={0} | all-to-all | bytes 1048576 | tf_op jit(solution)/shard_map/all_to_all | solution.py:386
  230.4 3.0 shard_map.175
  233.4 12.2 %all_to_all.44 = bf16[8,32,1024]{2,1,0:T(8,128)(2,1)S(1)} all-to-all(bf16[8,32,1024]{2,1,0:T(8,128)(2,1)S(1)} %shard_map.175), channel_id=1, replica_groups=mesh['seq'=8,'chan'=4] {'seq'}, dimensions={0} | all-to-all | bytes 1048576 | tf_op jit(solution)/shard_map/all_to_all | solution.py:387
  245.5 1.2 shard_map.176
  246.7 0.0 all-gather.9.cloned.1.call-update
  246.8 3.9 %all-gather.11.cloned.1.call-done = bf16[4096,256]{1,0:T(8,128)(2,1)} async-done(((bf16[1024,256]{1,0:T(8,128)(2,1)}), bf16[4096,256]{1,0:T(8,128)(2,1)}) %all-gather.11.cloned.1.call-update) | async-done | bytes 2097168 | tf_op jit(solution)/shard_map/all_gather | solution.py:390
  250.7 5.8 %shard_map.180.refs_0_ = f32[1024,1024]{1,0:T(8,128)} custom-call(bf16[4,1024,256]{2,1,0:T(8,128)(2,1)} %bitcast.92, bf16[2,1024,1024]{2,1,0:T(8,128)(2,1)} %bitcast.86), custom_call_target="tpu_custom_call" | custom-call | flops 2147483648 | bytes 10485760 | tf_op jit(solution)/shard_map/pallas_call | solution.py:338
  256.5 40.5 %all-gather.9.cloned.1.call-done = bf16[4096,256]{1,0:T(8,128)(2,1)} async-done(((bf16[1024,256]{1,0:T(8,128)(2,1)}), bf16[4096,256]{1,0:T(8,128)(2,1)}) %all-gather.9.cloned.1.call-update) | async-done | bytes 2097168 | tf_op jit(solution)/shard_map/all_gather | solution.py:390
  297.0 6.0 %shard_map.181 = bf16[1024,1024]{1,0:T(8,128)(2,1)} custom-call(bf16[4,1024,256]{2,1,0:T(8,128)(2,1)} %bitcast.96, bf16[2,1024,1024]{2,1,0:T(8,128)(2,1)} %bitcast.87, f32[1024,1024]{1,0:T(8,128)} %shard_map.180.refs_0_), custom_call_target="tpu_custom_call" | custom-call | flops 2147483648 | bytes 10485760 | tf_op jit(solution)/shard_map/pallas_call | solution.py:338
  (12 shorter events, 0.1 us)
Async XLA Ops:
  6.5 160.5 %all-gather.7.cloned.1.call-start = ((), (), s32[]{:S(2)}) async-start(), calls=%async_computation.6 | async-start | bytes 10485760 | tf_op jit(solution)/shard_map/all_gather | solution.py:364
  9.2 29.7 %all-to-all-start = ((bf16[64,4,1024]{2,0,1:T(8,128)(2,1)}), bf16[64,4,1024]{2,0,1:T(8,128)(2,1)S(1)}, u32[]{:S(2)}, u32[]{:S(2)}) async-start(bf16[64,4,1024]{2,0,1:T(8,128)(2,1)} %bitcast.76), calls=%async_computation | async-start | bytes 1048576 | tf_op jit(solution)/shard_map/all_to_all | solution.py:318
  38.9 2.1 collective-permute-start
  41.0 11.7 %collective-permute-start.1 = (bf16[1,16,1024]{2,1,0:T(8,128)(2,1)S(1)}, bf16[1,16,1024]{2,1,0:T(8,128)(2,1)S(1)}, u32[]{:S(2)}, u32[]{:S(2)}) collective-permute-start(bf16[1,16,1024]{2,1,0:T(8,128)(2,1)S(1)} %bitcast.98), channel_id=1, source_target_pairs={{0,2},{1,3},{2,0},{3,1},{4,6},{5,7},{6,4},{7,5},{8,10},{9,11},{10,... | collective-permute-start | bytes 98312 | tf_op jit(solution)/shard_map/ppermute | solution.py:29
  52.7 17.7 %collective-permute-start.2 = (bf16[2,16,1024]{2,1,0:T(8,128)(2,1)S(1)}, bf16[2,16,1024]{2,1,0:T(8,128)(2,1)S(1)}, u32[]{:S(2)}, u32[]{:S(2)}) collective-permute-start(bf16[2,16,1024]{2,1,0:T(8,128)(2,1)S(1)} %maximum_bitcast_fusion.1), channel_id=1, source_target_pairs={{0,1},{1,0},{2,3},{3,2},{4,5},{5,4},{6,7},{7,6},{8,9},{9,8},{10,11... | collective-permute-start | bytes 196616 | tf_op jit(solution)/shard_map/ppermute | solution.py:29
  70.4 15.4 %collective-permute-start.3 = (bf16[1,4,64,1024]{3,2,1,0:T(8,128)(2,1)S(1)}, bf16[1,4,64,1024]{3,2,1,0:T(8,128)(2,1)S(1)}, u32[]{:S(2)}, u32[]{:S(2)}) collective-permute-start(bf16[1,4,64,1024]{3,2,1,0:T(8,128)(2,1)S(1)} %bitcast.93), channel_id=1, source_target_pairs={{0,16},{4,20},{8,24},{12,28},{16,0},{20,4},{24,8},{28,12},{1,17},{... | collective-permute-start | bytes 1572872 | tf_op jit(solution)/shard_map/ppermute | solution.py:29
  86.0 26.2 %collective-permute-start.4 = (bf16[2,4,64,1024]{3,2,1,0:T(8,128)(2,1)S(1)}, bf16[2,4,64,1024]{3,2,1,0:T(8,128)(2,1)S(1)}, u32[]{:S(2)}, u32[]{:S(2)}) collective-permute-start(bf16[2,4,64,1024]{3,2,1,0:T(8,128)(2,1)S(1)} %maximum_bitcast_fusion), channel_id=1, source_target_pairs={{0,8},{4,12},{8,0},{12,4},{16,24},{20,28},{24,16},{28,20},{1,9},{5... | collective-permute-start | bytes 3145736 | tf_op jit(solution)/shard_map/ppermute | solution.py:29
  87.6 65.6 %all-to-all-start.1 = ((bf16[8,2,2,64,1024]{4,3,2,1,0:T(8,128)(2,1)}), bf16[8,2,2,64,1024]{4,3,2,1,0:T(8,128)(2,1)}, u32[]{:S(2)}, u32[]{:S(2)}) async-start(bf16[8,2,2,64,1024]{4,3,2,1,0:T(8,128)(2,1)} %shard_map.172), calls=%async_computation.1 | async-start | bytes 8388608 | tf_op jit(solution)/shard_map/all_to_all | solution.py:297
  92.2 158.5 %all-gather.11.cloned.1.call-start = ((), (), s32[]{:S(2)}) async-start(), calls=%async_computation.8 | async-start | bytes 2621440 | tf_op jit(solution)/shard_map/all_gather | solution.py:390
  112.5 6.4 %collective-permute-start.5 = (bf16[4,4,64,1024]{3,2,1,0:T(8,128)(2,1)S(1)}, bf16[4,4,64,1024]{3,2,1,0:T(8,128)(2,1)}, u32[]{:S(2)}, u32[]{:S(2)}) collective-permute-start(bf16[4,4,64,1024]{3,2,1,0:T(8,128)(2,1)S(1)} %bitcast.91), channel_id=1, source_target_pairs={{0,4},{4,0},{8,12},{12,8},{16,20},{20,16},{24,28},{28,24},{1,5},{5... | collective-permute-start | bytes 6291464 | tf_op jit(solution)/shard_map/ppermute | solution.py:29
  124.4 42.6 %copy-start.6 = (f32[3,3,512]{2,1,0:T(4,128)S(1)}, f32[3,3,512]{2,1,0:T(4,128)}, u32[]{:S(2)}) copy-start(f32[3,3,512]{2,1,0:T(4,128)} %refs_4_.3) | copy-start | bytes 55300
  167.0 23.9 %copy-start = (bf16[256,256]{1,0:T(8,128)(2,1)S(1)}, bf16[256,256]{1,0:T(8,128)(2,1)}, u32[]{:S(2)}) copy-start(bf16[256,256]{1,0:T(8,128)(2,1)} %constant.138.clone.fwd_ref) | copy-start | bytes 393220
  167.0 23.9 %copy-start.1 = (bf16[256,256]{1,0:T(8,128)(2,1)S(1)}, bf16[256,256]{1,0:T(8,128)(2,1)}, u32[]{:S(2)}) copy-start(bf16[256,256]{1,0:T(8,128)(2,1)} %constant.139.clone.bwd_ref) | copy-start | bytes 393220
  167.0 23.9 %copy-start.2 = (bf16[144,64]{1,0:T(8,128)(2,1)S(1)}, bf16[144,64]{1,0:T(8,128)(2,1)}, u32[]{:S(2)}) copy-start(bf16[144,64]{1,0:T(8,128)(2,1)} %constant.134.clone.first_ref) | copy-start | bytes 55300
  167.0 23.9 %copy-start.3 = (f32[72,128]{1,0:T(8,128)S(1)}, f32[72,128]{1,0:T(8,128)}, u32[]{:S(2)}) copy-start(f32[72,128]{1,0:T(8,128)} %constant.136.clone.cos_ref) | copy-start | bytes 110596
  167.0 23.9 %copy-start.4 = (f32[72,128]{1,0:T(8,128)S(1)}, f32[72,128]{1,0:T(8,128)}, u32[]{:S(2)}) copy-start(f32[72,128]{1,0:T(8,128)} %constant.137.clone.sin_ref) | copy-start | bytes 110596
  167.0 23.9 %copy-start.5 = (bf16[64,144]{1,0:T(8,128)(2,1)S(1)}, bf16[64,144]{1,0:T(8,128)(2,1)}, u32[]{:S(2)}) copy-start(bf16[64,144]{1,0:T(8,128)(2,1)} %constant.135.clone.last_ref) | copy-start | bytes 55300
  177.6 28.5 %copy-start.7 = (f32[512]{0:T(512)S(1)}, f32[512]{0:T(512)}, u32[]{:S(2)}) copy-start(f32[512]{0:T(512)} %param.22) | copy-start | bytes 6148
  207.3 89.6 %all-gather.9.cloned.1.call-start = ((), (), s32[]{:S(2)}) async-start(), calls=%async_computation.7 | async-start | bytes 2621440 | tf_op jit(solution)/shard_map/all_gather | solution.py:390
Sparse Core Ops, SparseCore 0:
  8.9 158.0 all-gather.6
  207.5 43.1 all-gather.10
  252.3 44.6 all-gather.8

commit v17 on v16

--- a/solution.py
+++ b/solution.py
@@ -46,9 +46,9 @@
     last = pl.num_programs(0) - 1
     rows, size = query_t_ref.shape
 
-    def part():
+    def part(first=0, count=rows):
         weight = jnp.concatenate([wq_ref[0], wk_ref[0], wv_ref[0]], axis=1)
-        return jnp.dot(tok_ref[0], weight, preferred_element_type=jnp.float32)
+        return jnp.dot(tok_ref[0, first : first + count], weight, preferred_element_type=jnp.float32)
 
     def filtered(p, r):
         lanes = slice(p * size, (p + 1) * size)
@@ -69,12 +69,15 @@
 
     @pl.when(step == last)
     def _():
-        acc[HALO:, :] = (acc[HALO:, :] + part()).astype(jnp.bfloat16).astype(jnp.float32)
-        for r in range(0, rows, LANES):
-            query_t_ref[r : r + LANES, :] = filtered(0, r).astype(query_t_ref.dtype)
-            signal = filtered(1, r) * filtered(2, r)
-            signal_t_ref[r : r + LANES, :] = signal.astype(signal_t_ref.dtype)
-            signal_ref[:, r : r + LANES] = signal.T.astype(signal_ref.dtype)
+        half = rows // 2
+        for first in (0, half):
+            held = slice(HALO + first, HALO + first + half)
+            acc[held, :] = (acc[held, :] + part(first, half)).astype(jnp.bfloat16).astype(jnp.float32)
+            for r in range(first, first + half, LANES):
+                query_t_ref[r : r + LANES, :] = filtered(0, r).astype(query_t_ref.dtype)
+                signal = filtered(1, r) * filtered(2, r)
+                signal_t_ref[r : r + LANES, :] = signal.astype(signal_t_ref.dtype)
+                signal_ref[:, r : r + LANES] = signal.T.astype(signal_ref.dtype)
 
 
 def project(gathered, in_weight, conv_weight, halo, lo, size, *after):
@@ -324,11 +327,11 @@
     gated = jnp.concatenate([gated_ref[z] for z in range(gated_ref.shape[0])], axis=1)
     total = jnp.dot(gated, w_ref[0], preferred_element_type=jnp.float32)
     if len(refs) == 2:
-        total = total + refs[0][...]
+        total = total + refs[0][...].astype(jnp.float32)
     out_ref[...] = total.astype(out_ref.dtype)
 
 
-def combine(gathered, weight, chunk, total, dtype):
+def combine(gathered, weight, chunk, total):
     count, tok_rows, size = gathered.shape
     depth = count * size
     features = weight.shape[2]
@@ -344,7 +347,7 @@
             *[block for _ in given],
         ],
         out_specs=block,
-        out_shape=jax.ShapeDtypeStruct((tok_rows, features), dtype),
+        out_shape=jax.ShapeDtypeStruct((tok_rows, features), jnp.bfloat16),
         compiler_params=pltpu.CompilerParams(vmem_limit_bytes=60 * MIB),
         cost_estimate=pl.CostEstimate(
             flops=2 * tok_rows * depth * features,
@@ -388,8 +391,7 @@
             long_conv(values, response, lo // seq_count), "seq", split_axis=0, concat_axis=0, tiled=True
         ).reshape(size, tok_rows)
         gated = lax.all_gather(gate(longconv, skip, lo, signal_t, query_t), "chan")
-        dtype = jnp.bfloat16 if lo + size == chans else jnp.float32
-        total = combine(gated, weight, j, total, dtype)
+        total = combine(gated, weight, j, total)
     return total
 
 

time: 310 us -> 310 us (level)
  no operation moved by 1% of the time
where the time goes in v17:
time: 310 us; the launch traced here: 309 us
  waiting for transfers between devices  136 us (44%)
  Pallas kernels  53.1 us (17%)
  blocking collectives  49.7 us (16%)
  starting transfers between devices  30.1 us (10%)
  local copies, waits for them, and re-layouts  16.8 us (5%)
  between operations  13.4 us (4%)
  matrix products  6.3 us (2%)
  other arithmetic  3.57 us (1%)
    all_gather x2, waiting for transfers between devices, shards(): gated = lax.all_gather(gate(longconv, skip, lo, signal_t, query_t), 'chan')  44.8 us
    all_to_all x1, waiting for transfers between devices, folded_response(): got = lax.all_to_all(sent, 'seq', split_axis=0, concat_axis=0, tiled=True)  28.8 us
    ppermute x5, waiting for transfers between devices, gather_by_doubling(): other = lax.ppermute(held, axis, [(i, i ^ bit) for i in range(size)])  28.5 us
    all_to_all x2, blocking collectives, shards(): lax.all_to_all(values, 'seq', split_axis=0, concat_axis=0, tiled=True)  25.4 us
    all_to_all x2, blocking collectives, shards(): lax.all_to_all(long_conv(values, response, lo // seq_count), 'seq', split...  24.3 us
    all_to_all x1, waiting for transfers between devices, feature_rows(): own = lax.all_to_all(own, 'chan', split_axis=1, concat_axis=0, tiled=True)  22.6 us
    pallas_call x2, Pallas kernels, project(): pl.pallas_call(lambda *refs: project_kernel(len(after), *refs), grid=(cou...  21 us
    ppermute x5, starting transfers between devices, gather_by_doubling(): other = lax.ppermute(held, axis, [(i, i ^ bit) for i in range(size)])  17.4 us
  transfers between devices with their start and end apart: 11, of which 8 were waited for; matrix products, arithmetic and copies ran while one was open for 9% of the time, Pallas kernels for 11%

profile of v17, /device:TPU:0, one launch (start us, length us, event | category | flops | bytes accessed | tf_op | source)
XLA Modules:
  0.0 309.0 jit_solution(7092828307110037471)
XLA Ops:
  6.5 0.0 all-gather.7.cloned.1.call-start
  6.5 0.7 all-gather.7.cloned.1.call-update
  7.3 1.1 constant_dynamic-slice_fusion
  8.3 0.8 copy.35
  9.2 6.3 %all-to-all-start = ((bf16[64,4,1024]{2,0,1:T(8,128)(2,1)}), bf16[64,4,1024]{2,0,1:T(8,128)(2,1)S(1)}, u32[]{:S(2)}, u32[]{:S(2)}) async-start(bf16[64,4,1024]{2,0,1:T(8,128)(2,1)} %bitcast.76), calls=%async_computation | async-start | bytes 1048576 | tf_op jit(solution)/shard_map/all_to_all | solution.py:321
  15.5 0.8 slice.3
  16.3 22.6 %all-to-all-done = bf16[64,4,1024]{2,0,1:T(8,128)(2,1)S(1)} async-done(((bf16[64,4,1024]{2,0,1:T(8,128)(2,1)}), bf16[64,4,1024]{2,0,1:T(8,128)(2,1)S(1)}, u32[]{:S(2)}, u32[]{:S(2)}) %all-to-all-start) | async-done | bytes 524320 | tf_op jit(solution)/shard_map/all_to_all | solution.py:321
  38.9 1.3 collective-permute-start
  40.2 0.8 collective-permute-done
  41.0 0.0 collective-permute-start.1
  41.0 0.7 fusion.1.order_ref
  41.7 10.9 %reshape.40.spec_ref = f32[2,1024,1024]{2,1,0:T(8,128)} reshape(f32[2,512,2,1024]{3,2,1,0:T(2,128)} %param.21) | data formatting | bytes 16777216 | tf_op jit(solution)/shard_map/reshape | solution.py:293
  52.6 0.0 collective-permute-done.1
  52.7 9.1 %collective-permute-start.2 = (bf16[2,16,1024]{2,1,0:T(8,128)(2,1)S(1)}, bf16[2,16,1024]{2,1,0:T(8,128)(2,1)S(1)}, u32[]{:S(2)}, u32[]{:S(2)}) collective-permute-start(bf16[2,16,1024]{2,1,0:T(8,128)(2,1)S(1)} %maximum_bitcast_fusion.1), channel_id=1, source_target_pairs={{0,1},{1,0},{2,3},{3,2},{4,5},{5,4},{6,7},{7,6},{8,9},{9,8},{10,11... | collective-permute-start | bytes 196616 | tf_op jit(solution)/shard_map/ppermute | solution.py:29
  61.8 8.6 %shard_map.172 = bf16[8,2,2,64,1024]{4,3,2,1,0:T(8,128)(2,1)} custom-call(f32[2,1024,1024]{2,1,0:T(8,128)} %reshape.40.spec_ref, bf16[1024,1024]{1,0:T(8,128)(2,1)S(1)} %fusion.1.order_ref), custom_call_target="tpu_custom_call" | custom-call | flops 4294967296 | bytes 12582912 | tf_op jit(solution)/shard_map/pallas_call | solution.py:280
  70.4 0.0 collective-permute-done.2
  70.4 6.6 %collective-permute-start.3 = (bf16[1,4,64,1024]{3,2,1,0:T(8,128)(2,1)S(1)}, bf16[1,4,64,1024]{3,2,1,0:T(8,128)(2,1)S(1)}, u32[]{:S(2)}, u32[]{:S(2)}) collective-permute-start(bf16[1,4,64,1024]{3,2,1,0:T(8,128)(2,1)S(1)} %bitcast.93), channel_id=1, source_target_pairs={{0,16},{4,20},{8,24},{12,28},{16,0},{20,4},{24,8},{28,12},{1,17},{... | collective-permute-start | bytes 1572872 | tf_op jit(solution)/shard_map/ppermute | solution.py:29
  77.1 8.7 %collective-permute-done.3 = bf16[1,4,64,1024]{3,2,1,0:T(8,128)(2,1)S(1)} collective-permute-done((bf16[1,4,64,1024]{3,2,1,0:T(8,128)(2,1)S(1)}, bf16[1,4,64,1024]{3,2,1,0:T(8,128)(2,1)S(1)}, u32[]{:S(2)}, u32[]{:S(2)}) %collective-permute-start.3) | collective-permute-done | bytes 524320 | tf_op jit(solution)/shard_map/ppermute | solution.py:29
  85.8 0.1 select_bitcast_fusion.5
  85.9 0.1 maximum_bitcast_fusion
  86.0 1.6 collective-permute-start.4
  87.6 4.6 %all-to-all-start.1 = ((bf16[8,2,2,64,1024]{4,3,2,1,0:T(8,128)(2,1)}), bf16[8,2,2,64,1024]{4,3,2,1,0:T(8,128)(2,1)}, u32[]{:S(2)}, u32[]{:S(2)}) async-start(bf16[8,2,2,64,1024]{4,3,2,1,0:T(8,128)(2,1)} %shard_map.172), calls=%async_computation.1 | async-start | bytes 8388608 | tf_op jit(solution)/shard_map/all_to_all | solution.py:300
  92.2 0.2 all-gather.11.cloned.1.call-start
  92.4 19.7 %collective-permute-done.4 = bf16[2,4,64,1024]{3,2,1,0:T(8,128)(2,1)S(1)} collective-permute-done((bf16[2,4,64,1024]{3,2,1,0:T(8,128)(2,1)S(1)}, bf16[2,4,64,1024]{3,2,1,0:T(8,128)(2,1)S(1)}, u32[]{:S(2)}, u32[]{:S(2)}) %collective-permute-start.4) | collective-permute-done | bytes 1048608 | tf_op jit(solution)/shard_map/ppermute | solution.py:29
  112.2 0.1 select_bitcast_fusion.3
  112.3 0.2 pad_maximum_fusion.1
  112.5 0.1 collective-permute-start.5
  112.6 6.3 %fusion.3.refs_5_ = bf16[3,16,512]{2,1,0:T(8,128)(2,1)S(1)} fusion(bf16[3,4,1024,512]{3,2,1,0:T(8,128)(2,1)} %bitcast.83, bf16[4,16,1024]{2,1,0:T(8,128)(2,1)S(1)} %bitcast.97), kind=kOutput, calls=%fused_computation.9 | convolution fusion | flops 201351168 | bytes 12763136 | tf_op jit(solution)/shard_map/ztd,pzdc->ptc/dot_general | solution.py:378
  118.9 0.0 collective-permute-done.5
  118.9 1.9 select_bitcast_fusion.1
  120.8 0.4 pad_maximum_fusion
  121.2 0.7 copy.30
  121.9 2.4 copy.31
  124.4 28.8 %all-to-all-done.1.got_ref = bf16[8,2,2,64,1024]{4,3,2,1,0:T(8,128)(2,1)} async-done(((bf16[8,2,2,64,1024]{4,3,2,1,0:T(8,128)(2,1)}), bf16[8,2,2,64,1024]{4,3,2,1,0:T(8,128)(2,1)}, u32[]{:S(2)}, u32[]{:S(2)}) %all-to-all-start.1) | async-done | bytes 4194336 | tf_op jit(solution)/shard_map/all_to_all | solution.py:300
  153.2 4.0 %shard_map.173.refs_6_.resp_ref = bf16[2,64,72,128]{3,2,1,0:T(8,128)(2,1)S(1)} custom-call(bf16[8,2,2,64,1024]{4,3,2,1,0:T(8,128)(2,1)} %all-to-all-done.1.got_ref), custom_call_target="tpu_custom_call" | custom-call | flops 2097152 | bytes 6291456 | tf_op jit(solution)/shard_map/pallas_call | solution.py:303
  157.2 9.8 %all-gather.7.cloned.1.call-done = bf16[4096,1024]{1,0:T(8,128)(2,1)} async-done(((bf16[1024,1024]{1,0:T(8,128)(2,1)}), bf16[4096,1024]{1,0:T(8,128)(2,1)}) %all-gather.7.cloned.1.call-update) | async-done | bytes 8388624 | tf_op jit(solution)/shard_map/all_gather | solution.py:367
  167.0 0.0 copy-done.6
  167.0 0.0 copy-start.3
  167.0 0.0 copy-start.4
  167.0 0.0 copy-start.5
  167.0 10.5 %shard_map.177 = (bf16[1024,256]{1,0:T(8,128)(2,1)S(1)}, bf16[256,1024]{1,0:T(8,128)(2,1)S(1)}, bf16[1024,256]{1,0:T(8,128)(2,1)S(1)}) custom-call(bf16[4,1024,1024]{2,1,0:T(8,128)(2,1)} %bitcast.88, bf16[3,4096,512]{2,1,0:T(8,128)(2,1)} %refs_3_.3, bf16[3,4096,512]{2,1,0:T(8,128)(2,1)} %refs_3_.3, bf16[3,4096,512]{2,1,0:T(8,128)(2,1)} %refs_3_.3, ...), custom_call_target="tpu_custom_call" | custom-call | flops 6442450944 | bytes 14680064 | tf_op jit(solution)/shard_map/pallas_call | solution.py:92
  177.5 0.0 copy-start.7
  177.5 13.3 %all_to_all.41.signal_ref = bf16[8,32,1024]{2,1,0:T(8,128)(2,1)S(1)} all-to-all(bf16[8,32,1024]{2,1,0:T(8,128)(2,1)S(1)} %bitcast.80), channel_id=1, replica_groups=mesh['seq'=8,'chan'=4] {'seq'}, dimensions={0} | all-to-all | bytes 1048576 | tf_op jit(solution)/shard_map/all_to_all | solution.py:389
  190.8 0.0 copy-done
  190.8 0.0 copy-done.1
  190.8 0.0 copy-done.3
  190.8 0.0 copy-done.4
  190.8 0.0 copy-done.5
  190.8 3.0 shard_map.178
  193.8 12.2 %all_to_all.42 = bf16[8,32,1024]{2,1,0:T(8,128)(2,1)S(1)} all-to-all(bf16[8,32,1024]{2,1,0:T(8,128)(2,1)S(1)} %shard_map.178), channel_id=1, replica_groups=mesh['seq'=8,'chan'=4] {'seq'}, dimensions={0} | all-to-all | bytes 1048576 | tf_op jit(solution)/shard_map/all_to_all | solution.py:390
  206.0 0.0 copy-done.7
  206.0 1.2 shard_map.179
  207.2 0.0 all-gather.11.cloned.1.call-update
  207.2 0.3 all-gather.9.cloned.1.call-start
  207.5 10.5 %shard_map.174 = (bf16[1024,256]{1,0:T(8,128)(2,1)S(1)}, bf16[256,1024]{1,0:T(8,128)(2,1)S(1)}, bf16[1024,256]{1,0:T(8,128)(2,1)S(1)}) custom-call(bf16[4,1024,1024]{2,1,0:T(8,128)(2,1)} %bitcast.89, bf16[3,4096,512]{2,1,0:T(8,128)(2,1)} %refs_3_.3, bf16[3,4096,512]{2,1,0:T(8,128)(2,1)} %refs_3_.3, bf16[3,4096,512]{2,1,0:T(8,128)(2,1)} %refs_3_.3, ...), custom_call_target="tpu_custom_call" | custom-call | flops 6442450944 | bytes 14680064 | tf_op jit(solution)/shard_map/pallas_call | solution.py:92
  218.0 12.2 %all_to_all.43.signal_ref = bf16[8,32,1024]{2,1,0:T(8,128)(2,1)S(1)} all-to-all(bf16[8,32,1024]{2,1,0:T(8,128)(2,1)S(1)} %bitcast.79), channel_id=1, replica_groups=mesh['seq'=8,'chan'=4] {'seq'}, dimensions={0} | all-to-all | bytes 1048576 | tf_op jit(solution)/shard_map/all_to_all | solution.py:389
  230.2 3.0 shard_map.175
  233.2 12.2 %all_to_all.44 = bf16[8,32,1024]{2,1,0:T(8,128)(2,1)S(1)} all-to-all(bf16[8,32,1024]{2,1,0:T(8,128)(2,1)S(1)} %shard_map.175), channel_id=1, replica_groups=mesh['seq'=8,'chan'=4] {'seq'}, dimensions={0} | all-to-all | bytes 1048576 | tf_op jit(solution)/shard_map/all_to_all | solution.py:390
  245.3 1.2 shard_map.176
  246.5 0.0 all-gather.9.cloned.1.call-update
  246.6 4.0 %all-gather.11.cloned.1.call-done = bf16[4096,256]{1,0:T(8,128)(2,1)} async-done(((bf16[1024,256]{1,0:T(8,128)(2,1)}), bf16[4096,256]{1,0:T(8,128)(2,1)}) %all-gather.11.cloned.1.call-update) | async-done | bytes 2097168 | tf_op jit(solution)/shard_map/all_gather | solution.py:393
  250.5 5.4 %shard_map.180.refs_0_ = bf16[1024,1024]{1,0:T(8,128)(2,1)} custom-call(bf16[4,1024,256]{2,1,0:T(8,128)(2,1)} %bitcast.96, bf16[2,1024,1024]{2,1,0:T(8,128)(2,1)} %bitcast.86), custom_call_target="tpu_custom_call" | custom-call | flops 2147483648 | bytes 10485760 | tf_op jit(solution)/shard_map/pallas_call | solution.py:341
  256.0 40.8 %all-gather.9.cloned.1.call-done = bf16[4096,256]{1,0:T(8,128)(2,1)} async-done(((bf16[1024,256]{1,0:T(8,128)(2,1)}), bf16[4096,256]{1,0:T(8,128)(2,1)}) %all-gather.9.cloned.1.call-update) | async-done | bytes 2097168 | tf_op jit(solution)/shard_map/all_gather | solution.py:393
  296.8 5.7 %shard_map.181 = bf16[1024,1024]{1,0:T(8,128)(2,1)} custom-call(bf16[4,1024,256]{2,1,0:T(8,128)(2,1)} %bitcast.92, bf16[2,1024,1024]{2,1,0:T(8,128)(2,1)} %bitcast.87, bf16[1024,1024]{1,0:T(8,128)(2,1)} %shard_map.180.refs_0_), custom_call_target="tpu_custom_call" | custom-call | flops 2147483648 | bytes 10485760 | tf_op jit(solution)/shard_map/pallas_call | solution.py:341
  (12 shorter events, 0.1 us)
Async XLA Ops:
  6.5 160.5 %all-gather.7.cloned.1.call-start = ((), (), s32[]{:S(2)}) async-start(), calls=%async_computation.6 | async-start | bytes 10485760 | tf_op jit(solution)/shard_map/all_gather | solution.py:367
  9.2 29.7 %all-to-all-start = ((bf16[64,4,1024]{2,0,1:T(8,128)(2,1)}), bf16[64,4,1024]{2,0,1:T(8,128)(2,1)S(1)}, u32[]{:S(2)}, u32[]{:S(2)}) async-start(bf16[64,4,1024]{2,0,1:T(8,128)(2,1)} %bitcast.76), calls=%async_computation | async-start | bytes 1048576 | tf_op jit(solution)/shard_map/all_to_all | solution.py:321
  38.9 2.1 collective-permute-start
  41.0 11.7 %collective-permute-start.1 = (bf16[1,16,1024]{2,1,0:T(8,128)(2,1)S(1)}, bf16[1,16,1024]{2,1,0:T(8,128)(2,1)S(1)}, u32[]{:S(2)}, u32[]{:S(2)}) collective-permute-start(bf16[1,16,1024]{2,1,0:T(8,128)(2,1)S(1)} %bitcast.98), channel_id=1, source_target_pairs={{0,2},{1,3},{2,0},{3,1},{4,6},{5,7},{6,4},{7,5},{8,10},{9,11},{10,... | collective-permute-start | bytes 98312 | tf_op jit(solution)/shard_map/ppermute | solution.py:29
  52.7 17.7 %collective-permute-start.2 = (bf16[2,16,1024]{2,1,0:T(8,128)(2,1)S(1)}, bf16[2,16,1024]{2,1,0:T(8,128)(2,1)S(1)}, u32[]{:S(2)}, u32[]{:S(2)}) collective-permute-start(bf16[2,16,1024]{2,1,0:T(8,128)(2,1)S(1)} %maximum_bitcast_fusion.1), channel_id=1, source_target_pairs={{0,1},{1,0},{2,3},{3,2},{4,5},{5,4},{6,7},{7,6},{8,9},{9,8},{10,11... | collective-permute-start | bytes 196616 | tf_op jit(solution)/shard_map/ppermute | solution.py:29
  70.4 15.4 %collective-permute-start.3 = (bf16[1,4,64,1024]{3,2,1,0:T(8,128)(2,1)S(1)}, bf16[1,4,64,1024]{3,2,1,0:T(8,128)(2,1)S(1)}, u32[]{:S(2)}, u32[]{:S(2)}) collective-permute-start(bf16[1,4,64,1024]{3,2,1,0:T(8,128)(2,1)S(1)} %bitcast.93), channel_id=1, source_target_pairs={{0,16},{4,20},{8,24},{12,28},{16,0},{20,4},{24,8},{28,12},{1,17},{... | collective-permute-start | bytes 1572872 | tf_op jit(solution)/shard_map/ppermute | solution.py:29
  86.0 26.2 %collective-permute-start.4 = (bf16[2,4,64,1024]{3,2,1,0:T(8,128)(2,1)S(1)}, bf16[2,4,64,1024]{3,2,1,0:T(8,128)(2,1)S(1)}, u32[]{:S(2)}, u32[]{:S(2)}) collective-permute-start(bf16[2,4,64,1024]{3,2,1,0:T(8,128)(2,1)S(1)} %maximum_bitcast_fusion), channel_id=1, source_target_pairs={{0,8},{4,12},{8,0},{12,4},{16,24},{20,28},{24,16},{28,20},{1,9},{5... | collective-permute-start | bytes 3145736 | tf_op jit(solution)/shard_map/ppermute | solution.py:29
  87.6 65.6 %all-to-all-start.1 = ((bf16[8,2,2,64,1024]{4,3,2,1,0:T(8,128)(2,1)}), bf16[8,2,2,64,1024]{4,3,2,1,0:T(8,128)(2,1)}, u32[]{:S(2)}, u32[]{:S(2)}) async-start(bf16[8,2,2,64,1024]{4,3,2,1,0:T(8,128)(2,1)} %shard_map.172), calls=%async_computation.1 | async-start | bytes 8388608 | tf_op jit(solution)/shard_map/all_to_all | solution.py:300
  92.2 158.4 %all-gather.11.cloned.1.call-start = ((), (), s32[]{:S(2)}) async-start(), calls=%async_computation.8 | async-start | bytes 2621440 | tf_op jit(solution)/shard_map/all_gather | solution.py:393
  112.5 6.4 %collective-permute-start.5 = (bf16[4,4,64,1024]{3,2,1,0:T(8,128)(2,1)S(1)}, bf16[4,4,64,1024]{3,2,1,0:T(8,128)(2,1)}, u32[]{:S(2)}, u32[]{:S(2)}) collective-permute-start(bf16[4,4,64,1024]{3,2,1,0:T(8,128)(2,1)S(1)} %bitcast.91), channel_id=1, source_target_pairs={{0,4},{4,0},{8,12},{12,8},{16,20},{20,16},{24,28},{28,24},{1,5},{5... | collective-permute-start | bytes 6291464 | tf_op jit(solution)/shard_map/ppermute | solution.py:29
  124.4 42.6 %copy-start.6 = (f32[3,3,512]{2,1,0:T(4,128)S(1)}, f32[3,3,512]{2,1,0:T(4,128)}, u32[]{:S(2)}) copy-start(f32[3,3,512]{2,1,0:T(4,128)} %refs_4_.3) | copy-start | bytes 55300
  167.0 23.8 %copy-start = (bf16[256,256]{1,0:T(8,128)(2,1)S(1)}, bf16[256,256]{1,0:T(8,128)(2,1)}, u32[]{:S(2)}) copy-start(bf16[256,256]{1,0:T(8,128)(2,1)} %constant.138.clone.fwd_ref) | copy-start | bytes 393220
  167.0 23.8 %copy-start.1 = (bf16[256,256]{1,0:T(8,128)(2,1)S(1)}, bf16[256,256]{1,0:T(8,128)(2,1)}, u32[]{:S(2)}) copy-start(bf16[256,256]{1,0:T(8,128)(2,1)} %constant.139.clone.bwd_ref) | copy-start | bytes 393220
  167.0 23.8 %copy-start.2 = (bf16[144,64]{1,0:T(8,128)(2,1)S(1)}, bf16[144,64]{1,0:T(8,128)(2,1)}, u32[]{:S(2)}) copy-start(bf16[144,64]{1,0:T(8,128)(2,1)} %constant.134.clone.first_ref) | copy-start | bytes 55300
  167.0 23.8 %copy-start.3 = (f32[72,128]{1,0:T(8,128)S(1)}, f32[72,128]{1,0:T(8,128)}, u32[]{:S(2)}) copy-start(f32[72,128]{1,0:T(8,128)} %constant.136.clone.cos_ref) | copy-start | bytes 110596
  167.0 23.8 %copy-start.4 = (f32[72,128]{1,0:T(8,128)S(1)}, f32[72,128]{1,0:T(8,128)}, u32[]{:S(2)}) copy-start(f32[72,128]{1,0:T(8,128)} %constant.137.clone.sin_ref) | copy-start | bytes 110596
  167.0 23.8 %copy-start.5 = (bf16[64,144]{1,0:T(8,128)(2,1)S(1)}, bf16[64,144]{1,0:T(8,128)(2,1)}, u32[]{:S(2)}) copy-start(bf16[64,144]{1,0:T(8,128)(2,1)} %constant.135.clone.last_ref) | copy-start | bytes 55300
  177.5 28.4 %copy-start.7 = (f32[512]{0:T(512)S(1)}, f32[512]{0:T(512)}, u32[]{:S(2)}) copy-start(f32[512]{0:T(512)} %param.22) | copy-start | bytes 6148
  207.2 89.6 %all-gather.9.cloned.1.call-start = ((), (), s32[]{:S(2)}) async-start(), calls=%async_computation.7 | async-start | bytes 2621440 | tf_op jit(solution)/shard_map/all_gather | solution.py:393
Sparse Core Ops, SparseCore 0:
  8.9 158.0 all-gather.6
  207.3 43.1 all-gather.10
  252.1 44.6 all-gather.8

commit v18 on v17

--- a/solution.py
+++ b/solution.py
@@ -335,7 +335,7 @@
     count, tok_rows, size = gathered.shape
     depth = count * size
     features = weight.shape[2]
-    tile = min(4 * LANES, features)
+    tile = min(8 * LANES, features)
     block = pl.BlockSpec((tok_rows, tile), lambda i: (0, i))
     given = [] if total is None else [total]
     return pl.pallas_call(

time: 310 us -> 311 us (level)
  no operation moved by 1% of the time
where the time goes in v18:
time: 311 us; the launch traced here: 310 us
  waiting for transfers between devices  136 us (44%)
  Pallas kernels  54.4 us (17%)
  blocking collectives  49.7 us (16%)
  starting transfers between devices  30.1 us (10%)
  local copies, waits for them, and re-layouts  16.8 us (5%)
  between operations  13.4 us (4%)
  matrix products  6.3 us (2%)
  other arithmetic  3.57 us (1%)
    all_gather x2, waiting for transfers between devices, shards(): gated = lax.all_gather(gate(longconv, skip, lo, signal_t, query_t), 'chan')  44.3 us
    all_to_all x1, waiting for transfers between devices, folded_response(): got = lax.all_to_all(sent, 'seq', split_axis=0, concat_axis=0, tiled=True)  28.8 us
    ppermute x5, waiting for transfers between devices, gather_by_doubling(): other = lax.ppermute(held, axis, [(i, i ^ bit) for i in range(size)])  28.5 us
    all_to_all x2, blocking collectives, shards(): lax.all_to_all(values, 'seq', split_axis=0, concat_axis=0, tiled=True)  25.4 us
    all_to_all x2, blocking collectives, shards(): lax.all_to_all(long_conv(values, response, lo // seq_count), 'seq', split...  24.3 us
    all_to_all x1, waiting for transfers between devices, feature_rows(): own = lax.all_to_all(own, 'chan', split_axis=1, concat_axis=0, tiled=True)  22.6 us
    pallas_call x2, Pallas kernels, project(): pl.pallas_call(lambda *refs: project_kernel(len(after), *refs), grid=(cou...  21 us
    ppermute x5, starting transfers between devices, gather_by_doubling(): other = lax.ppermute(held, axis, [(i, i ^ bit) for i in range(size)])  17.4 us
  transfers between devices with their start and end apart: 11, of which 8 were waited for; matrix products, arithmetic and copies ran while one was open for 9% of the time, Pallas kernels for 11%

profile of v18, /device:TPU:0, one launch (start us, length us, event | category | flops | bytes accessed | tf_op | source)
XLA Modules:
  0.0 309.8 jit_solution(12346849109595642215)
XLA Ops:
  6.5 0.0 all-gather.7.cloned.1.call-start
  6.5 0.7 all-gather.7.cloned.1.call-update
  7.3 1.1 constant_dynamic-slice_fusion
  8.3 0.8 copy.35
  9.2 6.3 %all-to-all-start = ((bf16[64,4,1024]{2,0,1:T(8,128)(2,1)}), bf16[64,4,1024]{2,0,1:T(8,128)(2,1)S(1)}, u32[]{:S(2)}, u32[]{:S(2)}) async-start(bf16[64,4,1024]{2,0,1:T(8,128)(2,1)} %bitcast.76), calls=%async_computation | async-start | bytes 1048576 | tf_op jit(solution)/shard_map/all_to_all | solution.py:321
  15.5 0.8 slice.3
  16.3 22.6 %all-to-all-done = bf16[64,4,1024]{2,0,1:T(8,128)(2,1)S(1)} async-done(((bf16[64,4,1024]{2,0,1:T(8,128)(2,1)}), bf16[64,4,1024]{2,0,1:T(8,128)(2,1)S(1)}, u32[]{:S(2)}, u32[]{:S(2)}) %all-to-all-start) | async-done | bytes 524320 | tf_op jit(solution)/shard_map/all_to_all | solution.py:321
  38.9 1.3 collective-permute-start
  40.2 0.8 collective-permute-done
  41.0 0.0 collective-permute-start.1
  41.0 0.7 fusion.1.order_ref
  41.7 10.9 %reshape.40.spec_ref = f32[2,1024,1024]{2,1,0:T(8,128)} reshape(f32[2,512,2,1024]{3,2,1,0:T(2,128)} %param.21) | data formatting | bytes 16777216 | tf_op jit(solution)/shard_map/reshape | solution.py:293
  52.6 0.0 collective-permute-done.1
  52.7 9.1 %collective-permute-start.2 = (bf16[2,16,1024]{2,1,0:T(8,128)(2,1)S(1)}, bf16[2,16,1024]{2,1,0:T(8,128)(2,1)S(1)}, u32[]{:S(2)}, u32[]{:S(2)}) collective-permute-start(bf16[2,16,1024]{2,1,0:T(8,128)(2,1)S(1)} %maximum_bitcast_fusion.1), channel_id=1, source_target_pairs={{0,1},{1,0},{2,3},{3,2},{4,5},{5,4},{6,7},{7,6},{8,9},{9,8},{10,11... | collective-permute-start | bytes 196616 | tf_op jit(solution)/shard_map/ppermute | solution.py:29
  61.8 8.6 %shard_map.172 = bf16[8,2,2,64,1024]{4,3,2,1,0:T(8,128)(2,1)} custom-call(f32[2,1024,1024]{2,1,0:T(8,128)} %reshape.40.spec_ref, bf16[1024,1024]{1,0:T(8,128)(2,1)S(1)} %fusion.1.order_ref), custom_call_target="tpu_custom_call" | custom-call | flops 4294967296 | bytes 12582912 | tf_op jit(solution)/shard_map/pallas_call | solution.py:280
  70.4 0.0 collective-permute-done.2
  70.4 6.6 %collective-permute-start.3 = (bf16[1,4,64,1024]{3,2,1,0:T(8,128)(2,1)S(1)}, bf16[1,4,64,1024]{3,2,1,0:T(8,128)(2,1)S(1)}, u32[]{:S(2)}, u32[]{:S(2)}) collective-permute-start(bf16[1,4,64,1024]{3,2,1,0:T(8,128)(2,1)S(1)} %bitcast.93), channel_id=1, source_target_pairs={{0,16},{4,20},{8,24},{12,28},{16,0},{20,4},{24,8},{28,12},{1,17},{... | collective-permute-start | bytes 1572872 | tf_op jit(solution)/shard_map/ppermute | solution.py:29
  77.1 8.7 %collective-permute-done.3 = bf16[1,4,64,1024]{3,2,1,0:T(8,128)(2,1)S(1)} collective-permute-done((bf16[1,4,64,1024]{3,2,1,0:T(8,128)(2,1)S(1)}, bf16[1,4,64,1024]{3,2,1,0:T(8,128)(2,1)S(1)}, u32[]{:S(2)}, u32[]{:S(2)}) %collective-permute-start.3) | collective-permute-done | bytes 524320 | tf_op jit(solution)/shard_map/ppermute | solution.py:29
  85.8 0.1 select_bitcast_fusion.5
  85.9 0.1 maximum_bitcast_fusion
  86.0 1.6 collective-permute-start.4
  87.6 4.6 %all-to-all-start.1 = ((bf16[8,2,2,64,1024]{4,3,2,1,0:T(8,128)(2,1)}), bf16[8,2,2,64,1024]{4,3,2,1,0:T(8,128)(2,1)}, u32[]{:S(2)}, u32[]{:S(2)}) async-start(bf16[8,2,2,64,1024]{4,3,2,1,0:T(8,128)(2,1)} %shard_map.172), calls=%async_computation.1 | async-start | bytes 8388608 | tf_op jit(solution)/shard_map/all_to_all | solution.py:300
  92.2 0.2 all-gather.11.cloned.1.call-start
  92.4 19.7 %collective-permute-done.4 = bf16[2,4,64,1024]{3,2,1,0:T(8,128)(2,1)S(1)} collective-permute-done((bf16[2,4,64,1024]{3,2,1,0:T(8,128)(2,1)S(1)}, bf16[2,4,64,1024]{3,2,1,0:T(8,128)(2,1)S(1)}, u32[]{:S(2)}, u32[]{:S(2)}) %collective-permute-start.4) | collective-permute-done | bytes 1048608 | tf_op jit(solution)/shard_map/ppermute | solution.py:29
  112.2 0.1 select_bitcast_fusion.3
  112.3 0.2 pad_maximum_fusion.1
  112.5 0.1 collective-permute-start.5
  112.6 6.3 %fusion.3.refs_5_ = bf16[3,16,512]{2,1,0:T(8,128)(2,1)S(1)} fusion(bf16[3,4,1024,512]{3,2,1,0:T(8,128)(2,1)} %bitcast.83, bf16[4,16,1024]{2,1,0:T(8,128)(2,1)S(1)} %bitcast.97), kind=kOutput, calls=%fused_computation.9 | convolution fusion | flops 201351168 | bytes 12763136 | tf_op jit(solution)/shard_map/ztd,pzdc->ptc/dot_general | solution.py:378
  118.9 0.0 collective-permute-done.5
  118.9 1.9 select_bitcast_fusion.1
  120.8 0.4 pad_maximum_fusion
  121.2 0.7 copy.30
  121.9 2.4 copy.31
  124.4 28.8 %all-to-all-done.1.got_ref = bf16[8,2,2,64,1024]{4,3,2,1,0:T(8,128)(2,1)} async-done(((bf16[8,2,2,64,1024]{4,3,2,1,0:T(8,128)(2,1)}), bf16[8,2,2,64,1024]{4,3,2,1,0:T(8,128)(2,1)}, u32[]{:S(2)}, u32[]{:S(2)}) %all-to-all-start.1) | async-done | bytes 4194336 | tf_op jit(solution)/shard_map/all_to_all | solution.py:300
  153.2 4.0 %shard_map.173.refs_6_.resp_ref = bf16[2,64,72,128]{3,2,1,0:T(8,128)(2,1)S(1)} custom-call(bf16[8,2,2,64,1024]{4,3,2,1,0:T(8,128)(2,1)} %all-to-all-done.1.got_ref), custom_call_target="tpu_custom_call" | custom-call | flops 2097152 | bytes 6291456 | tf_op jit(solution)/shard_map/pallas_call | solution.py:303
  157.2 9.8 %all-gather.7.cloned.1.call-done = bf16[4096,1024]{1,0:T(8,128)(2,1)} async-done(((bf16[1024,1024]{1,0:T(8,128)(2,1)}), bf16[4096,1024]{1,0:T(8,128)(2,1)}) %all-gather.7.cloned.1.call-update) | async-done | bytes 8388624 | tf_op jit(solution)/shard_map/all_gather | solution.py:367
  167.0 0.0 copy-done.6
  167.0 0.0 copy-start.3
  167.0 0.0 copy-start.4
  167.0 0.0 copy-start.5
  167.0 10.5 %shard_map.177 = (bf16[1024,256]{1,0:T(8,128)(2,1)S(1)}, bf16[256,1024]{1,0:T(8,128)(2,1)S(1)}, bf16[1024,256]{1,0:T(8,128)(2,1)S(1)}) custom-call(bf16[4,1024,1024]{2,1,0:T(8,128)(2,1)} %bitcast.88, bf16[3,4096,512]{2,1,0:T(8,128)(2,1)} %refs_3_.3, bf16[3,4096,512]{2,1,0:T(8,128)(2,1)} %refs_3_.3, bf16[3,4096,512]{2,1,0:T(8,128)(2,1)} %refs_3_.3, ...), custom_call_target="tpu_custom_call" | custom-call | flops 6442450944 | bytes 14680064 | tf_op jit(solution)/shard_map/pallas_call | solution.py:92
  177.5 0.0 copy-start.7
  177.5 13.3 %all_to_all.41.signal_ref = bf16[8,32,1024]{2,1,0:T(8,128)(2,1)S(1)} all-to-all(bf16[8,32,1024]{2,1,0:T(8,128)(2,1)S(1)} %bitcast.80), channel_id=1, replica_groups=mesh['seq'=8,'chan'=4] {'seq'}, dimensions={0} | all-to-all | bytes 1048576 | tf_op jit(solution)/shard_map/all_to_all | solution.py:389
  190.8 0.0 copy-done
  190.8 0.0 copy-done.1
  190.8 0.0 copy-done.2
  190.8 0.0 copy-done.3
  190.8 0.0 copy-done.4
  190.8 0.0 copy-done.5
  190.8 3.0 shard_map.178
  193.8 12.2 %all_to_all.42 = bf16[8,32,1024]{2,1,0:T(8,128)(2,1)S(1)} all-to-all(bf16[8,32,1024]{2,1,0:T(8,128)(2,1)S(1)} %shard_map.178), channel_id=1, replica_groups=mesh['seq'=8,'chan'=4] {'seq'}, dimensions={0} | all-to-all | bytes 1048576 | tf_op jit(solution)/shard_map/all_to_all | solution.py:390
  206.0 1.2 shard_map.179
  207.2 0.0 all-gather.11.cloned.1.call-update
  207.2 0.3 all-gather.9.cloned.1.call-start
  207.5 10.5 %shard_map.174 = (bf16[1024,256]{1,0:T(8,128)(2,1)S(1)}, bf16[256,1024]{1,0:T(8,128)(2,1)S(1)}, bf16[1024,256]{1,0:T(8,128)(2,1)S(1)}) custom-call(bf16[4,1024,1024]{2,1,0:T(8,128)(2,1)} %bitcast.89, bf16[3,4096,512]{2,1,0:T(8,128)(2,1)} %refs_3_.3, bf16[3,4096,512]{2,1,0:T(8,128)(2,1)} %refs_3_.3, bf16[3,4096,512]{2,1,0:T(8,128)(2,1)} %refs_3_.3, ...), custom_call_target="tpu_custom_call" | custom-call | flops 6442450944 | bytes 14680064 | tf_op jit(solution)/shard_map/pallas_call | solution.py:92
  218.0 12.2 %all_to_all.43.signal_ref = bf16[8,32,1024]{2,1,0:T(8,128)(2,1)S(1)} all-to-all(bf16[8,32,1024]{2,1,0:T(8,128)(2,1)S(1)} %bitcast.79), channel_id=1, replica_groups=mesh['seq'=8,'chan'=4] {'seq'}, dimensions={0} | all-to-all | bytes 1048576 | tf_op jit(solution)/shard_map/all_to_all | solution.py:389
  230.2 3.0 shard_map.175
  233.2 12.2 %all_to_all.44 = bf16[8,32,1024]{2,1,0:T(8,128)(2,1)S(1)} all-to-all(bf16[8,32,1024]{2,1,0:T(8,128)(2,1)S(1)} %shard_map.175), channel_id=1, replica_groups=mesh['seq'=8,'chan'=4] {'seq'}, dimensions={0} | all-to-all | bytes 1048576 | tf_op jit(solution)/shard_map/all_to_all | solution.py:390
  245.3 1.2 shard_map.176
  246.5 0.0 all-gather.9.cloned.1.call-update
  246.6 4.0 %all-gather.11.cloned.1.call-done = bf16[4096,256]{1,0:T(8,128)(2,1)} async-done(((bf16[1024,256]{1,0:T(8,128)(2,1)}), bf16[4096,256]{1,0:T(8,128)(2,1)}) %all-gather.11.cloned.1.call-update) | async-done | bytes 2097168 | tf_op jit(solution)/shard_map/all_gather | solution.py:393
  250.5 5.9 %shard_map.180.refs_0_ = bf16[1024,1024]{1,0:T(8,128)(2,1)} custom-call(bf16[4,1024,256]{2,1,0:T(8,128)(2,1)} %bitcast.96, bf16[2,1024,1024]{2,1,0:T(8,128)(2,1)} %bitcast.86), custom_call_target="tpu_custom_call" | custom-call | flops 2147483648 | bytes 10485760 | tf_op jit(solution)/shard_map/pallas_call | solution.py:341
  256.4 40.4 %all-gather.9.cloned.1.call-done = bf16[4096,256]{1,0:T(8,128)(2,1)} async-done(((bf16[1024,256]{1,0:T(8,128)(2,1)}), bf16[4096,256]{1,0:T(8,128)(2,1)}) %all-gather.9.cloned.1.call-update) | async-done | bytes 2097168 | tf_op jit(solution)/shard_map/all_gather | solution.py:393
  296.8 6.5 %shard_map.181 = bf16[1024,1024]{1,0:T(8,128)(2,1)} custom-call(bf16[4,1024,256]{2,1,0:T(8,128)(2,1)} %bitcast.92, bf16[2,1024,1024]{2,1,0:T(8,128)(2,1)} %bitcast.87, bf16[1024,1024]{1,0:T(8,128)(2,1)} %shard_map.180.refs_0_), custom_call_target="tpu_custom_call" | custom-call | flops 2147483648 | bytes 10485760 | tf_op jit(solution)/shard_map/pallas_call | solution.py:341
  (12 shorter events, 0.1 us)
Async XLA Ops:
  6.5 160.5 %all-gather.7.cloned.1.call-start = ((), (), s32[]{:S(2)}) async-start(), calls=%async_computation.6 | async-start | bytes 10485760 | tf_op jit(solution)/shard_map/all_gather | solution.py:367
  9.2 29.7 %all-to-all-start = ((bf16[64,4,1024]{2,0,1:T(8,128)(2,1)}), bf16[64,4,1024]{2,0,1:T(8,128)(2,1)S(1)}, u32[]{:S(2)}, u32[]{:S(2)}) async-start(bf16[64,4,1024]{2,0,1:T(8,128)(2,1)} %bitcast.76), calls=%async_computation | async-start | bytes 1048576 | tf_op jit(solution)/shard_map/all_to_all | solution.py:321
  38.9 2.1 collective-permute-start
  41.0 11.7 %collective-permute-start.1 = (bf16[1,16,1024]{2,1,0:T(8,128)(2,1)S(1)}, bf16[1,16,1024]{2,1,0:T(8,128)(2,1)S(1)}, u32[]{:S(2)}, u32[]{:S(2)}) collective-permute-start(bf16[1,16,1024]{2,1,0:T(8,128)(2,1)S(1)} %bitcast.98), channel_id=1, source_target_pairs={{0,2},{1,3},{2,0},{3,1},{4,6},{5,7},{6,4},{7,5},{8,10},{9,11},{10,... | collective-permute-start | bytes 98312 | tf_op jit(solution)/shard_map/ppermute | solution.py:29
  52.7 17.7 %collective-permute-start.2 = (bf16[2,16,1024]{2,1,0:T(8,128)(2,1)S(1)}, bf16[2,16,1024]{2,1,0:T(8,128)(2,1)S(1)}, u32[]{:S(2)}, u32[]{:S(2)}) collective-permute-start(bf16[2,16,1024]{2,1,0:T(8,128)(2,1)S(1)} %maximum_bitcast_fusion.1), channel_id=1, source_target_pairs={{0,1},{1,0},{2,3},{3,2},{4,5},{5,4},{6,7},{7,6},{8,9},{9,8},{10,11... | collective-permute-start | bytes 196616 | tf_op jit(solution)/shard_map/ppermute | solution.py:29
  70.4 15.4 %collective-permute-start.3 = (bf16[1,4,64,1024]{3,2,1,0:T(8,128)(2,1)S(1)}, bf16[1,4,64,1024]{3,2,1,0:T(8,128)(2,1)S(1)}, u32[]{:S(2)}, u32[]{:S(2)}) collective-permute-start(bf16[1,4,64,1024]{3,2,1,0:T(8,128)(2,1)S(1)} %bitcast.93), channel_id=1, source_target_pairs={{0,16},{4,20},{8,24},{12,28},{16,0},{20,4},{24,8},{28,12},{1,17},{... | collective-permute-start | bytes 1572872 | tf_op jit(solution)/shard_map/ppermute | solution.py:29
  86.0 26.2 %collective-permute-start.4 = (bf16[2,4,64,1024]{3,2,1,0:T(8,128)(2,1)S(1)}, bf16[2,4,64,1024]{3,2,1,0:T(8,128)(2,1)S(1)}, u32[]{:S(2)}, u32[]{:S(2)}) collective-permute-start(bf16[2,4,64,1024]{3,2,1,0:T(8,128)(2,1)S(1)} %maximum_bitcast_fusion), channel_id=1, source_target_pairs={{0,8},{4,12},{8,0},{12,4},{16,24},{20,28},{24,16},{28,20},{1,9},{5... | collective-permute-start | bytes 3145736 | tf_op jit(solution)/shard_map/ppermute | solution.py:29
  87.6 65.6 %all-to-all-start.1 = ((bf16[8,2,2,64,1024]{4,3,2,1,0:T(8,128)(2,1)}), bf16[8,2,2,64,1024]{4,3,2,1,0:T(8,128)(2,1)}, u32[]{:S(2)}, u32[]{:S(2)}) async-start(bf16[8,2,2,64,1024]{4,3,2,1,0:T(8,128)(2,1)} %shard_map.172), calls=%async_computation.1 | async-start | bytes 8388608 | tf_op jit(solution)/shard_map/all_to_all | solution.py:300
  92.2 158.4 %all-gather.11.cloned.1.call-start = ((), (), s32[]{:S(2)}) async-start(), calls=%async_computation.8 | async-start | bytes 2621440 | tf_op jit(solution)/shard_map/all_gather | solution.py:393
  112.5 6.4 %collective-permute-start.5 = (bf16[4,4,64,1024]{3,2,1,0:T(8,128)(2,1)S(1)}, bf16[4,4,64,1024]{3,2,1,0:T(8,128)(2,1)}, u32[]{:S(2)}, u32[]{:S(2)}) collective-permute-start(bf16[4,4,64,1024]{3,2,1,0:T(8,128)(2,1)S(1)} %bitcast.91), channel_id=1, source_target_pairs={{0,4},{4,0},{8,12},{12,8},{16,20},{20,16},{24,28},{28,24},{1,5},{5... | collective-permute-start | bytes 6291464 | tf_op jit(solution)/shard_map/ppermute | solution.py:29
  124.4 42.6 %copy-start.6 = (f32[3,3,512]{2,1,0:T(4,128)S(1)}, f32[3,3,512]{2,1,0:T(4,128)}, u32[]{:S(2)}) copy-start(f32[3,3,512]{2,1,0:T(4,128)} %refs_4_.3) | copy-start | bytes 55300
  167.0 23.8 %copy-start = (bf16[256,256]{1,0:T(8,128)(2,1)S(1)}, bf16[256,256]{1,0:T(8,128)(2,1)}, u32[]{:S(2)}) copy-start(bf16[256,256]{1,0:T(8,128)(2,1)} %constant.138.clone.fwd_ref) | copy-start | bytes 393220
  167.0 23.8 %copy-start.1 = (bf16[256,256]{1,0:T(8,128)(2,1)S(1)}, bf16[256,256]{1,0:T(8,128)(2,1)}, u32[]{:S(2)}) copy-start(bf16[256,256]{1,0:T(8,128)(2,1)} %constant.139.clone.bwd_ref) | copy-start | bytes 393220
  167.0 23.8 %copy-start.2 = (bf16[144,64]{1,0:T(8,128)(2,1)S(1)}, bf16[144,64]{1,0:T(8,128)(2,1)}, u32[]{:S(2)}) copy-start(bf16[144,64]{1,0:T(8,128)(2,1)} %constant.134.clone.first_ref) | copy-start | bytes 55300
  167.0 23.8 %copy-start.3 = (f32[72,128]{1,0:T(8,128)S(1)}, f32[72,128]{1,0:T(8,128)}, u32[]{:S(2)}) copy-start(f32[72,128]{1,0:T(8,128)} %constant.136.clone.cos_ref) | copy-start | bytes 110596
  167.0 23.8 %copy-start.4 = (f32[72,128]{1,0:T(8,128)S(1)}, f32[72,128]{1,0:T(8,128)}, u32[]{:S(2)}) copy-start(f32[72,128]{1,0:T(8,128)} %constant.137.clone.sin_ref) | copy-start | bytes 110596
  167.0 23.8 %copy-start.5 = (bf16[64,144]{1,0:T(8,128)(2,1)S(1)}, bf16[64,144]{1,0:T(8,128)(2,1)}, u32[]{:S(2)}) copy-start(bf16[64,144]{1,0:T(8,128)(2,1)} %constant.135.clone.last_ref) | copy-start | bytes 55300
  177.5 28.4 %copy-start.7 = (f32[512]{0:T(512)S(1)}, f32[512]{0:T(512)}, u32[]{:S(2)}) copy-start(f32[512]{0:T(512)} %param.22) | copy-start | bytes 6148
  207.2 89.5 %all-gather.9.cloned.1.call-start = ((), (), s32[]{:S(2)}) async-start(), calls=%async_computation.7 | async-start | bytes 2621440 | tf_op jit(solution)/shard_map/all_gather | solution.py:393
Sparse Core Ops, SparseCore 0:
  8.9 158.0 all-gather.6
  207.3 43.1 all-gather.10
  252.1 44.6 all-gather.8
